TPU v7x, 32 devices: a whole 2x2x4 slice. The times are simulated.
32 devices in a mesh: clip: 4 (over x, core), tm: 8 (over z, y).
Axes of the slice: x: 2, y: 2, z: 4, core: 2. Of those that a mesh axis runs over, the one named last changes fastest.
Arguments:
- clips: bfloat16 [16, 8, 128, 1024], P('clip', 'tm'), may hold values from -6 to 6
- w_qkv: bfloat16 [1024, 3072], replicated, may hold values from -8 to 8
- w_out: bfloat16 [1024, 1024], replicated, may hold values from -0.1875 to 0.1875
- cotangent: bfloat16 [16, 8, 128, 1024], P('clip', 'tm'), may hold values from -6 to 6
Outputs:
- grad_clips: bfloat16 [16, 8, 128, 1024], P('clip', 'tm')
- grad_qkv: float32 [1024, 3072], P(('clip', 'tm'))
- grad_out: float32 [1024, 1024], P(('clip', 'tm'))
All inputs are finite; a program needn't handle non-finite values.
Results may differ from a plain program's by a relative error of at most 0.0093.
Values may be sent and summed in bfloat16 or wider, within the bound.
No kernel may reach another device: no remote copies, remote signals or barrier semaphores. Data moves between devices by JAX's collectives and lax.ppermute only.
A program may use at most 128 MiB of HBM per device.

v0:
```python
import jax
import jax.numpy as jnp
from jax import lax
from jax.sharding import PartitionSpec as P

D = 1024
HEADS = 16


epsilon = 1e-06


def normalize(clips):
    values32 = clips.astype(jnp.float32)
    centred = values32 - jnp.mean(values32, axis=-1, keepdims=True)
    inverse = lax.rsqrt(jnp.mean(centred * centred, axis=-1, keepdims=True) + epsilon)
    return (centred * inverse, inverse)


def split_heads(array):
    return array.reshape(array.shape[:-1] + (HEADS, array.shape[-1] // HEADS))


def unpack(packed):
    width = packed.shape[-1] // 3
    queries = split_heads(packed[..., :width])
    key_rows = split_heads(packed[..., width : 2 * width])
    value_rows = split_heads(packed[..., 2 * width :])
    return (queries, key_rows, value_rows, width)


def attend(packed):
    queries, key_rows, value_rows, width = unpack(packed)
    scaling = (width // HEADS) ** (-0.5)
    scores = (
        jnp.einsum("cfphd,cgphd->cphfg", queries, key_rows, preferred_element_type=jnp.float32)
        * scaling
    )
    highest = jnp.max(scores, axis=-1, keepdims=True)
    expo = jnp.exp(scores - highest)
    full_weights = expo / jnp.sum(expo, axis=-1, keepdims=True)
    low_weights = full_weights.astype(jnp.bfloat16)
    mixed = jnp.einsum(
        "cphfg,cgphd->cfphd", low_weights, value_rows, preferred_element_type=jnp.float32
    )
    mixed = mixed.astype(jnp.bfloat16).reshape(packed.shape[:3] + (width,))
    return (mixed, full_weights, low_weights)


def attend_back(packed, full_weights, low_weights, mixed_grad):
    queries, key_rows, value_rows, width = unpack(packed)
    scaling = (width // HEADS) ** (-0.5)
    grad_heads = split_heads(mixed_grad)
    dots = jnp.einsum(
        "cfphd,cgphd->cphfg", grad_heads, value_rows, preferred_element_type=jnp.float32
    )
    score_grad = full_weights * (dots - jnp.sum(full_weights * dots, axis=-1, keepdims=True))
    score_grad = (score_grad * scaling).astype(jnp.bfloat16)
    query_grad = jnp.einsum(
        "cphfg,cgphd->cfphd", score_grad, key_rows, preferred_element_type=jnp.float32
    )
    key_grad = jnp.einsum(
        "cphfg,cfphd->cgphd", score_grad, queries, preferred_element_type=jnp.float32
    )
    value_grad = jnp.einsum(
        "cphfg,cfphd->cgphd", low_weights, grad_heads, preferred_element_type=jnp.float32
    )
    lead = packed.shape[:3] + (width,)
    return jnp.concatenate(
        [
            query_grad.astype(jnp.bfloat16).reshape(lead),
            key_grad.astype(jnp.bfloat16).reshape(lead),
            value_grad.astype(jnp.bfloat16).reshape(lead),
        ],
        axis=-1,
    )


def row_product(left, right):
    return lax.dot_general(
        left, right, (((0,), (0,)), ((), ())), preferred_element_type=jnp.float32
    )


def shards(clips, w_qkv, w_out, cotangent):
    unit_rows, inverse = normalize(clips)
    normed = unit_rows.astype(jnp.bfloat16)
    flat_normed = normed.reshape(-1, D)
    packed = jnp.dot(flat_normed, w_qkv, preferred_element_type=jnp.float32).astype(jnp.bfloat16)
    packed = packed.reshape(clips.shape[:3] + (3 * D,))
    gathered = lax.all_to_all(packed, "tm", split_axis=2, concat_axis=1, tiled=True)
    mixed, full_weights, low_weights = attend(gathered)
    mixed_pos, full_weights, low_weights, packed_pos = (mixed, full_weights, low_weights, gathered)
    mixed_frames = lax.all_to_all(mixed_pos, "tm", split_axis=1, concat_axis=2, tiled=True)
    mixed_rows = mixed_frames.reshape(-1, D)
    cot_rows = cotangent.reshape(-1, D)
    grad_frames = jnp.dot(cot_rows, w_out.T, preferred_element_type=jnp.float32).astype(
        jnp.bfloat16
    )
    grad_frames = grad_frames.reshape(clips.shape)
    mixed_grad = lax.all_to_all(grad_frames, "tm", split_axis=2, concat_axis=1, tiled=True)
    grad_out = lax.psum_scatter(
        row_product(mixed_rows, cot_rows), ("clip", "tm"), scatter_dimension=0, tiled=True
    )
    packed_grad_pos = attend_back(packed_pos, full_weights, low_weights, mixed_grad)
    packed_grad = lax.all_to_all(packed_grad_pos, "tm", split_axis=1, concat_axis=2, tiled=True)
    flat_grad = packed_grad.reshape(-1, 3 * D)
    grad_qkv = lax.psum_scatter(
        row_product(flat_normed, flat_grad), ("clip", "tm"), scatter_dimension=0, tiled=True
    )
    normed_grad = lax.dot_general(
        flat_grad, w_qkv, (((1,), (1,)), ((), ())), preferred_element_type=jnp.float32
    )
    normed_grad = normed_grad.reshape(clips.shape)
    input_grad = inverse * (
        normed_grad
        - jnp.mean(normed_grad, axis=-1, keepdims=True)
        - unit_rows * jnp.mean(normed_grad * unit_rows, axis=-1, keepdims=True)
    )
    grad_clips = (cotangent.astype(jnp.float32) + input_grad).astype(jnp.bfloat16)
    return (grad_clips, grad_qkv, grad_out)


def solution(mesh):
    return jax.shard_map(
        shards,
        mesh=mesh,
        in_specs=(P("clip", "tm", None, None), P(), P(), P("clip", "tm", None, None)),
        out_specs=(P("clip", "tm", None, None), P(("clip", "tm"), None), P(("clip", "tm"), None)),
        check_vma=False,
    )
```

profile of v0, /device:TPU:0, one launch (start us, length us, event | category | flops | bytes accessed | tf_op | source)
XLA Modules:
  0.0 526.1 jit_solution(13870645170249759700)
XLA Ops:
  10.8 6.8 %convolution_convert_fusion = bf16[512,3072]{1,0:T(8,128)(2,1)S(1)} fusion(bf16[512,1024]{1,0:T(8,128)(2,1)S(1)} %bitcast.59, bf16[1024,3072]{1,0:T(8,128)(2,1)} %param.5), kind=kOutput, calls=%fused_computation.2 | convolution fusion | flops 3222798336 | bytes 10485760 | tf_op jit(solution)/shard_map/dot_general | solution.py:89
  17.6 4.1 copy.51
  21.7 7.3 %all-to-all-start = ((bf16[4,1,128,3072]{3,0,1,2:T(4,128)(2,1)}), bf16[4,1,128,3072]{3,0,1,2:T(4,128)(2,1)}, u32[]{:S(2)}, u32[]{:S(2)}) async-start(bf16[4,1,128,3072]{3,0,1,2:T(4,128)(2,1)} %copy.51), calls=%async_computation | async-start | bytes 6291456 | tf_op jit(solution)/shard_map/all_to_all | solution.py:91
  33.3 66.5 %all-to-all-done = bf16[4,1,128,3072]{3,0,1,2:T(4,128)(2,1)} async-done(((bf16[4,1,128,3072]{3,0,1,2:T(4,128)(2,1)}), bf16[4,1,128,3072]{3,0,1,2:T(4,128)(2,1)}, u32[]{:S(2)}, u32[]{:S(2)}) %all-to-all-start) | async-done | bytes 3145760 | tf_op jit(solution)/shard_map/all_to_all | solution.py:91
  99.8 4.8 all-to-all-start.1
  104.6 4.5 fusion.33
  116.7 4.1 fusion.24
  120.8 32.5 %fusion.34 = (f32[4,16,16,8]{3,2,1,0:T(8,128)S(1)}, f32[4,16,16,8,8]{3,4,2,1,0:T(8,128)S(1)}) fusion(f32[4,16,16,8,8]{3,4,2,1,0:T(8,128)S(1)} %fusion.24), kind=kOutput, calls=%fused_computation.48 | output fusion | flops 262151 | bytes 557056 | tf_op jit(solution)/shard_map/sub | solution.py:40
  157.3 4.1 reshape.147
  161.4 6.0 %all-to-all-start.3 = ((bf16[4,8,16,1024]{3,2,0,1:T(8,128)(2,1)}), bf16[4,8,16,1024]{3,2,0,1:T(8,128)(2,1)}, u32[]{:S(2)}, u32[]{:S(2)}) async-start(bf16[4,8,16,1024]{3,2,0,1:T(8,128)(2,1)} %reshape.147), calls=%async_computation.4 | async-start | bytes 2097152 | tf_op jit(solution)/shard_map/all_to_all | solution.py:94
  167.6 4.2 reshape.148
  171.7 4.7 convert_bitcast_fusion.1
  178.3 4.1 reshape.142
  182.3 6.7 %fusion.21 = f32[4,16,16,8,8]{3,4,2,1,0:T(8,128)} fusion(bf16[4,8,16,16,64]{4,3,0,2,1:T(8,128)(2,1)} %reshape.151, bf16[4,8,16,16,64]{4,3,0,2,1:T(8,128)(2,1)} %reshape.148), kind=kOutput, calls=%fused_computation.30 | convolution fusion | flops 8388608 | bytes 2359296 | tf_op jit(solution)/shard_map/cfphd,cgphd->cphfg/dot_general | solution.py:54
  189.0 3.5 all-to-all-done.3
  194.1 3.2 fusion.37
  197.6 8.5 %multiply_convert_fusion = bf16[4,16,16,8,8]{3,4,2,1,0:T(8,128)(2,1)S(1)} fusion(f32[4,16,16,8,8]{3,4,2,1,0:T(8,128)} %fusion.21, f32[4,16,16,8,8]{3,4,2,1,0:T(8,128)} %copy-done.11, f32[4,16,16,8]{3,2,1,0:T(8,128)} %copy-done.12), kind=kOutput, calls=%fused_computation.3 | output fusion | flops 466951 | bytes 688128 | tf_op jit(solution)/shard_map/sub | solution.py:57
  209.7 4.2 reshape.140
  213.9 3.2 convert_bitcast_fusion.2
  222.2 96.7 %all_to_all.19 = bf16[4,8,16,3072]{3,2,0,1:T(8,128)(2,1)S(1)} all-to-all(bf16[4,8,16,3072]{3,2,0,1:T(8,128)(2,1)S(1)} %copy.68), channel_id=1, replica_groups=mesh['clip'=4,'tm'=8] {'tm'}, dimensions={1} | all-to-all | bytes 6291456 | tf_op jit(solution)/shard_map/all_to_all | solution.py:106
  320.9 6.4 %fusion.36 = f32[1024,3072]{1,0:T(8,128)} fusion(bf16[512,1024]{1,0:T(8,128)(2,1)S(1)} %bitcast.60, bf16[512,3072]{1,0:T(8,128)(2,1)S(1)} %bitcast.56), kind=kOutput, calls=%fused_computation.50 | convolution fusion | flops 3221225472 | bytes 16777216 | tf_op jit(solution)/shard_map/dot_general | solution.py:80
  327.4 6.7 %fusion.35 = (f32[512]{0:T(512)S(1)}, f32[512,1024]{1,0:T(8,128)S(1)}) fusion(bf16[512,3072]{1,0:T(8,128)(2,1)} %bitcast.57, bf16[1024,3072]{1,0:T(8,128)(2,1)} %param.5), kind=kOutput, calls=%fused_computation.49 | convolution fusion | flops 3221749248 | bytes 11536384 | tf_op jit(solution)/shard_map/dot_general | solution.py:111
  337.1 21.3 %reduce-scatter.5.cloned.1.call-done = f32[32,1024]{1,0:T(8,128)} async-done(((f32[1024,1024]{1,0:T(8,128)}), f32[32,1024]{1,0:T(8,128)}) %reduce-scatter.5.cloned.1.call-update) | async-done | bytes 131088 | tf_op jit(solution)/shard_map/reduce_scatter | solution.py:102
  358.4 160.5 %reduce-scatter.3.cloned.1.call-done = f32[32,3072]{1,0:T(8,128)} async-done(((f32[1024,3072]{1,0:T(8,128)}), f32[32,3072]{1,0:T(8,128)}) %reduce-scatter.3.cloned.1.call-update) | async-done | bytes 393232 | tf_op jit(solution)/shard_map/reduce_scatter | solution.py:108
  (56 shorter events, 36.8 us)
Async XLA Ops:
  7.2 21.8 %copy-start = (bf16[1024,1024]{1,0:T(8,128)(2,1)S(1)}, bf16[1024,1024]{1,0:T(8,128)(2,1)}, u32[]{:S(2)}) copy-start(bf16[1024,1024]{1,0:T(8,128)(2,1)} %param.6) | copy-start | bytes 6291460
  7.2 3.3 copy-start.2
  10.8 6.8 %copy-start.9 = (bf16[4,1,128,1024]{3,2,1,0:T(8,128)(2,1)}, bf16[4,1,128,1024]{3,2,1,0:T(8,128)(2,1)S(1)}, u32[]{:S(2)}) copy-start(bf16[4,1,128,1024]{3,2,1,0:T(8,128)(2,1)S(1)} %fusion.12) | copy-start | bytes 3145732
  21.7 78.1 %all-to-all-start = ((bf16[4,1,128,3072]{3,0,1,2:T(4,128)(2,1)}), bf16[4,1,128,3072]{3,0,1,2:T(4,128)(2,1)}, u32[]{:S(2)}, u32[]{:S(2)}) async-start(bf16[4,1,128,3072]{3,0,1,2:T(4,128)(2,1)} %copy.51), calls=%async_computation | async-start | bytes 6291456 | tf_op jit(solution)/shard_map/all_to_all | solution.py:91
  99.8 61.6 %all-to-all-start.1 = ((bf16[4,1,128,1024]{3,0,1,2:T(4,128)(2,1)}), bf16[4,1,128,1024]{3,0,1,2:T(4,128)(2,1)}, u32[]{:S(2)}, u32[]{:S(2)}) async-start(bf16[4,1,128,1024]{3,0,1,2:T(4,128)(2,1)} %copy.56), calls=%async_computation.1 | async-start | bytes 2097152 | tf_op jit(solution)/shard_map/all_to_all | solution.py:101
  120.8 32.6 %copy-start.5 = (bf16[4,8,16,16,64]{4,3,0,2,1:T(8,128)(2,1)S(1)}, bf16[4,8,16,16,64]{4,3,0,2,1:T(8,128)(2,1)}, u32[]{:S(2)}) copy-start(bf16[4,8,16,16,64]{4,3,0,2,1:T(8,128)(2,1)} %reshape.151) | copy-start | bytes 3145732
  153.3 1.9 copy-start.11
  153.3 2.1 copy-start.12
  161.4 31.2 %all-to-all-start.3 = ((bf16[4,8,16,1024]{3,2,0,1:T(8,128)(2,1)}), bf16[4,8,16,1024]{3,2,0,1:T(8,128)(2,1)}, u32[]{:S(2)}, u32[]{:S(2)}) async-start(bf16[4,8,16,1024]{3,2,0,1:T(8,128)(2,1)} %reshape.147), calls=%async_computation.4 | async-start | bytes 2097152 | tf_op jit(solution)/shard_map/all_to_all | solution.py:94
  167.3 191.1 %reduce-scatter.5.cloned.1.call-start = ((), (), s32[]{:S(2)}) async-start(), calls=%async_computation.7 | async-start | bytes 4325376 | tf_op jit(solution)/shard_map/reduce_scatter | solution.py:102
  192.5 1.5 copy-start.6
  197.3 321.6 %reduce-scatter.3.cloned.1.call-start = ((), (), s32[]{:S(2)}) async-start(), calls=%async_computation.6 | async-start | bytes 12976128 | tf_op jit(solution)/shard_map/reduce_scatter | solution.py:108
  206.1 1.7 copy-start.4
  209.7 4.2 copy-start.3
  318.9 2.0 copy-start.10
  319.2 1.7 copy-start.8
  334.1 1.2 copy-start.7
  334.6 184.3 %copy-start.1 = (bf16[1024,1024]{1,0:T(8,128)(2,1)S(1)}, bf16[1024,1024]{1,0:T(8,128)(2,1)}, u32[]{:S(2)}) copy-start(bf16[1024,1024]{1,0:T(8,128)(2,1)} %param.6) | copy-start | bytes 6291460
Sparse Core Ops, SparseCore 0:
  197.5 160.9 reduce-scatter.4
  365.0 153.8 reduce-scatter.2
where the time goes:
time: 532 us; the launch traced here: 526 us
  waiting for transfers between devices  252 us (47%)
  blocking collectives  96.7 us (18%)
  other arithmetic  49 us (9%)
  matrix products  48 us (9%)
  local copies, waits for them, and re-layouts  47.5 us (9%)
  starting transfers between devices  18.5 us (3%)
  between operations  14.6 us (3%)
    reduce_scatter x1, waiting for transfers between devices, shards(): lax.psum_scatter(row_product(flat_normed, flat_grad), ('clip', 'tm'), sca...  161 us
    all_to_all x1, blocking collectives, shards(): lax.all_to_all(packed_grad_pos, 'tm', split_axis=1, concat_axis=2, tiled=...  96.7 us
    all_to_all x1, waiting for transfers between devices, shards(): lax.all_to_all(packed, 'tm', split_axis=2, concat_axis=1, tiled=True)  66.5 us
    sub x1, other arithmetic, attend(): expo = jnp.exp(scores - highest)  32.5 us
    reduce_scatter x1, waiting for transfers between devices, shards(): lax.psum_scatter(row_product(mixed_rows, cot_rows), ('clip', 'tm'), scatt...  21.3 us
    reshape x4, local copies, waits for them, and re-layouts, split_heads(): return array.reshape(array.shape[:-1] + (HEADS, array.shape[-1] // HEADS))  11.8 us
  transfers between devices with their start and end apart: 5, of which 4 were waited for; matrix products, arithmetic and copies ran while one was open for 23% of the time, Pallas kernels for 0%

commit v1 on v0

v1 whole, which is shorter than its diff:
```python
import functools

import jax
import jax.numpy as jnp
from jax import lax
from jax.experimental import pallas as pl
from jax.experimental.pallas import tpu as pltpu
from jax.sharding import PartitionSpec as P

HEADS = 16
GROUP = 4
CHUNKS = 2
EPSILON = 1e-06
LOWEST = -1e30
VMEM_LIMIT = 48 * 1024 * 1024


def contract(left, right, dims):
    return lax.dot_general(left, right, (dims, ((), ())), preferred_element_type=jnp.float32)


def statistics(rows32):
    mean = jnp.mean(rows32, axis=-1, keepdims=True)
    centred = rows32 - mean
    inverse = lax.rsqrt(jnp.mean(centred * centred, axis=-1, keepdims=True) + EPSILON)
    return centred * inverse, inverse


def pick_kernel(n_slots, n_chunks, me_ref, x_ref, cot_ref, *out_refs):
    depth = x_ref.shape[0] // n_chunks
    for chunk in range(n_chunks):
        here = pl.ds(chunk * depth, depth)
        for slot in range(n_slots):
            out = out_refs[chunk * n_slots + slot]
            block = me_ref[0] ^ slot
            out[0] = x_ref[here, block]
            out[1] = cot_ref[here, block]


def pick(me, clips, cotangent, n_slots, n_chunks):
    n_clips, _, n_patches, width = clips.shape
    cut = (n_clips, n_slots, n_patches // n_slots, width)
    piece = jax.ShapeDtypeStruct((2, n_clips // n_chunks) + cut[2:], clips.dtype)
    out = pl.pallas_call(
        functools.partial(pick_kernel, n_slots, n_chunks),
        out_shape=[piece] * (n_slots * n_chunks),
        in_specs=[
            pl.BlockSpec(memory_space=pltpu.SMEM),
            pl.BlockSpec(memory_space=pltpu.VMEM),
            pl.BlockSpec(memory_space=pltpu.VMEM),
        ],
        out_specs=[pl.BlockSpec(memory_space=pltpu.VMEM)] * (n_slots * n_chunks),
        compiler_params=pltpu.CompilerParams(vmem_limit_bytes=VMEM_LIMIT),
    )(me, clips.reshape(cut), cotangent.reshape(cut))
    return [out[chunk * n_slots : (chunk + 1) * n_slots] for chunk in range(n_chunks)]


def place_kernel(n_slots, me_ref, *refs):
    out_ref = refs[n_slots]
    for slot in range(n_slots):
        out_ref[:, me_ref[0] ^ slot] = refs[slot][...]


def place(me, blocks):
    n_slots = len(blocks)
    n_clips, n_positions, width = blocks[0].shape
    return pl.pallas_call(
        functools.partial(place_kernel, n_slots),
        out_shape=jax.ShapeDtypeStruct((n_clips, n_slots, n_positions, width), blocks[0].dtype),
        in_specs=[pl.BlockSpec(memory_space=pltpu.SMEM)]
        + [pl.BlockSpec(memory_space=pltpu.VMEM)] * n_slots,
        out_specs=pl.BlockSpec(memory_space=pltpu.VMEM),
        compiler_params=pltpu.CompilerParams(vmem_limit_bytes=VMEM_LIMIT),
    )(me, *blocks)


def sublayer_kernel(n_clips, n_positions, n_pieces, n_aliased, *refs):
    pieces, refs = refs[:n_pieces], refs[n_pieces:]
    wq_ref, wk_ref, wv_ref, wo_ref = refs[:4]
    refs = refs[4 + n_aliased :]
    normed_ref, cot_ref, mixed_ref, grads_ref = refs[:4]
    dx_refs, total_ref = refs[4:-1], refs[-1]
    step = pl.program_id(0)
    rows = normed_ref.shape[0] // n_clips
    span = rows // n_pieces
    wide = wo_ref.shape[0]
    depth = wide // GROUP
    scaling = depth**-0.5

    def raw_rows():
        return jnp.concatenate(
            [pieces[k][0, clip] for clip in range(n_clips) for k in range(n_pieces)], axis=0
        ).astype(jnp.float32)

    @pl.when(step == 0)
    def _():
        unit, _ = statistics(raw_rows())
        normed_ref[...] = unit.astype(jnp.bfloat16)
        for clip in range(n_clips):
            for k in range(n_pieces):
                cot_ref[pl.ds(clip * rows + k * span, span)] = pieces[k][1, clip]

    normed = normed_ref[...]
    all_queries = contract(normed, wq_ref[...], ((1,), (0,))).astype(jnp.bfloat16)
    all_keys = contract(normed, wk_ref[...], ((1,), (0,))).astype(jnp.bfloat16)
    all_values = contract(normed, wv_ref[...], ((1,), (0,))).astype(jnp.bfloat16)
    mixed_grad = contract(cot_ref[...], wo_ref[...], ((1,), (1,))).astype(jnp.bfloat16)

    lane_head = lax.broadcasted_iota(jnp.int32, (rows, wide), 1) // depth
    head_masks = [(lane_head == h).astype(jnp.float32).astype(jnp.bfloat16) for h in range(GROUP)]
    key_pos = lax.broadcasted_iota(jnp.int32, (rows, rows), 0) % n_positions
    query_pos = lax.broadcasted_iota(jnp.int32, (rows, rows), 1) % n_positions
    same = (key_pos == query_pos)[None]

    def stacked(block):
        return jnp.concatenate([block * mask for mask in head_masks], axis=0)

    def side_by_side(blocks):
        return jnp.concatenate([blocks[h] for h in range(GROUP)], axis=1)

    for clip in range(n_clips):
        here = slice(clip * rows, (clip + 1) * rows)
        queries = all_queries[here]
        keys = stacked(all_keys[here])
        values = stacked(all_values[here])
        upstream = mixed_grad[here]
        scores = contract(keys, queries, ((1,), (1,))).reshape(GROUP, rows, rows)
        scores = jnp.where(same, scores * scaling, LOWEST)
        expo = jnp.exp(scores - jnp.max(scores, axis=1, keepdims=True))
        full = expo * (1.0 / jnp.sum(expo, axis=1, keepdims=True))
        low = full.astype(jnp.bfloat16)
        dots = contract(values, upstream, ((1,), (1,))).reshape(GROUP, rows, rows)
        score_grad = full * (dots - jnp.sum(full * dots, axis=1, keepdims=True))
        score_grad = (score_grad * scaling).astype(jnp.bfloat16)
        mixed = contract(low.reshape(GROUP * rows, rows), values, ((0,), (0,)))
        mixed_ref[here] = mixed.astype(jnp.bfloat16)
        dq = contract(score_grad.reshape(GROUP * rows, rows), keys, ((0,), (0,)))
        grads_ref[here, :wide] = dq.astype(jnp.bfloat16)
        dk = contract(side_by_side(score_grad), stacked(queries), ((1,), (0,)))
        grads_ref[here, wide : 2 * wide] = dk.astype(jnp.bfloat16)
        dv = contract(side_by_side(low), stacked(upstream), ((1,), (0,)))
        grads_ref[here, 2 * wide :] = dv.astype(jnp.bfloat16)

    part = contract(grads_ref[:, :wide], wq_ref[...], ((1,), (1,)))
    part += contract(grads_ref[:, wide : 2 * wide], wk_ref[...], ((1,), (1,)))
    part += contract(grads_ref[:, 2 * wide :], wv_ref[...], ((1,), (1,)))

    @pl.when(step == 0)
    def _():
        total_ref[...] = part

    @pl.when(step > 0)
    def _():
        total_ref[...] += part

    @pl.when(step == pl.num_programs(0) - 1)
    def _():
        unit, inverse = statistics(raw_rows())
        total = total_ref[...]
        grad = inverse * (
            total
            - jnp.mean(total, axis=-1, keepdims=True)
            - unit * jnp.mean(total * unit, axis=-1, keepdims=True)
        )
        dx = (cot_ref[...].astype(jnp.float32) + grad).astype(jnp.bfloat16)
        for clip in range(n_clips):
            for k in range(n_pieces):
                start = clip * rows + k * span
                dx_refs[k][clip] = dx[start : start + span]


def sublayer(pieces, w_qkv, w_out, chunk, n_chunks, n_positions, before):
    n_pieces = len(pieces)
    _, n_clips, span, width = pieces[0].shape
    rows = n_clips * n_pieces * span
    groups = HEADS // GROUP
    wide = width // groups

    def whole(shape):
        return pl.BlockSpec(shape, lambda j: (0,) * len(shape))

    flat = jax.ShapeDtypeStruct((n_chunks * rows, width), jnp.bfloat16)
    grads = jax.ShapeDtypeStruct((n_chunks * rows, 3 * width), jnp.bfloat16)
    dx = jax.ShapeDtypeStruct((n_chunks * n_clips, span, width), jnp.bfloat16)
    out_shape = [flat, flat, flat, grads] + [dx] * n_pieces
    aliased = [] if before is None else list(before)
    first = n_pieces + 4
    return pl.pallas_call(
        functools.partial(sublayer_kernel, n_clips, n_positions, n_pieces, len(aliased)),
        grid=(groups,),
        out_shape=out_shape,
        in_specs=[whole(piece.shape) for piece in pieces]
        + [pl.BlockSpec((width, wide), lambda j, i=i: (0, i * groups + j)) for i in range(3)]
        + [pl.BlockSpec((wide, width), lambda j: (j, 0))]
        + [pl.BlockSpec(memory_space=pl.ANY)] * len(aliased),
        out_specs=[
            pl.BlockSpec((rows, width), lambda j: (chunk, 0)),
            pl.BlockSpec((rows, width), lambda j: (chunk, 0)),
            pl.BlockSpec((rows, wide), lambda j: (chunk, j)),
            pl.BlockSpec((rows, 3 * wide), lambda j: (chunk, j)),
        ]
        + [pl.BlockSpec((n_clips, span, width), lambda j: (chunk, 0, 0))] * n_pieces,
        scratch_shapes=[pltpu.VMEM((rows, width), jnp.float32)],
        input_output_aliases={first + i: i for i in range(len(aliased))},
        compiler_params=pltpu.CompilerParams(vmem_limit_bytes=VMEM_LIMIT),
        cost_estimate=pl.CostEstimate(
            flops=2 * rows * width * (7 * width + 24 * 128),
            bytes_accessed=16 * rows * width + 8 * width * width,
            transcendentals=rows * 128 * HEADS,
        ),
    )(*pieces, w_qkv, w_qkv, w_qkv, w_out, *aliased)


def swap(block, axis, size, distance):
    return lax.ppermute(block, axis, [(i, i ^ distance) for i in range(size)])


def scatter_sum(parts, axis, size, stride, count):
    me = lax.axis_index(axis) // stride % count
    total = lax.dynamic_index_in_dim(parts, me, 0, keepdims=False).astype(jnp.float32)
    for j in range(1, count):
        block = lax.dynamic_index_in_dim(parts, me ^ j, 0, keepdims=False)
        total += swap(block.astype(jnp.bfloat16), axis, size, j * stride).astype(jnp.float32)
    return total


def shards(n_clip_devices, n_tm, clips, w_qkv, w_out, cotangent):
    n_clips, _, n_patches, width = clips.shape
    n_positions = n_patches // n_tm
    me = lax.axis_index("tm").reshape(1)

    chunks = pick(me, clips, cotangent, n_tm, CHUNKS)
    joined = n_positions % 16 != 0
    results = None
    for chunk, blocks in enumerate(chunks):
        pieces = [blocks[0]] + [swap(blocks[k], "tm", n_tm, k) for k in range(1, n_tm)]
        if joined:
            pieces = [jnp.stack(pieces, axis=2).reshape(2, n_clips // CHUNKS, -1, width)]
        results = sublayer(pieces, w_qkv, w_out, chunk, CHUNKS, n_positions, results)
    normed, cot, mixed, grads = results[:4]
    dx = list(results[4:])
    if joined:
        cut = dx[0].reshape(n_clips, n_tm, n_positions, width)
        dx = [cut[:, k] for k in range(n_tm)]
    dx = [dx[0]] + [swap(dx[k], "tm", n_tm, k) for k in range(1, n_tm)]
    grad_clips = place(me, dx).reshape(clips.shape)

    cores = 2
    n_x = n_clip_devices // cores
    n_y = 2
    n_z = n_tm // n_y
    core = lax.axis_index("clip") % cores
    rest = width // (n_x * cores)

    def chosen(rows, which):
        cut = rows.reshape(rows.shape[0], n_x, cores, rest)
        return lax.dynamic_index_in_dim(cut, which, 2, keepdims=False).reshape(rows.shape[0], -1)

    half = 2 * width

    def first_half(which):
        left = chosen(normed, which)
        return contract(left, grads[:, :half], ((0,), (0,))).astype(jnp.bfloat16)

    def second_half(which):
        left = contract(chosen(normed, which), grads[:, half:], ((0,), (0,)))
        right = contract(chosen(mixed, which), cot, ((0,), (0,)))
        return jnp.concatenate([left, right], axis=1).astype(jnp.bfloat16)

    sums = []
    for product in (first_half, second_half):
        other = swap(product(1 - core), "clip", n_clip_devices, 1)
        total = product(core).astype(jnp.float32) + other.astype(jnp.float32)
        sums.append(total.reshape(n_x, n_z, n_y, -1, half))
    first, second = sums
    first = scatter_sum(first, "clip", n_clip_devices, cores, n_x)
    second = scatter_sum(second.transpose(2, 0, 1, 3, 4), "tm", n_tm, 1, n_y)
    first = scatter_sum(first.transpose(1, 0, 2, 3), "tm", n_tm, 1, n_y)
    second = scatter_sum(second, "clip", n_clip_devices, cores, n_x)
    first = scatter_sum(first, "tm", n_tm, n_y, n_z)
    second = scatter_sum(second, "tm", n_tm, n_y, n_z)

    groups = HEADS // GROUP
    grad_qkv = jnp.concatenate([first, second[:, :width]], axis=1)
    grad_qkv = grad_qkv.reshape(-1, groups, 3, width // groups).transpose(0, 2, 1, 3)
    return (grad_clips, grad_qkv.reshape(-1, 3 * width), second[:, width:])


def solution(mesh):
    return jax.shard_map(
        functools.partial(shards, mesh.shape["clip"], mesh.shape["tm"]),
        mesh=mesh,
        in_specs=(P("clip", "tm", None, None), P(), P(), P("clip", "tm", None, None)),
        out_specs=(P("clip", "tm", None, None), P(("clip", "tm"), None), P(("clip", "tm"), None)),
        check_vma=False,
    )
```

time: 532 us -> 200 us (0.38); the launches traced: 526 us -> 199 us
  waiting for transfers between devices: 252 us -> 46.2 us
  blocking collectives: 96.7 us -> 0 us
  starting transfers between devices: 18.5 us -> 59.6 us
  other arithmetic: 49 us -> 11 us
  matrix products: 48 us -> 11.5 us
  Pallas kernels: 0 us -> 26.9 us
  between operations: 14.6 us -> 1.05 us
    reduce_scatter x2 -> x0, waiting for transfers between devices: 182 us -> none  [the longest x1 161 us: shards(): lax.psum_scatter(row_product(flat_normed, flat_grad), ('clip', 'tm'), sca...]
    all_to_all x1 -> x0, blocking collectives: 96.7 us -> none  [shards(): lax.all_to_all(packed_grad_pos, 'tm', split_axis=1, concat_axis=2, tiled=...]
    all_to_all x3 -> x0, waiting for transfers between devices: 70 us -> none  [the longest x1 66.5 us: shards(): lax.all_to_all(packed, 'tm', split_axis=2, concat_axis=1, tiled=True)]
    ppermute x0 -> x33, starting transfers between devices: none -> 59.6 us  [swap(): return lax.ppermute(block, axis, [(i, i ^ distance) for i in range(size)])]
    ppermute x0 -> x33, waiting for transfers between devices: none -> 46.2 us  [swap(): return lax.ppermute(block, axis, [(i, i ^ distance) for i in range(size)])]
    sub x2 -> x0, other arithmetic: 41.1 us -> none  [the longest x1 32.5 us: attend(): expo = jnp.exp(scores - highest)]
    dot_general x11 -> x6, matrix products: 48 us -> 11.5 us  [contract(): lax.dot_general(left, right, (dims, ((), ())), preferred_element_type=jnp...]
    reshape x11 -> x4, local copies, waits for them, and re-layouts: 34.2 us -> 4.36 us  [the longest x2 3.13 us: chosen(): cut = rows.reshape(rows.shape[0], n_x, cores, rest)]
  transfers between devices with their start and end apart: 5 -> 33, of which waited for: 4 -> 8; matrix products, arithmetic and copies ran while one was open for 23% -> 11% of each run, Pallas kernels for 0% -> 7%
where the time goes in v1:
time: 200 us; the launch traced here: 199 us
  starting transfers between devices  59.6 us (30%)
  waiting for transfers between devices  46.2 us (23%)
  local copies, waits for them, and re-layouts  43.1 us (22%)
  Pallas kernels  26.9 us (13%)
  matrix products  11.5 us (6%)
  other arithmetic  11 us (6%)
    ppermute x33, starting transfers between devices, swap(): return lax.ppermute(block, axis, [(i, i ^ distance) for i in range(size)])  59.6 us
    ppermute x33, waiting for transfers between devices, swap(): return lax.ppermute(block, axis, [(i, i ^ distance) for i in range(size)])  46.2 us
    unnamed x90, local copies, waits for them, and re-layouts  30.7 us
    pallas_call x2, Pallas kernels, sublayer(): pl.pallas_call(functools.partial(sublayer_kernel, n_clips, n_positions, n...  25 us
    dot_general x6, matrix products, contract(): lax.dot_general(left, right, (dims, ((), ())), preferred_element_type=jnp...  11.5 us
    dynamic_slice x1, local copies, waits for them, and re-layouts, chosen(): lax.dynamic_index_in_dim(cut, which, 2, keepdims=False)  6.76 us
    add x2, other arithmetic, shards(): total = product(core).astype(jnp.float32) + other.astype(jnp.float32)  5.37 us
    add x6, other arithmetic, scatter_sum(): total += swap(block.astype(jnp.bfloat16), axis, size, j * stride).astype(...  4.11 us
  transfers between devices with their start and end apart: 33, of which 8 were waited for; matrix products, arithmetic and copies ran while one was open for 11% of the time, Pallas kernels for 7%

profile of v1, /device:TPU:0, one launch (start us, length us, event | category | flops | bytes accessed | tf_op | source)
XLA Modules:
  0.0 199.4 jit_solution(12393376775399001953)
XLA Ops:
  4.6 3.0 %collective-permute-start = (bf16[2,2,16,1024]{3,2,1,0:T(8,128)(2,1)S(1)}, bf16[2,2,16,1024]{3,2,1,0:T(8,128)(2,1)S(1)}, u32[]{:S(2)}, u32[]{:S(2)}) collective-permute-start(bf16[2,2,16,1024]{3,2,1,0:T(8,128)(2,1)S(1)} %get-tuple-element.44), channel_id=1, source_target_pairs={{0,1},{1,0},{2,3},{3,2},{4,5},{5,4},{6,7},{7,6},{8,9},{9,8},{10,11... | collective-permute-start | bytes 393224 | tf_op jit(solution)/shard_map/ppermute | solution.py:215
  9.7 3.0 %collective-permute-start.9 = (bf16[2,2,16,1024]{3,2,1,0:T(8,128)(2,1)S(1)}, bf16[2,2,16,1024]{3,2,1,0:T(8,128)(2,1)S(1)}, u32[]{:S(2)}, u32[]{:S(2)}) collective-permute-start(bf16[2,2,16,1024]{3,2,1,0:T(8,128)(2,1)S(1)} %get-tuple-element.54), channel_id=1, source_target_pairs={{0,3},{1,2},{2,1},{3,0},{4,7},{5,6},{6,5},{7,4},{8,11},{9,10},{10,... | collective-permute-start | bytes 393224 | tf_op jit(solution)/shard_map/ppermute | solution.py:215
  12.7 2.6 %collective-permute-start.10 = (bf16[2,2,16,1024]{3,2,1,0:T(8,128)(2,1)S(1)}, bf16[2,2,16,1024]{3,2,1,0:T(8,128)(2,1)S(1)}, u32[]{:S(2)}, u32[]{:S(2)}) collective-permute-start(bf16[2,2,16,1024]{3,2,1,0:T(8,128)(2,1)S(1)} %get-tuple-element.55), channel_id=1, source_target_pairs={{0,4},{1,5},{2,6},{3,7},{4,0},{5,1},{6,2},{7,3},{8,12},{9,13},{10,... | collective-permute-start | bytes 393224 | tf_op jit(solution)/shard_map/ppermute | solution.py:215
  17.6 3.6 %collective-permute-start.12 = (bf16[2,2,16,1024]{3,2,1,0:T(8,128)(2,1)S(1)}, bf16[2,2,16,1024]{3,2,1,0:T(8,128)(2,1)S(1)}, u32[]{:S(2)}, u32[]{:S(2)}) collective-permute-start(bf16[2,2,16,1024]{3,2,1,0:T(8,128)(2,1)S(1)} %get-tuple-element.57), channel_id=1, source_target_pairs={{0,6},{1,7},{2,4},{3,5},{4,2},{5,3},{6,0},{7,1},{8,14},{9,15},{10,... | collective-permute-start | bytes 393224 | tf_op jit(solution)/shard_map/ppermute | solution.py:215
  25.4 3.1 %collective-permute-start.3 = (bf16[2,2,16,1024]{3,2,1,0:T(8,128)(2,1)}, bf16[2,2,16,1024]{3,2,1,0:T(8,128)(2,1)S(1)}, u32[]{:S(2)}, u32[]{:S(2)}) collective-permute-start(bf16[2,2,16,1024]{3,2,1,0:T(8,128)(2,1)} %get-tuple-element.47), channel_id=1, source_target_pairs={{0,4},{1,5},{2,6},{3,7},{4,0},{5,1},{6,2},{7,3},{8,12},{9,13},{10,... | collective-permute-start | bytes 393224 | tf_op jit(solution)/shard_map/ppermute | solution.py:215
  28.5 12.8 %collective-permute-done.11.refs_5_ = bf16[2,2,16,1024]{3,2,1,0:T(8,128)(2,1)S(1)} collective-permute-done((bf16[2,2,16,1024]{3,2,1,0:T(8,128)(2,1)S(1)}, bf16[2,2,16,1024]{3,2,1,0:T(8,128)(2,1)S(1)}, u32[]{:S(2)}, u32[]{:S(2)}) %collective-permute-start.11) | collective-permute-done | bytes 131104 | tf_op jit(solution)/shard_map/ppermute | solution.py:215
  42.6 4.9 %collective-permute-start.5 = (bf16[2,2,16,1024]{3,2,1,0:T(8,128)(2,1)}, bf16[2,2,16,1024]{3,2,1,0:T(8,128)(2,1)S(1)}, u32[]{:S(2)}, u32[]{:S(2)}) collective-permute-start(bf16[2,2,16,1024]{3,2,1,0:T(8,128)(2,1)} %get-tuple-element.49), channel_id=1, source_target_pairs={{0,6},{1,7},{2,4},{3,5},{4,2},{5,3},{6,0},{7,1},{8,14},{9,15},{10,... | collective-permute-start | bytes 393224 | tf_op jit(solution)/shard_map/ppermute | solution.py:215
  55.3 12.5 %shard_map.68 = (bf16[512,1024]{1,0:T(8,128)(2,1)S(1)}, bf16[512,1024]{1,0:T(8,128)(2,1)S(1)}, bf16[512,1024]{1,0:T(8,128)(2,1)S(1)}, bf16[512,3072]{1,0:T(8,128...) custom-call(bf16[2,2,16,1024]{3,2,1,0:T(8,128)(2,1)S(1)} %copy-done., ...), custom_call_target="tpu_custom_call" | custom-call | flops 5368709120 | bytes 12582912 | tf_op jit(solution)/shard_map/pallas_call | solution.py:188
  67.9 12.5 %shard_map.69 = (bf16[512,1024]{1,0:T(8,128)(2,1)S(1)}, bf16[512,1024]{1,0:T(8,128)(2,1)S(1)}, bf16[512,1024]{1,0:T(8,128)(2,1)S(1)}, bf16[512,3072]{1,0:T(8,128...) custom-call(bf16[2,2,16,1024]{3,2,1,0:T(8,128)(2,1)S(1)} %get-tuple-, ...), custom_call_target="tpu_custom_call", output_to_operand_aliasing={{0}: (12, {}), {1}: (13, {}), {2}: (14, {}), {3}: (15, {}),... | custom-call | flops 5368709120 | bytes 12582912 | tf_op jit(solution)/shard_map/pallas_call | solution.py:188
  88.1 6.8 %constant_dynamic-slice_fusion.1 = (bf16[512,2,1,256]{3,2,1,0:T(2,128)(2,1)}, bf16[512,2,1,256]{3,2,1,0:T(2,128)(2,1)}, bf16[512,2,1,256]{3,2,1,0:T(2,128)(2,1)}, bf16[512,2,1,256]{3,2,1,0:T(2,128)(2,1)S(1)}) fusion(bf16[512,2,2,256]{3,2,1,0:T(2,128)(2,1)S(1)} %copy-done.37, s32[]{:T(128)S(6)} %select_n.84, s32[]{:T(128)S(6)} %select_n.85, ...), kind=kLoop, calls=%fused_computation.45 | loop fusion | bytes 4194312 | tf_op jit(solution)/shard_map/jit(dynamic_index_in_dim)/dynamic_slice | solution.py:257
  94.9 3.6 %copy.43 = bf16[512,2,1,256]{0,3,1,2:T(8,128)(2,1)} copy(bf16[512,2,1,256]{3,2,1,0:T(2,128)(2,1)} %get-tuple-element.101) | data formatting | bytes 1048576
  107.2 2.6 %convolution_convert_fusion = bf16[512,2048]{1,0:T(8,128)(2,1)} fusion(bf16[512,512]{0,1:T(8,128)(2,1)S(1)} %bitcast.74, bf16[512,3072]{1,0:T(8,128)(2,1)S(1)} %copy-done.40), kind=kOutput, calls=%fused_computation.2 | convolution fusion | flops 1074790400 | bytes 4718592 | tf_op jit(solution)/shard_map/dot_general | solution.py:19
  120.0 2.4 %convert_add_fusion = f32[512,2048]{1,0:T(8,128)S(1)} fusion(bf16[512,2048]{1,0:T(8,128)(2,1)} %collective-permute-done.27, bf16[512,1024]{1,0:T(8,128)(2,1)S(1)} %convolution_convert_fusion.4, bf16[512,1024]{1,0:T(8,128)(2,1)S(1)} %convolution_convert_fusion.5), kind=kLoop, calls=%fused_computation | loop fusion | flops 6291456 | bytes 8388608 | tf_op jit(solution)/shard_map/add | solution.py:273
  123.2 3.0 %convert_add_fusion.1 = f32[512,2048]{1,0:T(8,128)S(1)} fusion(bf16[512,2048]{1,0:T(8,128)(2,1)} %collective-permute-done.21, bf16[512,2048]{1,0:T(8,128)(2,1)S(1)} %convolution_convert_fusion.1), kind=kLoop, calls=%fused_computation.1 | loop fusion | flops 3145728 | bytes 8388608 | tf_op jit(solution)/shard_map/add | solution.py:273
  128.0 3.9 %collective-permute-start.15 = (bf16[4,16,1024]{2,1,0:T(8,128)(2,1)S(1)}, bf16[4,16,1024]{2,1,0:T(8,128)(2,1)S(1)}, u32[]{:S(2)}, u32[]{:S(2)}) collective-permute-start(bf16[4,16,1024]{2,1,0:T(8,128)(2,1)S(1)} %copy-done.23), channel_id=1, source_target_pairs={{0,2},{1,3},{2,0},{3,1},{4,6},{5,7},{6,4},{7,5},{8,10},{9,11},{10,... | collective-permute-start | bytes 393224 | tf_op jit(solution)/shard_map/ppermute | solution.py:215
  133.5 5.3 %collective-permute-done.15.refs_2_ = bf16[4,16,1024]{2,1,0:T(8,128)(2,1)S(1)} collective-permute-done((bf16[4,16,1024]{2,1,0:T(8,128)(2,1)S(1)}, bf16[4,16,1024]{2,1,0:T(8,128)(2,1)S(1)}, u32[]{:S(2)}, u32[]{:S(2)}) %collective-permute-start.15) | collective-permute-done | bytes 131104 | tf_op jit(solution)/shard_map/ppermute | solution.py:215
  141.8 2.4 %collective-permute-start.19 = (bf16[4,16,1024]{2,1,0:T(8,128)(2,1)S(1)}, bf16[4,16,1024]{2,1,0:T(8,128)(2,1)S(1)}, u32[]{:S(2)}, u32[]{:S(2)}) collective-permute-start(bf16[4,16,1024]{2,1,0:T(8,128)(2,1)S(1)} %copy-done.31), channel_id=1, source_target_pairs={{0,6},{1,7},{2,4},{3,5},{4,2},{5,3},{6,0},{7,1},{8,14},{9,15},{10,... | collective-permute-start | bytes 393224 | tf_op jit(solution)/shard_map/ppermute | solution.py:215
  146.2 7.6 %collective-permute-done.18.refs_5_ = bf16[4,16,1024]{2,1,0:T(8,128)(2,1)S(1)} collective-permute-done((bf16[4,16,1024]{2,1,0:T(8,128)(2,1)S(1)}, bf16[4,16,1024]{2,1,0:T(8,128)(2,1)S(1)}, u32[]{:S(2)}, u32[]{:S(2)}) %collective-permute-start.18) | collective-permute-done | bytes 131104 | tf_op jit(solution)/shard_map/ppermute | solution.py:215
  162.6 9.4 %collective-permute-done.29 = bf16[4,32,2048]{2,1,0:T(8,128)(2,1)S(1)} collective-permute-done((bf16[4,32,2048]{2,1,0:T(8,128)(2,1)S(1)}, bf16[4,32,2048]{2,1,0:T(8,128)(2,1)S(1)}, u32[]{:S(2)}, u32[]{:S(2)}) %collective-permute-start.29) | collective-permute-done | bytes 524320 | tf_op jit(solution)/shard_map/ppermute | solution.py:215
  172.2 3.9 %collective-permute-start.32 = (bf16[32,2048]{1,0:T(8,128)(2,1)S(1)}, bf16[32,2048]{1,0:T(8,128)(2,1)S(1)}, u32[]{:S(2)}, u32[]{:S(2)}) collective-permute-start(bf16[32,2048]{1,0:T(8,128)(2,1)S(1)} %get-tuple-element.96), channel_id=1, source_target_pairs={{0,6},{1,7},{2,4},{3,5},{4,2},{5,3},{6,0},{7,1},{8,14},{9,15},{10,... | collective-permute-start | bytes 393224 | tf_op jit(solution)/shard_map/ppermute | solution.py:215
  178.1 2.7 %collective-permute-start.26 = (bf16[32,2048]{1,0:T(8,128)(2,1)S(1)}, bf16[32,2048]{1,0:T(8,128)(2,1)S(1)}, u32[]{:S(2)}, u32[]{:S(2)}) collective-permute-start(bf16[32,2048]{1,0:T(8,128)(2,1)S(1)} %get-tuple-element.93), channel_id=1, source_target_pairs={{0,6},{1,7},{2,4},{3,5},{4,2},{5,3},{6,0},{7,1},{8,14},{9,15},{10,... | collective-permute-start | bytes 393224 | tf_op jit(solution)/shard_map/ppermute | solution.py:215
  181.6 8.1 %collective-permute-start.24 = (bf16[32,2048]{1,0:T(8,128)(2,1)S(1)}, bf16[32,2048]{1,0:T(8,128)(2,1)S(1)}, u32[]{:S(2)}, u32[]{:S(2)}) collective-permute-start(bf16[32,2048]{1,0:T(8,128)(2,1)S(1)} %get-tuple-element.92), channel_id=1, source_target_pairs={{0,2},{1,3},{2,0},{3,1},{4,6},{5,7},{6,4},{7,5},{8,10},{9,11},{10,... | collective-permute-start | bytes 393224 | tf_op jit(solution)/shard_map/ppermute | solution.py:215
  189.7 3.5 %collective-permute-done.31 = bf16[32,2048]{1,0:T(8,128)(2,1)S(1)} collective-permute-done((bf16[32,2048]{1,0:T(8,128)(2,1)S(1)}, bf16[32,2048]{1,0:T(8,128)(2,1)S(1)}, u32[]{:S(2)}, u32[]{:S(2)}) %collective-permute-start.31) | collective-permute-done | bytes 131104 | tf_op jit(solution)/shard_map/ppermute | solution.py:215
  194.0 4.0 %collective-permute-done.25 = bf16[32,2048]{1,0:T(8,128)(2,1)S(1)} collective-permute-done((bf16[32,2048]{1,0:T(8,128)(2,1)S(1)}, bf16[32,2048]{1,0:T(8,128)(2,1)S(1)}, u32[]{:S(2)}, u32[]{:S(2)}) %collective-permute-start.25) | collective-permute-done | bytes 131104 | tf_op jit(solution)/shard_map/ppermute | solution.py:215
  (165 shorter events, 71.3 us)
Async XLA Ops:
  9.7 14.4 %collective-permute-start.9 = (bf16[2,2,16,1024]{3,2,1,0:T(8,128)(2,1)S(1)}, bf16[2,2,16,1024]{3,2,1,0:T(8,128)(2,1)S(1)}, u32[]{:S(2)}, u32[]{:S(2)}) collective-permute-start(bf16[2,2,16,1024]{3,2,1,0:T(8,128)(2,1)S(1)} %get-tuple-element.54), channel_id=1, source_target_pairs={{0,3},{1,2},{2,1},{3,0},{4,7},{5,6},{6,5},{7,4},{8,11},{9,10},{10,... | collective-permute-start | bytes 393224 | tf_op jit(solution)/shard_map/ppermute | solution.py:215
  12.7 12.1 %collective-permute-start.10 = (bf16[2,2,16,1024]{3,2,1,0:T(8,128)(2,1)S(1)}, bf16[2,2,16,1024]{3,2,1,0:T(8,128)(2,1)S(1)}, u32[]{:S(2)}, u32[]{:S(2)}) collective-permute-start(bf16[2,2,16,1024]{3,2,1,0:T(8,128)(2,1)S(1)} %get-tuple-element.55), channel_id=1, source_target_pairs={{0,4},{1,5},{2,6},{3,7},{4,0},{5,1},{6,2},{7,3},{8,12},{9,13},{10,... | collective-permute-start | bytes 393224 | tf_op jit(solution)/shard_map/ppermute | solution.py:215
  15.9 25.4 %collective-permute-start.11 = (bf16[2,2,16,1024]{3,2,1,0:T(8,128)(2,1)S(1)}, bf16[2,2,16,1024]{3,2,1,0:T(8,128)(2,1)S(1)}, u32[]{:S(2)}, u32[]{:S(2)}) collective-permute-start(bf16[2,2,16,1024]{3,2,1,0:T(8,128)(2,1)S(1)} %get-tuple-element.56), channel_id=1, source_target_pairs={{0,5},{1,4},{2,7},{3,6},{4,1},{5,0},{6,3},{7,2},{8,13},{9,12},{10,... | collective-permute-start | bytes 393224 | tf_op jit(solution)/shard_map/ppermute | solution.py:215
  17.6 24.3 %collective-permute-start.12 = (bf16[2,2,16,1024]{3,2,1,0:T(8,128)(2,1)S(1)}, bf16[2,2,16,1024]{3,2,1,0:T(8,128)(2,1)S(1)}, u32[]{:S(2)}, u32[]{:S(2)}) collective-permute-start(bf16[2,2,16,1024]{3,2,1,0:T(8,128)(2,1)S(1)} %get-tuple-element.57), channel_id=1, source_target_pairs={{0,6},{1,7},{2,4},{3,5},{4,2},{5,3},{6,0},{7,1},{8,14},{9,15},{10,... | collective-permute-start | bytes 393224 | tf_op jit(solution)/shard_map/ppermute | solution.py:215
  21.9 25.6 %collective-permute-start.13 = (bf16[2,2,16,1024]{3,2,1,0:T(8,128)(2,1)S(1)}, bf16[2,2,16,1024]{3,2,1,0:T(8,128)(2,1)S(1)}, u32[]{:S(2)}, u32[]{:S(2)}) collective-permute-start(bf16[2,2,16,1024]{3,2,1,0:T(8,128)(2,1)S(1)} %get-tuple-element.58), channel_id=1, source_target_pairs={{0,7},{1,6},{2,5},{3,4},{4,3},{5,2},{6,1},{7,0},{8,15},{9,14},{10,... | collective-permute-start | bytes 393224 | tf_op jit(solution)/shard_map/ppermute | solution.py:215
  24.7 43.1 %collective-permute-start.2 = (bf16[2,2,16,1024]{3,2,1,0:T(8,128)(2,1)}, bf16[2,2,16,1024]{3,2,1,0:T(8,128)(2,1)S(1)}, u32[]{:S(2)}, u32[]{:S(2)}) collective-permute-start(bf16[2,2,16,1024]{3,2,1,0:T(8,128)(2,1)} %get-tuple-element.46), channel_id=1, source_target_pairs={{0,3},{1,2},{2,1},{3,0},{4,7},{5,6},{6,5},{7,4},{8,11},{9,10},{10,... | collective-permute-start | bytes 393224 | tf_op jit(solution)/shard_map/ppermute | solution.py:215
  25.4 42.5 %collective-permute-start.3 = (bf16[2,2,16,1024]{3,2,1,0:T(8,128)(2,1)}, bf16[2,2,16,1024]{3,2,1,0:T(8,128)(2,1)S(1)}, u32[]{:S(2)}, u32[]{:S(2)}) collective-permute-start(bf16[2,2,16,1024]{3,2,1,0:T(8,128)(2,1)} %get-tuple-element.47), channel_id=1, source_target_pairs={{0,4},{1,5},{2,6},{3,7},{4,0},{5,1},{6,2},{7,3},{8,12},{9,13},{10,... | collective-permute-start | bytes 393224 | tf_op jit(solution)/shard_map/ppermute | solution.py:215
  41.9 25.9 %collective-permute-start.4 = (bf16[2,2,16,1024]{3,2,1,0:T(8,128)(2,1)}, bf16[2,2,16,1024]{3,2,1,0:T(8,128)(2,1)S(1)}, u32[]{:S(2)}, u32[]{:S(2)}) collective-permute-start(bf16[2,2,16,1024]{3,2,1,0:T(8,128)(2,1)} %get-tuple-element.48), channel_id=1, source_target_pairs={{0,5},{1,4},{2,7},{3,6},{4,1},{5,0},{6,3},{7,2},{8,13},{9,12},{10,... | collective-permute-start | bytes 393224 | tf_op jit(solution)/shard_map/ppermute | solution.py:215
  42.6 25.3 %collective-permute-start.5 = (bf16[2,2,16,1024]{3,2,1,0:T(8,128)(2,1)}, bf16[2,2,16,1024]{3,2,1,0:T(8,128)(2,1)S(1)}, u32[]{:S(2)}, u32[]{:S(2)}) collective-permute-start(bf16[2,2,16,1024]{3,2,1,0:T(8,128)(2,1)} %get-tuple-element.49), channel_id=1, source_target_pairs={{0,6},{1,7},{2,4},{3,5},{4,2},{5,3},{6,0},{7,1},{8,14},{9,15},{10,... | collective-permute-start | bytes 393224 | tf_op jit(solution)/shard_map/ppermute | solution.py:215
  48.1 19.8 %collective-permute-start.6 = (bf16[2,2,16,1024]{3,2,1,0:T(8,128)(2,1)}, bf16[2,2,16,1024]{3,2,1,0:T(8,128)(2,1)S(1)}, u32[]{:S(2)}, u32[]{:S(2)}) collective-permute-start(bf16[2,2,16,1024]{3,2,1,0:T(8,128)(2,1)} %get-tuple-element.50), channel_id=1, source_target_pairs={{0,7},{1,6},{2,5},{3,4},{4,3},{5,2},{6,1},{7,0},{8,15},{9,14},{10,... | collective-permute-start | bytes 393224 | tf_op jit(solution)/shard_map/ppermute | solution.py:215
  106.1 13.9 %collective-permute-start.27 = (bf16[512,2048]{1,0:T(8,128)(2,1)}, bf16[512,2048]{1,0:T(8,128)(2,1)}, u32[]{:S(2)}, u32[]{:S(2)}) collective-permute-start(bf16[512,2048]{1,0:T(8,128)(2,1)} %pad_maximum_fusion), channel_id=1, source_target_pairs={{0,8},{8,0},{16,24},{24,16},{1,9},{9,1},{17,25},{25,17},{2,10},{10... | collective-permute-start | bytes 6291464 | tf_op jit(solution)/shard_map/ppermute | solution.py:215
  109.8 13.4 %collective-permute-start.21 = (bf16[512,2048]{1,0:T(8,128)(2,1)}, bf16[512,2048]{1,0:T(8,128)(2,1)}, u32[]{:S(2)}, u32[]{:S(2)}) collective-permute-start(bf16[512,2048]{1,0:T(8,128)(2,1)} %convolution_convert_fusion), channel_id=1, source_target_pairs={{0,8},{8,0},{16,24},{24,16},{1,9},{9,1},{17,25},{25,17},{2,10},{10... | collective-permute-start | bytes 6291464 | tf_op jit(solution)/shard_map/ppermute | solution.py:215
  109.8 22.6 %collective-permute-start.14 = (bf16[4,16,1024]{2,1,0:T(8,128)(2,1)S(1)}, bf16[4,16,1024]{2,1,0:T(8,128)(2,1)S(1)}, u32[]{:S(2)}, u32[]{:S(2)}) collective-permute-start(bf16[4,16,1024]{2,1,0:T(8,128)(2,1)S(1)} %copy-done.21), channel_id=1, source_target_pairs={{0,1},{1,0},{2,3},{3,2},{4,5},{5,4},{6,7},{7,6},{8,9},{9,8},{10,11... | collective-permute-start | bytes 393224 | tf_op jit(solution)/shard_map/ppermute | solution.py:215
  122.6 33.9 %collective-permute-start.28 = (bf16[2,4,32,2048]{3,2,1,0:T(8,128)(2,1)S(1)}, bf16[2,4,32,2048]{3,2,1,0:T(8,128)(2,1)}, u32[]{:S(2)}, u32[]{:S(2)}) collective-permute-start(bf16[2,4,32,2048]{3,2,1,0:T(8,128)(2,1)S(1)} %fusion.3), channel_id=1, source_target_pairs={{0,1},{1,0},{2,3},{3,2},{4,5},{5,4},{6,7},{7,6},{8,9},{9,8},{10,11... | collective-permute-start | bytes 3145736 | tf_op jit(solution)/shard_map/ppermute | solution.py:215
  126.5 33.8 %collective-permute-start.22 = (bf16[4,2,32,2048]{3,2,0,1:T(8,128)(2,1)S(1)}, bf16[4,2,32,2048]{3,2,0,1:T(8,128)(2,1)}, u32[]{:S(2)}, u32[]{:S(2)}) collective-permute-start(bf16[4,2,32,2048]{3,2,0,1:T(8,128)(2,1)S(1)} %fusion.2), channel_id=1, source_target_pairs={{0,16},{8,24},{16,0},{24,8},{1,17},{9,25},{17,1},{25,9},{2,18},{10... | collective-permute-start | bytes 3145736 | tf_op jit(solution)/shard_map/ppermute | solution.py:215
  138.7 15.1 %collective-permute-start.18 = (bf16[4,16,1024]{2,1,0:T(8,128)(2,1)S(1)}, bf16[4,16,1024]{2,1,0:T(8,128)(2,1)S(1)}, u32[]{:S(2)}, u32[]{:S(2)}) collective-permute-start(bf16[4,16,1024]{2,1,0:T(8,128)(2,1)S(1)} %copy-done.29), channel_id=1, source_target_pairs={{0,5},{1,4},{2,7},{3,6},{4,1},{5,0},{6,3},{7,2},{8,13},{9,12},{10,... | collective-permute-start | bytes 393224 | tf_op jit(solution)/shard_map/ppermute | solution.py:215
  141.8 12.0 %collective-permute-start.19 = (bf16[4,16,1024]{2,1,0:T(8,128)(2,1)S(1)}, bf16[4,16,1024]{2,1,0:T(8,128)(2,1)S(1)}, u32[]{:S(2)}, u32[]{:S(2)}) collective-permute-start(bf16[4,16,1024]{2,1,0:T(8,128)(2,1)S(1)} %copy-done.31), channel_id=1, source_target_pairs={{0,6},{1,7},{2,4},{3,5},{4,2},{5,3},{6,0},{7,1},{8,14},{9,15},{10,... | collective-permute-start | bytes 393224 | tf_op jit(solution)/shard_map/ppermute | solution.py:215
  158.7 13.3 %collective-permute-start.29 = (bf16[4,32,2048]{2,1,0:T(8,128)(2,1)S(1)}, bf16[4,32,2048]{2,1,0:T(8,128)(2,1)S(1)}, u32[]{:S(2)}, u32[]{:S(2)}) collective-permute-start(bf16[4,32,2048]{2,1,0:T(8,128)(2,1)S(1)} %fusion.7), channel_id=1, source_target_pairs={{0,16},{8,24},{16,0},{24,8},{1,17},{9,25},{17,1},{25,9},{2,18},{10... | collective-permute-start | bytes 1572872 | tf_op jit(solution)/shard_map/ppermute | solution.py:215
  162.0 15.9 %collective-permute-start.23 = (bf16[4,32,2048]{2,1,0:T(8,128)(2,1)S(1)}, bf16[4,32,2048]{2,1,0:T(8,128)(2,1)S(1)}, u32[]{:S(2)}, u32[]{:S(2)}) collective-permute-start(bf16[4,32,2048]{2,1,0:T(8,128)(2,1)S(1)} %fusion.6), channel_id=1, source_target_pairs={{0,1},{1,0},{2,3},{3,2},{4,5},{5,4},{6,7},{7,6},{8,9},{9,8},{10,11... | collective-permute-start | bytes 1572872 | tf_op jit(solution)/shard_map/ppermute | solution.py:215
  176.1 17.2 %collective-permute-start.31 = (bf16[32,2048]{1,0:T(8,128)(2,1)S(1)}, bf16[32,2048]{1,0:T(8,128)(2,1)S(1)}, u32[]{:S(2)}, u32[]{:S(2)}) collective-permute-start(bf16[32,2048]{1,0:T(8,128)(2,1)S(1)} %get-tuple-element.97), channel_id=1, source_target_pairs={{0,4},{1,5},{2,6},{3,7},{4,0},{5,1},{6,2},{7,3},{8,12},{9,13},{10,... | collective-permute-start | bytes 393224 | tf_op jit(solution)/shard_map/ppermute | solution.py:215
  177.9 15.4 %collective-permute-start.30 = (bf16[32,2048]{1,0:T(8,128)(2,1)S(1)}, bf16[32,2048]{1,0:T(8,128)(2,1)S(1)}, u32[]{:S(2)}, u32[]{:S(2)}) collective-permute-start(bf16[32,2048]{1,0:T(8,128)(2,1)S(1)} %get-tuple-element.95), channel_id=1, source_target_pairs={{0,2},{1,3},{2,0},{3,1},{4,6},{5,7},{6,4},{7,5},{8,10},{9,11},{10,... | collective-permute-start | bytes 393224 | tf_op jit(solution)/shard_map/ppermute | solution.py:215
  178.1 15.9 %collective-permute-start.26 = (bf16[32,2048]{1,0:T(8,128)(2,1)S(1)}, bf16[32,2048]{1,0:T(8,128)(2,1)S(1)}, u32[]{:S(2)}, u32[]{:S(2)}) collective-permute-start(bf16[32,2048]{1,0:T(8,128)(2,1)S(1)} %get-tuple-element.93), channel_id=1, source_target_pairs={{0,6},{1,7},{2,4},{3,5},{4,2},{5,3},{6,0},{7,1},{8,14},{9,15},{10,... | collective-permute-start | bytes 393224 | tf_op jit(solution)/shard_map/ppermute | solution.py:215
  180.7 17.2 %collective-permute-start.25 = (bf16[32,2048]{1,0:T(8,128)(2,1)S(1)}, bf16[32,2048]{1,0:T(8,128)(2,1)S(1)}, u32[]{:S(2)}, u32[]{:S(2)}) collective-permute-start(bf16[32,2048]{1,0:T(8,128)(2,1)S(1)} %get-tuple-element.94), channel_id=1, source_target_pairs={{0,4},{1,5},{2,6},{3,7},{4,0},{5,1},{6,2},{7,3},{8,12},{9,13},{10,... | collective-permute-start | bytes 393224 | tf_op jit(solution)/shard_map/ppermute | solution.py:215
  181.6 16.4 %collective-permute-start.24 = (bf16[32,2048]{1,0:T(8,128)(2,1)S(1)}, bf16[32,2048]{1,0:T(8,128)(2,1)S(1)}, u32[]{:S(2)}, u32[]{:S(2)}) collective-permute-start(bf16[32,2048]{1,0:T(8,128)(2,1)S(1)} %get-tuple-element.92), channel_id=1, source_target_pairs={{0,2},{1,3},{2,0},{3,1},{4,6},{5,7},{6,4},{7,5},{8,10},{9,11},{10,... | collective-permute-start | bytes 393224 | tf_op jit(solution)/shard_map/ppermute | solution.py:215
  (52 other events, 228.3 us)

commit v2 on v1

--- a/solution.py
+++ b/solution.py
@@ -12,7 +12,7 @@
 CHUNKS = 2
 EPSILON = 1e-06
 LOWEST = -1e30
-VMEM_LIMIT = 48 * 1024 * 1024
+MIB = 1024 * 1024
 
 
 def contract(left, right, dims):
@@ -50,36 +50,71 @@
             pl.BlockSpec(memory_space=pltpu.VMEM),
         ],
         out_specs=[pl.BlockSpec(memory_space=pltpu.VMEM)] * (n_slots * n_chunks),
-        compiler_params=pltpu.CompilerParams(vmem_limit_bytes=VMEM_LIMIT),
+        compiler_params=pltpu.CompilerParams(vmem_limit_bytes=16 * MIB),
     )(me, clips.reshape(cut), cotangent.reshape(cut))
     return [out[chunk * n_slots : (chunk + 1) * n_slots] for chunk in range(n_chunks)]
 
 
 def place_kernel(n_slots, me_ref, *refs):
-    out_ref = refs[n_slots]
-    for slot in range(n_slots):
-        out_ref[:, me_ref[0] ^ slot] = refs[slot][...]
-
-
-def place(me, blocks):
-    n_slots = len(blocks)
-    n_clips, n_positions, width = blocks[0].shape
+    out_ref = refs[-1]
+    for i, ref in enumerate(refs[:-1]):
+        depth = ref.shape[0]
+        here = pl.ds(i // n_slots * depth, depth)
+        out_ref[here, me_ref[0] ^ (i % n_slots)] = ref[...]
+
+
+def place(me, chunks):
+    n_slots = len(chunks[0])
+    n_clips, n_positions, width = chunks[0][0].shape
+    blocks = [block for chunk in chunks for block in chunk]
+    shape = (n_clips * len(chunks), n_slots, n_positions, width)
     return pl.pallas_call(
         functools.partial(place_kernel, n_slots),
-        out_shape=jax.ShapeDtypeStruct((n_clips, n_slots, n_positions, width), blocks[0].dtype),
+        out_shape=jax.ShapeDtypeStruct(shape, blocks[0].dtype),
         in_specs=[pl.BlockSpec(memory_space=pltpu.SMEM)]
-        + [pl.BlockSpec(memory_space=pltpu.VMEM)] * n_slots,
+        + [pl.BlockSpec(memory_space=pltpu.VMEM)] * len(blocks),
         out_specs=pl.BlockSpec(memory_space=pltpu.VMEM),
-        compiler_params=pltpu.CompilerParams(vmem_limit_bytes=VMEM_LIMIT),
+        compiler_params=pltpu.CompilerParams(vmem_limit_bytes=16 * MIB),
     )(me, *blocks)
+
+
+def product_kernel(n_x, which_ref, normed_ref, mixed_ref, dq_ref, dk_ref, dv_ref, cot_ref, first_ref, second_ref):
+    width = normed_ref.shape[1]
+    rest = width // (2 * n_x)
+    for x in range(n_x):
+        columns = pl.ds(pl.multiple_of((2 * x + which_ref[0]) * rest, rest), rest)
+        rows = pl.ds(x * rest, rest)
+        left = normed_ref[:, columns].T
+        for ref, right, start in ((first_ref, dq_ref, 0), (first_ref, dk_ref, width), (second_ref, dv_ref, 0)):
+            ref[rows, pl.ds(start, width)] = contract(left, right[...], ((1,), (0,))).astype(jnp.bfloat16)
+        left = mixed_ref[:, columns].T
+        second_ref[rows, pl.ds(width, width)] = contract(left, cot_ref[...], ((1,), (0,))).astype(jnp.bfloat16)
+
+
+def products(which, n_x, normed, mixed, dq, dk, dv, cot):
+    rows, width = normed.shape
+    half = jax.ShapeDtypeStruct((width // 2, 2 * width), jnp.bfloat16)
+    return pl.pallas_call(
+        functools.partial(product_kernel, n_x),
+        out_shape=[half, half],
+        in_specs=[pl.BlockSpec(memory_space=pltpu.SMEM)]
+        + [pl.BlockSpec(memory_space=pltpu.VMEM)] * 6,
+        out_specs=[pl.BlockSpec(memory_space=pltpu.VMEM)] * 2,
+        compiler_params=pltpu.CompilerParams(vmem_limit_bytes=24 * MIB),
+        cost_estimate=pl.CostEstimate(
+            flops=4 * rows * width * width,
+            bytes_accessed=12 * rows * width + 4 * width * width,
+            transcendentals=0,
+        ),
+    )(which, normed, mixed, dq, dk, dv, cot)
 
 
 def sublayer_kernel(n_clips, n_positions, n_pieces, n_aliased, *refs):
     pieces, refs = refs[:n_pieces], refs[n_pieces:]
     wq_ref, wk_ref, wv_ref, wo_ref = refs[:4]
     refs = refs[4 + n_aliased :]
-    normed_ref, cot_ref, mixed_ref, grads_ref = refs[:4]
-    dx_refs, total_ref = refs[4:-1], refs[-1]
+    normed_ref, cot_ref, mixed_ref, dq_ref, dk_ref, dv_ref = refs[:6]
+    dx_refs, total_ref = refs[6:-1], refs[-1]
     step = pl.program_id(0)
     rows = normed_ref.shape[0] // n_clips
     span = rows // n_pieces
@@ -135,15 +170,15 @@
         mixed = contract(low.reshape(GROUP * rows, rows), values, ((0,), (0,)))
         mixed_ref[here] = mixed.astype(jnp.bfloat16)
         dq = contract(score_grad.reshape(GROUP * rows, rows), keys, ((0,), (0,)))
-        grads_ref[here, :wide] = dq.astype(jnp.bfloat16)
+        dq_ref[here] = dq.astype(jnp.bfloat16)
         dk = contract(side_by_side(score_grad), stacked(queries), ((1,), (0,)))
-        grads_ref[here, wide : 2 * wide] = dk.astype(jnp.bfloat16)
+        dk_ref[here] = dk.astype(jnp.bfloat16)
         dv = contract(side_by_side(low), stacked(upstream), ((1,), (0,)))
-        grads_ref[here, 2 * wide :] = dv.astype(jnp.bfloat16)
-
-    part = contract(grads_ref[:, :wide], wq_ref[...], ((1,), (1,)))
-    part += contract(grads_ref[:, wide : 2 * wide], wk_ref[...], ((1,), (1,)))
-    part += contract(grads_ref[:, 2 * wide :], wv_ref[...], ((1,), (1,)))
+        dv_ref[here] = dv.astype(jnp.bfloat16)
+
+    part = contract(dq_ref[...], wq_ref[...], ((1,), (1,)))
+    part += contract(dk_ref[...], wk_ref[...], ((1,), (1,)))
+    part += contract(dv_ref[...], wv_ref[...], ((1,), (1,)))
 
     @pl.when(step == 0)
     def _():
@@ -180,9 +215,8 @@
         return pl.BlockSpec(shape, lambda j: (0,) * len(shape))
 
     flat = jax.ShapeDtypeStruct((n_chunks * rows, width), jnp.bfloat16)
-    grads = jax.ShapeDtypeStruct((n_chunks * rows, 3 * width), jnp.bfloat16)
-    dx = jax.ShapeDtypeStruct((n_chunks * n_clips, span, width), jnp.bfloat16)
-    out_shape = [flat, flat, flat, grads] + [dx] * n_pieces
+    dx = jax.ShapeDtypeStruct((n_clips, span, width), jnp.bfloat16)
+    out_shape = [flat] * 6 + [dx] * n_pieces
     aliased = [] if before is None else list(before)
     first = n_pieces + 4
     return pl.pallas_call(
@@ -196,13 +230,12 @@
         out_specs=[
             pl.BlockSpec((rows, width), lambda j: (chunk, 0)),
             pl.BlockSpec((rows, width), lambda j: (chunk, 0)),
-            pl.BlockSpec((rows, wide), lambda j: (chunk, j)),
-            pl.BlockSpec((rows, 3 * wide), lambda j: (chunk, j)),
         ]
-        + [pl.BlockSpec((n_clips, span, width), lambda j: (chunk, 0, 0))] * n_pieces,
+        + [pl.BlockSpec((rows, wide), lambda j: (chunk, j))] * 4
+        + [whole(dx.shape)] * n_pieces,
         scratch_shapes=[pltpu.VMEM((rows, width), jnp.float32)],
         input_output_aliases={first + i: i for i in range(len(aliased))},
-        compiler_params=pltpu.CompilerParams(vmem_limit_bytes=VMEM_LIMIT),
+        compiler_params=pltpu.CompilerParams(vmem_limit_bytes=28 * MIB),
         cost_estimate=pl.CostEstimate(
             flops=2 * rows * width * (7 * width + 24 * 128),
             bytes_accessed=16 * rows * width + 8 * width * width,
@@ -215,75 +248,94 @@
     return lax.ppermute(block, axis, [(i, i ^ distance) for i in range(size)])
 
 
-def scatter_sum(parts, axis, size, stride, count):
-    me = lax.axis_index(axis) // stride % count
-    total = lax.dynamic_index_in_dim(parts, me, 0, keepdims=False).astype(jnp.float32)
+def digit(axis, stride, count):
+    return lax.axis_index(axis) // stride % count
+
+
+def part(addends, index, dim):
+    return [lax.dynamic_index_in_dim(a, index, dim, keepdims=False) for a in addends]
+
+
+def summed(addends):
+    total = addends[0].astype(jnp.float32)
+    for a in addends[1:]:
+        total += a.astype(jnp.float32)
+    return total
+
+
+def scatter(addends, dim, axis, size, stride, count):
+    me = digit(axis, stride, count)
+    kept = part(addends, me, dim)
     for j in range(1, count):
-        block = lax.dynamic_index_in_dim(parts, me ^ j, 0, keepdims=False)
-        total += swap(block.astype(jnp.bfloat16), axis, size, j * stride).astype(jnp.float32)
-    return total
+        sent = summed(part(addends, me ^ j, dim)).astype(jnp.bfloat16)
+        kept.append(swap(sent, axis, size, j * stride))
+    return kept
+
+
+def after(values, done):
+    values, _ = lax.optimization_barrier((values, done))
+    return values
 
 
 def shards(n_clip_devices, n_tm, clips, w_qkv, w_out, cotangent):
     n_clips, _, n_patches, width = clips.shape
     n_positions = n_patches // n_tm
     me = lax.axis_index("tm").reshape(1)
-
-    chunks = pick(me, clips, cotangent, n_tm, CHUNKS)
     joined = n_positions % 16 != 0
-    results = None
-    for chunk, blocks in enumerate(chunks):
-        pieces = [blocks[0]] + [swap(blocks[k], "tm", n_tm, k) for k in range(1, n_tm)]
+    order = range(n_tm - 1, 0, -1)
+    far = range(n_tm // 2, n_tm)
+
+    def exchanged(blocks):
+        return {0: blocks[0]} | {k: swap(blocks[k], "tm", n_tm, k) for k in order}
+
+    arrived = []
+    for blocks in pick(me, clips, cotangent, n_tm, CHUNKS):
+        if arrived:
+            blocks = after(blocks, [arrived[-1][k] for k in far])
+        arrived.append(exchanged(blocks))
+    results, dx = None, []
+    for chunk, pieces in enumerate(arrived):
+        pieces = [pieces[k] for k in range(n_tm)]
         if joined:
             pieces = [jnp.stack(pieces, axis=2).reshape(2, n_clips // CHUNKS, -1, width)]
-        results = sublayer(pieces, w_qkv, w_out, chunk, CHUNKS, n_positions, results)
-    normed, cot, mixed, grads = results[:4]
-    dx = list(results[4:])
-    if joined:
-        cut = dx[0].reshape(n_clips, n_tm, n_positions, width)
-        dx = [cut[:, k] for k in range(n_tm)]
-    dx = [dx[0]] + [swap(dx[k], "tm", n_tm, k) for k in range(1, n_tm)]
-    grad_clips = place(me, dx).reshape(clips.shape)
-
-    cores = 2
-    n_x = n_clip_devices // cores
-    n_y = 2
-    n_z = n_tm // n_y
-    core = lax.axis_index("clip") % cores
-    rest = width // (n_x * cores)
-
-    def chosen(rows, which):
-        cut = rows.reshape(rows.shape[0], n_x, cores, rest)
-        return lax.dynamic_index_in_dim(cut, which, 2, keepdims=False).reshape(rows.shape[0], -1)
-
-    half = 2 * width
-
-    def first_half(which):
-        left = chosen(normed, which)
-        return contract(left, grads[:, :half], ((0,), (0,))).astype(jnp.bfloat16)
-
-    def second_half(which):
-        left = contract(chosen(normed, which), grads[:, half:], ((0,), (0,)))
-        right = contract(chosen(mixed, which), cot, ((0,), (0,)))
-        return jnp.concatenate([left, right], axis=1).astype(jnp.bfloat16)
-
-    sums = []
-    for product in (first_half, second_half):
-        other = swap(product(1 - core), "clip", n_clip_devices, 1)
-        total = product(core).astype(jnp.float32) + other.astype(jnp.float32)
-        sums.append(total.reshape(n_x, n_z, n_y, -1, half))
-    first, second = sums
-    first = scatter_sum(first, "clip", n_clip_devices, cores, n_x)
-    second = scatter_sum(second.transpose(2, 0, 1, 3, 4), "tm", n_tm, 1, n_y)
-    first = scatter_sum(first.transpose(1, 0, 2, 3), "tm", n_tm, 1, n_y)
-    second = scatter_sum(second, "clip", n_clip_devices, cores, n_x)
-    first = scatter_sum(first, "tm", n_tm, n_y, n_z)
-    second = scatter_sum(second, "tm", n_tm, n_y, n_z)
-
-    groups = HEADS // GROUP
-    grad_qkv = jnp.concatenate([first, second[:, :width]], axis=1)
-    grad_qkv = grad_qkv.reshape(-1, groups, 3, width // groups).transpose(0, 2, 1, 3)
-    return (grad_clips, grad_qkv.reshape(-1, 3 * width), second[:, width:])
+        out = sublayer(pieces, w_qkv, w_out, chunk, CHUNKS, n_positions, results)
+        results, blocks = out[:6], list(out[6:])
+        if joined:
+            cut = blocks[0].reshape(n_clips // CHUNKS, n_tm, n_positions, width)
+            blocks = [cut[:, k] for k in range(n_tm)]
+        dx.append(blocks)
+    normed, cot, mixed, dq, dk, dv = results
+
+    cores, n_y = 2, 2
+    n_x, n_z = n_clip_devices // cores, n_tm // n_y
+    core = digit("clip", 1, cores)
+    rest = width // (cores * n_x * n_z * n_y)
+    factors = (normed, mixed, dq, dk, dv, cot)
+    sent = products((1 - core).reshape(1), n_x, *factors)
+    kept = products(core.reshape(1), n_x, *after(factors, sent))
+    first, second = (
+        [a.reshape(n_x, n_z, n_y, rest, -1) for a in (mine, swap(theirs, "clip", n_clip_devices, 1))]
+        for mine, theirs in zip(kept, sent)
+    )
+    for chunk in range(CHUNKS):
+        done = [arrived[-1][k] for k in far] if chunk < CHUNKS - 1 else sent
+        dx[chunk] = exchanged(after(dx[chunk], done))
+    grad_clips = place(me, [[d[k] for k in range(n_tm)] for d in dx]).reshape(clips.shape)
+
+    first = scatter(first, 0, "clip", n_clip_devices, cores, n_x)
+    second = scatter(second, 2, "tm", n_tm, 1, n_y)
+    first = scatter(first, 1, "tm", n_tm, 1, n_y)
+    second = scatter(second, 0, "clip", n_clip_devices, cores, n_x)
+    z = digit("tm", n_y, n_z)
+
+    def both(index):
+        return jnp.concatenate([summed(part(a, index, 0)) for a in (first, second)], axis=-1)
+
+    total = both(z)
+    for j in range(1, n_z):
+        other = swap(both(z ^ j).astype(jnp.bfloat16), "tm", n_tm, j * n_y)
+        total += other.astype(jnp.float32)
+    return (grad_clips, total[:, : 3 * width], total[:, 3 * width :])
 
 
 def solution(mesh):

time: 200 us -> 203 us (1.015)
  waiting for transfers between devices: 46.2 us -> 68.9 us
  local copies, waits for them, and re-layouts: 43.1 us -> 24.3 us
  matrix products: 11.5 us -> 0 us
  Pallas kernels: 26.9 us -> 31.1 us
  other arithmetic: 11 us -> 14.3 us
  starting transfers between devices: 59.6 us -> 62.7 us
    ppermute x33 -> x37, waiting for transfers between devices: 46.2 us -> 68.9 us  [swap(): return lax.ppermute(block, axis, [(i, i ^ distance) for i in range(size)])]
    dot_general x6 -> x0, matrix products: 11.5 us -> none  [contract(): lax.dot_general(left, right, (dims, ((), ())), preferred_element_type=jnp...]
    convert_element_type x0 -> x4, other arithmetic: none -> 10.6 us  [scatter(): sent = summed(part(addends, me ^ j, dim)).astype(jnp.bfloat16)]
    add x8 -> x1, other arithmetic: 9.48 us -> 0.12 us  [shards(): total += other.astype(jnp.float32)]
    unnamed x90 -> x112, local copies, waits for them, and re-layouts: 30.7 us -> 22.9 us
    dynamic_slice x1 -> x0, local copies, waits for them, and re-layouts: 6.76 us -> none  [chosen(): lax.dynamic_index_in_dim(cut, which, 2, keepdims=False)]
    pallas_call x0 -> x2, Pallas kernels: none -> 6.5 us  [products(): pl.pallas_call(functools.partial(product_kernel, n_x), out_shape=[half, h...]
    reshape x4 -> x0, local copies, waits for them, and re-layouts: 4.36 us -> none  [the longest x2 3.13 us: chosen(): cut = rows.reshape(rows.shape[0], n_x, cores, rest)]
  transfers between devices with their start and end apart: 33 -> 37, of which waited for: 8 -> 13; matrix products, arithmetic and copies ran while one was open for 11% -> 7% of each run, Pallas kernels for 7% -> 7%
where the time goes in v2:
time: 203 us
  waiting for transfers between devices  68.9 us (34%)
  starting transfers between devices  62.7 us (31%)
  Pallas kernels  31.1 us (15%)
  local copies, waits for them, and re-layouts  24.3 us (12%)
  other arithmetic  14.3 us (7%)
    ppermute x37, waiting for transfers between devices, swap(): return lax.ppermute(block, axis, [(i, i ^ distance) for i in range(size)])  68.9 us
    ppermute x37, starting transfers between devices, swap(): return lax.ppermute(block, axis, [(i, i ^ distance) for i in range(size)])  62.7 us
    unnamed x112, local copies, waits for them, and re-layouts  22.9 us
    pallas_call x2, Pallas kernels, sublayer(): pl.pallas_call(functools.partial(sublayer_kernel, n_clips, n_positions, n...  22.6 us
    convert_element_type x4, other arithmetic, scatter(): sent = summed(part(addends, me ^ j, dim)).astype(jnp.bfloat16)  10.6 us
    pallas_call x2, Pallas kernels, products(): pl.pallas_call(functools.partial(product_kernel, n_x), out_shape=[half, h...  6.5 us
  transfers between devices with their start and end apart: 37, of which 13 were waited for; matrix products, arithmetic and copies ran while one was open for 7% of the time, Pallas kernels for 7%

profile of v2, /device:TPU:0, one launch (start us, length us, event | category | flops | bytes accessed | tf_op | source)
XLA Modules:
  0.0 202.5 jit_solution(4760158910825404998)
XLA Ops:
  4.3 4.0 %collective-permute-start.3 = (bf16[2,2,16,1024]{3,2,1,0:T(8,128)(2,1)S(1)}, bf16[2,2,16,1024]{3,2,1,0:T(8,128)(2,1)S(1)}, u32[]{:S(2)}, u32[]{:S(2)}) collective-permute-start(bf16[2,2,16,1024]{3,2,1,0:T(8,128)(2,1)S(1)} %get-tuple-element.85), channel_id=1, source_target_pairs={{0,4},{1,5},{2,6},{3,7},{4,0},{5,1},{6,2},{7,3},{8,12},{9,13},{10,... | collective-permute-start | bytes 393224 | tf_op jit(solution)/shard_map/ppermute | solution.py:248
  9.6 3.6 %collective-permute-start.5 = (bf16[2,2,16,1024]{3,2,1,0:T(8,128)(2,1)S(1)}, bf16[2,2,16,1024]{3,2,1,0:T(8,128)(2,1)S(1)}, u32[]{:S(2)}, u32[]{:S(2)}) collective-permute-start(bf16[2,2,16,1024]{3,2,1,0:T(8,128)(2,1)S(1)} %get-tuple-element.87), channel_id=1, source_target_pairs={{0,6},{1,7},{2,4},{3,5},{4,2},{5,3},{6,0},{7,1},{8,14},{9,15},{10,... | collective-permute-start | bytes 393224 | tf_op jit(solution)/shard_map/ppermute | solution.py:248
  14.9 9.0 %collective-permute-done.3.refs_4_ = bf16[2,2,16,1024]{3,2,1,0:T(8,128)(2,1)S(1)} collective-permute-done((bf16[2,2,16,1024]{3,2,1,0:T(8,128)(2,1)S(1)}, bf16[2,2,16,1024]{3,2,1,0:T(8,128)(2,1)S(1)}, u32[]{:S(2)}, u32[]{:S(2)}) %collective-permute-start.3) | collective-permute-done | bytes 131104 | tf_op jit(solution)/shard_map/ppermute | solution.py:248
  23.9 4.1 %collective-permute-done.4.refs_5_ = bf16[2,2,16,1024]{3,2,1,0:T(8,128)(2,1)S(1)} collective-permute-done((bf16[2,2,16,1024]{3,2,1,0:T(8,128)(2,1)S(1)}, bf16[2,2,16,1024]{3,2,1,0:T(8,128)(2,1)S(1)}, u32[]{:S(2)}, u32[]{:S(2)}) %collective-permute-start.4) | collective-permute-done | bytes 131104 | tf_op jit(solution)/shard_map/ppermute | solution.py:248
  29.9 8.3 %collective-permute-start.7 = (bf16[2,2,16,1024]{3,2,1,0:T(8,128)(2,1)S(1)}, bf16[2,2,16,1024]{3,2,1,0:T(8,128)(2,1)S(1)}, u32[]{:S(2)}, u32[]{:S(2)}) collective-permute-start(bf16[2,2,16,1024]{3,2,1,0:T(8,128)(2,1)S(1)} %get-tuple-element.105), channel_id=1, source_target_pairs={{0,4},{1,5},{2,6},{3,7},{4,0},{5,1},{6,2},{7,3},{8,12},{9,13},{10,... | collective-permute-start | bytes 393224 | tf_op jit(solution)/shard_map/ppermute | solution.py:248
  39.5 4.7 %collective-permute-start.10 = (bf16[2,2,16,1024]{3,2,1,0:T(8,128)(2,1)}, bf16[2,2,16,1024]{3,2,1,0:T(8,128)(2,1)S(1)}, u32[]{:S(2)}, u32[]{:S(2)}) collective-permute-start(bf16[2,2,16,1024]{3,2,1,0:T(8,128)(2,1)} %get-tuple-element.108), channel_id=1, source_target_pairs={{0,7},{1,6},{2,5},{3,4},{4,3},{5,2},{6,1},{7,0},{8,15},{9,14},{10,... | collective-permute-start | bytes 393224 | tf_op jit(solution)/shard_map/ppermute | solution.py:248
  45.5 5.4 %collective-permute-done.7.refs_4_ = bf16[2,2,16,1024]{3,2,1,0:T(8,128)(2,1)S(1)} collective-permute-done((bf16[2,2,16,1024]{3,2,1,0:T(8,128)(2,1)S(1)}, bf16[2,2,16,1024]{3,2,1,0:T(8,128)(2,1)S(1)}, u32[]{:S(2)}, u32[]{:S(2)}) %collective-permute-start.7) | collective-permute-done | bytes 131104 | tf_op jit(solution)/shard_map/ppermute | solution.py:248
  51.6 3.5 %collective-permute-done.8.refs_5_ = bf16[2,2,16,1024]{3,2,1,0:T(8,128)(2,1)S(1)} collective-permute-done((bf16[2,2,16,1024]{3,2,1,0:T(8,128)(2,1)S(1)}, bf16[2,2,16,1024]{3,2,1,0:T(8,128)(2,1)S(1)}, u32[]{:S(2)}, u32[]{:S(2)}) %collective-permute-start.8) | collective-permute-done | bytes 131104 | tf_op jit(solution)/shard_map/ppermute | solution.py:248
  55.7 2.8 %copy-done = bf16[1024,3072]{1,0:T(8,128)(2,1)S(1)} copy-done((bf16[1024,3072]{1,0:T(8,128)(2,1)S(1)}, bf16[1024,3072]{1,0:T(8,128)(2,1)}, u32[]{:S(2)}) %copy-start) | copy-done | bytes 6291480
  63.9 11.2 %shard_map.68 = (bf16[512,1024]{1,0:T(8,128)(2,1)S(1)}, bf16[512,1024]{1,0:T(8,128)(2,1)S(1)}, bf16[512,1024]{1,0:T(8,128)(2,1)S(1)}, bf16[512,1024]{1,0:T(8,128...) custom-call(bf16[2,2,16,1024]{3,2,1,0:T(8,128)(2,1)S(1)} %get-tuple-, ...), custom_call_target="tpu_custom_call" | custom-call | flops 5368709120 | bytes 12582912 | tf_op jit(solution)/shard_map/pallas_call | solution.py:222
  75.9 11.4 %shard_map.69 = (bf16[512,1024]{1,0:T(8,128)(2,1)S(1)}, bf16[512,1024]{1,0:T(8,128)(2,1)S(1)}, bf16[512,1024]{1,0:T(8,128)(2,1)S(1)}, bf16[512,1024]{1,0:T(8,128...) custom-call(bf16[2,2,16,1024]{3,2,1,0:T(8,128)(2,1)S(1)} %get-tuple-, ...), custom_call_target="tpu_custom_call", output_to_operand_aliasing={{0}: (12, {}), {1}: (13, {}), {2}: (14, {}), {3}: (15, {}),... | custom-call | flops 5368709120 | bytes 12582912 | tf_op jit(solution)/shard_map/pallas_call | solution.py:222
  87.4 4.1 %shard_map.70 = (bf16[512,2048]{1,0:T(8,128)(2,1)}, bf16[512,2048]{1,0:T(8,128)(2,1)}) custom-call(s32[1]{0:T(128)} %bitcast.3.which_ref, bf16[512,1024]{1,0:T(8,128)(2,1)S(1)} %get-tuple-element.151.normed_ref, bf16[512,1024]{1,0:T(8,128)(2,1)S(1)} %get-tuple-element.152.mixed_ref, bf16[512,1024]{1,0:T(8,128)(2,1)S(1)} %get-tuple-element.153.dq_ref, ...), custom_call_target="tpu_custom_call" | custom-call | flops 2147483648 | bytes 10485760 | tf_op jit(solution)/shard_map/pallas_call | solution.py:97
  100.7 3.3 %fusion.1 = bf16[2,4,32,2048]{3,2,1,0:T(8,128)(2,1)} fusion(bf16[2,4,2,32,2048]{4,3,2,1,0:T(8,128)(2,1)} %bitcast.16, s32[]{:T(128)S(6)} %select_n.136, bf16[2,4,2,32,2048]{4,3,2,1,0:T(8,128)(2,1)S(1)} %bitcast.95), kind=kLoop, calls=%fused_computation.3 | loop fusion | flops 2097152 | bytes 3145732 | tf_op jit(solution)/shard_map/convert_element_type | solution.py:270
  104.2 2.6 %fusion = bf16[4,2,32,2048]{3,2,1,0:T(8,128)(2,1)} fusion(bf16[2,4,2,32,2048]{4,3,2,1,0:T(8,128)(2,1)} %bitcast.8, s32[]{:T(128)S(6)} %select_n.135, bf16[2,4,2,32,2048]{4,3,2,1,0:T(8,128)(2,1)S(1)} %bitcast.92), kind=kLoop, calls=%fused_computation.2 | loop fusion | flops 2097152 | bytes 3145732 | tf_op jit(solution)/shard_map/convert_element_type | solution.py:270
  108.3 21.3 %collective-permute-done.32 = bf16[2,4,32,2048]{3,2,1,0:T(8,128)(2,1)} collective-permute-done((bf16[2,4,32,2048]{3,2,1,0:T(8,128)(2,1)}, bf16[2,4,32,2048]{3,2,1,0:T(8,128)(2,1)}, u32[]{:S(2)}, u32[]{:S(2)}) %collective-permute-start.32) | collective-permute-done | bytes 1048608 | tf_op jit(solution)/shard_map/ppermute | solution.py:248
  140.8 4.5 %collective-permute-done.33 = bf16[4,32,2048]{2,1,0:T(8,128)(2,1)S(1)} collective-permute-done((bf16[4,32,2048]{2,1,0:T(8,128)(2,1)}, bf16[4,32,2048]{2,1,0:T(8,128)(2,1)S(1)}, u32[]{:S(2)}, u32[]{:S(2)}) %collective-permute-start.33) | collective-permute-done | bytes 524320 | tf_op jit(solution)/shard_map/ppermute | solution.py:248
  145.3 2.6 %collective-permute-start.14 = (bf16[2,16,1024]{2,1,0:T(8,128)(2,1)S(1)}, bf16[2,16,1024]{2,1,0:T(8,128)(2,1)S(1)}, u32[]{:S(2)}, u32[]{:S(2)}) collective-permute-start(bf16[2,16,1024]{2,1,0:T(8,128)(2,1)S(1)} %copy-done.45), channel_id=1, source_target_pairs={{0,4},{1,5},{2,6},{3,7},{4,0},{5,1},{6,2},{7,3},{8,12},{9,13},{10,... | collective-permute-start | bytes 196616 | tf_op jit(solution)/shard_map/ppermute | solution.py:248
  155.3 2.9 %collective-permute-start.16 = (bf16[2,16,1024]{2,1,0:T(8,128)(2,1)S(1)}, bf16[2,16,1024]{2,1,0:T(8,128)(2,1)S(1)}, u32[]{:S(2)}, u32[]{:S(2)}) collective-permute-start(bf16[2,16,1024]{2,1,0:T(8,128)(2,1)S(1)} %copy-done.37), channel_id=1, source_target_pairs={{0,6},{1,7},{2,4},{3,5},{4,2},{5,3},{6,0},{7,1},{8,14},{9,15},{10,... | collective-permute-start | bytes 196616 | tf_op jit(solution)/shard_map/ppermute | solution.py:248
  160.7 2.9 %collective-permute-start.36 = (bf16[32,4096]{1,0:T(8,128)(2,1)S(1)}, bf16[32,4096]{1,0:T(8,128)(2,1)S(1)}, u32[]{:S(2)}, u32[]{:S(2)}) collective-permute-start(bf16[32,4096]{1,0:T(8,128)(2,1)S(1)} %pad_maximum_fusion.2), channel_id=1, source_target_pairs={{0,6},{1,7},{2,4},{3,5},{4,2},{5,3},{6,0},{7,1},{8,14},{9,15},{10,... | collective-permute-start | bytes 786440 | tf_op jit(solution)/shard_map/ppermute | solution.py:248
  166.1 7.0 %collective-permute-start.22 = (bf16[2,16,1024]{2,1,0:T(8,128)(2,1)S(1)}, bf16[2,16,1024]{2,1,0:T(8,128)(2,1)S(1)}, u32[]{:S(2)}, u32[]{:S(2)}) collective-permute-start(bf16[2,16,1024]{2,1,0:T(8,128)(2,1)S(1)} %copy-done.47), channel_id=1, source_target_pairs={{0,2},{1,3},{2,0},{3,1},{4,6},{5,7},{6,4},{7,5},{8,10},{9,11},{10,... | collective-permute-start | bytes 196616 | tf_op jit(solution)/shard_map/ppermute | solution.py:248
  173.7 7.4 %collective-permute-done.22.refs_10_ = bf16[2,16,1024]{2,1,0:T(8,128)(2,1)S(1)} collective-permute-done((bf16[2,16,1024]{2,1,0:T(8,128)(2,1)S(1)}, bf16[2,16,1024]{2,1,0:T(8,128)(2,1)S(1)}, u32[]{:S(2)}, u32[]{:S(2)}) %collective-permute-start.22) | collective-permute-done | bytes 65568 | tf_op jit(solution)/shard_map/ppermute | solution.py:248
  184.0 5.3 %collective-permute-done.24.refs_12_ = bf16[2,16,1024]{2,1,0:T(8,128)(2,1)S(1)} collective-permute-done((bf16[2,16,1024]{2,1,0:T(8,128)(2,1)S(1)}, bf16[2,16,1024]{2,1,0:T(8,128)(2,1)S(1)}, u32[]{:S(2)}, u32[]{:S(2)}) %collective-permute-start.24) | collective-permute-done | bytes 65568 | tf_op jit(solution)/shard_map/ppermute | solution.py:248
  189.3 2.5 %collective-permute-start.26 = (bf16[2,16,1024]{2,1,0:T(8,128)(2,1)S(1)}, bf16[2,16,1024]{2,1,0:T(8,128)(2,1)S(1)}, u32[]{:S(2)}, u32[]{:S(2)}) collective-permute-start(bf16[2,16,1024]{2,1,0:T(8,128)(2,1)S(1)} %get-tuple-element.149), channel_id=1, source_target_pairs={{0,6},{1,7},{2,4},{3,5},{4,2},{5,3},{6,0},{7,1},{8,14},{9,15},{10,... | collective-permute-start | bytes 196616 | tf_op jit(solution)/shard_map/ppermute | solution.py:248
  195.4 4.5 %collective-permute-done.27.refs_15_ = bf16[2,16,1024]{2,1,0:T(8,128)(2,1)S(1)} collective-permute-done((bf16[2,16,1024]{2,1,0:T(8,128)(2,1)S(1)}, bf16[2,16,1024]{2,1,0:T(8,128)(2,1)S(1)}, u32[]{:S(2)}, u32[]{:S(2)}) %collective-permute-start.27) | collective-permute-done | bytes 65568 | tf_op jit(solution)/shard_map/ppermute | solution.py:248
  (180 shorter events, 62.3 us)
Async XLA Ops:
  4.3 19.6 %collective-permute-start.3 = (bf16[2,2,16,1024]{3,2,1,0:T(8,128)(2,1)S(1)}, bf16[2,2,16,1024]{3,2,1,0:T(8,128)(2,1)S(1)}, u32[]{:S(2)}, u32[]{:S(2)}) collective-permute-start(bf16[2,2,16,1024]{3,2,1,0:T(8,128)(2,1)S(1)} %get-tuple-element.85), channel_id=1, source_target_pairs={{0,4},{1,5},{2,6},{3,7},{4,0},{5,1},{6,2},{7,3},{8,12},{9,13},{10,... | collective-permute-start | bytes 393224 | tf_op jit(solution)/shard_map/ppermute | solution.py:248
  8.3 19.7 %collective-permute-start.4 = (bf16[2,2,16,1024]{3,2,1,0:T(8,128)(2,1)S(1)}, bf16[2,2,16,1024]{3,2,1,0:T(8,128)(2,1)S(1)}, u32[]{:S(2)}, u32[]{:S(2)}) collective-permute-start(bf16[2,2,16,1024]{3,2,1,0:T(8,128)(2,1)S(1)} %get-tuple-element.86), channel_id=1, source_target_pairs={{0,5},{1,4},{2,7},{3,6},{4,1},{5,0},{6,3},{7,2},{8,13},{9,12},{10,... | collective-permute-start | bytes 393224 | tf_op jit(solution)/shard_map/ppermute | solution.py:248
  9.6 19.0 %collective-permute-start.5 = (bf16[2,2,16,1024]{3,2,1,0:T(8,128)(2,1)S(1)}, bf16[2,2,16,1024]{3,2,1,0:T(8,128)(2,1)S(1)}, u32[]{:S(2)}, u32[]{:S(2)}) collective-permute-start(bf16[2,2,16,1024]{3,2,1,0:T(8,128)(2,1)S(1)} %get-tuple-element.87), channel_id=1, source_target_pairs={{0,6},{1,7},{2,4},{3,5},{4,2},{5,3},{6,0},{7,1},{8,14},{9,15},{10,... | collective-permute-start | bytes 393224 | tf_op jit(solution)/shard_map/ppermute | solution.py:248
  13.2 16.1 %collective-permute-start.6 = (bf16[2,2,16,1024]{3,2,1,0:T(8,128)(2,1)S(1)}, bf16[2,2,16,1024]{3,2,1,0:T(8,128)(2,1)S(1)}, u32[]{:S(2)}, u32[]{:S(2)}) collective-permute-start(bf16[2,2,16,1024]{3,2,1,0:T(8,128)(2,1)S(1)} %get-tuple-element.88), channel_id=1, source_target_pairs={{0,7},{1,6},{2,5},{3,4},{4,3},{5,2},{6,1},{7,0},{8,15},{9,14},{10,... | collective-permute-start | bytes 393224 | tf_op jit(solution)/shard_map/ppermute | solution.py:248
  13.2 25.0 %collective-permute-start = (bf16[2,2,16,1024]{3,2,1,0:T(8,128)(2,1)}, bf16[2,2,16,1024]{3,2,1,0:T(8,128)(2,1)S(1)}, u32[]{:S(2)}, u32[]{:S(2)}) collective-permute-start(bf16[2,2,16,1024]{3,2,1,0:T(8,128)(2,1)} %get-tuple-element.82), channel_id=1, source_target_pairs={{0,1},{1,0},{2,3},{3,2},{4,5},{5,4},{6,7},{7,6},{8,9},{9,8},{10,11... | collective-permute-start | bytes 393224 | tf_op jit(solution)/shard_map/ppermute | solution.py:248
  28.6 15.6 %collective-permute-start.2 = (bf16[2,2,16,1024]{3,2,1,0:T(8,128)(2,1)}, bf16[2,2,16,1024]{3,2,1,0:T(8,128)(2,1)S(1)}, u32[]{:S(2)}, u32[]{:S(2)}) collective-permute-start(bf16[2,2,16,1024]{3,2,1,0:T(8,128)(2,1)} %get-tuple-element.84), channel_id=1, source_target_pairs={{0,3},{1,2},{2,1},{3,0},{4,7},{5,6},{6,5},{7,4},{8,11},{9,10},{10,... | collective-permute-start | bytes 393224 | tf_op jit(solution)/shard_map/ppermute | solution.py:248
  29.9 21.0 %collective-permute-start.7 = (bf16[2,2,16,1024]{3,2,1,0:T(8,128)(2,1)S(1)}, bf16[2,2,16,1024]{3,2,1,0:T(8,128)(2,1)S(1)}, u32[]{:S(2)}, u32[]{:S(2)}) collective-permute-start(bf16[2,2,16,1024]{3,2,1,0:T(8,128)(2,1)S(1)} %get-tuple-element.105), channel_id=1, source_target_pairs={{0,4},{1,5},{2,6},{3,7},{4,0},{5,1},{6,2},{7,3},{8,12},{9,13},{10,... | collective-permute-start | bytes 393224 | tf_op jit(solution)/shard_map/ppermute | solution.py:248
  38.2 16.9 %collective-permute-start.8 = (bf16[2,2,16,1024]{3,2,1,0:T(8,128)(2,1)S(1)}, bf16[2,2,16,1024]{3,2,1,0:T(8,128)(2,1)S(1)}, u32[]{:S(2)}, u32[]{:S(2)}) collective-permute-start(bf16[2,2,16,1024]{3,2,1,0:T(8,128)(2,1)S(1)} %get-tuple-element.106), channel_id=1, source_target_pairs={{0,5},{1,4},{2,7},{3,6},{4,1},{5,0},{6,3},{7,2},{8,13},{9,12},{10,... | collective-permute-start | bytes 393224 | tf_op jit(solution)/shard_map/ppermute | solution.py:248
  38.9 36.9 %collective-permute-start.9 = (bf16[2,2,16,1024]{3,2,1,0:T(8,128)(2,1)}, bf16[2,2,16,1024]{3,2,1,0:T(8,128)(2,1)S(1)}, u32[]{:S(2)}, u32[]{:S(2)}) collective-permute-start(bf16[2,2,16,1024]{3,2,1,0:T(8,128)(2,1)} %get-tuple-element.107), channel_id=1, source_target_pairs={{0,6},{1,7},{2,4},{3,5},{4,2},{5,3},{6,0},{7,1},{8,14},{9,15},{10,... | collective-permute-start | bytes 393224 | tf_op jit(solution)/shard_map/ppermute | solution.py:248
  39.5 36.3 %collective-permute-start.10 = (bf16[2,2,16,1024]{3,2,1,0:T(8,128)(2,1)}, bf16[2,2,16,1024]{3,2,1,0:T(8,128)(2,1)S(1)}, u32[]{:S(2)}, u32[]{:S(2)}) collective-permute-start(bf16[2,2,16,1024]{3,2,1,0:T(8,128)(2,1)} %get-tuple-element.108), channel_id=1, source_target_pairs={{0,7},{1,6},{2,5},{3,4},{4,3},{5,2},{6,1},{7,0},{8,15},{9,14},{10,... | collective-permute-start | bytes 393224 | tf_op jit(solution)/shard_map/ppermute | solution.py:248
  44.9 30.9 %collective-permute-start.18 = (bf16[2,2,16,1024]{3,2,1,0:T(8,128)(2,1)}, bf16[2,2,16,1024]{3,2,1,0:T(8,128)(2,1)S(1)}, u32[]{:S(2)}, u32[]{:S(2)}) collective-permute-start(bf16[2,2,16,1024]{3,2,1,0:T(8,128)(2,1)} %get-tuple-element.118), channel_id=1, source_target_pairs={{0,1},{1,0},{2,3},{3,2},{4,5},{5,4},{6,7},{7,6},{8,9},{9,8},{10,11... | collective-permute-start | bytes 393224 | tf_op jit(solution)/shard_map/ppermute | solution.py:248
  51.6 24.3 %collective-permute-start.19 = (bf16[2,2,16,1024]{3,2,1,0:T(8,128)(2,1)}, bf16[2,2,16,1024]{3,2,1,0:T(8,128)(2,1)S(1)}, u32[]{:S(2)}, u32[]{:S(2)}) collective-permute-start(bf16[2,2,16,1024]{3,2,1,0:T(8,128)(2,1)} %get-tuple-element.119), channel_id=1, source_target_pairs={{0,2},{1,3},{2,0},{3,1},{4,6},{5,7},{6,4},{7,5},{8,10},{9,11},{10,... | collective-permute-start | bytes 393224 | tf_op jit(solution)/shard_map/ppermute | solution.py:248
  55.7 20.1 %collective-permute-start.20 = (bf16[2,2,16,1024]{3,2,1,0:T(8,128)(2,1)}, bf16[2,2,16,1024]{3,2,1,0:T(8,128)(2,1)S(1)}, u32[]{:S(2)}, u32[]{:S(2)}) collective-permute-start(bf16[2,2,16,1024]{3,2,1,0:T(8,128)(2,1)} %get-tuple-element.120), channel_id=1, source_target_pairs={{0,3},{1,2},{2,1},{3,0},{4,7},{5,6},{6,5},{7,4},{8,11},{9,10},{10,... | collective-permute-start | bytes 393224 | tf_op jit(solution)/shard_map/ppermute | solution.py:248
  104.1 25.5 %collective-permute-start.32 = (bf16[2,4,32,2048]{3,2,1,0:T(8,128)(2,1)}, bf16[2,4,32,2048]{3,2,1,0:T(8,128)(2,1)}, u32[]{:S(2)}, u32[]{:S(2)}) collective-permute-start(bf16[2,4,32,2048]{3,2,1,0:T(8,128)(2,1)} %fusion.1), channel_id=1, source_target_pairs={{0,1},{1,0},{2,3},{3,2},{4,5},{5,4},{6,7},{7,6},{8,9},{9,8},{10,11... | collective-permute-start | bytes 3145736 | tf_op jit(solution)/shard_map/ppermute | solution.py:248
  106.8 26.7 %collective-permute-start.29 = (bf16[4,2,32,2048]{3,2,1,0:T(8,128)(2,1)}, bf16[4,2,32,2048]{3,2,1,0:T(8,128)(2,1)}, u32[]{:S(2)}, u32[]{:S(2)}) collective-permute-start(bf16[4,2,32,2048]{3,2,1,0:T(8,128)(2,1)} %fusion), channel_id=1, source_target_pairs={{0,16},{8,24},{16,0},{24,8},{1,17},{9,25},{17,1},{25,9},{2,18},{10... | collective-permute-start | bytes 3145736 | tf_op jit(solution)/shard_map/ppermute | solution.py:248
  135.7 15.2 %collective-permute-start.30 = (bf16[4,32,2048]{2,1,0:T(8,128)(2,1)}, bf16[4,32,2048]{2,1,0:T(8,128)(2,1)}, u32[]{:S(2)}, u32[]{:S(2)}) collective-permute-start(bf16[4,32,2048]{2,1,0:T(8,128)(2,1)} %fusion.3), channel_id=1, source_target_pairs={{0,1},{1,0},{2,3},{3,2},{4,5},{5,4},{6,7},{7,6},{8,9},{9,8},{10,11... | collective-permute-start | bytes 1572872 | tf_op jit(solution)/shard_map/ppermute | solution.py:248
  136.2 19.0 %collective-permute-start.11 = (bf16[2,16,1024]{2,1,0:T(8,128)(2,1)S(1)}, bf16[2,16,1024]{2,1,0:T(8,128)(2,1)S(1)}, u32[]{:S(2)}, u32[]{:S(2)}) collective-permute-start(bf16[2,16,1024]{2,1,0:T(8,128)(2,1)S(1)} %copy-done.55), channel_id=1, source_target_pairs={{0,1},{1,0},{2,3},{3,2},{4,5},{5,4},{6,7},{7,6},{8,9},{9,8},{10,11... | collective-permute-start | bytes 196616 | tf_op jit(solution)/shard_map/ppermute | solution.py:248
  137.8 20.4 %collective-permute-start.12 = (bf16[2,16,1024]{2,1,0:T(8,128)(2,1)S(1)}, bf16[2,16,1024]{2,1,0:T(8,128)(2,1)S(1)}, u32[]{:S(2)}, u32[]{:S(2)}) collective-permute-start(bf16[2,16,1024]{2,1,0:T(8,128)(2,1)S(1)} %copy-done.53), channel_id=1, source_target_pairs={{0,2},{1,3},{2,0},{3,1},{4,6},{5,7},{6,4},{7,5},{8,10},{9,11},{10,... | collective-permute-start | bytes 196616 | tf_op jit(solution)/shard_map/ppermute | solution.py:248
  139.7 20.5 %collective-permute-start.13 = (bf16[2,16,1024]{2,1,0:T(8,128)(2,1)S(1)}, bf16[2,16,1024]{2,1,0:T(8,128)(2,1)S(1)}, u32[]{:S(2)}, u32[]{:S(2)}) collective-permute-start(bf16[2,16,1024]{2,1,0:T(8,128)(2,1)S(1)} %copy-done.51), channel_id=1, source_target_pairs={{0,3},{1,2},{2,1},{3,0},{4,7},{5,6},{6,5},{7,4},{8,11},{9,10},{10,... | collective-permute-start | bytes 196616 | tf_op jit(solution)/shard_map/ppermute | solution.py:248
  145.3 15.4 %collective-permute-start.14 = (bf16[2,16,1024]{2,1,0:T(8,128)(2,1)S(1)}, bf16[2,16,1024]{2,1,0:T(8,128)(2,1)S(1)}, u32[]{:S(2)}, u32[]{:S(2)}) collective-permute-start(bf16[2,16,1024]{2,1,0:T(8,128)(2,1)S(1)} %copy-done.45), channel_id=1, source_target_pairs={{0,4},{1,5},{2,6},{3,7},{4,0},{5,1},{6,2},{7,3},{8,12},{9,13},{10,... | collective-permute-start | bytes 196616 | tf_op jit(solution)/shard_map/ppermute | solution.py:248
  160.7 40.3 %collective-permute-start.36 = (bf16[32,4096]{1,0:T(8,128)(2,1)S(1)}, bf16[32,4096]{1,0:T(8,128)(2,1)S(1)}, u32[]{:S(2)}, u32[]{:S(2)}) collective-permute-start(bf16[32,4096]{1,0:T(8,128)(2,1)S(1)} %pad_maximum_fusion.2), channel_id=1, source_target_pairs={{0,6},{1,7},{2,4},{3,5},{4,2},{5,3},{6,0},{7,1},{8,14},{9,15},{10,... | collective-permute-start | bytes 786440 | tf_op jit(solution)/shard_map/ppermute | solution.py:248
  163.6 37.4 %collective-permute-start.35 = (bf16[32,4096]{1,0:T(8,128)(2,1)S(1)}, bf16[32,4096]{1,0:T(8,128)(2,1)S(1)}, u32[]{:S(2)}, u32[]{:S(2)}) collective-permute-start(bf16[32,4096]{1,0:T(8,128)(2,1)S(1)} %pad_maximum_fusion.1), channel_id=1, source_target_pairs={{0,4},{1,5},{2,6},{3,7},{4,0},{5,1},{6,2},{7,3},{8,12},{9,13},{10,... | collective-permute-start | bytes 786440 | tf_op jit(solution)/shard_map/ppermute | solution.py:248
  163.6 37.4 %collective-permute-start.34 = (bf16[32,4096]{1,0:T(8,128)(2,1)S(1)}, bf16[32,4096]{1,0:T(8,128)(2,1)S(1)}, u32[]{:S(2)}, u32[]{:S(2)}) collective-permute-start(bf16[32,4096]{1,0:T(8,128)(2,1)S(1)} %pad_maximum_fusion), channel_id=1, source_target_pairs={{0,2},{1,3},{2,0},{3,1},{4,6},{5,7},{6,4},{7,5},{8,10},{9,11},{10,... | collective-permute-start | bytes 786440 | tf_op jit(solution)/shard_map/ppermute | solution.py:248
  166.1 15.0 %collective-permute-start.22 = (bf16[2,16,1024]{2,1,0:T(8,128)(2,1)S(1)}, bf16[2,16,1024]{2,1,0:T(8,128)(2,1)S(1)}, u32[]{:S(2)}, u32[]{:S(2)}) collective-permute-start(bf16[2,16,1024]{2,1,0:T(8,128)(2,1)S(1)} %copy-done.47), channel_id=1, source_target_pairs={{0,2},{1,3},{2,0},{3,1},{4,6},{5,7},{6,4},{7,5},{8,10},{9,11},{10,... | collective-permute-start | bytes 196616 | tf_op jit(solution)/shard_map/ppermute | solution.py:248
  (69 other events, 660.4 us)

commit v3 on v2

--- a/solution.py
+++ b/solution.py
@@ -1,4 +1,5 @@
 import functools
+import itertools
 
 import jax
 import jax.numpy as jnp
@@ -10,6 +11,9 @@
 HEADS = 16
 GROUP = 4
 CHUNKS = 2
+WINDOW = 5
+CORES = 2
+N_Y = 2
 EPSILON = 1e-06
 LOWEST = -1e30
 MIB = 1024 * 1024
@@ -26,18 +30,18 @@
     return centred * inverse, inverse
 
 
-def pick_kernel(n_slots, n_chunks, me_ref, x_ref, cot_ref, *out_refs):
+def pick_kernel(n_slots, n_chunks, ids_ref, x_ref, cot_ref, *out_refs):
     depth = x_ref.shape[0] // n_chunks
     for chunk in range(n_chunks):
         here = pl.ds(chunk * depth, depth)
         for slot in range(n_slots):
             out = out_refs[chunk * n_slots + slot]
-            block = me_ref[0] ^ slot
+            block = ids_ref[1] ^ slot
             out[0] = x_ref[here, block]
             out[1] = cot_ref[here, block]
 
 
-def pick(me, clips, cotangent, n_slots, n_chunks):
+def pick(ids, clips, cotangent, n_slots, n_chunks):
     n_clips, _, n_patches, width = clips.shape
     cut = (n_clips, n_slots, n_patches // n_slots, width)
     piece = jax.ShapeDtypeStruct((2, n_clips // n_chunks) + cut[2:], clips.dtype)
@@ -51,51 +55,53 @@
         ],
         out_specs=[pl.BlockSpec(memory_space=pltpu.VMEM)] * (n_slots * n_chunks),
         compiler_params=pltpu.CompilerParams(vmem_limit_bytes=16 * MIB),
-    )(me, clips.reshape(cut), cotangent.reshape(cut))
+    )(ids, clips.reshape(cut), cotangent.reshape(cut))
     return [out[chunk * n_slots : (chunk + 1) * n_slots] for chunk in range(n_chunks)]
 
 
-def place_kernel(n_slots, me_ref, *refs):
-    out_ref = refs[-1]
-    for i, ref in enumerate(refs[:-1]):
-        depth = ref.shape[0]
-        here = pl.ds(i // n_slots * depth, depth)
-        out_ref[here, me_ref[0] ^ (i % n_slots)] = ref[...]
-
-
-def place(me, chunks):
-    n_slots = len(chunks[0])
-    n_clips, n_positions, width = chunks[0][0].shape
-    blocks = [block for chunk in chunks for block in chunk]
-    shape = (n_clips * len(chunks), n_slots, n_positions, width)
-    return pl.pallas_call(
-        functools.partial(place_kernel, n_slots),
-        out_shape=jax.ShapeDtypeStruct(shape, blocks[0].dtype),
+def place_kernel(ids_ref, *refs):
+    for slot, ref in enumerate(refs[:-1]):
+        refs[-1][:, ids_ref[1] ^ slot] = ref[...]
+
+
+def place(ids, blocks):
+    n_clips, n_positions, width = blocks[0].shape
+    return pl.pallas_call(
+        place_kernel,
+        out_shape=jax.ShapeDtypeStruct((n_clips, len(blocks), n_positions, width), blocks[0].dtype),
         in_specs=[pl.BlockSpec(memory_space=pltpu.SMEM)]
         + [pl.BlockSpec(memory_space=pltpu.VMEM)] * len(blocks),
         out_specs=pl.BlockSpec(memory_space=pltpu.VMEM),
-        compiler_params=pltpu.CompilerParams(vmem_limit_bytes=16 * MIB),
-    )(me, *blocks)
-
-
-def product_kernel(n_x, which_ref, normed_ref, mixed_ref, dq_ref, dk_ref, dv_ref, cot_ref, first_ref, second_ref):
+        compiler_params=pltpu.CompilerParams(vmem_limit_bytes=8 * MIB),
+    )(ids, *blocks)
+
+
+def product_kernel(n_x, flip, ids_ref, normed_ref, mixed_ref, dq_ref, dk_ref, dv_ref, cot_ref, first_ref, second_ref):
     width = normed_ref.shape[1]
-    rest = width // (2 * n_x)
+    rest = width // (CORES * n_x)
+    core = lax.rem(ids_ref[0], CORES) ^ flip
+    cut = first_ref.shape[1:4]
     for x in range(n_x):
-        columns = pl.ds(pl.multiple_of((2 * x + which_ref[0]) * rest, rest), rest)
-        rows = pl.ds(x * rest, rest)
+        columns = pl.ds(pl.multiple_of((CORES * x + core) * rest, rest), rest)
+
+        def store(ref, start, left, right):
+            product = contract(left, right[...], ((1,), (0,)))
+            product = product.reshape(cut + (width,)).astype(jnp.bfloat16)
+            ref[x, :, :, :, pl.ds(start, width)] = product
+
         left = normed_ref[:, columns].T
-        for ref, right, start in ((first_ref, dq_ref, 0), (first_ref, dk_ref, width), (second_ref, dv_ref, 0)):
-            ref[rows, pl.ds(start, width)] = contract(left, right[...], ((1,), (0,))).astype(jnp.bfloat16)
-        left = mixed_ref[:, columns].T
-        second_ref[rows, pl.ds(width, width)] = contract(left, cot_ref[...], ((1,), (0,))).astype(jnp.bfloat16)
-
-
-def products(which, n_x, normed, mixed, dq, dk, dv, cot):
+        store(first_ref, 0, left, dq_ref)
+        store(first_ref, width, left, dk_ref)
+        store(second_ref, 0, left, dv_ref)
+        store(second_ref, width, mixed_ref[:, columns].T, cot_ref)
+
+
+def products(ids, flip, n_x, n_z, normed, mixed, dq, dk, dv, cot):
     rows, width = normed.shape
-    half = jax.ShapeDtypeStruct((width // 2, 2 * width), jnp.bfloat16)
-    return pl.pallas_call(
-        functools.partial(product_kernel, n_x),
+    rest = width // (CORES * n_x * n_z * N_Y)
+    half = jax.ShapeDtypeStruct((n_x, n_z, N_Y, rest, 2 * width), jnp.bfloat16)
+    return pl.pallas_call(
+        functools.partial(product_kernel, n_x, flip),
         out_shape=[half, half],
         in_specs=[pl.BlockSpec(memory_space=pltpu.SMEM)]
         + [pl.BlockSpec(memory_space=pltpu.VMEM)] * 6,
@@ -106,7 +112,81 @@
             bytes_accessed=12 * rows * width + 4 * width * width,
             transcendentals=0,
         ),
-    )(which, normed, mixed, dq, dk, dv, cot)
+    )(ids, normed, mixed, dq, dk, dv, cot)
+
+
+def summed(refs, index):
+    total = refs[0][index].astype(jnp.float32)
+    for ref in refs[1:]:
+        total += ref[index].astype(jnp.float32)
+    return total
+
+
+def halve_kernel(dim, axis, stride, ids_ref, *refs):
+    addends, sent_ref, kept_ref = refs[:-2], refs[-2], refs[-1]
+    me = lax.rem(lax.div(ids_ref[axis], stride), 2)
+    for index in itertools.product(*(range(n) for n in sent_ref.shape[:-2])):
+        sent_ref[index] = summed(addends, index[:dim] + (me ^ 1,) + index[dim:]).astype(jnp.bfloat16)
+    for index in itertools.product(*(range(n) for n in sent_ref.shape[:-2])):
+        kept_ref[index] = summed(addends, index[:dim] + (me,) + index[dim:])
+
+
+def halve(ids, addends, dim, axis, stride):
+    shape = addends[0].shape[:dim] + addends[0].shape[dim + 1 :]
+    return pl.pallas_call(
+        functools.partial(halve_kernel, dim, axis, stride),
+        out_shape=[jax.ShapeDtypeStruct(shape, jnp.bfloat16), jax.ShapeDtypeStruct(shape, jnp.float32)],
+        in_specs=[pl.BlockSpec(memory_space=pltpu.SMEM)]
+        + [pl.BlockSpec(memory_space=pltpu.VMEM)] * len(addends),
+        out_specs=[pl.BlockSpec(memory_space=pltpu.VMEM)] * 2,
+        compiler_params=pltpu.CompilerParams(vmem_limit_bytes=16 * MIB),
+    )(ids, *addends)
+
+
+def join_kernel(n_z, n_first, ids_ref, *refs):
+    addends, outs = refs[:-n_z], refs[-n_z:]
+    me = lax.div(ids_ref[1], N_Y)
+    half = addends[0].shape[-1]
+    for j in [*range(1, n_z), 0]:
+        for side, part in enumerate((addends[:n_first], addends[n_first:])):
+            total = summed(part, (me ^ j,))
+            outs[j][:, pl.ds(side * half, half)] = total.astype(outs[j].dtype)
+
+
+def join(ids, first, second, n_z):
+    rows, half = first[0].shape[1:]
+    own = jax.ShapeDtypeStruct((rows, 2 * half), jnp.float32)
+    other = jax.ShapeDtypeStruct((rows, 2 * half), jnp.bfloat16)
+    return pl.pallas_call(
+        functools.partial(join_kernel, n_z, len(first)),
+        out_shape=[own] + [other] * (n_z - 1),
+        in_specs=[pl.BlockSpec(memory_space=pltpu.SMEM)]
+        + [pl.BlockSpec(memory_space=pltpu.VMEM)] * (len(first) + len(second)),
+        out_specs=[pl.BlockSpec(memory_space=pltpu.VMEM)] * n_z,
+        compiler_params=pltpu.CompilerParams(vmem_limit_bytes=12 * MIB),
+    )(ids, *first, *second)
+
+
+def finish_kernel(*refs):
+    addends, (grad_qkv_ref, grad_out_ref) = refs[:-2], refs[-2:]
+    wide = grad_qkv_ref.shape[1]
+    everything = slice(None)
+    grad_qkv_ref[...] = summed(addends, (everything, pl.ds(0, wide)))
+    grad_out_ref[...] = summed(addends, (everything, pl.ds(wide, grad_out_ref.shape[1])))
+
+
+def finish(addends):
+    rows, columns = addends[0].shape
+    return pl.pallas_call(
+        finish_kernel,
+        out_shape=[
+            jax.ShapeDtypeStruct((rows, columns // 4 * 3), jnp.float32),
+            jax.ShapeDtypeStruct((rows, columns // 4), jnp.float32),
+        ],
+        in_specs=[pl.BlockSpec(memory_space=pltpu.VMEM)] * len(addends),
+        out_specs=[pl.BlockSpec(memory_space=pltpu.VMEM)] * 2,
+        compiler_params=pltpu.CompilerParams(vmem_limit_bytes=8 * MIB),
+    )(*addends)
 
 
 def sublayer_kernel(n_clips, n_positions, n_pieces, n_aliased, *refs):
@@ -215,7 +295,7 @@
         return pl.BlockSpec(shape, lambda j: (0,) * len(shape))
 
     flat = jax.ShapeDtypeStruct((n_chunks * rows, width), jnp.bfloat16)
-    dx = jax.ShapeDtypeStruct((n_clips, span, width), jnp.bfloat16)
+    dx = jax.ShapeDtypeStruct((n_chunks * n_clips, span, width), jnp.bfloat16)
     out_shape = [flat] * 6 + [dx] * n_pieces
     aliased = [] if before is None else list(before)
     first = n_pieces + 4
@@ -232,7 +312,7 @@
             pl.BlockSpec((rows, width), lambda j: (chunk, 0)),
         ]
         + [pl.BlockSpec((rows, wide), lambda j: (chunk, j))] * 4
-        + [whole(dx.shape)] * n_pieces,
+        + [pl.BlockSpec((n_clips, span, width), lambda j: (chunk, 0, 0))] * n_pieces,
         scratch_shapes=[pltpu.VMEM((rows, width), jnp.float32)],
         input_output_aliases={first + i: i for i in range(len(aliased))},
         compiler_params=pltpu.CompilerParams(vmem_limit_bytes=28 * MIB),
@@ -248,94 +328,68 @@
     return lax.ppermute(block, axis, [(i, i ^ distance) for i in range(size)])
 
 
-def digit(axis, stride, count):
-    return lax.axis_index(axis) // stride % count
-
-
-def part(addends, index, dim):
-    return [lax.dynamic_index_in_dim(a, index, dim, keepdims=False) for a in addends]
-
-
-def summed(addends):
-    total = addends[0].astype(jnp.float32)
-    for a in addends[1:]:
-        total += a.astype(jnp.float32)
-    return total
-
-
-def scatter(addends, dim, axis, size, stride, count):
-    me = digit(axis, stride, count)
-    kept = part(addends, me, dim)
-    for j in range(1, count):
-        sent = summed(part(addends, me ^ j, dim)).astype(jnp.bfloat16)
-        kept.append(swap(sent, axis, size, j * stride))
-    return kept
-
-
 def after(values, done):
     values, _ = lax.optimization_barrier((values, done))
     return values
 
 
+def inbound_order(n_tm, chunk):
+    far, near = list(range(n_tm - 1, n_tm // 2 - 1, -1)), list(range(1, n_tm // 2))
+    if chunk == CHUNKS - 1:
+        return far + near
+    cut = len(far) // 2
+    return far[:cut] + near[:1] + far[cut:] + near[1:]
+
+
 def shards(n_clip_devices, n_tm, clips, w_qkv, w_out, cotangent):
     n_clips, _, n_patches, width = clips.shape
     n_positions = n_patches // n_tm
-    me = lax.axis_index("tm").reshape(1)
+    n_x, n_z = n_clip_devices // CORES, n_tm // N_Y
     joined = n_positions % 16 != 0
-    order = range(n_tm - 1, 0, -1)
-    far = range(n_tm // 2, n_tm)
-
-    def exchanged(blocks):
-        return {0: blocks[0]} | {k: swap(blocks[k], "tm", n_tm, k) for k in order}
-
-    arrived = []
-    for blocks in pick(me, clips, cotangent, n_tm, CHUNKS):
-        if arrived:
-            blocks = after(blocks, [arrived[-1][k] for k in far])
-        arrived.append(exchanged(blocks))
-    results, dx = None, []
+    ids = jnp.stack([lax.axis_index("clip"), lax.axis_index("tm")]).astype(jnp.int32)
+
+    arrived, line = [], []
+    for chunk, blocks in enumerate(pick(ids, clips, cotangent, n_tm, CHUNKS)):
+        pieces = {0: blocks[0]}
+        for k in inbound_order(n_tm, chunk):
+            block = blocks[k]
+            if len(line) >= WINDOW:
+                block = after(block, line[-WINDOW])
+            pieces[k] = swap(block, "tm", n_tm, k)
+            line.append(pieces[k])
+        arrived.append([pieces[k] for k in range(n_tm)])
+    results = None
     for chunk, pieces in enumerate(arrived):
-        pieces = [pieces[k] for k in range(n_tm)]
         if joined:
             pieces = [jnp.stack(pieces, axis=2).reshape(2, n_clips // CHUNKS, -1, width)]
-        out = sublayer(pieces, w_qkv, w_out, chunk, CHUNKS, n_positions, results)
-        results, blocks = out[:6], list(out[6:])
-        if joined:
-            cut = blocks[0].reshape(n_clips // CHUNKS, n_tm, n_positions, width)
-            blocks = [cut[:, k] for k in range(n_tm)]
-        dx.append(blocks)
-    normed, cot, mixed, dq, dk, dv = results
-
-    cores, n_y = 2, 2
-    n_x, n_z = n_clip_devices // cores, n_tm // n_y
-    core = digit("clip", 1, cores)
-    rest = width // (cores * n_x * n_z * n_y)
+        results = sublayer(pieces, w_qkv, w_out, chunk, CHUNKS, n_positions, results)
+    normed, cot, mixed, dq, dk, dv = results[:6]
+    dx = list(results[6:])
+    if joined:
+        cut = dx[0].reshape(n_clips, n_tm, n_positions, width)
+        dx = [cut[:, k] for k in range(n_tm)]
+
     factors = (normed, mixed, dq, dk, dv, cot)
-    sent = products((1 - core).reshape(1), n_x, *factors)
-    kept = products(core.reshape(1), n_x, *after(factors, sent))
-    first, second = (
-        [a.reshape(n_x, n_z, n_y, rest, -1) for a in (mine, swap(theirs, "clip", n_clip_devices, 1))]
-        for mine, theirs in zip(kept, sent)
-    )
-    for chunk in range(CHUNKS):
-        done = [arrived[-1][k] for k in far] if chunk < CHUNKS - 1 else sent
-        dx[chunk] = exchanged(after(dx[chunk], done))
-    grad_clips = place(me, [[d[k] for k in range(n_tm)] for d in dx]).reshape(clips.shape)
-
-    first = scatter(first, 0, "clip", n_clip_devices, cores, n_x)
-    second = scatter(second, 2, "tm", n_tm, 1, n_y)
-    first = scatter(first, 1, "tm", n_tm, 1, n_y)
-    second = scatter(second, 0, "clip", n_clip_devices, cores, n_x)
-    z = digit("tm", n_y, n_z)
-
-    def both(index):
-        return jnp.concatenate([summed(part(a, index, 0)) for a in (first, second)], axis=-1)
-
-    total = both(z)
-    for j in range(1, n_z):
-        other = swap(both(z ^ j).astype(jnp.bfloat16), "tm", n_tm, j * n_y)
-        total += other.astype(jnp.float32)
-    return (grad_clips, total[:, : 3 * width], total[:, 3 * width :])
+    sent = products(ids, 1, n_x, n_z, *factors)
+    first, second = (swap(half, "clip", n_clip_devices, 1) for half in sent)
+    dx = after(dx, sent)
+    dx = [dx[0]] + [swap(dx[k], "tm", n_tm, k) for k in range(1, n_tm)]
+    own_first, own_second = products(ids, 0, n_x, n_z, *after(factors, sent))
+
+    sent, own_first = halve(ids, (own_first, first), 0, 0, CORES)
+    first = swap(sent, "clip", n_clip_devices, CORES)
+    sent, own_second = halve(ids, (own_second, second), 2, 1, 1)
+    second = swap(sent, "tm", n_tm, 1)
+    first, second = after((first, second), dx)
+    sent, own_first = halve(ids, (own_first, first), 1, 1, 1)
+    first = swap(sent, "tm", n_tm, 1)
+    sent, own_second = halve(ids, (own_second, second), 0, 0, CORES)
+    second = swap(sent, "clip", n_clip_devices, CORES)
+    total, *sent = join(ids, (own_first, first), (own_second, second), n_z)
+    grad_clips = place(ids, dx).reshape(clips.shape)
+    others = [swap(block, "tm", n_tm, (j + 1) * N_Y) for j, block in enumerate(sent)]
+    grad_qkv, grad_out = finish((total, *others))
+    return (grad_clips, grad_qkv, grad_out)
 
 
 def solution(mesh):

time: 203 us -> 181 us (0.89)
  local copies, waits for them, and re-layouts: 24.3 us -> 5.37 us
  other arithmetic: 14.3 us -> 0.08 us
  starting transfers between devices: 62.7 us -> 69.5 us
  Pallas kernels: 31.1 us -> 35.7 us
    unnamed x112 -> x10, local copies, waits for them, and re-layouts: 22.9 us -> 5.37 us
    convert_element_type x4 -> x0, other arithmetic: 10.6 us -> none  [scatter(): sent = summed(part(addends, me ^ j, dim)).astype(jnp.bfloat16)]
    ppermute x37 -> x30, starting transfers between devices: 62.7 us -> 69.5 us  [swap(): return lax.ppermute(block, axis, [(i, i ^ distance) for i in range(size)])]
    pallas_call x3 -> x9, Pallas kernels: 7.54 us -> 12.5 us  [the longest x2 5.88 us: products(): pl.pallas_call(functools.partial(product_kernel, n_x, flip), out_shape=[h...]
    another operation x2 -> x1, other arithmetic: 3.52 us -> 0.08 us  [shards(): jnp.stack([lax.axis_index('clip'), lax.axis_index('tm')]).astype(jnp.int32)]
    ppermute x37 -> x30, waiting for transfers between devices: 68.9 us -> 67.9 us  [swap(): return lax.ppermute(block, axis, [(i, i ^ distance) for i in range(size)])]
  transfers between devices with their start and end apart: 37 -> 30, of which waited for: 13 -> 11; matrix products, arithmetic and copies ran while one was open for 7% -> 0% of each run, Pallas kernels for 7% -> 10%
where the time goes in v3:
time: 181 us; the launch traced here: 179 us
  starting transfers between devices  69.5 us (38%)
  waiting for transfers between devices  67.9 us (38%)
  Pallas kernels  35.7 us (20%)
  local copies, waits for them, and re-layouts  5.37 us (3%)
    ppermute x30, starting transfers between devices, swap(): return lax.ppermute(block, axis, [(i, i ^ distance) for i in range(size)])  69.5 us
    ppermute x30, waiting for transfers between devices, swap(): return lax.ppermute(block, axis, [(i, i ^ distance) for i in range(size)])  67.9 us
    pallas_call x2, Pallas kernels, sublayer(): pl.pallas_call(functools.partial(sublayer_kernel, n_clips, n_positions, n...  22.6 us
    pallas_call x2, Pallas kernels, products(): pl.pallas_call(functools.partial(product_kernel, n_x, flip), out_shape=[h...  5.88 us
    unnamed x10, local copies, waits for them, and re-layouts  5.37 us
  transfers between devices with their start and end apart: 30, of which 11 were waited for; matrix products, arithmetic and copies ran while one was open for 0% of the time, Pallas kernels for 10%

profile of v3, /device:TPU:0, one launch (start us, length us, event | category | flops | bytes accessed | tf_op | source)
XLA Modules:
  0.0 179.5 jit_solution(6334542545774282929)
XLA Ops:
  4.0 5.1 %collective-permute-start = (bf16[2,2,16,1024]{3,2,1,0:T(8,128)(2,1)S(1)}, bf16[2,2,16,1024]{3,2,1,0:T(8,128)(2,1)S(1)}, u32[]{:S(2)}, u32[]{:S(2)}) collective-permute-start(bf16[2,2,16,1024]{3,2,1,0:T(8,128)(2,1)S(1)} %get-tuple-element.93), channel_id=1, source_target_pairs={{0,6},{1,7},{2,4},{3,5},{4,2},{5,3},{6,0},{7,1},{8,14},{9,15},{10,... | collective-permute-start | bytes 393224 | tf_op jit(solution)/shard_map/ppermute | solution.py:328
  10.6 2.8 %collective-permute-start.9 = (bf16[2,2,16,1024]{3,2,1,0:T(8,128)(2,1)S(1)}, bf16[2,2,16,1024]{3,2,1,0:T(8,128)(2,1)S(1)}, u32[]{:S(2)}, u32[]{:S(2)}) collective-permute-start(bf16[2,2,16,1024]{3,2,1,0:T(8,128)(2,1)S(1)} %get-tuple-element.108), channel_id=1, source_target_pairs={{0,7},{1,6},{2,5},{3,4},{4,3},{5,2},{6,1},{7,0},{8,15},{9,14},{10,... | collective-permute-start | bytes 393224 | tf_op jit(solution)/shard_map/ppermute | solution.py:328
  13.8 11.7 %collective-permute-start.1 = (bf16[2,2,16,1024]{3,2,1,0:T(8,128)(2,1)S(1)}, bf16[2,2,16,1024]{3,2,1,0:T(8,128)(2,1)S(1)}, u32[]{:S(2)}, u32[]{:S(2)}) collective-permute-start(bf16[2,2,16,1024]{3,2,1,0:T(8,128)(2,1)S(1)} %get-tuple-element.94), channel_id=1, source_target_pairs={{0,3},{1,2},{2,1},{3,0},{4,7},{5,6},{6,5},{7,4},{8,11},{9,10},{10,... | collective-permute-start | bytes 393224 | tf_op jit(solution)/shard_map/ppermute | solution.py:328
  27.7 3.7 %collective-permute-start.7 = (bf16[2,2,16,1024]{3,2,1,0:T(8,128)(2,1)S(1)}, bf16[2,2,16,1024]{3,2,1,0:T(8,128)(2,1)S(1)}, u32[]{:S(2)}, u32[]{:S(2)}) collective-permute-start(bf16[2,2,16,1024]{3,2,1,0:T(8,128)(2,1)S(1)} %get-tuple-element.104), channel_id=1, source_target_pairs={{0,6},{1,7},{2,4},{3,5},{4,2},{5,3},{6,0},{7,1},{8,14},{9,15},{10,... | collective-permute-start | bytes 393224 | tf_op jit(solution)/shard_map/ppermute | solution.py:328
  31.4 4.7 %collective-permute-start.10 = (bf16[2,2,16,1024]{3,2,1,0:T(8,128)(2,1)S(1)}, bf16[2,2,16,1024]{3,2,1,0:T(8,128)(2,1)S(1)}, u32[]{:S(2)}, u32[]{:S(2)}) collective-permute-start(bf16[2,2,16,1024]{3,2,1,0:T(8,128)(2,1)S(1)} %get-tuple-element.109), channel_id=1, source_target_pairs={{0,2},{1,3},{2,0},{3,1},{4,6},{5,7},{6,4},{7,5},{8,10},{9,11},{10,... | collective-permute-start | bytes 393224 | tf_op jit(solution)/shard_map/ppermute | solution.py:328
  39.8 5.6 %collective-permute-start.5 = (bf16[2,2,16,1024]{3,2,1,0:T(8,128)(2,1)S(1)}, bf16[2,2,16,1024]{3,2,1,0:T(8,128)(2,1)S(1)}, u32[]{:S(2)}, u32[]{:S(2)}) collective-permute-start(bf16[2,2,16,1024]{3,2,1,0:T(8,128)(2,1)S(1)} %get-tuple-element.100), channel_id=1, source_target_pairs={{0,2},{1,3},{2,0},{3,1},{4,6},{5,7},{6,4},{7,5},{8,10},{9,11},{10,... | collective-permute-start | bytes 393224 | tf_op jit(solution)/shard_map/ppermute | solution.py:328
  45.4 2.8 %collective-permute-start.8 = (bf16[2,2,16,1024]{3,2,1,0:T(8,128)(2,1)S(1)}, bf16[2,2,16,1024]{3,2,1,0:T(8,128)(2,1)S(1)}, u32[]{:S(2)}, u32[]{:S(2)}) collective-permute-start(bf16[2,2,16,1024]{3,2,1,0:T(8,128)(2,1)S(1)} %get-tuple-element.105), channel_id=1, source_target_pairs={{0,3},{1,2},{2,1},{3,0},{4,7},{5,6},{6,5},{7,4},{8,11},{9,10},{10,... | collective-permute-start | bytes 393224 | tf_op jit(solution)/shard_map/ppermute | solution.py:328
  48.2 2.8 %copy-done = bf16[1024,3072]{1,0:T(8,128)(2,1)S(1)} copy-done((bf16[1024,3072]{1,0:T(8,128)(2,1)S(1)}, bf16[1024,3072]{1,0:T(8,128)(2,1)}, u32[]{:S(2)}) %copy-start) | copy-done | bytes 6291480
  51.0 11.2 %shard_map.68 = (bf16[512,1024]{1,0:T(8,128)(2,1)S(1)}, bf16[512,1024]{1,0:T(8,128)(2,1)S(1)}, bf16[512,1024]{1,0:T(8,128)(2,1)S(1)}, bf16[512,1024]{1,0:T(8,128...) custom-call(bf16[2,2,16,1024]{3,2,1,0:T(8,128)(2,1)S(1)} %get-tuple-, ...), custom_call_target="tpu_custom_call" | custom-call | flops 5368709120 | bytes 12582912 | tf_op jit(solution)/shard_map/pallas_call | solution.py:302
  62.2 11.4 %shard_map.69 = (bf16[512,1024]{1,0:T(8,128)(2,1)S(1)}, bf16[512,1024]{1,0:T(8,128)(2,1)S(1)}, bf16[512,1024]{1,0:T(8,128)(2,1)S(1)}, bf16[512,1024]{1,0:T(8,128...) custom-call(bf16[2,2,16,1024]{3,2,1,0:T(8,128)(2,1)S(1)} %get-tuple-, ...), custom_call_target="tpu_custom_call", output_to_operand_aliasing={{0}: (12, {}), {1}: (13, {}), {2}: (14, {}), {3}: (15, {}),... | custom-call | flops 5368709120 | bytes 12582912 | tf_op jit(solution)/shard_map/pallas_call | solution.py:302
  73.6 2.9 %shard_map.70 = (bf16[2,4,2,32,2048]{4,3,2,1,0:T(8,128)(2,1)S(1)}, bf16[2,4,2,32,2048]{4,3,2,1,0:T(8,128)(2,1)S(1)}) custom-call(s32[2]{0:T(128)S(1)} %pad_add_fusion.ids_ref, bf16[512,1024]{1,0:T(8,128)(2,1)S(1)} %get-tuple-element.153.normed_ref, bf16[512,1024]{1,0:T(8,128)(2,1)S(1)} %get-tuple-element.154.mixed_ref, ...), custom_call_target="tpu_custom_call" | custom-call | flops 2147483648 | bytes 10485760 | tf_op jit(solution)/shard_map/pallas_call | solution.py:103
  77.2 2.9 %shard_map.72 = (bf16[2,4,2,32,2048]{4,3,2,1,0:T(8,128)(2,1)S(1)}, bf16[2,4,2,32,2048]{4,3,2,1,0:T(8,128)(2,1)S(1)}) custom-call(s32[2]{0:T(128)S(1)} %pad_add_fusion.ids_ref, bf16[512,1024]{1,0:T(8,128)(2,1)S(1)} %get-tuple-element.153.normed_ref, bf16[512,1024]{1,0:T(8,128)(2,1)S(1)} %get-tuple-element.154.mixed_ref, ...), custom_call_target="tpu_custom_call" | custom-call | flops 2147483648 | bytes 10485760 | tf_op jit(solution)/shard_map/pallas_call | solution.py:103
  86.9 2.7 %collective-permute-start.15 = (bf16[4,16,1024]{2,1,0:T(8,128)(2,1)S(1)}, bf16[4,16,1024]{2,1,0:T(8,128)(2,1)S(1)}, u32[]{:S(2)}, u32[]{:S(2)}) collective-permute-start(bf16[4,16,1024]{2,1,0:T(8,128)(2,1)S(1)} %get-tuple-element.147), channel_id=1, source_target_pairs={{0,2},{1,3},{2,0},{3,1},{4,6},{5,7},{6,4},{7,5},{8,10},{9,11},{10,... | collective-permute-start | bytes 393224 | tf_op jit(solution)/shard_map/ppermute | solution.py:328
  89.7 26.0 %collective-permute-done.14.refs_1_ = bf16[4,16,1024]{2,1,0:T(8,128)(2,1)S(1)} collective-permute-done((bf16[4,16,1024]{2,1,0:T(8,128)(2,1)S(1)}, bf16[4,16,1024]{2,1,0:T(8,128)(2,1)S(1)}, u32[]{:S(2)}, u32[]{:S(2)}) %collective-permute-start.14) | collective-permute-done | bytes 131104 | tf_op jit(solution)/shard_map/ppermute | solution.py:328
  115.7 2.9 %collective-permute-start.17 = (bf16[4,16,1024]{2,1,0:T(8,128)(2,1)S(1)}, bf16[4,16,1024]{2,1,0:T(8,128)(2,1)S(1)}, u32[]{:S(2)}, u32[]{:S(2)}) collective-permute-start(bf16[4,16,1024]{2,1,0:T(8,128)(2,1)S(1)} %get-tuple-element.149), channel_id=1, source_target_pairs={{0,4},{1,5},{2,6},{3,7},{4,0},{5,1},{6,2},{7,3},{8,12},{9,13},{10,... | collective-permute-start | bytes 393224 | tf_op jit(solution)/shard_map/ppermute | solution.py:328
  121.1 9.8 %collective-permute-done.17.refs_4_ = bf16[4,16,1024]{2,1,0:T(8,128)(2,1)S(1)} collective-permute-done((bf16[4,16,1024]{2,1,0:T(8,128)(2,1)S(1)}, bf16[4,16,1024]{2,1,0:T(8,128)(2,1)S(1)}, u32[]{:S(2)}, u32[]{:S(2)}) %collective-permute-start.17) | collective-permute-done | bytes 131104 | tf_op jit(solution)/shard_map/ppermute | solution.py:328
  130.9 2.7 %collective-permute-start.20 = (bf16[4,16,1024]{2,1,0:T(8,128)(2,1)S(1)}, bf16[4,16,1024]{2,1,0:T(8,128)(2,1)S(1)}, u32[]{:S(2)}, u32[]{:S(2)}) collective-permute-start(bf16[4,16,1024]{2,1,0:T(8,128)(2,1)S(1)} %get-tuple-element.152), channel_id=1, source_target_pairs={{0,7},{1,6},{2,5},{3,4},{4,3},{5,2},{6,1},{7,0},{8,15},{9,14},{10,... | collective-permute-start | bytes 393224 | tf_op jit(solution)/shard_map/ppermute | solution.py:328
  133.6 2.5 %collective-permute-done.18.refs_5_ = bf16[4,16,1024]{2,1,0:T(8,128)(2,1)S(1)} collective-permute-done((bf16[4,16,1024]{2,1,0:T(8,128)(2,1)S(1)}, bf16[4,16,1024]{2,1,0:T(8,128)(2,1)S(1)}, u32[]{:S(2)}, u32[]{:S(2)}) %collective-permute-start.18) | collective-permute-done | bytes 131104 | tf_op jit(solution)/shard_map/ppermute | solution.py:328
  136.1 2.6 %collective-permute-done.20.refs_7_ = bf16[4,16,1024]{2,1,0:T(8,128)(2,1)S(1)} collective-permute-done((bf16[4,16,1024]{2,1,0:T(8,128)(2,1)S(1)}, bf16[4,16,1024]{2,1,0:T(8,128)(2,1)S(1)}, u32[]{:S(2)}, u32[]{:S(2)}) %collective-permute-start.20) | collective-permute-done | bytes 131104 | tf_op jit(solution)/shard_map/ppermute | solution.py:328
  139.4 3.1 %collective-permute-start.25 = (bf16[4,32,2048]{2,1,0:T(8,128)(2,1)S(1)}, bf16[4,32,2048]{2,1,0:T(8,128)(2,1)S(1)}, u32[]{:S(2)}, u32[]{:S(2)}) collective-permute-start(bf16[4,32,2048]{2,1,0:T(8,128)(2,1)S(1)} %get-tuple-element.166), channel_id=1, source_target_pairs={{0,1},{1,0},{2,3},{3,2},{4,5},{5,4},{6,7},{7,6},{8,9},{9,8},{10,11... | collective-permute-start | bytes 1572872 | tf_op jit(solution)/shard_map/ppermute | solution.py:328
  144.8 5.3 %collective-permute-done.25.refs_1_ = bf16[4,32,2048]{2,1,0:T(8,128)(2,1)S(1)} collective-permute-done((bf16[4,32,2048]{2,1,0:T(8,128)(2,1)S(1)}, bf16[4,32,2048]{2,1,0:T(8,128)(2,1)S(1)}, u32[]{:S(2)}, u32[]{:S(2)}) %collective-permute-start.25) | collective-permute-done | bytes 524320 | tf_op jit(solution)/shard_map/ppermute | solution.py:328
  153.2 5.3 %collective-permute-start.27 = (bf16[32,4096]{1,0:T(8,128)(2,1)S(1)}, bf16[32,4096]{1,0:T(8,128)(2,1)S(1)}, u32[]{:S(2)}, u32[]{:S(2)}) collective-permute-start(bf16[32,4096]{1,0:T(8,128)(2,1)S(1)} %get-tuple-element.172), channel_id=1, source_target_pairs={{0,2},{1,3},{2,0},{3,1},{4,6},{5,7},{6,4},{7,5},{8,10},{9,11},{10,... | collective-permute-start | bytes 786440 | tf_op jit(solution)/shard_map/ppermute | solution.py:328
  162.5 5.2 %collective-permute-done.27.refs_1_ = bf16[32,4096]{1,0:T(8,128)(2,1)S(1)} collective-permute-done((bf16[32,4096]{1,0:T(8,128)(2,1)S(1)}, bf16[32,4096]{1,0:T(8,128)(2,1)S(1)}, u32[]{:S(2)}, u32[]{:S(2)}) %collective-permute-start.27) | collective-permute-done | bytes 262176 | tf_op jit(solution)/shard_map/ppermute | solution.py:328
  167.6 11.0 %collective-permute-done.28.refs_2_ = bf16[32,4096]{1,0:T(8,128)(2,1)S(1)} collective-permute-done((bf16[32,4096]{1,0:T(8,128)(2,1)S(1)}, bf16[32,4096]{1,0:T(8,128)(2,1)S(1)}, u32[]{:S(2)}, u32[]{:S(2)}) %collective-permute-start.28) | collective-permute-done | bytes 262176 | tf_op jit(solution)/shard_map/ppermute | solution.py:328
  (59 shorter events, 32.1 us)
Async XLA Ops:
  9.1 16.4 %collective-permute-start.3 = (bf16[2,2,16,1024]{3,2,1,0:T(8,128)(2,1)S(1)}, bf16[2,2,16,1024]{3,2,1,0:T(8,128)(2,1)S(1)}, u32[]{:S(2)}, u32[]{:S(2)}) collective-permute-start(bf16[2,2,16,1024]{3,2,1,0:T(8,128)(2,1)S(1)} %get-tuple-element.98), channel_id=1, source_target_pairs={{0,1},{1,0},{2,3},{3,2},{4,5},{5,4},{6,7},{7,6},{8,9},{9,8},{10,11... | collective-permute-start | bytes 393224 | tf_op jit(solution)/shard_map/ppermute | solution.py:328
  10.6 17.1 %collective-permute-start.6 = (bf16[2,2,16,1024]{3,2,1,0:T(8,128)(2,1)S(1)}, bf16[2,2,16,1024]{3,2,1,0:T(8,128)(2,1)S(1)}, u32[]{:S(2)}, u32[]{:S(2)}) collective-permute-start(bf16[2,2,16,1024]{3,2,1,0:T(8,128)(2,1)S(1)} %get-tuple-element.103), channel_id=1, source_target_pairs={{0,5},{1,4},{2,7},{3,6},{4,1},{5,0},{6,3},{7,2},{8,13},{9,12},{10,... | collective-permute-start | bytes 393224 | tf_op jit(solution)/shard_map/ppermute | solution.py:328
  10.6 20.8 %collective-permute-start.9 = (bf16[2,2,16,1024]{3,2,1,0:T(8,128)(2,1)S(1)}, bf16[2,2,16,1024]{3,2,1,0:T(8,128)(2,1)S(1)}, u32[]{:S(2)}, u32[]{:S(2)}) collective-permute-start(bf16[2,2,16,1024]{3,2,1,0:T(8,128)(2,1)S(1)} %get-tuple-element.108), channel_id=1, source_target_pairs={{0,7},{1,6},{2,5},{3,4},{4,3},{5,2},{6,1},{7,0},{8,15},{9,14},{10,... | collective-permute-start | bytes 393224 | tf_op jit(solution)/shard_map/ppermute | solution.py:328
  13.4 24.7 %collective-permute-start.12 = (bf16[2,2,16,1024]{3,2,1,0:T(8,128)(2,1)S(1)}, bf16[2,2,16,1024]{3,2,1,0:T(8,128)(2,1)S(1)}, u32[]{:S(2)}, u32[]{:S(2)}) collective-permute-start(bf16[2,2,16,1024]{3,2,1,0:T(8,128)(2,1)S(1)} %get-tuple-element.112), channel_id=1, source_target_pairs={{0,4},{1,5},{2,6},{3,7},{4,0},{5,1},{6,2},{7,3},{8,12},{9,13},{10,... | collective-permute-start | bytes 393224 | tf_op jit(solution)/shard_map/ppermute | solution.py:328
  13.8 24.9 %collective-permute-start.1 = (bf16[2,2,16,1024]{3,2,1,0:T(8,128)(2,1)S(1)}, bf16[2,2,16,1024]{3,2,1,0:T(8,128)(2,1)S(1)}, u32[]{:S(2)}, u32[]{:S(2)}) collective-permute-start(bf16[2,2,16,1024]{3,2,1,0:T(8,128)(2,1)S(1)} %get-tuple-element.94), channel_id=1, source_target_pairs={{0,3},{1,2},{2,1},{3,0},{4,7},{5,6},{6,5},{7,4},{8,11},{9,10},{10,... | collective-permute-start | bytes 393224 | tf_op jit(solution)/shard_map/ppermute | solution.py:328
  25.5 14.3 %collective-permute-start.4 = (bf16[2,2,16,1024]{3,2,1,0:T(8,128)(2,1)S(1)}, bf16[2,2,16,1024]{3,2,1,0:T(8,128)(2,1)S(1)}, u32[]{:S(2)}, u32[]{:S(2)}) collective-permute-start(bf16[2,2,16,1024]{3,2,1,0:T(8,128)(2,1)S(1)} %get-tuple-element.99), channel_id=1, source_target_pairs={{0,7},{1,6},{2,5},{3,4},{4,3},{5,2},{6,1},{7,0},{8,15},{9,14},{10,... | collective-permute-start | bytes 393224 | tf_op jit(solution)/shard_map/ppermute | solution.py:328
  27.7 17.6 %collective-permute-start.7 = (bf16[2,2,16,1024]{3,2,1,0:T(8,128)(2,1)S(1)}, bf16[2,2,16,1024]{3,2,1,0:T(8,128)(2,1)S(1)}, u32[]{:S(2)}, u32[]{:S(2)}) collective-permute-start(bf16[2,2,16,1024]{3,2,1,0:T(8,128)(2,1)S(1)} %get-tuple-element.104), channel_id=1, source_target_pairs={{0,6},{1,7},{2,4},{3,5},{4,2},{5,3},{6,0},{7,1},{8,14},{9,15},{10,... | collective-permute-start | bytes 393224 | tf_op jit(solution)/shard_map/ppermute | solution.py:328
  31.4 16.8 %collective-permute-start.10 = (bf16[2,2,16,1024]{3,2,1,0:T(8,128)(2,1)S(1)}, bf16[2,2,16,1024]{3,2,1,0:T(8,128)(2,1)S(1)}, u32[]{:S(2)}, u32[]{:S(2)}) collective-permute-start(bf16[2,2,16,1024]{3,2,1,0:T(8,128)(2,1)S(1)} %get-tuple-element.109), channel_id=1, source_target_pairs={{0,2},{1,3},{2,0},{3,1},{4,6},{5,7},{6,4},{7,5},{8,10},{9,11},{10,... | collective-permute-start | bytes 393224 | tf_op jit(solution)/shard_map/ppermute | solution.py:328
  38.2 24.0 %collective-permute-start.13 = (bf16[2,2,16,1024]{3,2,1,0:T(8,128)(2,1)S(1)}, bf16[2,2,16,1024]{3,2,1,0:T(8,128)(2,1)S(1)}, u32[]{:S(2)}, u32[]{:S(2)}) collective-permute-start(bf16[2,2,16,1024]{3,2,1,0:T(8,128)(2,1)S(1)} %get-tuple-element.113), channel_id=1, source_target_pairs={{0,5},{1,4},{2,7},{3,6},{4,1},{5,0},{6,3},{7,2},{8,13},{9,12},{10,... | collective-permute-start | bytes 393224 | tf_op jit(solution)/shard_map/ppermute | solution.py:328
  38.7 23.5 %collective-permute-start.2 = (bf16[2,2,16,1024]{3,2,1,0:T(8,128)(2,1)S(1)}, bf16[2,2,16,1024]{3,2,1,0:T(8,128)(2,1)S(1)}, u32[]{:S(2)}, u32[]{:S(2)}) collective-permute-start(bf16[2,2,16,1024]{3,2,1,0:T(8,128)(2,1)S(1)} %get-tuple-element.95), channel_id=1, source_target_pairs={{0,1},{1,0},{2,3},{3,2},{4,5},{5,4},{6,7},{7,6},{8,9},{9,8},{10,11... | collective-permute-start | bytes 393224 | tf_op jit(solution)/shard_map/ppermute | solution.py:328
  39.8 22.4 %collective-permute-start.5 = (bf16[2,2,16,1024]{3,2,1,0:T(8,128)(2,1)S(1)}, bf16[2,2,16,1024]{3,2,1,0:T(8,128)(2,1)S(1)}, u32[]{:S(2)}, u32[]{:S(2)}) collective-permute-start(bf16[2,2,16,1024]{3,2,1,0:T(8,128)(2,1)S(1)} %get-tuple-element.100), channel_id=1, source_target_pairs={{0,2},{1,3},{2,0},{3,1},{4,6},{5,7},{6,4},{7,5},{8,10},{9,11},{10,... | collective-permute-start | bytes 393224 | tf_op jit(solution)/shard_map/ppermute | solution.py:328
  45.4 16.8 %collective-permute-start.8 = (bf16[2,2,16,1024]{3,2,1,0:T(8,128)(2,1)S(1)}, bf16[2,2,16,1024]{3,2,1,0:T(8,128)(2,1)S(1)}, u32[]{:S(2)}, u32[]{:S(2)}) collective-permute-start(bf16[2,2,16,1024]{3,2,1,0:T(8,128)(2,1)S(1)} %get-tuple-element.105), channel_id=1, source_target_pairs={{0,3},{1,2},{2,1},{3,0},{4,7},{5,6},{6,5},{7,4},{8,11},{9,10},{10,... | collective-permute-start | bytes 393224 | tf_op jit(solution)/shard_map/ppermute | solution.py:328
  48.2 14.0 %collective-permute-start.11 = (bf16[2,2,16,1024]{3,2,1,0:T(8,128)(2,1)S(1)}, bf16[2,2,16,1024]{3,2,1,0:T(8,128)(2,1)S(1)}, u32[]{:S(2)}, u32[]{:S(2)}) collective-permute-start(bf16[2,2,16,1024]{3,2,1,0:T(8,128)(2,1)S(1)} %get-tuple-element.110), channel_id=1, source_target_pairs={{0,4},{1,5},{2,6},{3,7},{4,0},{5,1},{6,2},{7,3},{8,12},{9,13},{10,... | collective-permute-start | bytes 393224 | tf_op jit(solution)/shard_map/ppermute | solution.py:328
  81.8 56.9 %collective-permute-start.22 = (bf16[4,2,32,2048]{3,2,1,0:T(8,128)(2,1)S(1)}, bf16[4,2,32,2048]{3,2,1,0:T(8,128)(2,1)S(1)}, u32[]{:S(2)}, u32[]{:S(2)}) collective-permute-start(bf16[4,2,32,2048]{3,2,1,0:T(8,128)(2,1)S(1)} %get-tuple-element.161), channel_id=1, source_target_pairs={{0,16},{8,24},{16,0},{24,8},{1,17},{9,25},{17,1},{25,9},{2,18},{10... | collective-permute-start | bytes 3145736 | tf_op jit(solution)/shard_map/ppermute | solution.py:328
  84.8 53.9 %collective-permute-start.24 = (bf16[2,4,32,2048]{3,2,1,0:T(8,128)(2,1)S(1)}, bf16[2,4,32,2048]{3,2,1,0:T(8,128)(2,1)S(1)}, u32[]{:S(2)}, u32[]{:S(2)}) collective-permute-start(bf16[2,4,32,2048]{3,2,1,0:T(8,128)(2,1)S(1)} %get-tuple-element.163), channel_id=1, source_target_pairs={{0,1},{1,0},{2,3},{3,2},{4,5},{5,4},{6,7},{7,6},{8,9},{9,8},{10,11... | collective-permute-start | bytes 3145736 | tf_op jit(solution)/shard_map/ppermute | solution.py:328
  86.2 29.5 %collective-permute-start.14 = (bf16[4,16,1024]{2,1,0:T(8,128)(2,1)S(1)}, bf16[4,16,1024]{2,1,0:T(8,128)(2,1)S(1)}, u32[]{:S(2)}, u32[]{:S(2)}) collective-permute-start(bf16[4,16,1024]{2,1,0:T(8,128)(2,1)S(1)} %get-tuple-element.146), channel_id=1, source_target_pairs={{0,1},{1,0},{2,3},{3,2},{4,5},{5,4},{6,7},{7,6},{8,9},{9,8},{10,11... | collective-permute-start | bytes 393224 | tf_op jit(solution)/shard_map/ppermute | solution.py:328
  86.9 31.7 %collective-permute-start.15 = (bf16[4,16,1024]{2,1,0:T(8,128)(2,1)S(1)}, bf16[4,16,1024]{2,1,0:T(8,128)(2,1)S(1)}, u32[]{:S(2)}, u32[]{:S(2)}) collective-permute-start(bf16[4,16,1024]{2,1,0:T(8,128)(2,1)S(1)} %get-tuple-element.147), channel_id=1, source_target_pairs={{0,2},{1,3},{2,0},{3,1},{4,6},{5,7},{6,4},{7,5},{8,10},{9,11},{10,... | collective-permute-start | bytes 393224 | tf_op jit(solution)/shard_map/ppermute | solution.py:328
  89.6 29.8 %collective-permute-start.16 = (bf16[4,16,1024]{2,1,0:T(8,128)(2,1)S(1)}, bf16[4,16,1024]{2,1,0:T(8,128)(2,1)S(1)}, u32[]{:S(2)}, u32[]{:S(2)}) collective-permute-start(bf16[4,16,1024]{2,1,0:T(8,128)(2,1)S(1)} %get-tuple-element.148), channel_id=1, source_target_pairs={{0,3},{1,2},{2,1},{3,0},{4,7},{5,6},{6,5},{7,4},{8,11},{9,10},{10,... | collective-permute-start | bytes 393224 | tf_op jit(solution)/shard_map/ppermute | solution.py:328
  115.7 15.2 %collective-permute-start.17 = (bf16[4,16,1024]{2,1,0:T(8,128)(2,1)S(1)}, bf16[4,16,1024]{2,1,0:T(8,128)(2,1)S(1)}, u32[]{:S(2)}, u32[]{:S(2)}) collective-permute-start(bf16[4,16,1024]{2,1,0:T(8,128)(2,1)S(1)} %get-tuple-element.149), channel_id=1, source_target_pairs={{0,4},{1,5},{2,6},{3,7},{4,0},{5,1},{6,2},{7,3},{8,12},{9,13},{10,... | collective-permute-start | bytes 393224 | tf_op jit(solution)/shard_map/ppermute | solution.py:328
  118.6 17.5 %collective-permute-start.18 = (bf16[4,16,1024]{2,1,0:T(8,128)(2,1)S(1)}, bf16[4,16,1024]{2,1,0:T(8,128)(2,1)S(1)}, u32[]{:S(2)}, u32[]{:S(2)}) collective-permute-start(bf16[4,16,1024]{2,1,0:T(8,128)(2,1)S(1)} %get-tuple-element.150), channel_id=1, source_target_pairs={{0,5},{1,4},{2,7},{3,6},{4,1},{5,0},{6,3},{7,2},{8,13},{9,12},{10,... | collective-permute-start | bytes 393224 | tf_op jit(solution)/shard_map/ppermute | solution.py:328
  119.4 16.7 %collective-permute-start.19 = (bf16[4,16,1024]{2,1,0:T(8,128)(2,1)S(1)}, bf16[4,16,1024]{2,1,0:T(8,128)(2,1)S(1)}, u32[]{:S(2)}, u32[]{:S(2)}) collective-permute-start(bf16[4,16,1024]{2,1,0:T(8,128)(2,1)S(1)} %get-tuple-element.151), channel_id=1, source_target_pairs={{0,6},{1,7},{2,4},{3,5},{4,2},{5,3},{6,0},{7,1},{8,14},{9,15},{10,... | collective-permute-start | bytes 393224 | tf_op jit(solution)/shard_map/ppermute | solution.py:328
  153.2 14.4 %collective-permute-start.27 = (bf16[32,4096]{1,0:T(8,128)(2,1)S(1)}, bf16[32,4096]{1,0:T(8,128)(2,1)S(1)}, u32[]{:S(2)}, u32[]{:S(2)}) collective-permute-start(bf16[32,4096]{1,0:T(8,128)(2,1)S(1)} %get-tuple-element.172), channel_id=1, source_target_pairs={{0,2},{1,3},{2,0},{3,1},{4,6},{5,7},{6,4},{7,5},{8,10},{9,11},{10,... | collective-permute-start | bytes 786440 | tf_op jit(solution)/shard_map/ppermute | solution.py:328
  158.4 20.2 %collective-permute-start.28 = (bf16[32,4096]{1,0:T(8,128)(2,1)S(1)}, bf16[32,4096]{1,0:T(8,128)(2,1)S(1)}, u32[]{:S(2)}, u32[]{:S(2)}) collective-permute-start(bf16[32,4096]{1,0:T(8,128)(2,1)S(1)} %get-tuple-element.173), channel_id=1, source_target_pairs={{0,4},{1,5},{2,6},{3,7},{4,0},{5,1},{6,2},{7,3},{8,12},{9,13},{10,... | collective-permute-start | bytes 786440 | tf_op jit(solution)/shard_map/ppermute | solution.py:328
  158.7 19.8 %collective-permute-start.29 = (bf16[32,4096]{1,0:T(8,128)(2,1)S(1)}, bf16[32,4096]{1,0:T(8,128)(2,1)S(1)}, u32[]{:S(2)}, u32[]{:S(2)}) collective-permute-start(bf16[32,4096]{1,0:T(8,128)(2,1)S(1)} %get-tuple-element.174), channel_id=1, source_target_pairs={{0,6},{1,7},{2,4},{3,5},{4,2},{5,3},{6,0},{7,1},{8,14},{9,15},{10,... | collective-permute-start | bytes 786440 | tf_op jit(solution)/shard_map/ppermute | solution.py:328
  (11 other events, 113.0 us)

commit v4 on v3

--- a/solution.py
+++ b/solution.py
@@ -11,7 +11,6 @@
 HEADS = 16
 GROUP = 4
 CHUNKS = 2
-WINDOW = 5
 CORES = 2
 N_Y = 2
 EPSILON = 1e-06
@@ -76,43 +75,37 @@
     )(ids, *blocks)
 
 
-def product_kernel(n_x, flip, ids_ref, normed_ref, mixed_ref, dq_ref, dk_ref, dv_ref, cot_ref, first_ref, second_ref):
-    width = normed_ref.shape[1]
+def product_kernel(n_x, flip, n_lefts, ids_ref, *refs):
+    lefts, rights, out_ref = refs[:n_lefts], refs[n_lefts:-1], refs[-1]
+    width = lefts[0].shape[1]
     rest = width // (CORES * n_x)
     core = lax.rem(ids_ref[0], CORES) ^ flip
-    cut = first_ref.shape[1:4]
+    cut = out_ref.shape[1:4]
     for x in range(n_x):
         columns = pl.ds(pl.multiple_of((CORES * x + core) * rest, rest), rest)
-
-        def store(ref, start, left, right):
-            product = contract(left, right[...], ((1,), (0,)))
+        turned = [left[:, columns].T for left in lefts]
+        for i, right in enumerate(rights):
+            product = contract(turned[min(i, n_lefts - 1)], right[...], ((1,), (0,)))
             product = product.reshape(cut + (width,)).astype(jnp.bfloat16)
-            ref[x, :, :, :, pl.ds(start, width)] = product
-
-        left = normed_ref[:, columns].T
-        store(first_ref, 0, left, dq_ref)
-        store(first_ref, width, left, dk_ref)
-        store(second_ref, 0, left, dv_ref)
-        store(second_ref, width, mixed_ref[:, columns].T, cot_ref)
-
-
-def products(ids, flip, n_x, n_z, normed, mixed, dq, dk, dv, cot):
-    rows, width = normed.shape
+            out_ref[x, :, :, :, pl.ds(i * width, width)] = product
+
+
+def products(ids, flip, n_x, n_z, lefts, rights):
+    rows, width = rights[0].shape
     rest = width // (CORES * n_x * n_z * N_Y)
-    half = jax.ShapeDtypeStruct((n_x, n_z, N_Y, rest, 2 * width), jnp.bfloat16)
-    return pl.pallas_call(
-        functools.partial(product_kernel, n_x, flip),
-        out_shape=[half, half],
+    return pl.pallas_call(
+        functools.partial(product_kernel, n_x, flip, len(lefts)),
+        out_shape=jax.ShapeDtypeStruct((n_x, n_z, N_Y, rest, len(rights) * width), jnp.bfloat16),
         in_specs=[pl.BlockSpec(memory_space=pltpu.SMEM)]
-        + [pl.BlockSpec(memory_space=pltpu.VMEM)] * 6,
-        out_specs=[pl.BlockSpec(memory_space=pltpu.VMEM)] * 2,
-        compiler_params=pltpu.CompilerParams(vmem_limit_bytes=24 * MIB),
+        + [pl.BlockSpec(memory_space=pltpu.VMEM)] * (len(lefts) + len(rights)),
+        out_specs=pl.BlockSpec(memory_space=pltpu.VMEM),
+        compiler_params=pltpu.CompilerParams(vmem_limit_bytes=20 * MIB),
         cost_estimate=pl.CostEstimate(
-            flops=4 * rows * width * width,
-            bytes_accessed=12 * rows * width + 4 * width * width,
+            flops=2 * rows * width * width,
+            bytes_accessed=8 * rows * width + 2 * width * width,
             transcendentals=0,
         ),
-    )(ids, normed, mixed, dq, dk, dv, cot)
+    )(ids, *lefts, *rights)
 
 
 def summed(refs, index):
@@ -333,12 +326,21 @@
     return values
 
 
-def inbound_order(n_tm, chunk):
-    far, near = list(range(n_tm - 1, n_tm // 2 - 1, -1)), list(range(1, n_tm // 2))
-    if chunk == CHUNKS - 1:
-        return far + near
-    cut = len(far) // 2
-    return far[:cut] + near[:1] + far[cut:] + near[1:]
+def inbound(chunks, n_tm):
+    half = n_tm // 2
+    arrived = []
+    for blocks in chunks:
+        pieces = {0: blocks[0]}
+        for k in range(1, half):
+            gate = arrived[-1][k] if arrived else None
+            pieces[k] = swap(blocks[k] if gate is None else after(blocks[k], gate), "tm", n_tm, k)
+        for i, k in enumerate(range(n_tm - 1, half - 1, -1)):
+            gate = arrived[-1][k] if arrived else None
+            if not arrived and i >= half // 2:
+                gate = pieces[i - half // 2 + 1]
+            pieces[k] = swap(blocks[k] if gate is None else after(blocks[k], gate), "tm", n_tm, k)
+        arrived.append([pieces[k] for k in range(n_tm)])
+    return arrived
 
 
 def shards(n_clip_devices, n_tm, clips, w_qkv, w_out, cotangent):
@@ -348,16 +350,7 @@
     joined = n_positions % 16 != 0
     ids = jnp.stack([lax.axis_index("clip"), lax.axis_index("tm")]).astype(jnp.int32)
 
-    arrived, line = [], []
-    for chunk, blocks in enumerate(pick(ids, clips, cotangent, n_tm, CHUNKS)):
-        pieces = {0: blocks[0]}
-        for k in inbound_order(n_tm, chunk):
-            block = blocks[k]
-            if len(line) >= WINDOW:
-                block = after(block, line[-WINDOW])
-            pieces[k] = swap(block, "tm", n_tm, k)
-            line.append(pieces[k])
-        arrived.append([pieces[k] for k in range(n_tm)])
+    arrived = inbound(pick(ids, clips, cotangent, n_tm, CHUNKS), n_tm)
     results = None
     for chunk, pieces in enumerate(arrived):
         if joined:
@@ -369,25 +362,33 @@
         cut = dx[0].reshape(n_clips, n_tm, n_positions, width)
         dx = [cut[:, k] for k in range(n_tm)]
 
-    factors = (normed, mixed, dq, dk, dv, cot)
-    sent = products(ids, 1, n_x, n_z, *factors)
-    first, second = (swap(half, "clip", n_clip_devices, 1) for half in sent)
-    dx = after(dx, sent)
-    dx = [dx[0]] + [swap(dx[k], "tm", n_tm, k) for k in range(1, n_tm)]
-    own_first, own_second = products(ids, 0, n_x, n_z, *after(factors, sent))
+    halves = ([normed], [dq, dk]), ([normed, mixed], [dv, cot])
+    sent_first = products(ids, 1, n_x, n_z, *halves[0])
+    first = swap(sent_first, "clip", n_clip_devices, 1)
+    sent_second = products(ids, 1, n_x, n_z, *after(halves[1], sent_first))
+    second = swap(sent_second, "clip", n_clip_devices, 1)
+    dx = after(dx, sent_second)
+    back = {}
+    for k in range(n_tm - 1, 1, -1):
+        block = dx[k] if k + 3 >= n_tm else after(dx[k], back[k + 3])
+        back[k] = swap(block, "tm", n_tm, k)
+    own_first = products(ids, 0, n_x, n_z, *after(halves[0], sent_second))
+    own_second = products(ids, 0, n_x, n_z, *after(halves[1], own_first))
 
     sent, own_first = halve(ids, (own_first, first), 0, 0, CORES)
     first = swap(sent, "clip", n_clip_devices, CORES)
     sent, own_second = halve(ids, (own_second, second), 2, 1, 1)
     second = swap(sent, "tm", n_tm, 1)
-    first, second = after((first, second), dx)
+    first, second = after((first, second), back)
     sent, own_first = halve(ids, (own_first, first), 1, 1, 1)
     first = swap(sent, "tm", n_tm, 1)
     sent, own_second = halve(ids, (own_second, second), 0, 0, CORES)
     second = swap(sent, "clip", n_clip_devices, CORES)
     total, *sent = join(ids, (own_first, first), (own_second, second), n_z)
-    grad_clips = place(ids, dx).reshape(clips.shape)
     others = [swap(block, "tm", n_tm, (j + 1) * N_Y) for j, block in enumerate(sent)]
+    back[0] = dx[0]
+    back[1] = swap(after(dx[1], sent), "tm", n_tm, 1)
+    grad_clips = place(ids, [back[k] for k in range(n_tm)]).reshape(clips.shape)
     grad_qkv, grad_out = finish((total, *others))
     return (grad_clips, grad_qkv, grad_out)
 

time: 181 us -> 159 us (0.88)
  waiting for transfers between devices: 67.9 us -> 49.8 us
  starting transfers between devices: 69.5 us -> 64.1 us
    ppermute x30, waiting for transfers between devices: 67.9 us -> 49.8 us  [swap(): return lax.ppermute(block, axis, [(i, i ^ distance) for i in range(size)])]
    ppermute x30, starting transfers between devices: 69.5 us -> 64.1 us  [swap(): return lax.ppermute(block, axis, [(i, i ^ distance) for i in range(size)])]
    pallas_call x2 -> x4, Pallas kernels: 5.88 us -> 7.35 us  [products(): pl.pallas_call(functools.partial(product_kernel, n_x, flip, len(lefts)),...]
  transfers between devices with their start and end apart: 30 -> 30, of which waited for: 11 -> 13; matrix products, arithmetic and copies ran while one was open for 0% -> 0% of each run, Pallas kernels for 10% -> 12%
where the time goes in v4:
time: 159 us; the launch traced here: 157 us
  starting transfers between devices  64.1 us (40%)
  waiting for transfers between devices  49.8 us (31%)
  Pallas kernels  37.3 us (23%)
  local copies, waits for them, and re-layouts  5.37 us (3%)
    ppermute x30, starting transfers between devices, swap(): return lax.ppermute(block, axis, [(i, i ^ distance) for i in range(size)])  64.1 us
    ppermute x30, waiting for transfers between devices, swap(): return lax.ppermute(block, axis, [(i, i ^ distance) for i in range(size)])  49.8 us
    pallas_call x2, Pallas kernels, sublayer(): pl.pallas_call(functools.partial(sublayer_kernel, n_clips, n_positions, n...  22.6 us
    pallas_call x4, Pallas kernels, products(): pl.pallas_call(functools.partial(product_kernel, n_x, flip, len(lefts)),...  7.35 us
    unnamed x10, local copies, waits for them, and re-layouts  5.37 us
    pallas_call x4, Pallas kernels, halve(): pl.pallas_call(functools.partial(halve_kernel, dim, axis, stride), out_sh...  3.55 us
  transfers between devices with their start and end apart: 30, of which 13 were waited for; matrix products, arithmetic and copies ran while one was open for 0% of the time, Pallas kernels for 12%

profile of v4, /device:TPU:0, one launch (start us, length us, event | category | flops | bytes accessed | tf_op | source)
XLA Modules:
  0.0 157.5 jit_solution(6178498420073786444)
XLA Ops:
  4.0 3.0 %collective-permute-start = (bf16[2,2,16,1024]{3,2,1,0:T(8,128)(2,1)S(1)}, bf16[2,2,16,1024]{3,2,1,0:T(8,128)(2,1)S(1)}, u32[]{:S(2)}, u32[]{:S(2)}) collective-permute-start(bf16[2,2,16,1024]{3,2,1,0:T(8,128)(2,1)S(1)} %get-tuple-element.97), channel_id=1, source_target_pairs={{0,1},{1,0},{2,3},{3,2},{4,5},{5,4},{6,7},{7,6},{8,9},{9,8},{10,11... | collective-permute-start | bytes 393224 | tf_op jit(solution)/shard_map/ppermute | solution.py:321
  8.6 4.0 %collective-permute-start.10 = (bf16[2,2,16,1024]{3,2,1,0:T(8,128)(2,1)S(1)}, bf16[2,2,16,1024]{3,2,1,0:T(8,128)(2,1)S(1)}, u32[]{:S(2)}, u32[]{:S(2)}) collective-permute-start(bf16[2,2,16,1024]{3,2,1,0:T(8,128)(2,1)S(1)} %get-tuple-element.114), channel_id=1, source_target_pairs={{0,6},{1,7},{2,4},{3,5},{4,2},{5,3},{6,0},{7,1},{8,14},{9,15},{10,... | collective-permute-start | bytes 393224 | tf_op jit(solution)/shard_map/ppermute | solution.py:321
  14.6 1.9 %collective-permute-start.6 = (bf16[2,2,16,1024]{3,2,1,0:T(8,128)(2,1)S(1)}, bf16[2,2,16,1024]{3,2,1,0:T(8,128)(2,1)S(1)}, u32[]{:S(2)}, u32[]{:S(2)}) collective-permute-start(bf16[2,2,16,1024]{3,2,1,0:T(8,128)(2,1)S(1)} %get-tuple-element.107), channel_id=1, source_target_pairs={{0,4},{1,5},{2,6},{3,7},{4,0},{5,1},{6,2},{7,3},{8,12},{9,13},{10,... | collective-permute-start | bytes 393224 | tf_op jit(solution)/shard_map/ppermute | solution.py:321
  18.2 3.0 %collective-permute-done.10.refs_6_ = bf16[2,2,16,1024]{3,2,1,0:T(8,128)(2,1)S(1)} collective-permute-done((bf16[2,2,16,1024]{3,2,1,0:T(8,128)(2,1)S(1)}, bf16[2,2,16,1024]{3,2,1,0:T(8,128)(2,1)S(1)}, u32[]{:S(2)}, u32[]{:S(2)}) %collective-permute-start.10) | collective-permute-done | bytes 131104 | tf_op jit(solution)/shard_map/ppermute | solution.py:321
  21.2 2.5 %collective-permute-done.12.refs_7_ = bf16[2,2,16,1024]{3,2,1,0:T(8,128)(2,1)S(1)} collective-permute-done((bf16[2,2,16,1024]{3,2,1,0:T(8,128)(2,1)S(1)}, bf16[2,2,16,1024]{3,2,1,0:T(8,128)(2,1)S(1)}, u32[]{:S(2)}, u32[]{:S(2)}) %collective-permute-start.12) | collective-permute-done | bytes 131104 | tf_op jit(solution)/shard_map/ppermute | solution.py:321
  23.7 7.9 %collective-permute-start.5 = (bf16[2,2,16,1024]{3,2,1,0:T(8,128)(2,1)S(1)}, bf16[2,2,16,1024]{3,2,1,0:T(8,128)(2,1)S(1)}, u32[]{:S(2)}, u32[]{:S(2)}) collective-permute-start(bf16[2,2,16,1024]{3,2,1,0:T(8,128)(2,1)S(1)} %get-tuple-element.104), channel_id=1, source_target_pairs={{0,3},{1,2},{2,1},{3,0},{4,7},{5,6},{6,5},{7,4},{8,11},{9,10},{10,... | collective-permute-start | bytes 393224 | tf_op jit(solution)/shard_map/ppermute | solution.py:321
  31.6 2.7 %collective-permute-done.8.refs_5_ = bf16[2,2,16,1024]{3,2,1,0:T(8,128)(2,1)S(1)} collective-permute-done((bf16[2,2,16,1024]{3,2,1,0:T(8,128)(2,1)S(1)}, bf16[2,2,16,1024]{3,2,1,0:T(8,128)(2,1)S(1)}, u32[]{:S(2)}, u32[]{:S(2)}) %collective-permute-start.8) | collective-permute-done | bytes 131104 | tf_op jit(solution)/shard_map/ppermute | solution.py:321
  34.3 2.5 %collective-permute-start.11 = (bf16[2,2,16,1024]{3,2,1,0:T(8,128)(2,1)S(1)}, bf16[2,2,16,1024]{3,2,1,0:T(8,128)(2,1)S(1)}, u32[]{:S(2)}, u32[]{:S(2)}) collective-permute-start(bf16[2,2,16,1024]{3,2,1,0:T(8,128)(2,1)S(1)} %get-tuple-element.115), channel_id=1, source_target_pairs={{0,6},{1,7},{2,4},{3,5},{4,2},{5,3},{6,0},{7,1},{8,14},{9,15},{10,... | collective-permute-start | bytes 393224 | tf_op jit(solution)/shard_map/ppermute | solution.py:321
  37.2 10.8 %collective-permute-start.13 = (bf16[2,2,16,1024]{3,2,1,0:T(8,128)(2,1)S(1)}, bf16[2,2,16,1024]{3,2,1,0:T(8,128)(2,1)S(1)}, u32[]{:S(2)}, u32[]{:S(2)}) collective-permute-start(bf16[2,2,16,1024]{3,2,1,0:T(8,128)(2,1)S(1)} %get-tuple-element.118), channel_id=1, source_target_pairs={{0,7},{1,6},{2,5},{3,4},{4,3},{5,2},{6,1},{7,0},{8,15},{9,14},{10,... | collective-permute-start | bytes 393224 | tf_op jit(solution)/shard_map/ppermute | solution.py:321
  48.1 2.8 %copy-done = bf16[1024,3072]{1,0:T(8,128)(2,1)S(1)} copy-done((bf16[1024,3072]{1,0:T(8,128)(2,1)S(1)}, bf16[1024,3072]{1,0:T(8,128)(2,1)}, u32[]{:S(2)}) %copy-start) | copy-done | bytes 6291480
  50.9 11.2 %shard_map.68 = (bf16[512,1024]{1,0:T(8,128)(2,1)S(1)}, bf16[512,1024]{1,0:T(8,128)(2,1)S(1)}, bf16[512,1024]{1,0:T(8,128)(2,1)S(1)}, bf16[512,1024]{1,0:T(8,128...) custom-call(bf16[2,2,16,1024]{3,2,1,0:T(8,128)(2,1)S(1)} %get-tuple-, ...), custom_call_target="tpu_custom_call" | custom-call | flops 5368709120 | bytes 12582912 | tf_op jit(solution)/shard_map/pallas_call | solution.py:295
  62.2 11.4 %shard_map.69 = (bf16[512,1024]{1,0:T(8,128)(2,1)S(1)}, bf16[512,1024]{1,0:T(8,128)(2,1)S(1)}, bf16[512,1024]{1,0:T(8,128)(2,1)S(1)}, bf16[512,1024]{1,0:T(8,128...) custom-call(bf16[2,2,16,1024]{3,2,1,0:T(8,128)(2,1)S(1)} %get-tuple-, ...), custom_call_target="tpu_custom_call", output_to_operand_aliasing={{0}: (12, {}), {1}: (13, {}), {2}: (14, {}), {3}: (15, {}),... | custom-call | flops 5368709120 | bytes 12582912 | tf_op jit(solution)/shard_map/pallas_call | solution.py:295
  82.6 4.3 %collective-permute-start.17 = (bf16[2,4,32,2048]{3,2,1,0:T(8,128)(2,1)S(1)}, bf16[2,4,32,2048]{3,2,1,0:T(8,128)(2,1)S(1)}, u32[]{:S(2)}, u32[]{:S(2)}) collective-permute-start(bf16[2,4,32,2048]{3,2,1,0:T(8,128)(2,1)S(1)} %get-tuple-element.163), channel_id=1, source_target_pairs={{0,1},{1,0},{2,3},{3,2},{4,5},{5,4},{6,7},{7,6},{8,9},{9,8},{10,11... | collective-permute-start | bytes 3145736 | tf_op jit(solution)/shard_map/ppermute | solution.py:321
  90.8 3.9 %collective-permute-start.22 = (bf16[4,16,1024]{2,1,0:T(8,128)(2,1)S(1)}, bf16[4,16,1024]{2,1,0:T(8,128)(2,1)S(1)}, u32[]{:S(2)}, u32[]{:S(2)}) collective-permute-start(bf16[4,16,1024]{2,1,0:T(8,128)(2,1)S(1)} %get-tuple-element.171), channel_id=1, source_target_pairs={{0,7},{1,6},{2,5},{3,4},{4,3},{5,2},{6,1},{7,0},{8,15},{9,14},{10,... | collective-permute-start | bytes 393224 | tf_op jit(solution)/shard_map/ppermute | solution.py:321
  94.7 8.7 %collective-permute-done.18.refs_5_ = bf16[4,16,1024]{2,1,0:T(8,128)(2,1)S(1)} collective-permute-done((bf16[4,16,1024]{2,1,0:T(8,128)(2,1)S(1)}, bf16[4,16,1024]{2,1,0:T(8,128)(2,1)S(1)}, u32[]{:S(2)}, u32[]{:S(2)}) %collective-permute-start.18) | collective-permute-done | bytes 131104 | tf_op jit(solution)/shard_map/ppermute | solution.py:321
  103.4 3.4 %collective-permute-start.21 = (bf16[4,16,1024]{2,1,0:T(8,128)(2,1)S(1)}, bf16[4,16,1024]{2,1,0:T(8,128)(2,1)S(1)}, u32[]{:S(2)}, u32[]{:S(2)}) collective-permute-start(bf16[4,16,1024]{2,1,0:T(8,128)(2,1)S(1)} %get-tuple-element.169), channel_id=1, source_target_pairs={{0,3},{1,2},{2,1},{3,0},{4,7},{5,6},{6,5},{7,4},{8,11},{9,10},{10,... | collective-permute-start | bytes 393224 | tf_op jit(solution)/shard_map/ppermute | solution.py:321
  106.8 4.4 %collective-permute-start.23 = (bf16[4,16,1024]{2,1,0:T(8,128)(2,1)S(1)}, bf16[4,16,1024]{2,1,0:T(8,128)(2,1)S(1)}, u32[]{:S(2)}, u32[]{:S(2)}) collective-permute-start(bf16[4,16,1024]{2,1,0:T(8,128)(2,1)S(1)} %get-tuple-element.172), channel_id=1, source_target_pairs={{0,4},{1,5},{2,6},{3,7},{4,0},{5,1},{6,2},{7,3},{8,12},{9,13},{10,... | collective-permute-start | bytes 393224 | tf_op jit(solution)/shard_map/ppermute | solution.py:321
  112.9 2.8 %collective-permute-done.23.refs_4_ = bf16[4,16,1024]{2,1,0:T(8,128)(2,1)S(1)} collective-permute-done((bf16[4,16,1024]{2,1,0:T(8,128)(2,1)S(1)}, bf16[4,16,1024]{2,1,0:T(8,128)(2,1)S(1)}, u32[]{:S(2)}, u32[]{:S(2)}) %collective-permute-start.23) | collective-permute-done | bytes 131104 | tf_op jit(solution)/shard_map/ppermute | solution.py:321
  115.8 3.1 %collective-permute-done.17.refs_1_ = bf16[2,4,32,2048]{3,2,1,0:T(8,128)(2,1)S(1)} collective-permute-done((bf16[2,4,32,2048]{3,2,1,0:T(8,128)(2,1)S(1)}, bf16[2,4,32,2048]{3,2,1,0:T(8,128)(2,1)S(1)}, u32[]{:S(2)}, u32[]{:S(2)}) %collective-permute-start.17) | collective-permute-done | bytes 1048608 | tf_op jit(solution)/shard_map/ppermute | solution.py:321
  123.7 9.4 %collective-permute-done.25.refs_3_ = bf16[4,32,2048]{2,1,0:T(8,128)(2,1)S(1)} collective-permute-done((bf16[4,32,2048]{2,1,0:T(8,128)(2,1)S(1)}, bf16[4,32,2048]{2,1,0:T(8,128)(2,1)S(1)}, u32[]{:S(2)}, u32[]{:S(2)}) %collective-permute-start.25) | collective-permute-done | bytes 524320 | tf_op jit(solution)/shard_map/ppermute | solution.py:321
  133.1 2.0 %collective-permute-done.24.refs_1_ = bf16[4,32,2048]{2,1,0:T(8,128)(2,1)S(1)} collective-permute-done((bf16[4,32,2048]{2,1,0:T(8,128)(2,1)S(1)}, bf16[4,32,2048]{2,1,0:T(8,128)(2,1)S(1)}, u32[]{:S(2)}, u32[]{:S(2)}) %collective-permute-start.24) | collective-permute-done | bytes 524320 | tf_op jit(solution)/shard_map/ppermute | solution.py:321
  136.4 3.9 %collective-permute-start.29 = (bf16[32,4096]{1,0:T(8,128)(2,1)S(1)}, bf16[32,4096]{1,0:T(8,128)(2,1)S(1)}, u32[]{:S(2)}, u32[]{:S(2)}) collective-permute-start(bf16[32,4096]{1,0:T(8,128)(2,1)S(1)} %get-tuple-element.182), channel_id=1, source_target_pairs={{0,6},{1,7},{2,4},{3,5},{4,2},{5,3},{6,0},{7,1},{8,14},{9,15},{10,... | collective-permute-start | bytes 786440 | tf_op jit(solution)/shard_map/ppermute | solution.py:321
  141.7 3.5 %collective-permute-done.26.refs_1_ = bf16[4,16,1024]{2,1,0:T(8,128)(2,1)S(1)} collective-permute-done((bf16[4,16,1024]{2,1,0:T(8,128)(2,1)S(1)}, bf16[4,16,1024]{2,1,0:T(8,128)(2,1)S(1)}, u32[]{:S(2)}, u32[]{:S(2)}) %collective-permute-start.26) | collective-permute-done | bytes 131104 | tf_op jit(solution)/shard_map/ppermute | solution.py:321
  148.0 8.6 %collective-permute-done.28.refs_2_ = bf16[32,4096]{1,0:T(8,128)(2,1)S(1)} collective-permute-done((bf16[32,4096]{1,0:T(8,128)(2,1)S(1)}, bf16[32,4096]{1,0:T(8,128)(2,1)S(1)}, u32[]{:S(2)}, u32[]{:S(2)}) %collective-permute-start.28) | collective-permute-done | bytes 262176 | tf_op jit(solution)/shard_map/ppermute | solution.py:321
  (61 shorter events, 34.9 us)
Async XLA Ops:
  4.0 9.8 %collective-permute-start = (bf16[2,2,16,1024]{3,2,1,0:T(8,128)(2,1)S(1)}, bf16[2,2,16,1024]{3,2,1,0:T(8,128)(2,1)S(1)}, u32[]{:S(2)}, u32[]{:S(2)}) collective-permute-start(bf16[2,2,16,1024]{3,2,1,0:T(8,128)(2,1)S(1)} %get-tuple-element.97), channel_id=1, source_target_pairs={{0,1},{1,0},{2,3},{3,2},{4,5},{5,4},{6,7},{7,6},{8,9},{9,8},{10,11... | collective-permute-start | bytes 393224 | tf_op jit(solution)/shard_map/ppermute | solution.py:321
  8.6 12.6 %collective-permute-start.10 = (bf16[2,2,16,1024]{3,2,1,0:T(8,128)(2,1)S(1)}, bf16[2,2,16,1024]{3,2,1,0:T(8,128)(2,1)S(1)}, u32[]{:S(2)}, u32[]{:S(2)}) collective-permute-start(bf16[2,2,16,1024]{3,2,1,0:T(8,128)(2,1)S(1)} %get-tuple-element.114), channel_id=1, source_target_pairs={{0,6},{1,7},{2,4},{3,5},{4,2},{5,3},{6,0},{7,1},{8,14},{9,15},{10,... | collective-permute-start | bytes 393224 | tf_op jit(solution)/shard_map/ppermute | solution.py:321
  12.6 11.1 %collective-permute-start.12 = (bf16[2,2,16,1024]{3,2,1,0:T(8,128)(2,1)S(1)}, bf16[2,2,16,1024]{3,2,1,0:T(8,128)(2,1)S(1)}, u32[]{:S(2)}, u32[]{:S(2)}) collective-permute-start(bf16[2,2,16,1024]{3,2,1,0:T(8,128)(2,1)S(1)} %get-tuple-element.117), channel_id=1, source_target_pairs={{0,7},{1,6},{2,5},{3,4},{4,3},{5,2},{6,1},{7,0},{8,15},{9,14},{10,... | collective-permute-start | bytes 393224 | tf_op jit(solution)/shard_map/ppermute | solution.py:321
  13.8 20.5 %collective-permute-start.8 = (bf16[2,2,16,1024]{3,2,1,0:T(8,128)(2,1)S(1)}, bf16[2,2,16,1024]{3,2,1,0:T(8,128)(2,1)S(1)}, u32[]{:S(2)}, u32[]{:S(2)}) collective-permute-start(bf16[2,2,16,1024]{3,2,1,0:T(8,128)(2,1)S(1)} %get-tuple-element.111), channel_id=1, source_target_pairs={{0,5},{1,4},{2,7},{3,6},{4,1},{5,0},{6,3},{7,2},{8,13},{9,12},{10,... | collective-permute-start | bytes 393224 | tf_op jit(solution)/shard_map/ppermute | solution.py:321
  14.6 22.6 %collective-permute-start.6 = (bf16[2,2,16,1024]{3,2,1,0:T(8,128)(2,1)S(1)}, bf16[2,2,16,1024]{3,2,1,0:T(8,128)(2,1)S(1)}, u32[]{:S(2)}, u32[]{:S(2)}) collective-permute-start(bf16[2,2,16,1024]{3,2,1,0:T(8,128)(2,1)S(1)} %get-tuple-element.107), channel_id=1, source_target_pairs={{0,4},{1,5},{2,6},{3,7},{4,0},{5,1},{6,2},{7,3},{8,12},{9,13},{10,... | collective-permute-start | bytes 393224 | tf_op jit(solution)/shard_map/ppermute | solution.py:321
  16.5 31.5 %collective-permute-start.1 = (bf16[2,2,16,1024]{3,2,1,0:T(8,128)(2,1)S(1)}, bf16[2,2,16,1024]{3,2,1,0:T(8,128)(2,1)S(1)}, u32[]{:S(2)}, u32[]{:S(2)}) collective-permute-start(bf16[2,2,16,1024]{3,2,1,0:T(8,128)(2,1)S(1)} %get-tuple-element.98), channel_id=1, source_target_pairs={{0,1},{1,0},{2,3},{3,2},{4,5},{5,4},{6,7},{7,6},{8,9},{9,8},{10,11... | collective-permute-start | bytes 393224 | tf_op jit(solution)/shard_map/ppermute | solution.py:321
  21.2 26.8 %collective-permute-start.3 = (bf16[2,2,16,1024]{3,2,1,0:T(8,128)(2,1)S(1)}, bf16[2,2,16,1024]{3,2,1,0:T(8,128)(2,1)S(1)}, u32[]{:S(2)}, u32[]{:S(2)}) collective-permute-start(bf16[2,2,16,1024]{3,2,1,0:T(8,128)(2,1)S(1)} %get-tuple-element.101), channel_id=1, source_target_pairs={{0,2},{1,3},{2,0},{3,1},{4,6},{5,7},{6,4},{7,5},{8,10},{9,11},{10,... | collective-permute-start | bytes 393224 | tf_op jit(solution)/shard_map/ppermute | solution.py:321
  23.7 38.4 %collective-permute-start.5 = (bf16[2,2,16,1024]{3,2,1,0:T(8,128)(2,1)S(1)}, bf16[2,2,16,1024]{3,2,1,0:T(8,128)(2,1)S(1)}, u32[]{:S(2)}, u32[]{:S(2)}) collective-permute-start(bf16[2,2,16,1024]{3,2,1,0:T(8,128)(2,1)S(1)} %get-tuple-element.104), channel_id=1, source_target_pairs={{0,3},{1,2},{2,1},{3,0},{4,7},{5,6},{6,5},{7,4},{8,11},{9,10},{10,... | collective-permute-start | bytes 393224 | tf_op jit(solution)/shard_map/ppermute | solution.py:321
  34.3 27.8 %collective-permute-start.11 = (bf16[2,2,16,1024]{3,2,1,0:T(8,128)(2,1)S(1)}, bf16[2,2,16,1024]{3,2,1,0:T(8,128)(2,1)S(1)}, u32[]{:S(2)}, u32[]{:S(2)}) collective-permute-start(bf16[2,2,16,1024]{3,2,1,0:T(8,128)(2,1)S(1)} %get-tuple-element.115), channel_id=1, source_target_pairs={{0,6},{1,7},{2,4},{3,5},{4,2},{5,3},{6,0},{7,1},{8,14},{9,15},{10,... | collective-permute-start | bytes 393224 | tf_op jit(solution)/shard_map/ppermute | solution.py:321
  37.2 24.9 %collective-permute-start.13 = (bf16[2,2,16,1024]{3,2,1,0:T(8,128)(2,1)S(1)}, bf16[2,2,16,1024]{3,2,1,0:T(8,128)(2,1)S(1)}, u32[]{:S(2)}, u32[]{:S(2)}) collective-permute-start(bf16[2,2,16,1024]{3,2,1,0:T(8,128)(2,1)S(1)} %get-tuple-element.118), channel_id=1, source_target_pairs={{0,7},{1,6},{2,5},{3,4},{4,3},{5,2},{6,1},{7,0},{8,15},{9,14},{10,... | collective-permute-start | bytes 393224 | tf_op jit(solution)/shard_map/ppermute | solution.py:321
  48.0 14.1 %collective-permute-start.9 = (bf16[2,2,16,1024]{3,2,1,0:T(8,128)(2,1)S(1)}, bf16[2,2,16,1024]{3,2,1,0:T(8,128)(2,1)S(1)}, u32[]{:S(2)}, u32[]{:S(2)}) collective-permute-start(bf16[2,2,16,1024]{3,2,1,0:T(8,128)(2,1)S(1)} %get-tuple-element.112), channel_id=1, source_target_pairs={{0,5},{1,4},{2,7},{3,6},{4,1},{5,0},{6,3},{7,2},{8,13},{9,12},{10,... | collective-permute-start | bytes 393224 | tf_op jit(solution)/shard_map/ppermute | solution.py:321
  48.0 14.1 %collective-permute-start.7 = (bf16[2,2,16,1024]{3,2,1,0:T(8,128)(2,1)S(1)}, bf16[2,2,16,1024]{3,2,1,0:T(8,128)(2,1)S(1)}, u32[]{:S(2)}, u32[]{:S(2)}) collective-permute-start(bf16[2,2,16,1024]{3,2,1,0:T(8,128)(2,1)S(1)} %get-tuple-element.108), channel_id=1, source_target_pairs={{0,4},{1,5},{2,6},{3,7},{4,0},{5,1},{6,2},{7,3},{8,12},{9,13},{10,... | collective-permute-start | bytes 393224 | tf_op jit(solution)/shard_map/ppermute | solution.py:321
  77.4 9.6 %collective-permute-start.14 = (bf16[2,4,2,32,2048]{4,3,2,1,0:T(8,128)(2,1)S(1)}, bf16[2,4,2,32,2048]{4,3,2,1,0:T(8,128)(2,1)S(1)}, u32[]{:S(2)}, u32[]{:S(2)}) collective-permute-start(bf16[2,4,2,32,2048]{4,3,2,1,0:T(8,128)(2,1)S(1)} %shard_map.70), channel_id=1, source_target_pairs={{0,8},{8,0},{16,24},{24,16},{1,9},{9,1},{17,25},{25,17},{2,10},{10... | collective-permute-start | bytes 6291464 | tf_op jit(solution)/shard_map/ppermute | solution.py:321
  82.6 36.2 %collective-permute-start.17 = (bf16[2,4,32,2048]{3,2,1,0:T(8,128)(2,1)S(1)}, bf16[2,4,32,2048]{3,2,1,0:T(8,128)(2,1)S(1)}, u32[]{:S(2)}, u32[]{:S(2)}) collective-permute-start(bf16[2,4,32,2048]{3,2,1,0:T(8,128)(2,1)S(1)} %get-tuple-element.163), channel_id=1, source_target_pairs={{0,1},{1,0},{2,3},{3,2},{4,5},{5,4},{6,7},{7,6},{8,9},{9,8},{10,11... | collective-permute-start | bytes 3145736 | tf_op jit(solution)/shard_map/ppermute | solution.py:321
  88.0 30.9 %collective-permute-start.15 = (bf16[4,2,32,2048]{3,2,1,0:T(8,128)(2,1)S(1)}, bf16[4,2,32,2048]{3,2,1,0:T(8,128)(2,1)S(1)}, u32[]{:S(2)}, u32[]{:S(2)}) collective-permute-start(bf16[4,2,32,2048]{3,2,1,0:T(8,128)(2,1)S(1)} %get-tuple-element.158), channel_id=1, source_target_pairs={{0,16},{8,24},{16,0},{24,8},{1,17},{9,25},{17,1},{25,9},{2,18},{10... | collective-permute-start | bytes 3145736 | tf_op jit(solution)/shard_map/ppermute | solution.py:321
  89.5 13.9 %collective-permute-start.18 = (bf16[4,16,1024]{2,1,0:T(8,128)(2,1)S(1)}, bf16[4,16,1024]{2,1,0:T(8,128)(2,1)S(1)}, u32[]{:S(2)}, u32[]{:S(2)}) collective-permute-start(bf16[4,16,1024]{2,1,0:T(8,128)(2,1)S(1)} %get-tuple-element.165), channel_id=1, source_target_pairs={{0,5},{1,4},{2,7},{3,6},{4,1},{5,0},{6,3},{7,2},{8,13},{9,12},{10,... | collective-permute-start | bytes 393224 | tf_op jit(solution)/shard_map/ppermute | solution.py:321
  90.8 12.6 %collective-permute-start.20 = (bf16[4,16,1024]{2,1,0:T(8,128)(2,1)S(1)}, bf16[4,16,1024]{2,1,0:T(8,128)(2,1)S(1)}, u32[]{:S(2)}, u32[]{:S(2)}) collective-permute-start(bf16[4,16,1024]{2,1,0:T(8,128)(2,1)S(1)} %get-tuple-element.168), channel_id=1, source_target_pairs={{0,6},{1,7},{2,4},{3,5},{4,2},{5,3},{6,0},{7,1},{8,14},{9,15},{10,... | collective-permute-start | bytes 393224 | tf_op jit(solution)/shard_map/ppermute | solution.py:321
  90.8 16.0 %collective-permute-start.22 = (bf16[4,16,1024]{2,1,0:T(8,128)(2,1)S(1)}, bf16[4,16,1024]{2,1,0:T(8,128)(2,1)S(1)}, u32[]{:S(2)}, u32[]{:S(2)}) collective-permute-start(bf16[4,16,1024]{2,1,0:T(8,128)(2,1)S(1)} %get-tuple-element.171), channel_id=1, source_target_pairs={{0,7},{1,6},{2,5},{3,4},{4,3},{5,2},{6,1},{7,0},{8,15},{9,14},{10,... | collective-permute-start | bytes 393224 | tf_op jit(solution)/shard_map/ppermute | solution.py:321
  103.4 9.5 %collective-permute-start.21 = (bf16[4,16,1024]{2,1,0:T(8,128)(2,1)S(1)}, bf16[4,16,1024]{2,1,0:T(8,128)(2,1)S(1)}, u32[]{:S(2)}, u32[]{:S(2)}) collective-permute-start(bf16[4,16,1024]{2,1,0:T(8,128)(2,1)S(1)} %get-tuple-element.169), channel_id=1, source_target_pairs={{0,3},{1,2},{2,1},{3,0},{4,7},{5,6},{6,5},{7,4},{8,11},{9,10},{10,... | collective-permute-start | bytes 393224 | tf_op jit(solution)/shard_map/ppermute | solution.py:321
  119.6 13.5 %collective-permute-start.25 = (bf16[4,32,2048]{2,1,0:T(8,128)(2,1)S(1)}, bf16[4,32,2048]{2,1,0:T(8,128)(2,1)S(1)}, u32[]{:S(2)}, u32[]{:S(2)}) collective-permute-start(bf16[4,32,2048]{2,1,0:T(8,128)(2,1)S(1)} %get-tuple-element.179), channel_id=1, source_target_pairs={{0,16},{8,24},{16,0},{24,8},{1,17},{9,25},{17,1},{25,9},{2,18},{10... | collective-permute-start | bytes 1572872 | tf_op jit(solution)/shard_map/ppermute | solution.py:321
  121.9 13.2 %collective-permute-start.24 = (bf16[4,32,2048]{2,1,0:T(8,128)(2,1)S(1)}, bf16[4,32,2048]{2,1,0:T(8,128)(2,1)S(1)}, u32[]{:S(2)}, u32[]{:S(2)}) collective-permute-start(bf16[4,32,2048]{2,1,0:T(8,128)(2,1)S(1)} %get-tuple-element.175), channel_id=1, source_target_pairs={{0,1},{1,0},{2,3},{3,2},{4,5},{5,4},{6,7},{7,6},{8,9},{9,8},{10,11... | collective-permute-start | bytes 1572872 | tf_op jit(solution)/shard_map/ppermute | solution.py:321
  135.8 12.2 %collective-permute-start.27 = (bf16[32,4096]{1,0:T(8,128)(2,1)S(1)}, bf16[32,4096]{1,0:T(8,128)(2,1)S(1)}, u32[]{:S(2)}, u32[]{:S(2)}) collective-permute-start(bf16[32,4096]{1,0:T(8,128)(2,1)S(1)} %get-tuple-element.180), channel_id=1, source_target_pairs={{0,2},{1,3},{2,0},{3,1},{4,6},{5,7},{6,4},{7,5},{8,10},{9,11},{10,... | collective-permute-start | bytes 786440 | tf_op jit(solution)/shard_map/ppermute | solution.py:321
  135.9 20.7 %collective-permute-start.28 = (bf16[32,4096]{1,0:T(8,128)(2,1)S(1)}, bf16[32,4096]{1,0:T(8,128)(2,1)S(1)}, u32[]{:S(2)}, u32[]{:S(2)}) collective-permute-start(bf16[32,4096]{1,0:T(8,128)(2,1)S(1)} %get-tuple-element.181), channel_id=1, source_target_pairs={{0,4},{1,5},{2,6},{3,7},{4,0},{5,1},{6,2},{7,3},{8,12},{9,13},{10,... | collective-permute-start | bytes 786440 | tf_op jit(solution)/shard_map/ppermute | solution.py:321
  136.4 20.2 %collective-permute-start.29 = (bf16[32,4096]{1,0:T(8,128)(2,1)S(1)}, bf16[32,4096]{1,0:T(8,128)(2,1)S(1)}, u32[]{:S(2)}, u32[]{:S(2)}) collective-permute-start(bf16[32,4096]{1,0:T(8,128)(2,1)S(1)} %get-tuple-element.182), channel_id=1, source_target_pairs={{0,6},{1,7},{2,4},{3,5},{4,2},{5,3},{6,0},{7,1},{8,14},{9,15},{10,... | collective-permute-start | bytes 786440 | tf_op jit(solution)/shard_map/ppermute | solution.py:321
  (11 other events, 105.5 us)

commit v5 on v4

--- a/solution.py
+++ b/solution.py
@@ -29,33 +29,50 @@
     return centred * inverse, inverse
 
 
-def pick_kernel(n_slots, n_chunks, ids_ref, x_ref, cot_ref, *out_refs):
-    depth = x_ref.shape[0] // n_chunks
+def pick_kernel(n_slots, n_chunks, n_clips, ids_ref, x_ref, cot_ref, *out_refs):
+    clip = pl.program_id(0)
+    half = n_slots // 2
+    for slot in range(half):
+        out_refs[slot][0, 0] = x_ref[0, ids_ref[1] ^ slot]
+        out_refs[slot][1, 0] = cot_ref[0, ids_ref[1] ^ slot]
     for chunk in range(n_chunks):
-        here = pl.ds(chunk * depth, depth)
-        for slot in range(n_slots):
-            out = out_refs[chunk * n_slots + slot]
-            block = ids_ref[1] ^ slot
-            out[0] = x_ref[here, block]
-            out[1] = cot_ref[here, block]
+
+        @pl.when(clip // (n_clips // n_chunks) == chunk)
+        def _():
+            for slot in range(half, n_slots):
+                out = out_refs[chunk * half + slot]
+                out[0, 0] = x_ref[0, ids_ref[1] ^ slot]
+                out[1, 0] = cot_ref[0, ids_ref[1] ^ slot]
 
 
 def pick(ids, clips, cotangent, n_slots, n_chunks):
     n_clips, _, n_patches, width = clips.shape
-    cut = (n_clips, n_slots, n_patches // n_slots, width)
-    piece = jax.ShapeDtypeStruct((2, n_clips // n_chunks) + cut[2:], clips.dtype)
+    n_positions = n_patches // n_slots
+    cut = (n_clips, n_slots, n_positions, width)
+    half, depth = n_slots // 2, n_clips // n_chunks
+
+    def block(index):
+        return pl.BlockSpec((2, 1, n_positions, width), lambda c: (0, index(c), 0, 0))
+
+    def piece(count):
+        return jax.ShapeDtypeStruct((2, count, n_positions, width), clips.dtype)
+
     out = pl.pallas_call(
-        functools.partial(pick_kernel, n_slots, n_chunks),
-        out_shape=[piece] * (n_slots * n_chunks),
-        in_specs=[
-            pl.BlockSpec(memory_space=pltpu.SMEM),
-            pl.BlockSpec(memory_space=pltpu.VMEM),
-            pl.BlockSpec(memory_space=pltpu.VMEM),
+        functools.partial(pick_kernel, n_slots, n_chunks, n_clips),
+        grid=(n_clips,),
+        out_shape=[piece(n_clips)] * half + [piece(depth)] * (half * n_chunks),
+        in_specs=[pl.BlockSpec(memory_space=pltpu.SMEM)]
+        + [pl.BlockSpec((1,) + cut[1:], lambda c: (c, 0, 0, 0))] * 2,
+        out_specs=[block(lambda c: c)] * half
+        + [
+            block(lambda c, chunk=chunk: jnp.clip(c - chunk * depth, 0, depth - 1))
+            for chunk in range(n_chunks)
+            for _ in range(half)
         ],
-        out_specs=[pl.BlockSpec(memory_space=pltpu.VMEM)] * (n_slots * n_chunks),
-        compiler_params=pltpu.CompilerParams(vmem_limit_bytes=16 * MIB),
+        compiler_params=pltpu.CompilerParams(vmem_limit_bytes=12 * MIB),
     )(ids, clips.reshape(cut), cotangent.reshape(cut))
-    return [out[chunk * n_slots : (chunk + 1) * n_slots] for chunk in range(n_chunks)]
+    far = [out[half + chunk * half :][:half] for chunk in range(n_chunks)]
+    return out[:half], far
 
 
 def place_kernel(ids_ref, *refs):
@@ -277,15 +294,12 @@
                 dx_refs[k][clip] = dx[start : start + span]
 
 
-def sublayer(pieces, w_qkv, w_out, chunk, n_chunks, n_positions, before):
+def sublayer(pieces, n_clips, w_qkv, w_out, chunk, n_chunks, n_positions, before):
     n_pieces = len(pieces)
-    _, n_clips, span, width = pieces[0].shape
+    _, _, span, width = pieces[0].shape
     rows = n_clips * n_pieces * span
     groups = HEADS // GROUP
     wide = width // groups
-
-    def whole(shape):
-        return pl.BlockSpec(shape, lambda j: (0,) * len(shape))
 
     flat = jax.ShapeDtypeStruct((n_chunks * rows, width), jnp.bfloat16)
     dx = jax.ShapeDtypeStruct((n_chunks * n_clips, span, width), jnp.bfloat16)
@@ -296,7 +310,13 @@
         functools.partial(sublayer_kernel, n_clips, n_positions, n_pieces, len(aliased)),
         grid=(groups,),
         out_shape=out_shape,
-        in_specs=[whole(piece.shape) for piece in pieces]
+        in_specs=[
+            pl.BlockSpec(
+                (2, n_clips, span, width),
+                lambda j, i=chunk if piece.shape[1] > n_clips else 0: (0, i, 0, 0),
+            )
+            for piece in pieces
+        ]
         + [pl.BlockSpec((width, wide), lambda j, i=i: (0, i * groups + j)) for i in range(3)]
         + [pl.BlockSpec((wide, width), lambda j: (j, 0))]
         + [pl.BlockSpec(memory_space=pl.ANY)] * len(aliased),
@@ -308,7 +328,7 @@
         + [pl.BlockSpec((n_clips, span, width), lambda j: (chunk, 0, 0))] * n_pieces,
         scratch_shapes=[pltpu.VMEM((rows, width), jnp.float32)],
         input_output_aliases={first + i: i for i in range(len(aliased))},
-        compiler_params=pltpu.CompilerParams(vmem_limit_bytes=28 * MIB),
+        compiler_params=pltpu.CompilerParams(vmem_limit_bytes=50 * MIB),
         cost_estimate=pl.CostEstimate(
             flops=2 * rows * width * (7 * width + 24 * 128),
             bytes_accessed=16 * rows * width + 8 * width * width,
@@ -326,21 +346,16 @@
     return values
 
 
-def inbound(chunks, n_tm):
+def inbound(near, far, n_tm):
     half = n_tm // 2
+    near = [near[0]] + [swap(near[k], "tm", n_tm, k) for k in range(1, half)]
+    gates = [near[i + 1] if i < half // 2 else None for i in range(half)]
     arrived = []
-    for blocks in chunks:
-        pieces = {0: blocks[0]}
-        for k in range(1, half):
-            gate = arrived[-1][k] if arrived else None
-            pieces[k] = swap(blocks[k] if gate is None else after(blocks[k], gate), "tm", n_tm, k)
-        for i, k in enumerate(range(n_tm - 1, half - 1, -1)):
-            gate = arrived[-1][k] if arrived else None
-            if not arrived and i >= half // 2:
-                gate = pieces[i - half // 2 + 1]
-            pieces[k] = swap(blocks[k] if gate is None else after(blocks[k], gate), "tm", n_tm, k)
-        arrived.append([pieces[k] for k in range(n_tm)])
-    return arrived
+    for blocks in far:
+        blocks = [block if gate is None else after(block, gate) for block, gate in zip(blocks, gates)]
+        gates = [swap(block, "tm", n_tm, half + i) for i, block in enumerate(blocks)]
+        arrived.append(gates)
+    return near, arrived
 
 
 def shards(n_clip_devices, n_tm, clips, w_qkv, w_out, cotangent):
@@ -350,12 +365,15 @@
     joined = n_positions % 16 != 0
     ids = jnp.stack([lax.axis_index("clip"), lax.axis_index("tm")]).astype(jnp.int32)
 
-    arrived = inbound(pick(ids, clips, cotangent, n_tm, CHUNKS), n_tm)
+    near, far = inbound(*pick(ids, clips, cotangent, n_tm, CHUNKS), n_tm)
+    depth = n_clips // CHUNKS
     results = None
-    for chunk, pieces in enumerate(arrived):
+    for chunk in range(CHUNKS):
+        pieces = near + far[chunk]
         if joined:
-            pieces = [jnp.stack(pieces, axis=2).reshape(2, n_clips // CHUNKS, -1, width)]
-        results = sublayer(pieces, w_qkv, w_out, chunk, CHUNKS, n_positions, results)
+            pieces = [p[:, chunk * depth :][:, :depth] for p in near] + far[chunk]
+            pieces = [jnp.stack(pieces, axis=2).reshape(2, depth, -1, width)]
+        results = sublayer(pieces, depth, w_qkv, w_out, chunk, CHUNKS, n_positions, results)
     normed, cot, mixed, dq, dk, dv = results[:6]
     dx = list(results[6:])
     if joined:

time: 159 us -> 162 us (1.019)
  waiting for transfers between devices: 49.8 us -> 64.4 us
  starting transfers between devices: 64.1 us -> 50.3 us
  Pallas kernels: 37.3 us -> 40.7 us
    ppermute x30 -> x27, waiting for transfers between devices: 49.8 us -> 64.4 us  [swap(): return lax.ppermute(block, axis, [(i, i ^ distance) for i in range(size)])]
    ppermute x30 -> x27, starting transfers between devices: 64.1 us -> 50.3 us  [swap(): return lax.ppermute(block, axis, [(i, i ^ distance) for i in range(size)])]
    pallas_call x2, Pallas kernels: 22.6 us -> 25.6 us  [sublayer(): pl.pallas_call(functools.partial(sublayer_kernel, n_clips, n_positions, n...]
    unnamed x10 -> x14, local copies, waits for them, and re-layouts: 5.37 us -> 4.91 us
  transfers between devices with their start and end apart: 30 -> 27, of which waited for: 13 -> 13; matrix products, arithmetic and copies ran while one was open for 0% -> 0% of each run, Pallas kernels for 12% -> 13%
where the time goes in v5:
time: 162 us; the launch traced here: 161 us
  waiting for transfers between devices  64.4 us (40%)
  starting transfers between devices  50.3 us (31%)
  Pallas kernels  40.7 us (25%)
  local copies, waits for them, and re-layouts  4.91 us (3%)
    ppermute x27, waiting for transfers between devices, swap(): return lax.ppermute(block, axis, [(i, i ^ distance) for i in range(size)])  64.4 us
    ppermute x27, starting transfers between devices, swap(): return lax.ppermute(block, axis, [(i, i ^ distance) for i in range(size)])  50.3 us
    pallas_call x2, Pallas kernels, sublayer(): pl.pallas_call(functools.partial(sublayer_kernel, n_clips, n_positions, n...  25.6 us
    pallas_call x4, Pallas kernels, products(): pl.pallas_call(functools.partial(product_kernel, n_x, flip, len(lefts)),...  7.36 us
    unnamed x14, local copies, waits for them, and re-layouts  4.91 us
    pallas_call x4, Pallas kernels, halve(): pl.pallas_call(functools.partial(halve_kernel, dim, axis, stride), out_sh...  3.41 us
  transfers between devices with their start and end apart: 27, of which 13 were waited for; matrix products, arithmetic and copies ran while one was open for 0% of the time, Pallas kernels for 13%

profile of v5, /device:TPU:0, one launch (start us, length us, event | category | flops | bytes accessed | tf_op | source)
XLA Modules:
  0.0 161.1 jit_solution(5640542275727145327)
XLA Ops:
  4.3 3.0 %collective-permute-start = (bf16[2,4,16,1024]{3,2,1,0:T(8,128)(2,1)S(1)}, bf16[2,4,16,1024]{3,2,1,0:T(8,128)(2,1)S(1)}, u32[]{:S(2)}, u32[]{:S(2)}) collective-permute-start(bf16[2,4,16,1024]{3,2,1,0:T(8,128)(2,1)S(1)} %get-tuple-element.89), channel_id=1, source_target_pairs={{0,1},{1,0},{2,3},{3,2},{4,5},{5,4},{6,7},{7,6},{8,9},{9,8},{10,11... | collective-permute-start | bytes 786440 | tf_op jit(solution)/shard_map/ppermute | solution.py:341
  9.0 4.0 %collective-permute-start.7 = (bf16[2,2,16,1024]{3,2,1,0:T(8,128)(2,1)S(1)}, bf16[2,2,16,1024]{3,2,1,0:T(8,128)(2,1)S(1)}, u32[]{:S(2)}, u32[]{:S(2)}) collective-permute-start(bf16[2,2,16,1024]{3,2,1,0:T(8,128)(2,1)S(1)} %get-tuple-element.101), channel_id=1, source_target_pairs={{0,6},{1,7},{2,4},{3,5},{4,2},{5,3},{6,0},{7,1},{8,14},{9,15},{10,... | collective-permute-start | bytes 393224 | tf_op jit(solution)/shard_map/ppermute | solution.py:341
  14.1 9.8 %collective-permute-start.3 = (bf16[2,2,16,1024]{3,2,1,0:T(8,128)(2,1)S(1)}, bf16[2,2,16,1024]{3,2,1,0:T(8,128)(2,1)S(1)}, u32[]{:S(2)}, u32[]{:S(2)}) collective-permute-start(bf16[2,2,16,1024]{3,2,1,0:T(8,128)(2,1)S(1)} %get-tuple-element.94), channel_id=1, source_target_pairs={{0,4},{1,5},{2,6},{3,7},{4,0},{5,1},{6,2},{7,3},{8,12},{9,13},{10,... | collective-permute-start | bytes 393224 | tf_op jit(solution)/shard_map/ppermute | solution.py:341
  25.4 2.3 %collective-permute-done.7.refs_6_ = bf16[2,2,16,1024]{3,2,1,0:T(8,128)(2,1)S(1)} collective-permute-done((bf16[2,2,16,1024]{3,2,1,0:T(8,128)(2,1)S(1)}, bf16[2,2,16,1024]{3,2,1,0:T(8,128)(2,1)S(1)}, u32[]{:S(2)}, u32[]{:S(2)}) %collective-permute-start.7) | collective-permute-done | bytes 131104 | tf_op jit(solution)/shard_map/ppermute | solution.py:341
  27.7 1.9 %collective-permute-start.8 = (bf16[2,2,16,1024]{3,2,1,0:T(8,128)(2,1)S(1)}, bf16[2,2,16,1024]{3,2,1,0:T(8,128)(2,1)S(1)}, u32[]{:S(2)}, u32[]{:S(2)}) collective-permute-start(bf16[2,2,16,1024]{3,2,1,0:T(8,128)(2,1)S(1)} %get-tuple-element.102), channel_id=1, source_target_pairs={{0,6},{1,7},{2,4},{3,5},{4,2},{5,3},{6,0},{7,1},{8,14},{9,15},{10,... | collective-permute-start | bytes 393224 | tf_op jit(solution)/shard_map/ppermute | solution.py:341
  31.0 2.3 %collective-permute-start.10 = (bf16[2,2,16,1024]{3,2,1,0:T(8,128)(2,1)S(1)}, bf16[2,2,16,1024]{3,2,1,0:T(8,128)(2,1)S(1)}, u32[]{:S(2)}, u32[]{:S(2)}) collective-permute-start(bf16[2,2,16,1024]{3,2,1,0:T(8,128)(2,1)S(1)} %get-tuple-element.105), channel_id=1, source_target_pairs={{0,7},{1,6},{2,5},{3,4},{4,3},{5,2},{6,1},{7,0},{8,15},{9,14},{10,... | collective-permute-start | bytes 393224 | tf_op jit(solution)/shard_map/ppermute | solution.py:341
  33.4 12.6 %collective-permute-done.3.refs_4_ = bf16[2,2,16,1024]{3,2,1,0:T(8,128)(2,1)S(1)} collective-permute-done((bf16[2,2,16,1024]{3,2,1,0:T(8,128)(2,1)S(1)}, bf16[2,2,16,1024]{3,2,1,0:T(8,128)(2,1)S(1)}, u32[]{:S(2)}, u32[]{:S(2)}) %collective-permute-start.3) | collective-permute-done | bytes 131104 | tf_op jit(solution)/shard_map/ppermute | solution.py:341
  46.0 3.3 %collective-permute-done.5.refs_5_ = bf16[2,2,16,1024]{3,2,1,0:T(8,128)(2,1)S(1)} collective-permute-done((bf16[2,2,16,1024]{3,2,1,0:T(8,128)(2,1)S(1)}, bf16[2,2,16,1024]{3,2,1,0:T(8,128)(2,1)S(1)}, u32[]{:S(2)}, u32[]{:S(2)}) %collective-permute-start.5) | collective-permute-done | bytes 131104 | tf_op jit(solution)/shard_map/ppermute | solution.py:341
  49.4 12.7 %shard_map.68 = (bf16[512,1024]{1,0:T(8,128)(2,1)S(1)}, bf16[512,1024]{1,0:T(8,128)(2,1)}, bf16[512,1024]{1,0:T(8,128)(2,1)}, bf16[512,1024]{1,0:T(8,128)(2,1)},...) custom-call(bf16[2,4,16,1024]{3,2,1,0:T(8,128)(2,1)S(1)} %get-tuple-, ...), custom_call_target="tpu_custom_call" | custom-call | flops 5368709120 | bytes 12582912 | tf_op jit(solution)/shard_map/pallas_call | solution.py:309
  62.2 12.8 %shard_map.69 = (bf16[512,1024]{1,0:T(8,128)(2,1)S(1)}, bf16[512,1024]{1,0:T(8,128)(2,1)}, bf16[512,1024]{1,0:T(8,128)(2,1)}, bf16[512,1024]{1,0:T(8,128)(2,1)},...) custom-call(bf16[2,4,16,1024]{3,2,1,0:T(8,128)(2,1)S(1)} %get-tuple-, ...), custom_call_target="tpu_custom_call", output_to_operand_aliasing={{0}: (12, {}), {1}: (13, {}), {2}: (14, {}), {3}: (15, {}),... | custom-call | flops 5368709120 | bytes 12582912 | tf_op jit(solution)/shard_map/pallas_call | solution.py:309
  79.3 1.8 %shard_map.71 = bf16[2,4,2,32,2048]{4,3,2,1,0:T(8,128)(2,1)S(1)} custom-call(s32[2]{0:T(128)S(1)} %pad_add_fusion.ids_ref, bf16[512,1024]{1,0:T(8,128)(2,1)S(1)} %get-tuple-element.145.refs_0_, bf16[512,1024]{1,0:T(8,128)(2,1)S(1)} %copy-done.1, bf16[512,1024]{1,0:T(8,128)(2,1)S(1)} %copy-done.2, bf16[512,1024]{1,0:T(8,128)(2,1)S(1)} %copy-done), custom_call_target="tpu_custom_call" | custom-call | flops 1073741824 | bytes 6291456 | tf_op jit(solution)/shard_map/pallas_call | solution.py:113
  91.0 3.7 %collective-permute-start.15 = (bf16[4,16,1024]{2,1,0:T(8,128)(2,1)S(1)}, bf16[4,16,1024]{2,1,0:T(8,128)(2,1)S(1)}, u32[]{:S(2)}, u32[]{:S(2)}) collective-permute-start(bf16[4,16,1024]{2,1,0:T(8,128)(2,1)S(1)} %get-tuple-element.151), channel_id=1, source_target_pairs={{0,5},{1,4},{2,7},{3,6},{4,1},{5,0},{6,3},{7,2},{8,13},{9,12},{10,... | collective-permute-start | bytes 393224 | tf_op jit(solution)/shard_map/ppermute | solution.py:341
  96.0 2.9 %collective-permute-start.19 = (bf16[4,16,1024]{2,1,0:T(8,128)(2,1)S(1)}, bf16[4,16,1024]{2,1,0:T(8,128)(2,1)S(1)}, u32[]{:S(2)}, u32[]{:S(2)}) collective-permute-start(bf16[4,16,1024]{2,1,0:T(8,128)(2,1)S(1)} %get-tuple-element.157), channel_id=1, source_target_pairs={{0,7},{1,6},{2,5},{3,4},{4,3},{5,2},{6,1},{7,0},{8,15},{9,14},{10,... | collective-permute-start | bytes 393224 | tf_op jit(solution)/shard_map/ppermute | solution.py:341
  98.9 8.6 %collective-permute-done.15.refs_5_ = bf16[4,16,1024]{2,1,0:T(8,128)(2,1)S(1)} collective-permute-done((bf16[4,16,1024]{2,1,0:T(8,128)(2,1)S(1)}, bf16[4,16,1024]{2,1,0:T(8,128)(2,1)S(1)}, u32[]{:S(2)}, u32[]{:S(2)}) %collective-permute-start.15) | collective-permute-done | bytes 131104 | tf_op jit(solution)/shard_map/ppermute | solution.py:341
  107.6 3.4 %collective-permute-start.18 = (bf16[4,16,1024]{2,1,0:T(8,128)(2,1)S(1)}, bf16[4,16,1024]{2,1,0:T(8,128)(2,1)S(1)}, u32[]{:S(2)}, u32[]{:S(2)}) collective-permute-start(bf16[4,16,1024]{2,1,0:T(8,128)(2,1)S(1)} %get-tuple-element.155), channel_id=1, source_target_pairs={{0,3},{1,2},{2,1},{3,0},{4,7},{5,6},{6,5},{7,4},{8,11},{9,10},{10,... | collective-permute-start | bytes 393224 | tf_op jit(solution)/shard_map/ppermute | solution.py:341
  110.9 2.0 %collective-permute-start.20 = (bf16[4,16,1024]{2,1,0:T(8,128)(2,1)S(1)}, bf16[4,16,1024]{2,1,0:T(8,128)(2,1)S(1)}, u32[]{:S(2)}, u32[]{:S(2)}) collective-permute-start(bf16[4,16,1024]{2,1,0:T(8,128)(2,1)S(1)} %get-tuple-element.158), channel_id=1, source_target_pairs={{0,4},{1,5},{2,6},{3,7},{4,0},{5,1},{6,2},{7,3},{8,12},{9,13},{10,... | collective-permute-start | bytes 393224 | tf_op jit(solution)/shard_map/ppermute | solution.py:341
  112.9 3.0 %collective-permute-done.18.refs_3_ = bf16[4,16,1024]{2,1,0:T(8,128)(2,1)S(1)} collective-permute-done((bf16[4,16,1024]{2,1,0:T(8,128)(2,1)S(1)}, bf16[4,16,1024]{2,1,0:T(8,128)(2,1)S(1)}, u32[]{:S(2)}, u32[]{:S(2)}) %collective-permute-start.18) | collective-permute-done | bytes 131104 | tf_op jit(solution)/shard_map/ppermute | solution.py:341
  115.9 3.5 %collective-permute-done.20.refs_4_ = bf16[4,16,1024]{2,1,0:T(8,128)(2,1)S(1)} collective-permute-done((bf16[4,16,1024]{2,1,0:T(8,128)(2,1)S(1)}, bf16[4,16,1024]{2,1,0:T(8,128)(2,1)S(1)}, u32[]{:S(2)}, u32[]{:S(2)}) %collective-permute-start.20) | collective-permute-done | bytes 131104 | tf_op jit(solution)/shard_map/ppermute | solution.py:341
  124.1 9.8 %collective-permute-done.22.refs_3_ = bf16[4,32,2048]{2,1,0:T(8,128)(2,1)S(1)} collective-permute-done((bf16[4,32,2048]{2,1,0:T(8,128)(2,1)S(1)}, bf16[4,32,2048]{2,1,0:T(8,128)(2,1)S(1)}, u32[]{:S(2)}, u32[]{:S(2)}) %collective-permute-start.22) | collective-permute-done | bytes 524320 | tf_op jit(solution)/shard_map/ppermute | solution.py:341
  134.0 2.0 %collective-permute-done.21.refs_1_ = bf16[4,32,2048]{2,1,0:T(8,128)(2,1)S(1)} collective-permute-done((bf16[4,32,2048]{2,1,0:T(8,128)(2,1)S(1)}, bf16[4,32,2048]{2,1,0:T(8,128)(2,1)S(1)}, u32[]{:S(2)}, u32[]{:S(2)}) %collective-permute-start.21) | collective-permute-done | bytes 524320 | tf_op jit(solution)/shard_map/ppermute | solution.py:341
  136.7 2.8 %collective-permute-start.24 = (bf16[32,4096]{1,0:T(8,128)(2,1)S(1)}, bf16[32,4096]{1,0:T(8,128)(2,1)S(1)}, u32[]{:S(2)}, u32[]{:S(2)}) collective-permute-start(bf16[32,4096]{1,0:T(8,128)(2,1)S(1)} %get-tuple-element.166), channel_id=1, source_target_pairs={{0,2},{1,3},{2,0},{3,1},{4,6},{5,7},{6,4},{7,5},{8,10},{9,11},{10,... | collective-permute-start | bytes 786440 | tf_op jit(solution)/shard_map/ppermute | solution.py:341
  140.0 1.9 %collective-permute-start.26 = (bf16[32,4096]{1,0:T(8,128)(2,1)S(1)}, bf16[32,4096]{1,0:T(8,128)(2,1)S(1)}, u32[]{:S(2)}, u32[]{:S(2)}) collective-permute-start(bf16[32,4096]{1,0:T(8,128)(2,1)S(1)} %get-tuple-element.168), channel_id=1, source_target_pairs={{0,6},{1,7},{2,4},{3,5},{4,2},{5,3},{6,0},{7,1},{8,14},{9,15},{10,... | collective-permute-start | bytes 786440 | tf_op jit(solution)/shard_map/ppermute | solution.py:341
  142.5 4.4 %collective-permute-done.23.refs_1_ = bf16[4,16,1024]{2,1,0:T(8,128)(2,1)S(1)} collective-permute-done((bf16[4,16,1024]{2,1,0:T(8,128)(2,1)S(1)}, bf16[4,16,1024]{2,1,0:T(8,128)(2,1)S(1)}, u32[]{:S(2)}, u32[]{:S(2)}) %collective-permute-start.23) | collective-permute-done | bytes 131104 | tf_op jit(solution)/shard_map/ppermute | solution.py:341
  148.5 11.7 %collective-permute-done.25.refs_2_ = bf16[32,4096]{1,0:T(8,128)(2,1)S(1)} collective-permute-done((bf16[32,4096]{1,0:T(8,128)(2,1)S(1)}, bf16[32,4096]{1,0:T(8,128)(2,1)S(1)}, u32[]{:S(2)}, u32[]{:S(2)}) %collective-permute-start.25) | collective-permute-done | bytes 262176 | tf_op jit(solution)/shard_map/ppermute | solution.py:341
  (59 shorter events, 33.9 us)
Async XLA Ops:
  4.3 9.8 %collective-permute-start = (bf16[2,4,16,1024]{3,2,1,0:T(8,128)(2,1)S(1)}, bf16[2,4,16,1024]{3,2,1,0:T(8,128)(2,1)S(1)}, u32[]{:S(2)}, u32[]{:S(2)}) collective-permute-start(bf16[2,4,16,1024]{3,2,1,0:T(8,128)(2,1)S(1)} %get-tuple-element.89), channel_id=1, source_target_pairs={{0,1},{1,0},{2,3},{3,2},{4,5},{5,4},{6,7},{7,6},{8,9},{9,8},{10,11... | collective-permute-start | bytes 786440 | tf_op jit(solution)/shard_map/ppermute | solution.py:341
  7.4 16.6 %collective-permute-start.1 = (bf16[2,4,16,1024]{3,2,1,0:T(8,128)(2,1)S(1)}, bf16[2,4,16,1024]{3,2,1,0:T(8,128)(2,1)S(1)}, u32[]{:S(2)}, u32[]{:S(2)}) collective-permute-start(bf16[2,4,16,1024]{3,2,1,0:T(8,128)(2,1)S(1)} %get-tuple-element.90), channel_id=1, source_target_pairs={{0,2},{1,3},{2,0},{3,1},{4,6},{5,7},{6,4},{7,5},{8,10},{9,11},{10,... | collective-permute-start | bytes 786440 | tf_op jit(solution)/shard_map/ppermute | solution.py:341
  8.9 40.5 %collective-permute-start.2 = (bf16[2,4,16,1024]{3,2,1,0:T(8,128)(2,1)S(1)}, bf16[2,4,16,1024]{3,2,1,0:T(8,128)(2,1)S(1)}, u32[]{:S(2)}, u32[]{:S(2)}) collective-permute-start(bf16[2,4,16,1024]{3,2,1,0:T(8,128)(2,1)S(1)} %get-tuple-element.91), channel_id=1, source_target_pairs={{0,3},{1,2},{2,1},{3,0},{4,7},{5,6},{6,5},{7,4},{8,11},{9,10},{10,... | collective-permute-start | bytes 786440 | tf_op jit(solution)/shard_map/ppermute | solution.py:341
  9.0 18.8 %collective-permute-start.7 = (bf16[2,2,16,1024]{3,2,1,0:T(8,128)(2,1)S(1)}, bf16[2,2,16,1024]{3,2,1,0:T(8,128)(2,1)S(1)}, u32[]{:S(2)}, u32[]{:S(2)}) collective-permute-start(bf16[2,2,16,1024]{3,2,1,0:T(8,128)(2,1)S(1)} %get-tuple-element.101), channel_id=1, source_target_pairs={{0,6},{1,7},{2,4},{3,5},{4,2},{5,3},{6,0},{7,1},{8,14},{9,15},{10,... | collective-permute-start | bytes 393224 | tf_op jit(solution)/shard_map/ppermute | solution.py:341
  12.9 18.1 %collective-permute-start.9 = (bf16[2,2,16,1024]{3,2,1,0:T(8,128)(2,1)S(1)}, bf16[2,2,16,1024]{3,2,1,0:T(8,128)(2,1)S(1)}, u32[]{:S(2)}, u32[]{:S(2)}) collective-permute-start(bf16[2,2,16,1024]{3,2,1,0:T(8,128)(2,1)S(1)} %get-tuple-element.104), channel_id=1, source_target_pairs={{0,7},{1,6},{2,5},{3,4},{4,3},{5,2},{6,1},{7,0},{8,15},{9,14},{10,... | collective-permute-start | bytes 393224 | tf_op jit(solution)/shard_map/ppermute | solution.py:341
  14.1 31.9 %collective-permute-start.3 = (bf16[2,2,16,1024]{3,2,1,0:T(8,128)(2,1)S(1)}, bf16[2,2,16,1024]{3,2,1,0:T(8,128)(2,1)S(1)}, u32[]{:S(2)}, u32[]{:S(2)}) collective-permute-start(bf16[2,2,16,1024]{3,2,1,0:T(8,128)(2,1)S(1)} %get-tuple-element.94), channel_id=1, source_target_pairs={{0,4},{1,5},{2,6},{3,7},{4,0},{5,1},{6,2},{7,3},{8,12},{9,13},{10,... | collective-permute-start | bytes 393224 | tf_op jit(solution)/shard_map/ppermute | solution.py:341
  23.9 25.4 %collective-permute-start.5 = (bf16[2,2,16,1024]{3,2,1,0:T(8,128)(2,1)S(1)}, bf16[2,2,16,1024]{3,2,1,0:T(8,128)(2,1)S(1)}, u32[]{:S(2)}, u32[]{:S(2)}) collective-permute-start(bf16[2,2,16,1024]{3,2,1,0:T(8,128)(2,1)S(1)} %get-tuple-element.98), channel_id=1, source_target_pairs={{0,5},{1,4},{2,7},{3,6},{4,1},{5,0},{6,3},{7,2},{8,13},{9,12},{10,... | collective-permute-start | bytes 393224 | tf_op jit(solution)/shard_map/ppermute | solution.py:341
  27.7 34.4 %collective-permute-start.8 = (bf16[2,2,16,1024]{3,2,1,0:T(8,128)(2,1)S(1)}, bf16[2,2,16,1024]{3,2,1,0:T(8,128)(2,1)S(1)}, u32[]{:S(2)}, u32[]{:S(2)}) collective-permute-start(bf16[2,2,16,1024]{3,2,1,0:T(8,128)(2,1)S(1)} %get-tuple-element.102), channel_id=1, source_target_pairs={{0,6},{1,7},{2,4},{3,5},{4,2},{5,3},{6,0},{7,1},{8,14},{9,15},{10,... | collective-permute-start | bytes 393224 | tf_op jit(solution)/shard_map/ppermute | solution.py:341
  31.0 31.1 %collective-permute-start.10 = (bf16[2,2,16,1024]{3,2,1,0:T(8,128)(2,1)S(1)}, bf16[2,2,16,1024]{3,2,1,0:T(8,128)(2,1)S(1)}, u32[]{:S(2)}, u32[]{:S(2)}) collective-permute-start(bf16[2,2,16,1024]{3,2,1,0:T(8,128)(2,1)S(1)} %get-tuple-element.105), channel_id=1, source_target_pairs={{0,7},{1,6},{2,5},{3,4},{4,3},{5,2},{6,1},{7,0},{8,15},{9,14},{10,... | collective-permute-start | bytes 393224 | tf_op jit(solution)/shard_map/ppermute | solution.py:341
  46.0 16.2 %collective-permute-start.4 = (bf16[2,2,16,1024]{3,2,1,0:T(8,128)(2,1)S(1)}, bf16[2,2,16,1024]{3,2,1,0:T(8,128)(2,1)S(1)}, u32[]{:S(2)}, u32[]{:S(2)}) collective-permute-start(bf16[2,2,16,1024]{3,2,1,0:T(8,128)(2,1)S(1)} %get-tuple-element.95), channel_id=1, source_target_pairs={{0,4},{1,5},{2,6},{3,7},{4,0},{5,1},{6,2},{7,3},{8,12},{9,13},{10,... | collective-permute-start | bytes 393224 | tf_op jit(solution)/shard_map/ppermute | solution.py:341
  49.3 12.9 %collective-permute-start.6 = (bf16[2,2,16,1024]{3,2,1,0:T(8,128)(2,1)S(1)}, bf16[2,2,16,1024]{3,2,1,0:T(8,128)(2,1)S(1)}, u32[]{:S(2)}, u32[]{:S(2)}) collective-permute-start(bf16[2,2,16,1024]{3,2,1,0:T(8,128)(2,1)S(1)} %get-tuple-element.99), channel_id=1, source_target_pairs={{0,5},{1,4},{2,7},{3,6},{4,1},{5,0},{6,3},{7,2},{8,13},{9,12},{10,... | collective-permute-start | bytes 393224 | tf_op jit(solution)/shard_map/ppermute | solution.py:341
  81.3 7.1 %collective-permute-start.11 = (bf16[2,4,2,32,2048]{4,3,2,1,0:T(8,128)(2,1)S(1)}, bf16[2,4,2,32,2048]{4,3,2,1,0:T(8,128)(2,1)S(1)}, u32[]{:S(2)}, u32[]{:S(2)}) collective-permute-start(bf16[2,4,2,32,2048]{4,3,2,1,0:T(8,128)(2,1)S(1)} %shard_map.70), channel_id=1, source_target_pairs={{0,8},{8,0},{16,24},{24,16},{1,9},{9,1},{17,25},{25,17},{2,10},{10... | collective-permute-start | bytes 6291464 | tf_op jit(solution)/shard_map/ppermute | solution.py:341
  86.5 33.6 %collective-permute-start.14 = (bf16[2,4,32,2048]{3,2,1,0:T(8,128)(2,1)S(1)}, bf16[2,4,32,2048]{3,2,1,0:T(8,128)(2,1)S(1)}, u32[]{:S(2)}, u32[]{:S(2)}) collective-permute-start(bf16[2,4,32,2048]{3,2,1,0:T(8,128)(2,1)S(1)} %get-tuple-element.149), channel_id=1, source_target_pairs={{0,1},{1,0},{2,3},{3,2},{4,5},{5,4},{6,7},{7,6},{8,9},{9,8},{10,11... | collective-permute-start | bytes 3145736 | tf_op jit(solution)/shard_map/ppermute | solution.py:341
  89.4 30.7 %collective-permute-start.12 = (bf16[4,2,32,2048]{3,2,1,0:T(8,128)(2,1)S(1)}, bf16[4,2,32,2048]{3,2,1,0:T(8,128)(2,1)S(1)}, u32[]{:S(2)}, u32[]{:S(2)}) collective-permute-start(bf16[4,2,32,2048]{3,2,1,0:T(8,128)(2,1)S(1)} %get-tuple-element.144), channel_id=1, source_target_pairs={{0,16},{8,24},{16,0},{24,8},{1,17},{9,25},{17,1},{25,9},{2,18},{10... | collective-permute-start | bytes 3145736 | tf_op jit(solution)/shard_map/ppermute | solution.py:341
  91.0 16.6 %collective-permute-start.15 = (bf16[4,16,1024]{2,1,0:T(8,128)(2,1)S(1)}, bf16[4,16,1024]{2,1,0:T(8,128)(2,1)S(1)}, u32[]{:S(2)}, u32[]{:S(2)}) collective-permute-start(bf16[4,16,1024]{2,1,0:T(8,128)(2,1)S(1)} %get-tuple-element.151), channel_id=1, source_target_pairs={{0,5},{1,4},{2,7},{3,6},{4,1},{5,0},{6,3},{7,2},{8,13},{9,12},{10,... | collective-permute-start | bytes 393224 | tf_op jit(solution)/shard_map/ppermute | solution.py:341
  94.7 12.9 %collective-permute-start.17 = (bf16[4,16,1024]{2,1,0:T(8,128)(2,1)S(1)}, bf16[4,16,1024]{2,1,0:T(8,128)(2,1)S(1)}, u32[]{:S(2)}, u32[]{:S(2)}) collective-permute-start(bf16[4,16,1024]{2,1,0:T(8,128)(2,1)S(1)} %get-tuple-element.154), channel_id=1, source_target_pairs={{0,6},{1,7},{2,4},{3,5},{4,2},{5,3},{6,0},{7,1},{8,14},{9,15},{10,... | collective-permute-start | bytes 393224 | tf_op jit(solution)/shard_map/ppermute | solution.py:341
  96.0 14.9 %collective-permute-start.19 = (bf16[4,16,1024]{2,1,0:T(8,128)(2,1)S(1)}, bf16[4,16,1024]{2,1,0:T(8,128)(2,1)S(1)}, u32[]{:S(2)}, u32[]{:S(2)}) collective-permute-start(bf16[4,16,1024]{2,1,0:T(8,128)(2,1)S(1)} %get-tuple-element.157), channel_id=1, source_target_pairs={{0,7},{1,6},{2,5},{3,4},{4,3},{5,2},{6,1},{7,0},{8,15},{9,14},{10,... | collective-permute-start | bytes 393224 | tf_op jit(solution)/shard_map/ppermute | solution.py:341
  107.6 8.3 %collective-permute-start.18 = (bf16[4,16,1024]{2,1,0:T(8,128)(2,1)S(1)}, bf16[4,16,1024]{2,1,0:T(8,128)(2,1)S(1)}, u32[]{:S(2)}, u32[]{:S(2)}) collective-permute-start(bf16[4,16,1024]{2,1,0:T(8,128)(2,1)S(1)} %get-tuple-element.155), channel_id=1, source_target_pairs={{0,3},{1,2},{2,1},{3,0},{4,7},{5,6},{6,5},{7,4},{8,11},{9,10},{10,... | collective-permute-start | bytes 393224 | tf_op jit(solution)/shard_map/ppermute | solution.py:341
  110.9 8.4 %collective-permute-start.20 = (bf16[4,16,1024]{2,1,0:T(8,128)(2,1)S(1)}, bf16[4,16,1024]{2,1,0:T(8,128)(2,1)S(1)}, u32[]{:S(2)}, u32[]{:S(2)}) collective-permute-start(bf16[4,16,1024]{2,1,0:T(8,128)(2,1)S(1)} %get-tuple-element.158), channel_id=1, source_target_pairs={{0,4},{1,5},{2,6},{3,7},{4,0},{5,1},{6,2},{7,3},{8,12},{9,13},{10,... | collective-permute-start | bytes 393224 | tf_op jit(solution)/shard_map/ppermute | solution.py:341
  120.8 13.1 %collective-permute-start.22 = (bf16[4,32,2048]{2,1,0:T(8,128)(2,1)S(1)}, bf16[4,32,2048]{2,1,0:T(8,128)(2,1)S(1)}, u32[]{:S(2)}, u32[]{:S(2)}) collective-permute-start(bf16[4,32,2048]{2,1,0:T(8,128)(2,1)S(1)} %get-tuple-element.165), channel_id=1, source_target_pairs={{0,16},{8,24},{16,0},{24,8},{1,17},{9,25},{17,1},{25,9},{2,18},{10... | collective-permute-start | bytes 1572872 | tf_op jit(solution)/shard_map/ppermute | solution.py:341
  123.1 12.8 %collective-permute-start.21 = (bf16[4,32,2048]{2,1,0:T(8,128)(2,1)S(1)}, bf16[4,32,2048]{2,1,0:T(8,128)(2,1)S(1)}, u32[]{:S(2)}, u32[]{:S(2)}) collective-permute-start(bf16[4,32,2048]{2,1,0:T(8,128)(2,1)S(1)} %get-tuple-element.161), channel_id=1, source_target_pairs={{0,1},{1,0},{2,3},{3,2},{4,5},{5,4},{6,7},{7,6},{8,9},{9,8},{10,11... | collective-permute-start | bytes 1572872 | tf_op jit(solution)/shard_map/ppermute | solution.py:341
  136.7 11.8 %collective-permute-start.24 = (bf16[32,4096]{1,0:T(8,128)(2,1)S(1)}, bf16[32,4096]{1,0:T(8,128)(2,1)S(1)}, u32[]{:S(2)}, u32[]{:S(2)}) collective-permute-start(bf16[32,4096]{1,0:T(8,128)(2,1)S(1)} %get-tuple-element.166), channel_id=1, source_target_pairs={{0,2},{1,3},{2,0},{3,1},{4,6},{5,7},{6,4},{7,5},{8,10},{9,11},{10,... | collective-permute-start | bytes 786440 | tf_op jit(solution)/shard_map/ppermute | solution.py:341
  139.5 20.7 %collective-permute-start.25 = (bf16[32,4096]{1,0:T(8,128)(2,1)S(1)}, bf16[32,4096]{1,0:T(8,128)(2,1)S(1)}, u32[]{:S(2)}, u32[]{:S(2)}) collective-permute-start(bf16[32,4096]{1,0:T(8,128)(2,1)S(1)} %get-tuple-element.167), channel_id=1, source_target_pairs={{0,4},{1,5},{2,6},{3,7},{4,0},{5,1},{6,2},{7,3},{8,12},{9,13},{10,... | collective-permute-start | bytes 786440 | tf_op jit(solution)/shard_map/ppermute | solution.py:341
  140.0 20.2 %collective-permute-start.26 = (bf16[32,4096]{1,0:T(8,128)(2,1)S(1)}, bf16[32,4096]{1,0:T(8,128)(2,1)S(1)}, u32[]{:S(2)}, u32[]{:S(2)}) collective-permute-start(bf16[32,4096]{1,0:T(8,128)(2,1)S(1)} %get-tuple-element.168), channel_id=1, source_target_pairs={{0,6},{1,7},{2,4},{3,5},{4,2},{5,3},{6,0},{7,1},{8,14},{9,15},{10,... | collective-permute-start | bytes 786440 | tf_op jit(solution)/shard_map/ppermute | solution.py:341
  (10 other events, 25.1 us)

commit v6 on v4

--- a/solution.py
+++ b/solution.py
@@ -29,50 +29,55 @@
     return centred * inverse, inverse
 
 
-def pick_kernel(n_slots, n_chunks, ids_ref, x_ref, cot_ref, *out_refs):
+def pick_kernel(n_slots, n_chunks, ids_ref, x_ref, cot_ref, near_ref, *far_refs):
+    half = n_slots // 2
+    base = ids_ref[1] - lax.rem(ids_ref[1], half)
+    for j in range(half):
+        near_ref[j, 0] = x_ref[:, base + j]
+        near_ref[j, 1] = cot_ref[:, base + j]
     depth = x_ref.shape[0] // n_chunks
-    for chunk in range(n_chunks):
-        here = pl.ds(chunk * depth, depth)
-        for slot in range(n_slots):
-            out = out_refs[chunk * n_slots + slot]
-            block = ids_ref[1] ^ slot
-            out[0] = x_ref[here, block]
-            out[1] = cot_ref[here, block]
+    for i, ref in enumerate(far_refs):
+        here = pl.ds(i // half * depth, depth)
+        slot = ids_ref[1] ^ (half + i % half)
+        ref[0] = x_ref[here, slot]
+        ref[1] = cot_ref[here, slot]
 
 
 def pick(ids, clips, cotangent, n_slots, n_chunks):
     n_clips, _, n_patches, width = clips.shape
     cut = (n_clips, n_slots, n_patches // n_slots, width)
-    piece = jax.ShapeDtypeStruct((2, n_clips // n_chunks) + cut[2:], clips.dtype)
-    out = pl.pallas_call(
+    half = n_slots // 2
+    near = jax.ShapeDtypeStruct((half, 2, n_clips) + cut[2:], clips.dtype)
+    far = jax.ShapeDtypeStruct((2, n_clips // n_chunks) + cut[2:], clips.dtype)
+    near, *far = pl.pallas_call(
         functools.partial(pick_kernel, n_slots, n_chunks),
-        out_shape=[piece] * (n_slots * n_chunks),
-        in_specs=[
-            pl.BlockSpec(memory_space=pltpu.SMEM),
-            pl.BlockSpec(memory_space=pltpu.VMEM),
-            pl.BlockSpec(memory_space=pltpu.VMEM),
-        ],
-        out_specs=[pl.BlockSpec(memory_space=pltpu.VMEM)] * (n_slots * n_chunks),
-        compiler_params=pltpu.CompilerParams(vmem_limit_bytes=16 * MIB),
+        out_shape=[near] + [far] * (half * n_chunks),
+        in_specs=[pl.BlockSpec(memory_space=pltpu.SMEM)]
+        + [pl.BlockSpec(memory_space=pltpu.VMEM)] * 2,
+        out_specs=[pl.BlockSpec(memory_space=pltpu.VMEM)] * (1 + half * n_chunks),
+        compiler_params=pltpu.CompilerParams(vmem_limit_bytes=12 * MIB),
     )(ids, clips.reshape(cut), cotangent.reshape(cut))
-    return [out[chunk * n_slots : (chunk + 1) * n_slots] for chunk in range(n_chunks)]
-
-
-def place_kernel(ids_ref, *refs):
-    for slot, ref in enumerate(refs[:-1]):
-        refs[-1][:, ids_ref[1] ^ slot] = ref[...]
-
-
-def place(ids, blocks):
-    n_clips, n_positions, width = blocks[0].shape
+    return near, [far[chunk * half :][:half] for chunk in range(n_chunks)]
+
+
+def place_kernel(ids_ref, near_ref, *refs):
+    half = len(refs) - 1
+    base = ids_ref[1] - lax.rem(ids_ref[1], half)
+    for i in range(half):
+        refs[-1][:, base + i] = near_ref[i]
+        refs[-1][:, ids_ref[1] ^ (half + i)] = refs[i][...]
+
+
+def place(ids, near, far):
+    half, n_clips, n_positions, width = near.shape
     return pl.pallas_call(
         place_kernel,
-        out_shape=jax.ShapeDtypeStruct((n_clips, len(blocks), n_positions, width), blocks[0].dtype),
+        out_shape=jax.ShapeDtypeStruct((n_clips, 2 * half, n_positions, width), near.dtype),
         in_specs=[pl.BlockSpec(memory_space=pltpu.SMEM)]
-        + [pl.BlockSpec(memory_space=pltpu.VMEM)] * len(blocks),
+        + [pl.BlockSpec(memory_space=pltpu.VMEM)] * (1 + half),
         out_specs=pl.BlockSpec(memory_space=pltpu.VMEM),
         compiler_params=pltpu.CompilerParams(vmem_limit_bytes=8 * MIB),
-    )(ids, *blocks)
+    )(ids, near, *far)
 
 
 def product_kernel(n_x, flip, n_lefts, ids_ref, *refs):
@@ -182,12 +187,14 @@
     )(*addends)
 
 
-def sublayer_kernel(n_clips, n_positions, n_pieces, n_aliased, *refs):
-    pieces, refs = refs[:n_pieces], refs[n_pieces:]
+def sublayer_kernel(n_clips, n_positions, n_far, n_aliased, near_ref, *refs):
+    far_refs, refs = refs[:n_far], refs[n_far:]
     wq_ref, wk_ref, wv_ref, wo_ref = refs[:4]
     refs = refs[4 + n_aliased :]
     normed_ref, cot_ref, mixed_ref, dq_ref, dk_ref, dv_ref = refs[:6]
     dx_refs, total_ref = refs[6:-1], refs[-1]
+    n_near = near_ref.shape[0]
+    n_pieces = n_near + n_far
     step = pl.program_id(0)
     rows = normed_ref.shape[0] // n_clips
     span = rows // n_pieces
@@ -195,9 +202,12 @@
     depth = wide // GROUP
     scaling = depth**-0.5
 
+    def piece(k, which, clip):
+        return near_ref[k, which, clip] if k < n_near else far_refs[k - n_near][which, clip]
+
     def raw_rows():
         return jnp.concatenate(
-            [pieces[k][0, clip] for clip in range(n_clips) for k in range(n_pieces)], axis=0
+            [piece(k, 0, clip) for clip in range(n_clips) for k in range(n_pieces)], axis=0
         ).astype(jnp.float32)
 
     @pl.when(step == 0)
@@ -206,7 +216,7 @@
         normed_ref[...] = unit.astype(jnp.bfloat16)
         for clip in range(n_clips):
             for k in range(n_pieces):
-                cot_ref[pl.ds(clip * rows + k * span, span)] = pieces[k][1, clip]
+                cot_ref[pl.ds(clip * rows + k * span, span)] = piece(k, 1, clip)
 
     normed = normed_ref[...]
     all_queries = contract(normed, wq_ref[...], ((1,), (0,))).astype(jnp.bfloat16)
@@ -274,38 +284,36 @@
         for clip in range(n_clips):
             for k in range(n_pieces):
                 start = clip * rows + k * span
-                dx_refs[k][clip] = dx[start : start + span]
-
-
-def sublayer(pieces, w_qkv, w_out, chunk, n_chunks, n_positions, before):
-    n_pieces = len(pieces)
-    _, n_clips, span, width = pieces[0].shape
-    rows = n_clips * n_pieces * span
+                if k < n_near:
+                    dx_refs[0][k, clip] = dx[start : start + span]
+                else:
+                    dx_refs[1 + k - n_near][clip] = dx[start : start + span]
+
+
+def sublayer(near, far, n_clips, w_qkv, w_out, chunk, n_chunks, n_positions, before):
+    n_near, _, total_clips, span, width = near.shape
+    rows = n_clips * (n_near + len(far)) * span
     groups = HEADS // GROUP
     wide = width // groups
-
-    def whole(shape):
-        return pl.BlockSpec(shape, lambda j: (0,) * len(shape))
-
     flat = jax.ShapeDtypeStruct((n_chunks * rows, width), jnp.bfloat16)
     dx = jax.ShapeDtypeStruct((n_chunks * n_clips, span, width), jnp.bfloat16)
-    out_shape = [flat] * 6 + [dx] * n_pieces
+    dx_near = jax.ShapeDtypeStruct((n_near,) + dx.shape, jnp.bfloat16)
     aliased = [] if before is None else list(before)
-    first = n_pieces + 4
-    return pl.pallas_call(
-        functools.partial(sublayer_kernel, n_clips, n_positions, n_pieces, len(aliased)),
+    first = len(far) + 5
+    at = chunk if total_clips > n_clips else 0
+    return pl.pallas_call(
+        functools.partial(sublayer_kernel, n_clips, n_positions, len(far), len(aliased)),
         grid=(groups,),
-        out_shape=out_shape,
-        in_specs=[whole(piece.shape) for piece in pieces]
+        out_shape=[flat] * 6 + [dx_near] + [dx] * len(far),
+        in_specs=[pl.BlockSpec((n_near, 2, n_clips, span, width), lambda j: (0, 0, at, 0, 0))]
+        + [pl.BlockSpec(piece.shape, lambda j: (0, 0, 0, 0)) for piece in far]
         + [pl.BlockSpec((width, wide), lambda j, i=i: (0, i * groups + j)) for i in range(3)]
         + [pl.BlockSpec((wide, width), lambda j: (j, 0))]
         + [pl.BlockSpec(memory_space=pl.ANY)] * len(aliased),
-        out_specs=[
-            pl.BlockSpec((rows, width), lambda j: (chunk, 0)),
-            pl.BlockSpec((rows, width), lambda j: (chunk, 0)),
-        ]
+        out_specs=[pl.BlockSpec((rows, width), lambda j: (chunk, 0))] * 2
         + [pl.BlockSpec((rows, wide), lambda j: (chunk, j))] * 4
-        + [pl.BlockSpec((n_clips, span, width), lambda j: (chunk, 0, 0))] * n_pieces,
+        + [pl.BlockSpec((n_near, n_clips, span, width), lambda j: (0, chunk, 0, 0))]
+        + [pl.BlockSpec((n_clips, span, width), lambda j: (chunk, 0, 0))] * len(far),
         scratch_shapes=[pltpu.VMEM((rows, width), jnp.float32)],
         input_output_aliases={first + i: i for i in range(len(aliased))},
         compiler_params=pltpu.CompilerParams(vmem_limit_bytes=28 * MIB),
@@ -314,7 +322,7 @@
             bytes_accessed=16 * rows * width + 8 * width * width,
             transcendentals=rows * 128 * HEADS,
         ),
-    )(*pieces, w_qkv, w_qkv, w_qkv, w_out, *aliased)
+    )(near, *far, w_qkv, w_qkv, w_qkv, w_out, *aliased)
 
 
 def swap(block, axis, size, distance):
@@ -326,69 +334,64 @@
     return values
 
 
-def inbound(chunks, n_tm):
+def near_exchange(blocks, n_tm):
     half = n_tm // 2
-    arrived = []
-    for blocks in chunks:
-        pieces = {0: blocks[0]}
-        for k in range(1, half):
-            gate = arrived[-1][k] if arrived else None
-            pieces[k] = swap(blocks[k] if gate is None else after(blocks[k], gate), "tm", n_tm, k)
-        for i, k in enumerate(range(n_tm - 1, half - 1, -1)):
-            gate = arrived[-1][k] if arrived else None
-            if not arrived and i >= half // 2:
-                gate = pieces[i - half // 2 + 1]
-            pieces[k] = swap(blocks[k] if gate is None else after(blocks[k], gate), "tm", n_tm, k)
-        arrived.append([pieces[k] for k in range(n_tm)])
-    return arrived
+    groups = [list(range(half)), list(range(half, n_tm))]
+    return lax.all_to_all(blocks, "tm", 0, 0, axis_index_groups=groups, tiled=True)
 
 
 def shards(n_clip_devices, n_tm, clips, w_qkv, w_out, cotangent):
     n_clips, _, n_patches, width = clips.shape
     n_positions = n_patches // n_tm
     n_x, n_z = n_clip_devices // CORES, n_tm // N_Y
+    half = n_tm // 2
+    depth = n_clips // CHUNKS
     joined = n_positions % 16 != 0
     ids = jnp.stack([lax.axis_index("clip"), lax.axis_index("tm")]).astype(jnp.int32)
 
-    arrived = inbound(pick(ids, clips, cotangent, n_tm, CHUNKS), n_tm)
+    near, blocks = pick(ids, clips, cotangent, n_tm, CHUNKS)
+    near = near_exchange(near, n_tm)
+    far = []
+    for chunk in range(CHUNKS):
+        if far:
+            blocks[chunk] = [after(block, done) for block, done in zip(blocks[chunk], far[-1])]
+        far.append([swap(block, "tm", n_tm, half + i) for i, block in enumerate(blocks[chunk])])
     results = None
-    for chunk, pieces in enumerate(arrived):
+    for chunk in range(CHUNKS):
+        here, there = near, far[chunk]
         if joined:
-            pieces = [jnp.stack(pieces, axis=2).reshape(2, n_clips // CHUNKS, -1, width)]
-        results = sublayer(pieces, w_qkv, w_out, chunk, CHUNKS, n_positions, results)
+            here = near[:, :, chunk * depth :][:, :, :depth]
+            here = jnp.concatenate([here, jnp.stack(there)]).transpose(1, 2, 0, 3, 4)
+            here, there = here.reshape(1, 2, depth, -1, width), []
+        results = sublayer(here, there, depth, w_qkv, w_out, chunk, CHUNKS, n_positions, results)
     normed, cot, mixed, dq, dk, dv = results[:6]
-    dx = list(results[6:])
+    back_near, *back = results[6:]
     if joined:
-        cut = dx[0].reshape(n_clips, n_tm, n_positions, width)
-        dx = [cut[:, k] for k in range(n_tm)]
+        cut = back_near.reshape(n_clips, n_tm, n_positions, width).transpose(1, 0, 2, 3)
+        back_near, back = cut[:half], list(cut[half:])
 
     halves = ([normed], [dq, dk]), ([normed, mixed], [dv, cot])
-    sent_first = products(ids, 1, n_x, n_z, *halves[0])
+    sent_second = products(ids, 1, n_x, n_z, *halves[1])
+    second = swap(sent_second, "clip", n_clip_devices, 1)
+    sent_first = products(ids, 1, n_x, n_z, *after(halves[0], sent_second))
     first = swap(sent_first, "clip", n_clip_devices, 1)
-    sent_second = products(ids, 1, n_x, n_z, *after(halves[1], sent_first))
-    second = swap(sent_second, "clip", n_clip_devices, 1)
-    dx = after(dx, sent_second)
-    back = {}
-    for k in range(n_tm - 1, 1, -1):
-        block = dx[k] if k + 3 >= n_tm else after(dx[k], back[k + 3])
-        back[k] = swap(block, "tm", n_tm, k)
-    own_first = products(ids, 0, n_x, n_z, *after(halves[0], sent_second))
-    own_second = products(ids, 0, n_x, n_z, *after(halves[1], own_first))
-
+    own_second = products(ids, 0, n_x, n_z, *after(halves[1], sent_first))
+    sent, own_second = halve(ids, (own_second, second), 2, 1, 1)
+    second = swap(sent, "tm", n_tm, 1)
+    own_first = products(ids, 0, n_x, n_z, *after(halves[0], own_second))
     sent, own_first = halve(ids, (own_first, first), 0, 0, CORES)
     first = swap(sent, "clip", n_clip_devices, CORES)
-    sent, own_second = halve(ids, (own_second, second), 2, 1, 1)
-    second = swap(sent, "tm", n_tm, 1)
-    first, second = after((first, second), back)
+    back_near, back = after((back_near, back), sent_first)
+    back = [swap(block, "tm", n_tm, half + i) for i, block in enumerate(back)]
+    back_near = near_exchange(back_near, n_tm)
+    first, second = after((first, second), (back, back_near))
     sent, own_first = halve(ids, (own_first, first), 1, 1, 1)
     first = swap(sent, "tm", n_tm, 1)
     sent, own_second = halve(ids, (own_second, second), 0, 0, CORES)
     second = swap(sent, "clip", n_clip_devices, CORES)
     total, *sent = join(ids, (own_first, first), (own_second, second), n_z)
     others = [swap(block, "tm", n_tm, (j + 1) * N_Y) for j, block in enumerate(sent)]
-    back[0] = dx[0]
-    back[1] = swap(after(dx[1], sent), "tm", n_tm, 1)
-    grad_clips = place(ids, [back[k] for k in range(n_tm)]).reshape(clips.shape)
+    grad_clips = place(ids, back_near, back).reshape(clips.shape)
     grad_qkv, grad_out = finish((total, *others))
     return (grad_clips, grad_qkv, grad_out)
 

time: 159 us -> 179 us (1.13)
  local copies, waits for them, and re-layouts: 5.37 us -> 15.2 us
  Pallas kernels: 37.3 us -> 43.4 us
  starting transfers between devices: 64.1 us -> 67.2 us
    all_to_all x0 -> x2, starting transfers between devices: none -> 19.3 us  [near_exchange(): lax.all_to_all(blocks, 'tm', 0, 0, axis_index_groups=groups, tiled=True)]
    ppermute x30 -> x21, starting transfers between devices: 64.1 us -> 47.9 us  [swap(): return lax.ppermute(block, axis, [(i, i ^ distance) for i in range(size)])]
    unnamed x10 -> x52, local copies, waits for them, and re-layouts: 5.37 us -> 15.2 us
    pallas_call x4, Pallas kernels: 3.55 us -> 6.74 us  [halve(): pl.pallas_call(functools.partial(halve_kernel, dim, axis, stride), out_sh...]
    pallas_call x3, Pallas kernels: 24.2 us -> 26.4 us  [the longest x2 24.8 us: sublayer(): pl.pallas_call(functools.partial(sublayer_kernel, n_clips, n_positions, l...]
    ppermute x30 -> x21, waiting for transfers between devices: 49.8 us -> 49.8 us  [swap(): return lax.ppermute(block, axis, [(i, i ^ distance) for i in range(size)])]
  transfers between devices with their start and end apart: 30 -> 23, of which waited for: 13 -> 9; matrix products, arithmetic and copies ran while one was open for 0% -> 0% of each run, Pallas kernels for 12% -> 12%
where the time goes in v6:
time: 179 us; the launch traced here: 177 us
  starting transfers between devices  67.2 us (38%)
  waiting for transfers between devices  49.8 us (28%)
  Pallas kernels  43.4 us (24%)
  local copies, waits for them, and re-layouts  15.2 us (8%)
    ppermute x21, waiting for transfers between devices, swap(): return lax.ppermute(block, axis, [(i, i ^ distance) for i in range(size)])  49.8 us
    ppermute x21, starting transfers between devices, swap(): return lax.ppermute(block, axis, [(i, i ^ distance) for i in range(size)])  47.9 us
    pallas_call x2, Pallas kernels, sublayer(): pl.pallas_call(functools.partial(sublayer_kernel, n_clips, n_positions, l...  24.8 us
    all_to_all x2, starting transfers between devices, near_exchange(): lax.all_to_all(blocks, 'tm', 0, 0, axis_index_groups=groups, tiled=True)  19.3 us
    unnamed x52, local copies, waits for them, and re-layouts  15.2 us
    pallas_call x4, Pallas kernels, products(): pl.pallas_call(functools.partial(product_kernel, n_x, flip, len(lefts)),...  7.37 us
    pallas_call x4, Pallas kernels, halve(): pl.pallas_call(functools.partial(halve_kernel, dim, axis, stride), out_sh...  6.74 us
  transfers between devices with their start and end apart: 23, of which 9 were waited for; matrix products, arithmetic and copies ran while one was open for 0% of the time, Pallas kernels for 12%

profile of v6, /device:TPU:0, one launch (start us, length us, event | category | flops | bytes accessed | tf_op | source)
XLA Modules:
  0.0 176.7 jit_solution(7603373485280328378)
XLA Ops:
  8.1 5.2 %all-to-all-start = ((bf16[4,2,4,16,1024]{4,3,2,1,0:T(8,128)(2,1)}), bf16[4,2,4,16,1024]{4,3,2,1,0:T(8,128)(2,1)S(1)}, u32[]{:S(2)}, u32[]{:S(2)}) async-start(bf16[4,2,4,16,1024]{4,3,2,1,0:T(8,128)(2,1)} %copy-done.7), calls=%async_computation | async-start | bytes 2097152 | tf_op jit(solution)/shard_map/all_to_all | solution.py:340
  13.4 2.6 %collective-permute-start = (bf16[2,2,16,1024]{3,2,1,0:T(8,128)(2,1)S(1)}, bf16[2,2,16,1024]{3,2,1,0:T(8,128)(2,1)S(1)}, u32[]{:S(2)}, u32[]{:S(2)}) collective-permute-start(bf16[2,2,16,1024]{3,2,1,0:T(8,128)(2,1)S(1)} %get-tuple-element.71), channel_id=1, source_target_pairs={{0,4},{1,5},{2,6},{3,7},{4,0},{5,1},{6,2},{7,3},{8,12},{9,13},{10,... | collective-permute-start | bytes 393224 | tf_op jit(solution)/shard_map/ppermute | solution.py:329
  17.7 3.5 %collective-permute-start.4 = (bf16[2,2,16,1024]{3,2,1,0:T(8,128)(2,1)}, bf16[2,2,16,1024]{3,2,1,0:T(8,128)(2,1)S(1)}, u32[]{:S(2)}, u32[]{:S(2)}) collective-permute-start(bf16[2,2,16,1024]{3,2,1,0:T(8,128)(2,1)} %get-tuple-element.77), channel_id=1, source_target_pairs={{0,6},{1,7},{2,4},{3,5},{4,2},{5,3},{6,0},{7,1},{8,14},{9,15},{10,... | collective-permute-start | bytes 393224 | tf_op jit(solution)/shard_map/ppermute | solution.py:329
  21.2 7.6 %collective-permute-done.refs_0_ = bf16[2,2,16,1024]{3,2,1,0:T(8,128)(2,1)S(1)} collective-permute-done((bf16[2,2,16,1024]{3,2,1,0:T(8,128)(2,1)S(1)}, bf16[2,2,16,1024]{3,2,1,0:T(8,128)(2,1)S(1)}, u32[]{:S(2)}, u32[]{:S(2)}) %collective-permute-start) | collective-permute-done | bytes 131104 | tf_op jit(solution)/shard_map/ppermute | solution.py:329
  28.8 3.4 %collective-permute-start.1 = (bf16[2,2,16,1024]{3,2,1,0:T(8,128)(2,1)}, bf16[2,2,16,1024]{3,2,1,0:T(8,128)(2,1)S(1)}, u32[]{:S(2)}, u32[]{:S(2)}) collective-permute-start(bf16[2,2,16,1024]{3,2,1,0:T(8,128)(2,1)} %copy-done.25), channel_id=1, source_target_pairs={{0,4},{1,5},{2,6},{3,7},{4,0},{5,1},{6,2},{7,3},{8,12},{9,13},{10,... | collective-permute-start | bytes 393224 | tf_op jit(solution)/shard_map/ppermute | solution.py:329
  32.9 3.7 %collective-permute-start.3 = (bf16[2,2,16,1024]{3,2,1,0:T(8,128)(2,1)}, bf16[2,2,16,1024]{3,2,1,0:T(8,128)(2,1)S(1)}, u32[]{:S(2)}, u32[]{:S(2)}) collective-permute-start(bf16[2,2,16,1024]{3,2,1,0:T(8,128)(2,1)} %copy-done.24), channel_id=1, source_target_pairs={{0,5},{1,4},{2,7},{3,6},{4,1},{5,0},{6,3},{7,2},{8,13},{9,12},{10,... | collective-permute-start | bytes 393224 | tf_op jit(solution)/shard_map/ppermute | solution.py:329
  36.6 2.4 %collective-permute-done.4.refs_2_ = bf16[2,2,16,1024]{3,2,1,0:T(8,128)(2,1)S(1)} collective-permute-done((bf16[2,2,16,1024]{3,2,1,0:T(8,128)(2,1)}, bf16[2,2,16,1024]{3,2,1,0:T(8,128)(2,1)S(1)}, u32[]{:S(2)}, u32[]{:S(2)}) %collective-permute-start.4) | collective-permute-done | bytes 131104 | tf_op jit(solution)/shard_map/ppermute | solution.py:329
  45.0 2.8 %copy-done = bf16[1024,3072]{1,0:T(8,128)(2,1)S(1)} copy-done((bf16[1024,3072]{1,0:T(8,128)(2,1)S(1)}, bf16[1024,3072]{1,0:T(8,128)(2,1)}, u32[]{:S(2)}) %copy-start) | copy-done | bytes 6291480
  50.5 12.0 %shard_map.68 = (bf16[512,1024]{1,0:T(8,128)(2,1)S(1)}, bf16[512,1024]{1,0:T(8,128)(2,1)S(1)}, bf16[512,1024]{1,0:T(8,128)(2,1)S(1)}, bf16[512,1024]{1,0:T(8,128...) custom-call(bf16[4,2,4,16,1024]{4,3,2,1,0:T(8,128)(2,1)S(1)} %all-to, ...), custom_call_target="tpu_custom_call" | custom-call | flops 5368709120 | bytes 12582912 | tf_op jit(solution)/shard_map/pallas_call | solution.py:304
  62.6 12.8 %shard_map.69 = (bf16[512,1024]{1,0:T(8,128)(2,1)S(1)}, bf16[512,1024]{1,0:T(8,128)(2,1)S(1)}, bf16[512,1024]{1,0:T(8,128)(2,1)S(1)}, bf16[512,1024]{1,0:T(8,128...) custom-call(bf16[4,2,4,16,1024]{4,3,2,1,0:T(8,128)(2,1)S(1)} %all-to, ...), custom_call_target="tpu_custom_call", output_to_operand_aliasing={{0}: (9, {}), {1}: (10, {}), {2}: (11, {}), {3}: (12, {}), ... | custom-call | flops 5368709120 | bytes 12582912 | tf_op jit(solution)/shard_map/pallas_call | solution.py:304
  75.4 1.9 %shard_map.70 = bf16[2,4,2,32,2048]{4,3,2,1,0:T(8,128)(2,1)S(1)} custom-call(s32[2]{0:T(128)S(1)} %pad_add_fusion.ids_ref, bf16[512,1024]{1,0:T(8,128)(2,1)S(1)} %get-tuple-element.117.refs_0_, bf16[512,1024]{1,0:T(8,128)(2,1)S(1)} %get-tuple-element.113.refs_1_, bf16[512,1024]{1,0:T(8,128)(2,1)S(1)} %get-tuple-element.114.refs_2_, ...), custom_call_target="tpu_custom_call" | custom-call | flops 1073741824 | bytes 6291456 | tf_op jit(solution)/shard_map/pallas_call | solution.py:101
  77.3 1.8 %shard_map.71 = bf16[2,4,2,32,2048]{4,3,2,1,0:T(8,128)(2,1)S(1)} custom-call(s32[2]{0:T(128)S(1)} %pad_add_fusion.ids_ref, bf16[512,1024]{1,0:T(8,128)(2,1)S(1)} %get-tuple-element.117.refs_0_, bf16[512,1024]{1,0:T(8,128)(2,1)S(1)} %get-tuple-element.118.refs_1_, bf16[512,1024]{1,0:T(8,128)(2,1)S(1)} %get-tuple-element.119.refs_2_), custom_call_target="tpu_custom_call" | custom-call | flops 1073741824 | bytes 6291456 | tf_op jit(solution)/shard_map/pallas_call | solution.py:101
  81.6 1.9 %shard_map.74 = (bf16[2,4,32,2048]{3,2,1,0:T(8,128)(2,1)}, f32[2,4,32,2048]{3,2,1,0:T(8,128)S(1)}) custom-call(s32[2]{0:T(128)S(1)} %pad_add_fusion.ids_ref, bf16[2,4,2,32,2048]{4,3,2,1,0:T(8,128)(2,1)S(1)} %shard_map.73.refs_0_, bf16[2,4,2,32,2048]{4,3,2,1,0:T(8,128)(2,1)S(1)} %collective-permute-done.12.refs_1_), custom_call_target="tpu_custom_call" | custom-call | tf_op jit(solution)/shard_map/pallas_call | solution.py:134
  85.4 1.9 %shard_map.76 = (bf16[4,2,32,2048]{3,2,1,0:T(8,128)(2,1)}, f32[4,2,32,2048]{3,2,1,0:T(8,128)S(1)}) custom-call(s32[2]{0:T(128)S(1)} %pad_add_fusion.ids_ref, bf16[2,4,2,32,2048]{4,3,2,1,0:T(8,128)(2,1)S(1)} %shard_map.75.refs_0_, bf16[2,4,2,32,2048]{4,3,2,1,0:T(8,128)(2,1)S(1)} %collective-permute-done.13.refs_1_), custom_call_target="tpu_custom_call" | custom-call | tf_op jit(solution)/shard_map/pallas_call | solution.py:134
  90.7 14.0 %all-to-all-start.1 = ((bf16[4,4,16,1024]{3,2,1,0:T(8,128)(2,1)}), bf16[4,4,16,1024]{3,2,1,0:T(8,128)(2,1)S(1)}, u32[]{:S(2)}, u32[]{:S(2)}) async-start(bf16[4,4,16,1024]{3,2,1,0:T(8,128)(2,1)} %get-tuple-element.107), calls=%async_computation.1 | async-start | bytes 1048576 | tf_op jit(solution)/shard_map/all_to_all | solution.py:340
  105.5 3.6 %collective-permute-start.9 = (bf16[4,16,1024]{2,1,0:T(8,128)(2,1)S(1)}, bf16[4,16,1024]{2,1,0:T(8,128)(2,1)S(1)}, u32[]{:S(2)}, u32[]{:S(2)}) collective-permute-start(bf16[4,16,1024]{2,1,0:T(8,128)(2,1)S(1)} %copy-done.17), channel_id=1, source_target_pairs={{0,5},{1,4},{2,7},{3,6},{4,1},{5,0},{6,3},{7,2},{8,13},{9,12},{10,... | collective-permute-start | bytes 393224 | tf_op jit(solution)/shard_map/ppermute | solution.py:329
  110.7 3.8 %collective-permute-done.8.refs_0_ = bf16[4,16,1024]{2,1,0:T(8,128)(2,1)S(1)} collective-permute-done((bf16[4,16,1024]{2,1,0:T(8,128)(2,1)S(1)}, bf16[4,16,1024]{2,1,0:T(8,128)(2,1)S(1)}, u32[]{:S(2)}, u32[]{:S(2)}) %collective-permute-start.8) | collective-permute-done | bytes 131104 | tf_op jit(solution)/shard_map/ppermute | solution.py:329
  114.5 3.1 %collective-permute-start.11 = (bf16[4,16,1024]{2,1,0:T(8,128)(2,1)S(1)}, bf16[4,16,1024]{2,1,0:T(8,128)(2,1)S(1)}, u32[]{:S(2)}, u32[]{:S(2)}) collective-permute-start(bf16[4,16,1024]{2,1,0:T(8,128)(2,1)S(1)} %copy-done.21), channel_id=1, source_target_pairs={{0,7},{1,6},{2,5},{3,4},{4,3},{5,2},{6,1},{7,0},{8,15},{9,14},{10,... | collective-permute-start | bytes 393224 | tf_op jit(solution)/shard_map/ppermute | solution.py:329
  117.6 9.9 %collective-permute-done.9.refs_1_ = bf16[4,16,1024]{2,1,0:T(8,128)(2,1)S(1)} collective-permute-done((bf16[4,16,1024]{2,1,0:T(8,128)(2,1)S(1)}, bf16[4,16,1024]{2,1,0:T(8,128)(2,1)S(1)}, u32[]{:S(2)}, u32[]{:S(2)}) %collective-permute-start.9) | collective-permute-done | bytes 131104 | tf_op jit(solution)/shard_map/ppermute | solution.py:329
  131.6 9.0 %collective-permute-done.16.refs_1_ = bf16[4,32,2048]{2,1,0:T(8,128)(2,1)S(1)} collective-permute-done((bf16[4,32,2048]{2,1,0:T(8,128)(2,1)S(1)}, bf16[4,32,2048]{2,1,0:T(8,128)(2,1)S(1)}, u32[]{:S(2)}, u32[]{:S(2)}) %collective-permute-start.16) | collective-permute-done | bytes 524320 | tf_op jit(solution)/shard_map/ppermute | solution.py:329
  141.6 14.7 %collective-permute-start.18 = (bf16[32,4096]{1,0:T(8,128)(2,1)S(1)}, bf16[32,4096]{1,0:T(8,128)(2,1)S(1)}, u32[]{:S(2)}, u32[]{:S(2)}) collective-permute-start(bf16[32,4096]{1,0:T(8,128)(2,1)S(1)} %get-tuple-element.130), channel_id=1, source_target_pairs={{0,2},{1,3},{2,0},{3,1},{4,6},{5,7},{6,4},{7,5},{8,10},{9,11},{10,... | collective-permute-start | bytes 786440 | tf_op jit(solution)/shard_map/ppermute | solution.py:329
  156.3 2.4 %collective-permute-start.20 = (bf16[32,4096]{1,0:T(8,128)(2,1)S(1)}, bf16[32,4096]{1,0:T(8,128)(2,1)S(1)}, u32[]{:S(2)}, u32[]{:S(2)}) collective-permute-start(bf16[32,4096]{1,0:T(8,128)(2,1)S(1)} %get-tuple-element.132), channel_id=1, source_target_pairs={{0,6},{1,7},{2,4},{3,5},{4,2},{5,3},{6,0},{7,1},{8,14},{9,15},{10,... | collective-permute-start | bytes 786440 | tf_op jit(solution)/shard_map/ppermute | solution.py:329
  160.3 4.0 %collective-permute-done.18.refs_1_ = bf16[32,4096]{1,0:T(8,128)(2,1)S(1)} collective-permute-done((bf16[32,4096]{1,0:T(8,128)(2,1)S(1)}, bf16[32,4096]{1,0:T(8,128)(2,1)S(1)}, u32[]{:S(2)}, u32[]{:S(2)}) %collective-permute-start.18) | collective-permute-done | bytes 262176 | tf_op jit(solution)/shard_map/ppermute | solution.py:329
  164.4 11.4 %collective-permute-done.19.refs_2_ = bf16[32,4096]{1,0:T(8,128)(2,1)S(1)} collective-permute-done((bf16[32,4096]{1,0:T(8,128)(2,1)S(1)}, bf16[32,4096]{1,0:T(8,128)(2,1)S(1)}, u32[]{:S(2)}, u32[]{:S(2)}) %collective-permute-start.19) | collective-permute-done | bytes 262176 | tf_op jit(solution)/shard_map/ppermute | solution.py:329
  (89 shorter events, 36.3 us)
Async XLA Ops:
  3.2 41.9 %copy-start.2 = (bf16[1024,1024]{1,0:T(8,128)(2,1)S(1)}, bf16[1024,1024]{1,0:T(8,128)(2,1)}, u32[]{:S(2)}) copy-start(bf16[1024,1024]{1,0:T(8,128)(2,1)} %refs_7_.3) | copy-start | bytes 6291460
  8.1 36.9 %all-to-all-start = ((bf16[4,2,4,16,1024]{4,3,2,1,0:T(8,128)(2,1)}), bf16[4,2,4,16,1024]{4,3,2,1,0:T(8,128)(2,1)S(1)}, u32[]{:S(2)}, u32[]{:S(2)}) async-start(bf16[4,2,4,16,1024]{4,3,2,1,0:T(8,128)(2,1)} %copy-done.7), calls=%async_computation | async-start | bytes 2097152 | tf_op jit(solution)/shard_map/all_to_all | solution.py:340
  13.4 15.4 %collective-permute-start = (bf16[2,2,16,1024]{3,2,1,0:T(8,128)(2,1)S(1)}, bf16[2,2,16,1024]{3,2,1,0:T(8,128)(2,1)S(1)}, u32[]{:S(2)}, u32[]{:S(2)}) collective-permute-start(bf16[2,2,16,1024]{3,2,1,0:T(8,128)(2,1)S(1)} %get-tuple-element.71), channel_id=1, source_target_pairs={{0,4},{1,5},{2,6},{3,7},{4,0},{5,1},{6,2},{7,3},{8,12},{9,13},{10,... | collective-permute-start | bytes 393224 | tf_op jit(solution)/shard_map/ppermute | solution.py:329
  15.9 16.3 %collective-permute-start.2 = (bf16[2,2,16,1024]{3,2,1,0:T(8,128)(2,1)}, bf16[2,2,16,1024]{3,2,1,0:T(8,128)(2,1)S(1)}, u32[]{:S(2)}, u32[]{:S(2)}) collective-permute-start(bf16[2,2,16,1024]{3,2,1,0:T(8,128)(2,1)} %get-tuple-element.74), channel_id=1, source_target_pairs={{0,5},{1,4},{2,7},{3,6},{4,1},{5,0},{6,3},{7,2},{8,13},{9,12},{10,... | collective-permute-start | bytes 393224 | tf_op jit(solution)/shard_map/ppermute | solution.py:329
  17.7 21.2 %collective-permute-start.4 = (bf16[2,2,16,1024]{3,2,1,0:T(8,128)(2,1)}, bf16[2,2,16,1024]{3,2,1,0:T(8,128)(2,1)S(1)}, u32[]{:S(2)}, u32[]{:S(2)}) collective-permute-start(bf16[2,2,16,1024]{3,2,1,0:T(8,128)(2,1)} %get-tuple-element.77), channel_id=1, source_target_pairs={{0,6},{1,7},{2,4},{3,5},{4,2},{5,3},{6,0},{7,1},{8,14},{9,15},{10,... | collective-permute-start | bytes 393224 | tf_op jit(solution)/shard_map/ppermute | solution.py:329
  21.2 21.4 %collective-permute-start.6 = (bf16[2,2,16,1024]{3,2,1,0:T(8,128)(2,1)}, bf16[2,2,16,1024]{3,2,1,0:T(8,128)(2,1)S(1)}, u32[]{:S(2)}, u32[]{:S(2)}) collective-permute-start(bf16[2,2,16,1024]{3,2,1,0:T(8,128)(2,1)} %get-tuple-element.80), channel_id=1, source_target_pairs={{0,7},{1,6},{2,5},{3,4},{4,3},{5,2},{6,1},{7,0},{8,15},{9,14},{10,... | collective-permute-start | bytes 393224 | tf_op jit(solution)/shard_map/ppermute | solution.py:329
  28.8 33.7 %collective-permute-start.1 = (bf16[2,2,16,1024]{3,2,1,0:T(8,128)(2,1)}, bf16[2,2,16,1024]{3,2,1,0:T(8,128)(2,1)S(1)}, u32[]{:S(2)}, u32[]{:S(2)}) collective-permute-start(bf16[2,2,16,1024]{3,2,1,0:T(8,128)(2,1)} %copy-done.25), channel_id=1, source_target_pairs={{0,4},{1,5},{2,6},{3,7},{4,0},{5,1},{6,2},{7,3},{8,12},{9,13},{10,... | collective-permute-start | bytes 393224 | tf_op jit(solution)/shard_map/ppermute | solution.py:329
  32.9 29.6 %collective-permute-start.3 = (bf16[2,2,16,1024]{3,2,1,0:T(8,128)(2,1)}, bf16[2,2,16,1024]{3,2,1,0:T(8,128)(2,1)S(1)}, u32[]{:S(2)}, u32[]{:S(2)}) collective-permute-start(bf16[2,2,16,1024]{3,2,1,0:T(8,128)(2,1)} %copy-done.24), channel_id=1, source_target_pairs={{0,5},{1,4},{2,7},{3,6},{4,1},{5,0},{6,3},{7,2},{8,13},{9,12},{10,... | collective-permute-start | bytes 393224 | tf_op jit(solution)/shard_map/ppermute | solution.py:329
  39.6 22.9 %collective-permute-start.5 = (bf16[2,2,16,1024]{3,2,1,0:T(8,128)(2,1)}, bf16[2,2,16,1024]{3,2,1,0:T(8,128)(2,1)}, u32[]{:S(2)}, u32[]{:S(2)}) collective-permute-start(bf16[2,2,16,1024]{3,2,1,0:T(8,128)(2,1)} %copy-done.23), channel_id=1, source_target_pairs={{0,6},{1,7},{2,4},{3,5},{4,2},{5,3},{6,0},{7,1},{8,14},{9,15},{10,... | collective-permute-start | bytes 393224 | tf_op jit(solution)/shard_map/ppermute | solution.py:329
  43.3 19.2 %collective-permute-start.7 = (bf16[2,2,16,1024]{3,2,1,0:T(8,128)(2,1)}, bf16[2,2,16,1024]{3,2,1,0:T(8,128)(2,1)}, u32[]{:S(2)}, u32[]{:S(2)}) collective-permute-start(bf16[2,2,16,1024]{3,2,1,0:T(8,128)(2,1)} %copy-done.22), channel_id=1, source_target_pairs={{0,7},{1,6},{2,5},{3,4},{4,3},{5,2},{6,1},{7,0},{8,15},{9,14},{10,... | collective-permute-start | bytes 393224 | tf_op jit(solution)/shard_map/ppermute | solution.py:329
  77.3 4.3 %collective-permute-start.12 = (bf16[2,4,2,32,2048]{4,3,2,1,0:T(8,128)(2,1)S(1)}, bf16[2,4,2,32,2048]{4,3,2,1,0:T(8,128)(2,1)S(1)}, u32[]{:S(2)}, u32[]{:S(2)}) collective-permute-start(bf16[2,4,2,32,2048]{4,3,2,1,0:T(8,128)(2,1)S(1)} %shard_map.70), channel_id=1, source_target_pairs={{0,8},{8,0},{16,24},{24,16},{1,9},{9,1},{17,25},{25,17},{2,10},{10... | collective-permute-start | bytes 6291464 | tf_op jit(solution)/shard_map/ppermute | solution.py:329
  79.2 6.2 %collective-permute-start.13 = (bf16[2,4,2,32,2048]{4,3,2,1,0:T(8,128)(2,1)S(1)}, bf16[2,4,2,32,2048]{4,3,2,1,0:T(8,128)(2,1)S(1)}, u32[]{:S(2)}, u32[]{:S(2)}) collective-permute-start(bf16[2,4,2,32,2048]{4,3,2,1,0:T(8,128)(2,1)S(1)} %shard_map.71), channel_id=1, source_target_pairs={{0,8},{8,0},{16,24},{24,16},{1,9},{9,1},{17,25},{25,17},{2,10},{10... | collective-permute-start | bytes 6291464 | tf_op jit(solution)/shard_map/ppermute | solution.py:329
  88.6 38.9 %collective-permute-start.14 = (bf16[4,2,32,2048]{3,2,1,0:T(8,128)(2,1)}, bf16[4,2,32,2048]{3,2,1,0:T(8,128)(2,1)}, u32[]{:S(2)}, u32[]{:S(2)}) collective-permute-start(bf16[4,2,32,2048]{3,2,1,0:T(8,128)(2,1)} %get-tuple-element.121), channel_id=1, source_target_pairs={{0,16},{8,24},{16,0},{24,8},{1,17},{9,25},{17,1},{25,9},{2,18},{10... | collective-permute-start | bytes 3145736 | tf_op jit(solution)/shard_map/ppermute | solution.py:329
  90.1 37.5 %collective-permute-start.15 = (bf16[2,4,32,2048]{3,2,1,0:T(8,128)(2,1)}, bf16[2,4,32,2048]{3,2,1,0:T(8,128)(2,1)}, u32[]{:S(2)}, u32[]{:S(2)}) collective-permute-start(bf16[2,4,32,2048]{3,2,1,0:T(8,128)(2,1)} %get-tuple-element.122), channel_id=1, source_target_pairs={{0,1},{1,0},{2,3},{3,2},{4,5},{5,4},{6,7},{7,6},{8,9},{9,8},{10,11... | collective-permute-start | bytes 3145736 | tf_op jit(solution)/shard_map/ppermute | solution.py:329
  90.7 36.9 %all-to-all-start.1 = ((bf16[4,4,16,1024]{3,2,1,0:T(8,128)(2,1)}), bf16[4,4,16,1024]{3,2,1,0:T(8,128)(2,1)S(1)}, u32[]{:S(2)}, u32[]{:S(2)}) async-start(bf16[4,4,16,1024]{3,2,1,0:T(8,128)(2,1)} %get-tuple-element.107), calls=%async_computation.1 | async-start | bytes 1048576 | tf_op jit(solution)/shard_map/all_to_all | solution.py:340
  104.7 9.8 %collective-permute-start.8 = (bf16[4,16,1024]{2,1,0:T(8,128)(2,1)S(1)}, bf16[4,16,1024]{2,1,0:T(8,128)(2,1)S(1)}, u32[]{:S(2)}, u32[]{:S(2)}) collective-permute-start(bf16[4,16,1024]{2,1,0:T(8,128)(2,1)S(1)} %copy-done.15), channel_id=1, source_target_pairs={{0,4},{1,5},{2,6},{3,7},{4,0},{5,1},{6,2},{7,3},{8,12},{9,13},{10,... | collective-permute-start | bytes 393224 | tf_op jit(solution)/shard_map/ppermute | solution.py:329
  105.5 22.0 %collective-permute-start.9 = (bf16[4,16,1024]{2,1,0:T(8,128)(2,1)S(1)}, bf16[4,16,1024]{2,1,0:T(8,128)(2,1)S(1)}, u32[]{:S(2)}, u32[]{:S(2)}) collective-permute-start(bf16[4,16,1024]{2,1,0:T(8,128)(2,1)S(1)} %copy-done.17), channel_id=1, source_target_pairs={{0,5},{1,4},{2,7},{3,6},{4,1},{5,0},{6,3},{7,2},{8,13},{9,12},{10,... | collective-permute-start | bytes 393224 | tf_op jit(solution)/shard_map/ppermute | solution.py:329
  109.1 18.5 %collective-permute-start.10 = (bf16[4,16,1024]{2,1,0:T(8,128)(2,1)S(1)}, bf16[4,16,1024]{2,1,0:T(8,128)(2,1)S(1)}, u32[]{:S(2)}, u32[]{:S(2)}) collective-permute-start(bf16[4,16,1024]{2,1,0:T(8,128)(2,1)S(1)} %copy-done.19), channel_id=1, source_target_pairs={{0,6},{1,7},{2,4},{3,5},{4,2},{5,3},{6,0},{7,1},{8,14},{9,15},{10,... | collective-permute-start | bytes 393224 | tf_op jit(solution)/shard_map/ppermute | solution.py:329
  114.5 13.0 %collective-permute-start.11 = (bf16[4,16,1024]{2,1,0:T(8,128)(2,1)S(1)}, bf16[4,16,1024]{2,1,0:T(8,128)(2,1)S(1)}, u32[]{:S(2)}, u32[]{:S(2)}) collective-permute-start(bf16[4,16,1024]{2,1,0:T(8,128)(2,1)S(1)} %copy-done.21), channel_id=1, source_target_pairs={{0,7},{1,6},{2,5},{3,4},{4,3},{5,2},{6,1},{7,0},{8,15},{9,14},{10,... | collective-permute-start | bytes 393224 | tf_op jit(solution)/shard_map/ppermute | solution.py:329
  130.9 9.7 %collective-permute-start.16 = (bf16[4,32,2048]{2,1,0:T(8,128)(2,1)S(1)}, bf16[4,32,2048]{2,1,0:T(8,128)(2,1)S(1)}, u32[]{:S(2)}, u32[]{:S(2)}) collective-permute-start(bf16[4,32,2048]{2,1,0:T(8,128)(2,1)S(1)} %get-tuple-element.125), channel_id=1, source_target_pairs={{0,1},{1,0},{2,3},{3,2},{4,5},{5,4},{6,7},{7,6},{8,9},{9,8},{10,11... | collective-permute-start | bytes 1572872 | tf_op jit(solution)/shard_map/ppermute | solution.py:329
  131.0 9.9 %collective-permute-start.17 = (bf16[4,32,2048]{2,1,0:T(8,128)(2,1)S(1)}, bf16[4,32,2048]{2,1,0:T(8,128)(2,1)S(1)}, u32[]{:S(2)}, u32[]{:S(2)}) collective-permute-start(bf16[4,32,2048]{2,1,0:T(8,128)(2,1)S(1)} %get-tuple-element.128), channel_id=1, source_target_pairs={{0,16},{8,24},{16,0},{24,8},{1,17},{9,25},{17,1},{25,9},{2,18},{10... | collective-permute-start | bytes 1572872 | tf_op jit(solution)/shard_map/ppermute | solution.py:329
  141.6 22.7 %collective-permute-start.18 = (bf16[32,4096]{1,0:T(8,128)(2,1)S(1)}, bf16[32,4096]{1,0:T(8,128)(2,1)S(1)}, u32[]{:S(2)}, u32[]{:S(2)}) collective-permute-start(bf16[32,4096]{1,0:T(8,128)(2,1)S(1)} %get-tuple-element.130), channel_id=1, source_target_pairs={{0,2},{1,3},{2,0},{3,1},{4,6},{5,7},{6,4},{7,5},{8,10},{9,11},{10,... | collective-permute-start | bytes 786440 | tf_op jit(solution)/shard_map/ppermute | solution.py:329
  156.3 19.5 %collective-permute-start.19 = (bf16[32,4096]{1,0:T(8,128)(2,1)S(1)}, bf16[32,4096]{1,0:T(8,128)(2,1)S(1)}, u32[]{:S(2)}, u32[]{:S(2)}) collective-permute-start(bf16[32,4096]{1,0:T(8,128)(2,1)S(1)} %get-tuple-element.131), channel_id=1, source_target_pairs={{0,4},{1,5},{2,6},{3,7},{4,0},{5,1},{6,2},{7,3},{8,12},{9,13},{10,... | collective-permute-start | bytes 786440 | tf_op jit(solution)/shard_map/ppermute | solution.py:329
  156.3 19.5 %collective-permute-start.20 = (bf16[32,4096]{1,0:T(8,128)(2,1)S(1)}, bf16[32,4096]{1,0:T(8,128)(2,1)S(1)}, u32[]{:S(2)}, u32[]{:S(2)}) collective-permute-start(bf16[32,4096]{1,0:T(8,128)(2,1)S(1)} %get-tuple-element.132), channel_id=1, source_target_pairs={{0,6},{1,7},{2,4},{3,5},{4,2},{5,3},{6,0},{7,1},{8,14},{9,15},{10,... | collective-permute-start | bytes 786440 | tf_op jit(solution)/shard_map/ppermute | solution.py:329
  (25 other events, 128.8 us)

commit v7 on v5

--- a/solution.py
+++ b/solution.py
@@ -10,6 +10,7 @@
 
 HEADS = 16
 GROUP = 4
+STEP = 2
 CHUNKS = 2
 CORES = 2
 N_Y = 2
@@ -29,46 +30,31 @@
     return centred * inverse, inverse
 
 
-def pick_kernel(n_slots, n_chunks, n_clips, ids_ref, x_ref, cot_ref, *out_refs):
-    clip = pl.program_id(0)
+def pick_kernel(n_slots, n_chunks, ids_ref, x_ref, cot_ref, *out_refs):
     half = n_slots // 2
-    for slot in range(half):
-        out_refs[slot][0, 0] = x_ref[0, ids_ref[1] ^ slot]
-        out_refs[slot][1, 0] = cot_ref[0, ids_ref[1] ^ slot]
-    for chunk in range(n_chunks):
-
-        @pl.when(clip // (n_clips // n_chunks) == chunk)
-        def _():
-            for slot in range(half, n_slots):
-                out = out_refs[chunk * half + slot]
-                out[0, 0] = x_ref[0, ids_ref[1] ^ slot]
-                out[1, 0] = cot_ref[0, ids_ref[1] ^ slot]
+    depth = x_ref.shape[0] // n_chunks
+    for i, ref in enumerate(out_refs):
+        far = i - half
+        here = slice(None) if far < 0 else pl.ds(far // half * depth, depth)
+        slot = ids_ref[1] ^ (i if far < 0 else half + far % half)
+        ref[0] = x_ref[here, slot]
+        ref[1] = cot_ref[here, slot]
 
 
 def pick(ids, clips, cotangent, n_slots, n_chunks):
     n_clips, _, n_patches, width = clips.shape
-    n_positions = n_patches // n_slots
-    cut = (n_clips, n_slots, n_positions, width)
-    half, depth = n_slots // 2, n_clips // n_chunks
-
-    def block(index):
-        return pl.BlockSpec((2, 1, n_positions, width), lambda c: (0, index(c), 0, 0))
+    cut = (n_clips, n_slots, n_patches // n_slots, width)
+    half = n_slots // 2
 
     def piece(count):
-        return jax.ShapeDtypeStruct((2, count, n_positions, width), clips.dtype)
+        return jax.ShapeDtypeStruct((2, count) + cut[2:], clips.dtype)
 
     out = pl.pallas_call(
-        functools.partial(pick_kernel, n_slots, n_chunks, n_clips),
-        grid=(n_clips,),
-        out_shape=[piece(n_clips)] * half + [piece(depth)] * (half * n_chunks),
+        functools.partial(pick_kernel, n_slots, n_chunks),
+        out_shape=[piece(n_clips)] * half + [piece(n_clips // n_chunks)] * (half * n_chunks),
         in_specs=[pl.BlockSpec(memory_space=pltpu.SMEM)]
-        + [pl.BlockSpec((1,) + cut[1:], lambda c: (c, 0, 0, 0))] * 2,
-        out_specs=[block(lambda c: c)] * half
-        + [
-            block(lambda c, chunk=chunk: jnp.clip(c - chunk * depth, 0, depth - 1))
-            for chunk in range(n_chunks)
-            for _ in range(half)
-        ],
+        + [pl.BlockSpec(memory_space=pltpu.VMEM)] * 2,
+        out_specs=[pl.BlockSpec(memory_space=pltpu.VMEM)] * (half * (1 + n_chunks)),
         compiler_params=pltpu.CompilerParams(vmem_limit_bytes=12 * MIB),
     )(ids, clips.reshape(cut), cotangent.reshape(cut))
     far = [out[half + chunk * half :][:half] for chunk in range(n_chunks)]
@@ -208,7 +194,8 @@
     step = pl.program_id(0)
     rows = normed_ref.shape[0] // n_clips
     span = rows // n_pieces
-    wide = wo_ref.shape[0]
+    step_wide = wo_ref.shape[0]
+    wide = step_wide // STEP
     depth = wide // GROUP
     scaling = depth**-0.5
 
@@ -243,12 +230,13 @@
     def side_by_side(blocks):
         return jnp.concatenate([blocks[h] for h in range(GROUP)], axis=1)
 
-    for clip in range(n_clips):
+    for clip, group in itertools.product(range(n_clips), range(STEP)):
         here = slice(clip * rows, (clip + 1) * rows)
-        queries = all_queries[here]
-        keys = stacked(all_keys[here])
-        values = stacked(all_values[here])
-        upstream = mixed_grad[here]
+        columns = slice(group * wide, (group + 1) * wide)
+        queries = all_queries[here, columns]
+        keys = stacked(all_keys[here, columns])
+        values = stacked(all_values[here, columns])
+        upstream = mixed_grad[here, columns]
         scores = contract(keys, queries, ((1,), (1,))).reshape(GROUP, rows, rows)
         scores = jnp.where(same, scores * scaling, LOWEST)
         expo = jnp.exp(scores - jnp.max(scores, axis=1, keepdims=True))
@@ -258,13 +246,13 @@
         score_grad = full * (dots - jnp.sum(full * dots, axis=1, keepdims=True))
         score_grad = (score_grad * scaling).astype(jnp.bfloat16)
         mixed = contract(low.reshape(GROUP * rows, rows), values, ((0,), (0,)))
-        mixed_ref[here] = mixed.astype(jnp.bfloat16)
+        mixed_ref[here, columns] = mixed.astype(jnp.bfloat16)
         dq = contract(score_grad.reshape(GROUP * rows, rows), keys, ((0,), (0,)))
-        dq_ref[here] = dq.astype(jnp.bfloat16)
+        dq_ref[here, columns] = dq.astype(jnp.bfloat16)
         dk = contract(side_by_side(score_grad), stacked(queries), ((1,), (0,)))
-        dk_ref[here] = dk.astype(jnp.bfloat16)
+        dk_ref[here, columns] = dk.astype(jnp.bfloat16)
         dv = contract(side_by_side(low), stacked(upstream), ((1,), (0,)))
-        dv_ref[here] = dv.astype(jnp.bfloat16)
+        dv_ref[here, columns] = dv.astype(jnp.bfloat16)
 
     part = contract(dq_ref[...], wq_ref[...], ((1,), (1,)))
     part += contract(dk_ref[...], wk_ref[...], ((1,), (1,)))
@@ -298,7 +286,7 @@
     n_pieces = len(pieces)
     _, _, span, width = pieces[0].shape
     rows = n_clips * n_pieces * span
-    groups = HEADS // GROUP
+    groups = HEADS // (GROUP * STEP)
     wide = width // groups
 
     flat = jax.ShapeDtypeStruct((n_chunks * rows, width), jnp.bfloat16)
@@ -328,7 +316,7 @@
         + [pl.BlockSpec((n_clips, span, width), lambda j: (chunk, 0, 0))] * n_pieces,
         scratch_shapes=[pltpu.VMEM((rows, width), jnp.float32)],
         input_output_aliases={first + i: i for i in range(len(aliased))},
-        compiler_params=pltpu.CompilerParams(vmem_limit_bytes=50 * MIB),
+        compiler_params=pltpu.CompilerParams(vmem_limit_bytes=28 * MIB),
         cost_estimate=pl.CostEstimate(
             flops=2 * rows * width * (7 * width + 24 * 128),
             bytes_accessed=16 * rows * width + 8 * width * width,
@@ -349,12 +337,12 @@
 def inbound(near, far, n_tm):
     half = n_tm // 2
     near = [near[0]] + [swap(near[k], "tm", n_tm, k) for k in range(1, half)]
-    gates = [near[i + 1] if i < half // 2 else None for i in range(half)]
     arrived = []
     for blocks in far:
+        gates = arrived[-1] if arrived else [near[2]] + [None] * (half - 1)
         blocks = [block if gate is None else after(block, gate) for block, gate in zip(blocks, gates)]
-        gates = [swap(block, "tm", n_tm, half + i) for i, block in enumerate(blocks)]
-        arrived.append(gates)
+        done = {i: swap(blocks[i], "tm", n_tm, half + i) for i in reversed(range(half))}
+        arrived.append([done[i] for i in range(half)])
     return near, arrived
 
 
@@ -381,22 +369,21 @@
         dx = [cut[:, k] for k in range(n_tm)]
 
     halves = ([normed], [dq, dk]), ([normed, mixed], [dv, cot])
-    sent_first = products(ids, 1, n_x, n_z, *halves[0])
+    sent_second = products(ids, 1, n_x, n_z, *halves[1])
+    second = swap(sent_second, "clip", n_clip_devices, 1)
+    sent_first = products(ids, 1, n_x, n_z, *after(halves[0], sent_second))
     first = swap(sent_first, "clip", n_clip_devices, 1)
-    sent_second = products(ids, 1, n_x, n_z, *after(halves[1], sent_first))
-    second = swap(sent_second, "clip", n_clip_devices, 1)
-    dx = after(dx, sent_second)
+    own_second = products(ids, 0, n_x, n_z, *after(halves[1], sent_first))
+    sent, own_second = halve(ids, (own_second, second), 2, 1, 1)
+    second = swap(sent, "tm", n_tm, 1)
+    own_first = products(ids, 0, n_x, n_z, *after(halves[0], own_second))
+    sent, own_first = halve(ids, (own_first, first), 0, 0, CORES)
+    first = swap(sent, "clip", n_clip_devices, CORES)
+    dx = after(dx, sent_first)
     back = {}
     for k in range(n_tm - 1, 1, -1):
         block = dx[k] if k + 3 >= n_tm else after(dx[k], back[k + 3])
         back[k] = swap(block, "tm", n_tm, k)
-    own_first = products(ids, 0, n_x, n_z, *after(halves[0], sent_second))
-    own_second = products(ids, 0, n_x, n_z, *after(halves[1], own_first))
-
-    sent, own_first = halve(ids, (own_first, first), 0, 0, CORES)
-    first = swap(sent, "clip", n_clip_devices, CORES)
-    sent, own_second = halve(ids, (own_second, second), 2, 1, 1)
-    second = swap(sent, "tm", n_tm, 1)
     first, second = after((first, second), back)
     sent, own_first = halve(ids, (own_first, first), 1, 1, 1)
     first = swap(sent, "tm", n_tm, 1)

time: 162 us -> 155 us (0.957)
  Pallas kernels: 40.7 us -> 35.1 us
  starting transfers between devices: 50.3 us -> 46.2 us
  waiting for transfers between devices: 64.4 us -> 66.1 us
    pallas_call x2, Pallas kernels: 25.6 us -> 20.3 us  [sublayer(): pl.pallas_call(functools.partial(sublayer_kernel, n_clips, n_positions, n...]
    ppermute x27, starting transfers between devices: 50.3 us -> 46.2 us  [swap(): return lax.ppermute(block, axis, [(i, i ^ distance) for i in range(size)])]
    ppermute x27, waiting for transfers between devices: 64.4 us -> 66.1 us  [swap(): return lax.ppermute(block, axis, [(i, i ^ distance) for i in range(size)])]
    unnamed x14 -> x10, local copies, waits for them, and re-layouts: 4.91 us -> 5.37 us
  transfers between devices with their start and end apart: 27 -> 27, of which waited for: 13 -> 11; matrix products, arithmetic and copies ran while one was open for 0% -> 0% of each run, Pallas kernels for 13% -> 12%
where the time goes in v7:
time: 155 us; the launch traced here: 154 us
  waiting for transfers between devices  66.1 us (43%)
  starting transfers between devices  46.2 us (30%)
  Pallas kernels  35.1 us (23%)
  local copies, waits for them, and re-layouts  5.37 us (3%)
    ppermute x27, waiting for transfers between devices, swap(): return lax.ppermute(block, axis, [(i, i ^ distance) for i in range(size)])  66.1 us
    ppermute x27, starting transfers between devices, swap(): return lax.ppermute(block, axis, [(i, i ^ distance) for i in range(size)])  46.2 us
    pallas_call x2, Pallas kernels, sublayer(): pl.pallas_call(functools.partial(sublayer_kernel, n_clips, n_positions, n...  20.3 us
    pallas_call x4, Pallas kernels, products(): pl.pallas_call(functools.partial(product_kernel, n_x, flip, len(lefts)),...  7.35 us
    unnamed x10, local copies, waits for them, and re-layouts  5.37 us
    pallas_call x4, Pallas kernels, halve(): pl.pallas_call(functools.partial(halve_kernel, dim, axis, stride), out_sh...  3.61 us
  transfers between devices with their start and end apart: 27, of which 11 were waited for; matrix products, arithmetic and copies ran while one was open for 0% of the time, Pallas kernels for 12%

profile of v7, /device:TPU:0, one launch (start us, length us, event | category | flops | bytes accessed | tf_op | source)
XLA Modules:
  0.0 153.7 jit_solution(2718409019368562795)
XLA Ops:
  4.0 3.1 %collective-permute-start.1 = (bf16[2,4,16,1024]{3,2,1,0:T(8,128)(2,1)S(1)}, bf16[2,4,16,1024]{3,2,1,0:T(8,128)(2,1)S(1)}, u32[]{:S(2)}, u32[]{:S(2)}) collective-permute-start(bf16[2,4,16,1024]{3,2,1,0:T(8,128)(2,1)S(1)} %get-tuple-element.88), channel_id=1, source_target_pairs={{0,2},{1,3},{2,0},{3,1},{4,6},{5,7},{6,4},{7,5},{8,10},{9,11},{10,... | collective-permute-start | bytes 786440 | tf_op jit(solution)/shard_map/ppermute | solution.py:329
  7.1 3.5 %collective-permute-start.5 = (bf16[2,2,16,1024]{3,2,1,0:T(8,128)(2,1)S(1)}, bf16[2,2,16,1024]{3,2,1,0:T(8,128)(2,1)S(1)}, u32[]{:S(2)}, u32[]{:S(2)}) collective-permute-start(bf16[2,2,16,1024]{3,2,1,0:T(8,128)(2,1)S(1)} %get-tuple-element.95), channel_id=1, source_target_pairs={{0,5},{1,4},{2,7},{3,6},{4,1},{5,0},{6,3},{7,2},{8,13},{9,12},{10,... | collective-permute-start | bytes 393224 | tf_op jit(solution)/shard_map/ppermute | solution.py:329
  13.9 3.1 %collective-permute-done.1.refs_2_ = bf16[2,4,16,1024]{3,2,1,0:T(8,128)(2,1)S(1)} collective-permute-done((bf16[2,4,16,1024]{3,2,1,0:T(8,128)(2,1)S(1)}, bf16[2,4,16,1024]{3,2,1,0:T(8,128)(2,1)S(1)}, u32[]{:S(2)}, u32[]{:S(2)}) %collective-permute-start.1) | collective-permute-done | bytes 262176 | tf_op jit(solution)/shard_map/ppermute | solution.py:329
  17.0 5.0 %collective-permute-start.9 = (bf16[2,2,16,1024]{3,2,1,0:T(8,128)(2,1)S(1)}, bf16[2,2,16,1024]{3,2,1,0:T(8,128)(2,1)S(1)}, u32[]{:S(2)}, u32[]{:S(2)}) collective-permute-start(bf16[2,2,16,1024]{3,2,1,0:T(8,128)(2,1)S(1)} %get-tuple-element.101), channel_id=1, source_target_pairs={{0,7},{1,6},{2,5},{3,4},{4,3},{5,2},{6,1},{7,0},{8,15},{9,14},{10,... | collective-permute-start | bytes 393224 | tf_op jit(solution)/shard_map/ppermute | solution.py:329
  22.0 7.4 %collective-permute-done.7.refs_6_ = bf16[2,2,16,1024]{3,2,1,0:T(8,128)(2,1)S(1)} collective-permute-done((bf16[2,2,16,1024]{3,2,1,0:T(8,128)(2,1)S(1)}, bf16[2,2,16,1024]{3,2,1,0:T(8,128)(2,1)S(1)}, u32[]{:S(2)}, u32[]{:S(2)}) %collective-permute-start.7) | collective-permute-done | bytes 131104 | tf_op jit(solution)/shard_map/ppermute | solution.py:329
  29.4 4.4 %collective-permute-done.9.refs_7_ = bf16[2,2,16,1024]{3,2,1,0:T(8,128)(2,1)S(1)} collective-permute-done((bf16[2,2,16,1024]{3,2,1,0:T(8,128)(2,1)S(1)}, bf16[2,2,16,1024]{3,2,1,0:T(8,128)(2,1)S(1)}, u32[]{:S(2)}, u32[]{:S(2)}) %collective-permute-start.9) | collective-permute-done | bytes 131104 | tf_op jit(solution)/shard_map/ppermute | solution.py:329
  33.8 1.9 %collective-permute-start.8 = (bf16[2,2,16,1024]{3,2,1,0:T(8,128)(2,1)S(1)}, bf16[2,2,16,1024]{3,2,1,0:T(8,128)(2,1)S(1)}, u32[]{:S(2)}, u32[]{:S(2)}) collective-permute-start(bf16[2,2,16,1024]{3,2,1,0:T(8,128)(2,1)S(1)} %get-tuple-element.99), channel_id=1, source_target_pairs={{0,6},{1,7},{2,4},{3,5},{4,2},{5,3},{6,0},{7,1},{8,14},{9,15},{10,... | collective-permute-start | bytes 393224 | tf_op jit(solution)/shard_map/ppermute | solution.py:329
  35.8 9.2 %collective-permute-done.3.refs_4_ = bf16[2,2,16,1024]{3,2,1,0:T(8,128)(2,1)S(1)} collective-permute-done((bf16[2,2,16,1024]{3,2,1,0:T(8,128)(2,1)S(1)}, bf16[2,2,16,1024]{3,2,1,0:T(8,128)(2,1)S(1)}, u32[]{:S(2)}, u32[]{:S(2)}) %collective-permute-start.3) | collective-permute-done | bytes 131104 | tf_op jit(solution)/shard_map/ppermute | solution.py:329
  45.0 2.8 %copy-done = bf16[1024,3072]{1,0:T(8,128)(2,1)S(1)} copy-done((bf16[1024,3072]{1,0:T(8,128)(2,1)S(1)}, bf16[1024,3072]{1,0:T(8,128)(2,1)}, u32[]{:S(2)}) %copy-start) | copy-done | bytes 6291480
  47.8 10.0 %shard_map.68 = (bf16[512,1024]{1,0:T(8,128)(2,1)S(1)}, bf16[512,1024]{1,0:T(8,128)(2,1)S(1)}, bf16[512,1024]{1,0:T(8,128)(2,1)S(1)}, bf16[512,1024]{1,0:T(8,128...) custom-call(bf16[2,4,16,1024]{3,2,1,0:T(8,128)(2,1)S(1)} %get-tuple-, ...), custom_call_target="tpu_custom_call" | custom-call | flops 5368709120 | bytes 12582912 | tf_op jit(solution)/shard_map/pallas_call | solution.py:297
  57.9 10.3 %shard_map.69 = (bf16[512,1024]{1,0:T(8,128)(2,1)S(1)}, bf16[512,1024]{1,0:T(8,128)(2,1)S(1)}, bf16[512,1024]{1,0:T(8,128)(2,1)S(1)}, bf16[512,1024]{1,0:T(8,128...) custom-call(bf16[2,4,16,1024]{3,2,1,0:T(8,128)(2,1)S(1)} %get-tuple-, ...), custom_call_target="tpu_custom_call", output_to_operand_aliasing={{0}: (12, {}), {1}: (13, {}), {2}: (14, {}), {3}: (15, {}),... | custom-call | flops 5368709120 | bytes 12582912 | tf_op jit(solution)/shard_map/pallas_call | solution.py:297
  79.9 2.0 %collective-permute-start.14 = (bf16[2,4,32,2048]{3,2,1,0:T(8,128)(2,1)S(1)}, bf16[2,4,32,2048]{3,2,1,0:T(8,128)(2,1)S(1)}, u32[]{:S(2)}, u32[]{:S(2)}) collective-permute-start(bf16[2,4,32,2048]{3,2,1,0:T(8,128)(2,1)S(1)} %get-tuple-element.146), channel_id=1, source_target_pairs={{0,1},{1,0},{2,3},{3,2},{4,5},{5,4},{6,7},{7,6},{8,9},{9,8},{10,11... | collective-permute-start | bytes 3145736 | tf_op jit(solution)/shard_map/ppermute | solution.py:329
  81.8 2.4 %collective-permute-start.15 = (bf16[4,16,1024]{2,1,0:T(8,128)(2,1)S(1)}, bf16[4,16,1024]{2,1,0:T(8,128)(2,1)S(1)}, u32[]{:S(2)}, u32[]{:S(2)}) collective-permute-start(bf16[4,16,1024]{2,1,0:T(8,128)(2,1)S(1)} %get-tuple-element.148), channel_id=1, source_target_pairs={{0,5},{1,4},{2,7},{3,6},{4,1},{5,0},{6,3},{7,2},{8,13},{9,12},{10,... | collective-permute-start | bytes 393224 | tf_op jit(solution)/shard_map/ppermute | solution.py:329
  84.2 3.6 %collective-permute-start.17 = (bf16[4,16,1024]{2,1,0:T(8,128)(2,1)S(1)}, bf16[4,16,1024]{2,1,0:T(8,128)(2,1)S(1)}, u32[]{:S(2)}, u32[]{:S(2)}) collective-permute-start(bf16[4,16,1024]{2,1,0:T(8,128)(2,1)S(1)} %get-tuple-element.151), channel_id=1, source_target_pairs={{0,6},{1,7},{2,4},{3,5},{4,2},{5,3},{6,0},{7,1},{8,14},{9,15},{10,... | collective-permute-start | bytes 393224 | tf_op jit(solution)/shard_map/ppermute | solution.py:329
  89.5 8.3 %collective-permute-done.15.refs_5_ = bf16[4,16,1024]{2,1,0:T(8,128)(2,1)S(1)} collective-permute-done((bf16[4,16,1024]{2,1,0:T(8,128)(2,1)S(1)}, bf16[4,16,1024]{2,1,0:T(8,128)(2,1)S(1)}, u32[]{:S(2)}, u32[]{:S(2)}) %collective-permute-start.15) | collective-permute-done | bytes 131104 | tf_op jit(solution)/shard_map/ppermute | solution.py:329
  97.8 3.4 %collective-permute-start.18 = (bf16[4,16,1024]{2,1,0:T(8,128)(2,1)S(1)}, bf16[4,16,1024]{2,1,0:T(8,128)(2,1)S(1)}, u32[]{:S(2)}, u32[]{:S(2)}) collective-permute-start(bf16[4,16,1024]{2,1,0:T(8,128)(2,1)S(1)} %get-tuple-element.152), channel_id=1, source_target_pairs={{0,3},{1,2},{2,1},{3,0},{4,7},{5,6},{6,5},{7,4},{8,11},{9,10},{10,... | collective-permute-start | bytes 393224 | tf_op jit(solution)/shard_map/ppermute | solution.py:329
  101.1 4.0 %collective-permute-start.20 = (bf16[4,16,1024]{2,1,0:T(8,128)(2,1)S(1)}, bf16[4,16,1024]{2,1,0:T(8,128)(2,1)S(1)}, u32[]{:S(2)}, u32[]{:S(2)}) collective-permute-start(bf16[4,16,1024]{2,1,0:T(8,128)(2,1)S(1)} %get-tuple-element.155), channel_id=1, source_target_pairs={{0,4},{1,5},{2,6},{3,7},{4,0},{5,1},{6,2},{7,3},{8,12},{9,13},{10,... | collective-permute-start | bytes 393224 | tf_op jit(solution)/shard_map/ppermute | solution.py:329
  105.1 5.8 %collective-permute-done.20.refs_4_ = bf16[4,16,1024]{2,1,0:T(8,128)(2,1)S(1)} collective-permute-done((bf16[4,16,1024]{2,1,0:T(8,128)(2,1)S(1)}, bf16[4,16,1024]{2,1,0:T(8,128)(2,1)S(1)}, u32[]{:S(2)}, u32[]{:S(2)}) %collective-permute-start.20) | collective-permute-done | bytes 131104 | tf_op jit(solution)/shard_map/ppermute | solution.py:329
  111.0 2.4 %collective-permute-done.14.refs_1_ = bf16[2,4,32,2048]{3,2,1,0:T(8,128)(2,1)S(1)} collective-permute-done((bf16[2,4,32,2048]{3,2,1,0:T(8,128)(2,1)S(1)}, bf16[2,4,32,2048]{3,2,1,0:T(8,128)(2,1)S(1)}, u32[]{:S(2)}, u32[]{:S(2)}) %collective-permute-start.14) | collective-permute-done | bytes 1048608 | tf_op jit(solution)/shard_map/ppermute | solution.py:329
  117.3 10.0 %collective-permute-done.22.refs_3_ = bf16[4,32,2048]{2,1,0:T(8,128)(2,1)S(1)} collective-permute-done((bf16[4,32,2048]{2,1,0:T(8,128)(2,1)S(1)}, bf16[4,32,2048]{2,1,0:T(8,128)(2,1)S(1)}, u32[]{:S(2)}, u32[]{:S(2)}) %collective-permute-start.22) | collective-permute-done | bytes 524320 | tf_op jit(solution)/shard_map/ppermute | solution.py:329
  129.0 3.7 %collective-permute-start.24 = (bf16[32,4096]{1,0:T(8,128)(2,1)S(1)}, bf16[32,4096]{1,0:T(8,128)(2,1)S(1)}, u32[]{:S(2)}, u32[]{:S(2)}) collective-permute-start(bf16[32,4096]{1,0:T(8,128)(2,1)S(1)} %get-tuple-element.162), channel_id=1, source_target_pairs={{0,2},{1,3},{2,0},{3,1},{4,6},{5,7},{6,4},{7,5},{8,10},{9,11},{10,... | collective-permute-start | bytes 786440 | tf_op jit(solution)/shard_map/ppermute | solution.py:329
  132.8 2.4 %collective-permute-start.26 = (bf16[32,4096]{1,0:T(8,128)(2,1)S(1)}, bf16[32,4096]{1,0:T(8,128)(2,1)S(1)}, u32[]{:S(2)}, u32[]{:S(2)}) collective-permute-start(bf16[32,4096]{1,0:T(8,128)(2,1)S(1)} %get-tuple-element.164), channel_id=1, source_target_pairs={{0,6},{1,7},{2,4},{3,5},{4,2},{5,3},{6,0},{7,1},{8,14},{9,15},{10,... | collective-permute-start | bytes 786440 | tf_op jit(solution)/shard_map/ppermute | solution.py:329
  136.9 3.3 %collective-permute-done.23.refs_1_ = bf16[4,16,1024]{2,1,0:T(8,128)(2,1)S(1)} collective-permute-done((bf16[4,16,1024]{2,1,0:T(8,128)(2,1)S(1)}, bf16[4,16,1024]{2,1,0:T(8,128)(2,1)S(1)}, u32[]{:S(2)}, u32[]{:S(2)}) %collective-permute-start.23) | collective-permute-done | bytes 131104 | tf_op jit(solution)/shard_map/ppermute | solution.py:329
  141.8 11.1 %collective-permute-done.25.refs_2_ = bf16[32,4096]{1,0:T(8,128)(2,1)S(1)} collective-permute-done((bf16[32,4096]{1,0:T(8,128)(2,1)S(1)}, bf16[32,4096]{1,0:T(8,128)(2,1)S(1)}, u32[]{:S(2)}, u32[]{:S(2)}) %collective-permute-start.25) | collective-permute-done | bytes 262176 | tf_op jit(solution)/shard_map/ppermute | solution.py:329
  (55 shorter events, 29.8 us)
Async XLA Ops:
  4.0 13.0 %collective-permute-start.1 = (bf16[2,4,16,1024]{3,2,1,0:T(8,128)(2,1)S(1)}, bf16[2,4,16,1024]{3,2,1,0:T(8,128)(2,1)S(1)}, u32[]{:S(2)}, u32[]{:S(2)}) collective-permute-start(bf16[2,4,16,1024]{3,2,1,0:T(8,128)(2,1)S(1)} %get-tuple-element.88), channel_id=1, source_target_pairs={{0,2},{1,3},{2,0},{3,1},{4,6},{5,7},{6,4},{7,5},{8,10},{9,11},{10,... | collective-permute-start | bytes 786440 | tf_op jit(solution)/shard_map/ppermute | solution.py:329
  7.1 15.0 %collective-permute-start.5 = (bf16[2,2,16,1024]{3,2,1,0:T(8,128)(2,1)S(1)}, bf16[2,2,16,1024]{3,2,1,0:T(8,128)(2,1)S(1)}, u32[]{:S(2)}, u32[]{:S(2)}) collective-permute-start(bf16[2,2,16,1024]{3,2,1,0:T(8,128)(2,1)S(1)} %get-tuple-element.95), channel_id=1, source_target_pairs={{0,5},{1,4},{2,7},{3,6},{4,1},{5,0},{6,3},{7,2},{8,13},{9,12},{10,... | collective-permute-start | bytes 393224 | tf_op jit(solution)/shard_map/ppermute | solution.py:329
  10.6 34.4 %collective-permute-start = (bf16[2,4,16,1024]{3,2,1,0:T(8,128)(2,1)S(1)}, bf16[2,4,16,1024]{3,2,1,0:T(8,128)(2,1)S(1)}, u32[]{:S(2)}, u32[]{:S(2)}) collective-permute-start(bf16[2,4,16,1024]{3,2,1,0:T(8,128)(2,1)S(1)} %get-tuple-element.87), channel_id=1, source_target_pairs={{0,1},{1,0},{2,3},{3,2},{4,5},{5,4},{6,7},{7,6},{8,9},{9,8},{10,11... | collective-permute-start | bytes 786440 | tf_op jit(solution)/shard_map/ppermute | solution.py:329
  11.1 33.9 %collective-permute-start.2 = (bf16[2,4,16,1024]{3,2,1,0:T(8,128)(2,1)S(1)}, bf16[2,4,16,1024]{3,2,1,0:T(8,128)(2,1)S(1)}, u32[]{:S(2)}, u32[]{:S(2)}) collective-permute-start(bf16[2,4,16,1024]{3,2,1,0:T(8,128)(2,1)S(1)} %get-tuple-element.89), channel_id=1, source_target_pairs={{0,3},{1,2},{2,1},{3,0},{4,7},{5,6},{6,5},{7,4},{8,11},{9,10},{10,... | collective-permute-start | bytes 786440 | tf_op jit(solution)/shard_map/ppermute | solution.py:329
  12.5 16.9 %collective-permute-start.7 = (bf16[2,2,16,1024]{3,2,1,0:T(8,128)(2,1)S(1)}, bf16[2,2,16,1024]{3,2,1,0:T(8,128)(2,1)S(1)}, u32[]{:S(2)}, u32[]{:S(2)}) collective-permute-start(bf16[2,2,16,1024]{3,2,1,0:T(8,128)(2,1)S(1)} %get-tuple-element.98), channel_id=1, source_target_pairs={{0,6},{1,7},{2,4},{3,5},{4,2},{5,3},{6,0},{7,1},{8,14},{9,15},{10,... | collective-permute-start | bytes 393224 | tf_op jit(solution)/shard_map/ppermute | solution.py:329
  17.0 16.8 %collective-permute-start.9 = (bf16[2,2,16,1024]{3,2,1,0:T(8,128)(2,1)S(1)}, bf16[2,2,16,1024]{3,2,1,0:T(8,128)(2,1)S(1)}, u32[]{:S(2)}, u32[]{:S(2)}) collective-permute-start(bf16[2,2,16,1024]{3,2,1,0:T(8,128)(2,1)S(1)} %get-tuple-element.101), channel_id=1, source_target_pairs={{0,7},{1,6},{2,5},{3,4},{4,3},{5,2},{6,1},{7,0},{8,15},{9,14},{10,... | collective-permute-start | bytes 393224 | tf_op jit(solution)/shard_map/ppermute | solution.py:329
  22.0 22.9 %collective-permute-start.3 = (bf16[2,2,16,1024]{3,2,1,0:T(8,128)(2,1)S(1)}, bf16[2,2,16,1024]{3,2,1,0:T(8,128)(2,1)S(1)}, u32[]{:S(2)}, u32[]{:S(2)}) collective-permute-start(bf16[2,2,16,1024]{3,2,1,0:T(8,128)(2,1)S(1)} %get-tuple-element.92), channel_id=1, source_target_pairs={{0,4},{1,5},{2,6},{3,7},{4,0},{5,1},{6,2},{7,3},{8,12},{9,13},{10,... | collective-permute-start | bytes 393224 | tf_op jit(solution)/shard_map/ppermute | solution.py:329
  29.4 28.4 %collective-permute-start.6 = (bf16[2,2,16,1024]{3,2,1,0:T(8,128)(2,1)S(1)}, bf16[2,2,16,1024]{3,2,1,0:T(8,128)(2,1)S(1)}, u32[]{:S(2)}, u32[]{:S(2)}) collective-permute-start(bf16[2,2,16,1024]{3,2,1,0:T(8,128)(2,1)S(1)} %get-tuple-element.96), channel_id=1, source_target_pairs={{0,5},{1,4},{2,7},{3,6},{4,1},{5,0},{6,3},{7,2},{8,13},{9,12},{10,... | collective-permute-start | bytes 393224 | tf_op jit(solution)/shard_map/ppermute | solution.py:329
  33.8 24.0 %collective-permute-start.8 = (bf16[2,2,16,1024]{3,2,1,0:T(8,128)(2,1)S(1)}, bf16[2,2,16,1024]{3,2,1,0:T(8,128)(2,1)S(1)}, u32[]{:S(2)}, u32[]{:S(2)}) collective-permute-start(bf16[2,2,16,1024]{3,2,1,0:T(8,128)(2,1)S(1)} %get-tuple-element.99), channel_id=1, source_target_pairs={{0,6},{1,7},{2,4},{3,5},{4,2},{5,3},{6,0},{7,1},{8,14},{9,15},{10,... | collective-permute-start | bytes 393224 | tf_op jit(solution)/shard_map/ppermute | solution.py:329
  45.0 12.9 %collective-permute-start.10 = (bf16[2,2,16,1024]{3,2,1,0:T(8,128)(2,1)S(1)}, bf16[2,2,16,1024]{3,2,1,0:T(8,128)(2,1)S(1)}, u32[]{:S(2)}, u32[]{:S(2)}) collective-permute-start(bf16[2,2,16,1024]{3,2,1,0:T(8,128)(2,1)S(1)} %get-tuple-element.102), channel_id=1, source_target_pairs={{0,7},{1,6},{2,5},{3,4},{4,3},{5,2},{6,1},{7,0},{8,15},{9,14},{10,... | collective-permute-start | bytes 393224 | tf_op jit(solution)/shard_map/ppermute | solution.py:329
  45.0 12.9 %collective-permute-start.4 = (bf16[2,2,16,1024]{3,2,1,0:T(8,128)(2,1)S(1)}, bf16[2,2,16,1024]{3,2,1,0:T(8,128)(2,1)S(1)}, u32[]{:S(2)}, u32[]{:S(2)}) collective-permute-start(bf16[2,2,16,1024]{3,2,1,0:T(8,128)(2,1)S(1)} %get-tuple-element.93), channel_id=1, source_target_pairs={{0,4},{1,5},{2,6},{3,7},{4,0},{5,1},{6,2},{7,3},{8,12},{9,13},{10,... | collective-permute-start | bytes 393224 | tf_op jit(solution)/shard_map/ppermute | solution.py:329
  78.3 32.7 %collective-permute-start.13 = (bf16[4,2,32,2048]{3,2,1,0:T(8,128)(2,1)S(1)}, bf16[4,2,32,2048]{3,2,1,0:T(8,128)(2,1)S(1)}, u32[]{:S(2)}, u32[]{:S(2)}) collective-permute-start(bf16[4,2,32,2048]{3,2,1,0:T(8,128)(2,1)S(1)} %get-tuple-element.145), channel_id=1, source_target_pairs={{0,16},{8,24},{16,0},{24,8},{1,17},{9,25},{17,1},{25,9},{2,18},{10... | collective-permute-start | bytes 3145736 | tf_op jit(solution)/shard_map/ppermute | solution.py:329
  79.9 33.5 %collective-permute-start.14 = (bf16[2,4,32,2048]{3,2,1,0:T(8,128)(2,1)S(1)}, bf16[2,4,32,2048]{3,2,1,0:T(8,128)(2,1)S(1)}, u32[]{:S(2)}, u32[]{:S(2)}) collective-permute-start(bf16[2,4,32,2048]{3,2,1,0:T(8,128)(2,1)S(1)} %get-tuple-element.146), channel_id=1, source_target_pairs={{0,1},{1,0},{2,3},{3,2},{4,5},{5,4},{6,7},{7,6},{8,9},{9,8},{10,11... | collective-permute-start | bytes 3145736 | tf_op jit(solution)/shard_map/ppermute | solution.py:329
  81.8 16.0 %collective-permute-start.15 = (bf16[4,16,1024]{2,1,0:T(8,128)(2,1)S(1)}, bf16[4,16,1024]{2,1,0:T(8,128)(2,1)S(1)}, u32[]{:S(2)}, u32[]{:S(2)}) collective-permute-start(bf16[4,16,1024]{2,1,0:T(8,128)(2,1)S(1)} %get-tuple-element.148), channel_id=1, source_target_pairs={{0,5},{1,4},{2,7},{3,6},{4,1},{5,0},{6,3},{7,2},{8,13},{9,12},{10,... | collective-permute-start | bytes 393224 | tf_op jit(solution)/shard_map/ppermute | solution.py:329
  84.2 13.6 %collective-permute-start.17 = (bf16[4,16,1024]{2,1,0:T(8,128)(2,1)S(1)}, bf16[4,16,1024]{2,1,0:T(8,128)(2,1)S(1)}, u32[]{:S(2)}, u32[]{:S(2)}) collective-permute-start(bf16[4,16,1024]{2,1,0:T(8,128)(2,1)S(1)} %get-tuple-element.151), channel_id=1, source_target_pairs={{0,6},{1,7},{2,4},{3,5},{4,2},{5,3},{6,0},{7,1},{8,14},{9,15},{10,... | collective-permute-start | bytes 393224 | tf_op jit(solution)/shard_map/ppermute | solution.py:329
  87.8 13.4 %collective-permute-start.19 = (bf16[4,16,1024]{2,1,0:T(8,128)(2,1)S(1)}, bf16[4,16,1024]{2,1,0:T(8,128)(2,1)S(1)}, u32[]{:S(2)}, u32[]{:S(2)}) collective-permute-start(bf16[4,16,1024]{2,1,0:T(8,128)(2,1)S(1)} %get-tuple-element.154), channel_id=1, source_target_pairs={{0,7},{1,6},{2,5},{3,4},{4,3},{5,2},{6,1},{7,0},{8,15},{9,14},{10,... | collective-permute-start | bytes 393224 | tf_op jit(solution)/shard_map/ppermute | solution.py:329
  97.8 7.3 %collective-permute-start.16 = (bf16[4,16,1024]{2,1,0:T(8,128)(2,1)S(1)}, bf16[4,16,1024]{2,1,0:T(8,128)(2,1)S(1)}, u32[]{:S(2)}, u32[]{:S(2)}) collective-permute-start(bf16[4,16,1024]{2,1,0:T(8,128)(2,1)S(1)} %get-tuple-element.149), channel_id=1, source_target_pairs={{0,2},{1,3},{2,0},{3,1},{4,6},{5,7},{6,4},{7,5},{8,10},{9,11},{10,... | collective-permute-start | bytes 393224 | tf_op jit(solution)/shard_map/ppermute | solution.py:329
  97.8 7.3 %collective-permute-start.18 = (bf16[4,16,1024]{2,1,0:T(8,128)(2,1)S(1)}, bf16[4,16,1024]{2,1,0:T(8,128)(2,1)S(1)}, u32[]{:S(2)}, u32[]{:S(2)}) collective-permute-start(bf16[4,16,1024]{2,1,0:T(8,128)(2,1)S(1)} %get-tuple-element.152), channel_id=1, source_target_pairs={{0,3},{1,2},{2,1},{3,0},{4,7},{5,6},{6,5},{7,4},{8,11},{9,10},{10,... | collective-permute-start | bytes 393224 | tf_op jit(solution)/shard_map/ppermute | solution.py:329
  101.1 9.8 %collective-permute-start.20 = (bf16[4,16,1024]{2,1,0:T(8,128)(2,1)S(1)}, bf16[4,16,1024]{2,1,0:T(8,128)(2,1)S(1)}, u32[]{:S(2)}, u32[]{:S(2)}) collective-permute-start(bf16[4,16,1024]{2,1,0:T(8,128)(2,1)S(1)} %get-tuple-element.155), channel_id=1, source_target_pairs={{0,4},{1,5},{2,6},{3,7},{4,0},{5,1},{6,2},{7,3},{8,12},{9,13},{10,... | collective-permute-start | bytes 393224 | tf_op jit(solution)/shard_map/ppermute | solution.py:329
  114.2 13.1 %collective-permute-start.22 = (bf16[4,32,2048]{2,1,0:T(8,128)(2,1)S(1)}, bf16[4,32,2048]{2,1,0:T(8,128)(2,1)S(1)}, u32[]{:S(2)}, u32[]{:S(2)}) collective-permute-start(bf16[4,32,2048]{2,1,0:T(8,128)(2,1)S(1)} %get-tuple-element.161), channel_id=1, source_target_pairs={{0,16},{8,24},{16,0},{24,8},{1,17},{9,25},{17,1},{25,9},{2,18},{10... | collective-permute-start | bytes 1572872 | tf_op jit(solution)/shard_map/ppermute | solution.py:329
  115.5 12.8 %collective-permute-start.21 = (bf16[4,32,2048]{2,1,0:T(8,128)(2,1)S(1)}, bf16[4,32,2048]{2,1,0:T(8,128)(2,1)S(1)}, u32[]{:S(2)}, u32[]{:S(2)}) collective-permute-start(bf16[4,32,2048]{2,1,0:T(8,128)(2,1)S(1)} %get-tuple-element.158), channel_id=1, source_target_pairs={{0,1},{1,0},{2,3},{3,2},{4,5},{5,4},{6,7},{7,6},{8,9},{9,8},{10,11... | collective-permute-start | bytes 1572872 | tf_op jit(solution)/shard_map/ppermute | solution.py:329
  129.0 12.7 %collective-permute-start.24 = (bf16[32,4096]{1,0:T(8,128)(2,1)S(1)}, bf16[32,4096]{1,0:T(8,128)(2,1)S(1)}, u32[]{:S(2)}, u32[]{:S(2)}) collective-permute-start(bf16[32,4096]{1,0:T(8,128)(2,1)S(1)} %get-tuple-element.162), channel_id=1, source_target_pairs={{0,2},{1,3},{2,0},{3,1},{4,6},{5,7},{6,4},{7,5},{8,10},{9,11},{10,... | collective-permute-start | bytes 786440 | tf_op jit(solution)/shard_map/ppermute | solution.py:329
  132.8 20.1 %collective-permute-start.25 = (bf16[32,4096]{1,0:T(8,128)(2,1)S(1)}, bf16[32,4096]{1,0:T(8,128)(2,1)S(1)}, u32[]{:S(2)}, u32[]{:S(2)}) collective-permute-start(bf16[32,4096]{1,0:T(8,128)(2,1)S(1)} %get-tuple-element.163), channel_id=1, source_target_pairs={{0,4},{1,5},{2,6},{3,7},{4,0},{5,1},{6,2},{7,3},{8,12},{9,13},{10,... | collective-permute-start | bytes 786440 | tf_op jit(solution)/shard_map/ppermute | solution.py:329
  132.8 20.1 %collective-permute-start.26 = (bf16[32,4096]{1,0:T(8,128)(2,1)S(1)}, bf16[32,4096]{1,0:T(8,128)(2,1)S(1)}, u32[]{:S(2)}, u32[]{:S(2)}) collective-permute-start(bf16[32,4096]{1,0:T(8,128)(2,1)S(1)} %get-tuple-element.164), channel_id=1, source_target_pairs={{0,6},{1,7},{2,4},{3,5},{4,2},{5,3},{6,0},{7,1},{8,14},{9,15},{10,... | collective-permute-start | bytes 786440 | tf_op jit(solution)/shard_map/ppermute | solution.py:329
  (8 other events, 74.5 us)

commit v8 on v7

v8 whole, which is shorter than its diff:
```python
import functools
import itertools

import jax
import jax.numpy as jnp
from jax import lax
from jax.experimental import pallas as pl
from jax.experimental.pallas import tpu as pltpu
from jax.sharding import PartitionSpec as P

HEADS = 16
GROUP = 4
FIRST = 9 / 16
CHUNKS = 2
CORES = 2
N_Y = 2
EPSILON = 1e-06
LOWEST = -1e30
LOG2E = 1.4426950408889634
MIB = 1024 * 1024


def contract(left, right, dims):
    return lax.dot_general(left, right, (dims, ((), ())), preferred_element_type=jnp.float32)


def statistics(rows32):
    mean = jnp.mean(rows32, axis=-1, keepdims=True)
    centred = rows32 - mean
    inverse = lax.rsqrt(jnp.mean(centred * centred, axis=-1, keepdims=True) + EPSILON)
    return centred * inverse, inverse


def pick_kernel(n_slots, n_chunks, ids_ref, x_ref, cot_ref, *refs):
    out_refs, sem = refs[:-1], refs[-1]
    half = n_slots // 2
    depth = x_ref.shape[0] // n_chunks
    copies = []
    for i, ref in enumerate(out_refs):
        far = i - half
        here = slice(None) if far < 0 else pl.ds(far // half * depth, depth)
        slot = ids_ref[1] ^ (i if far < 0 else half + far % half)
        for which, source in enumerate((x_ref, cot_ref)):
            copy = pltpu.make_async_copy(source.at[here, slot], ref.at[which], sem.at[2 * i + which])
            copy.start()
            copies.append(copy)
    for copy in copies:
        copy.wait()


def pick(ids, clips, cotangent, n_slots, n_chunks):
    n_clips, _, n_patches, width = clips.shape
    cut = (n_clips, n_slots, n_patches // n_slots, width)
    half = n_slots // 2

    def piece(count):
        return jax.ShapeDtypeStruct((2, count) + cut[2:], clips.dtype)

    out = pl.pallas_call(
        functools.partial(pick_kernel, n_slots, n_chunks),
        out_shape=[piece(n_clips)] * half + [piece(n_clips // n_chunks)] * (half * n_chunks),
        in_specs=[pl.BlockSpec(memory_space=pltpu.SMEM)] + [pl.BlockSpec(memory_space=pl.ANY)] * 2,
        out_specs=[pl.BlockSpec(memory_space=pltpu.VMEM)] * (half * (1 + n_chunks)),
        scratch_shapes=[pltpu.SemaphoreType.DMA((2 * half * (1 + n_chunks),))],
        compiler_params=pltpu.CompilerParams(vmem_limit_bytes=12 * MIB),
    )(ids, clips.reshape(cut), cotangent.reshape(cut))
    far = [out[half + chunk * half :][:half] for chunk in range(n_chunks)]
    return out[:half], far


def place_kernel(ids_ref, *refs):
    for slot, ref in enumerate(refs[:-1]):
        refs[-1][:, ids_ref[1] ^ slot] = ref[...]


def place(ids, blocks):
    n_clips, n_positions, width = blocks[0].shape
    return pl.pallas_call(
        place_kernel,
        out_shape=jax.ShapeDtypeStruct((n_clips, len(blocks), n_positions, width), blocks[0].dtype),
        in_specs=[pl.BlockSpec(memory_space=pltpu.SMEM)]
        + [pl.BlockSpec(memory_space=pltpu.VMEM)] * len(blocks),
        out_specs=pl.BlockSpec(memory_space=pltpu.VMEM),
        compiler_params=pltpu.CompilerParams(vmem_limit_bytes=8 * MIB),
    )(ids, *blocks)


def product_kernel(n_x, flip, n_chunks, spans, ids_ref, *refs):
    lefts, rights, out_ref = refs[: -1 - len(spans) * n_chunks], refs[-1 - len(spans) * n_chunks : -1], refs[-1]
    width = lefts[0].shape[1]
    rest = width // (CORES * n_x)
    core = lax.rem(ids_ref[0], CORES) ^ flip
    starts = [pl.multiple_of((CORES * x + core) * rest, rest) for x in range(n_x)]
    turned = []
    for i in range(0, len(lefts), n_chunks):
        parts = [[left[:, pl.ds(start, rest)] for start in starts] for left in lefts[i : i + n_chunks]]
        turned.append(jnp.concatenate([jnp.concatenate(p, axis=1) for p in parts], axis=0).T)
    at = 0
    for i, (which, start, size) in enumerate(spans):
        right = [ref[:, pl.ds(start, size)] for ref in rights[i * n_chunks : (i + 1) * n_chunks]]
        product = contract(turned[which], jnp.concatenate(right, axis=0), ((1,), (0,)))
        out_ref[:, :, :, :, pl.ds(at, size)] = product.reshape(out_ref.shape[:4] + (size,)).astype(jnp.bfloat16)
        at += size


def products(ids, flip, n_x, n_z, lefts, rights, spans):
    n_chunks = len(rights[0])
    rows, width = rights[0][0].shape
    rest = width // (CORES * n_x * n_z * N_Y)
    columns = sum(size for _, _, size in spans)
    operands = [a for factor in lefts + rights for a in factor]
    return pl.pallas_call(
        functools.partial(product_kernel, n_x, flip, n_chunks, spans),
        out_shape=jax.ShapeDtypeStruct((n_x, n_z, N_Y, rest, columns), jnp.bfloat16),
        in_specs=[pl.BlockSpec(memory_space=pltpu.SMEM)]
        + [pl.BlockSpec(memory_space=pltpu.VMEM)] * len(operands),
        out_specs=pl.BlockSpec(memory_space=pltpu.VMEM),
        compiler_params=pltpu.CompilerParams(vmem_limit_bytes=24 * MIB),
        cost_estimate=pl.CostEstimate(
            flops=n_chunks * rows * width * columns,
            bytes_accessed=2 * n_chunks * rows * (width + columns) + width * columns,
            transcendentals=0,
        ),
    )(ids, *operands)


def summed(refs, index):
    total = refs[0][index].astype(jnp.float32)
    for ref in refs[1:]:
        total += ref[index].astype(jnp.float32)
    return total


def halve_kernel(dim, axis, stride, ids_ref, *refs):
    addends, sent_ref, kept_ref = refs[:-2], refs[-2], refs[-1]
    me = lax.rem(lax.div(ids_ref[axis], stride), 2)
    for index in itertools.product(*(range(n) for n in sent_ref.shape[:-2])):
        sent_ref[index] = summed(addends, index[:dim] + (me ^ 1,) + index[dim:]).astype(jnp.bfloat16)
    for index in itertools.product(*(range(n) for n in sent_ref.shape[:-2])):
        kept_ref[index] = summed(addends, index[:dim] + (me,) + index[dim:])


def halve(ids, addends, dim, axis, stride):
    shape = addends[0].shape[:dim] + addends[0].shape[dim + 1 :]
    return pl.pallas_call(
        functools.partial(halve_kernel, dim, axis, stride),
        out_shape=[jax.ShapeDtypeStruct(shape, jnp.bfloat16), jax.ShapeDtypeStruct(shape, jnp.float32)],
        in_specs=[pl.BlockSpec(memory_space=pltpu.SMEM)]
        + [pl.BlockSpec(memory_space=pltpu.VMEM)] * len(addends),
        out_specs=[pl.BlockSpec(memory_space=pltpu.VMEM)] * 2,
        compiler_params=pltpu.CompilerParams(vmem_limit_bytes=16 * MIB),
    )(ids, *addends)


def join_kernel(n_z, n_first, ids_ref, *refs):
    addends, outs = refs[:-n_z], refs[-n_z:]
    me = lax.div(ids_ref[1], N_Y)
    cut = addends[0].shape[-1]
    for j in [*range(1, n_z), 0]:
        outs[j][:, :cut] = summed(addends[:n_first], (me ^ j,)).astype(outs[j].dtype)
        outs[j][:, cut:] = summed(addends[n_first:], (me ^ j,)).astype(outs[j].dtype)


def join(ids, first, second, n_z):
    shape = (first[0].shape[1], first[0].shape[2] + second[0].shape[2])
    own = jax.ShapeDtypeStruct(shape, jnp.float32)
    other = jax.ShapeDtypeStruct(shape, jnp.bfloat16)
    return pl.pallas_call(
        functools.partial(join_kernel, n_z, len(first)),
        out_shape=[own] + [other] * (n_z - 1),
        in_specs=[pl.BlockSpec(memory_space=pltpu.SMEM)]
        + [pl.BlockSpec(memory_space=pltpu.VMEM)] * (len(first) + len(second)),
        out_specs=[pl.BlockSpec(memory_space=pltpu.VMEM)] * n_z,
        compiler_params=pltpu.CompilerParams(vmem_limit_bytes=12 * MIB),
    )(ids, *first, *second)


def finish_kernel(*refs):
    addends, (grad_qkv_ref, grad_out_ref) = refs[:-2], refs[-2:]
    wide = grad_qkv_ref.shape[1]
    everything = slice(None)
    grad_qkv_ref[...] = summed(addends, (everything, pl.ds(0, wide)))
    grad_out_ref[...] = summed(addends, (everything, pl.ds(wide, grad_out_ref.shape[1])))


def finish(addends):
    rows, columns = addends[0].shape
    return pl.pallas_call(
        finish_kernel,
        out_shape=[
            jax.ShapeDtypeStruct((rows, columns // 4 * 3), jnp.float32),
            jax.ShapeDtypeStruct((rows, columns // 4), jnp.float32),
        ],
        in_specs=[pl.BlockSpec(memory_space=pltpu.VMEM)] * len(addends),
        out_specs=[pl.BlockSpec(memory_space=pltpu.VMEM)] * 2,
        compiler_params=pltpu.CompilerParams(vmem_limit_bytes=8 * MIB),
    )(*addends)


def sublayer_kernel(at, n_clips, n_positions, n_pieces, n_before, *refs):
    pieces, refs = refs[:n_pieces], refs[n_pieces:]
    w_qkv_ref, w_out_ref = refs[:2]
    before, refs = refs[2 : 2 + n_before], refs[2 + n_before :]
    normed_ref, cot_ref, mixed_ref, dq_ref, dk_ref, dv_ref = refs[:6]
    dx_refs = refs[6:]
    rows = normed_ref.shape[0] // n_clips
    span = rows // n_pieces
    width = w_out_ref.shape[0]
    wide = width // HEADS * GROUP
    depth = wide // GROUP
    scaling = depth**-0.5

    def piece(k, which, clip):
        return pieces[k][which, clip if pieces[k].shape[1] == n_clips else at + clip]

    raw = jnp.concatenate([piece(k, 0, clip) for clip in range(n_clips) for k in range(n_pieces)], axis=0)
    unit, _ = statistics(raw.astype(jnp.float32))
    normed_ref[...] = unit.astype(jnp.bfloat16)
    for clip in range(n_clips):
        for k in range(n_pieces):
            cot_ref[pl.ds(clip * rows + k * span, span)] = piece(k, 1, clip)

    lane_head = lax.broadcasted_iota(jnp.int32, (rows, wide), 1) // depth
    head_masks = [(lane_head == h).astype(jnp.float32).astype(jnp.bfloat16) for h in range(GROUP)]
    key_pos = lax.broadcasted_iota(jnp.int32, (rows, rows), 0) % n_positions
    query_pos = lax.broadcasted_iota(jnp.int32, (rows, rows), 1) % n_positions
    same = (key_pos == query_pos)[None]

    def stacked(block):
        return jnp.concatenate([block * mask for mask in head_masks], axis=0)

    def side_by_side(blocks):
        return jnp.concatenate([blocks[h] for h in range(GROUP)], axis=1)

    for group in range(HEADS // GROUP):
        columns = slice(group * wide, (group + 1) * wide)
        all_queries, all_keys, all_values = (
            contract(normed_ref[...], w_qkv_ref[:, pl.ds(i * width + group * wide, wide)], ((1,), (0,))).astype(
                jnp.bfloat16
            )
            for i in range(3)
        )
        mixed_grad = contract(cot_ref[...], w_out_ref[columns, :], ((1,), (1,))).astype(jnp.bfloat16)
        for clip in range(n_clips):
            here = slice(clip * rows, (clip + 1) * rows)
            queries = all_queries[here]
            keys = stacked(all_keys[here])
            values = stacked(all_values[here])
            upstream = mixed_grad[here]
            scores = contract(keys, queries, ((1,), (1,))).reshape(GROUP, rows, rows)
            scores = jnp.where(same, scores, LOWEST)
            highest = jnp.max(scores, axis=1, keepdims=True)
            expo = jnp.exp2((scores - highest) * (scaling * LOG2E))
            full = expo * (1.0 / jnp.sum(expo, axis=1, keepdims=True))
            low = full.astype(jnp.bfloat16)
            dots = contract(values, upstream * jnp.bfloat16(scaling), ((1,), (1,)))
            dots = dots.reshape(GROUP, rows, rows)
            score_grad = full * (dots - jnp.sum(full * dots, axis=1, keepdims=True))
            score_grad = score_grad.astype(jnp.bfloat16)
            mixed = contract(low.reshape(GROUP * rows, rows), values, ((0,), (0,)))
            mixed_ref[here, columns] = mixed.astype(jnp.bfloat16)
            dq = contract(score_grad.reshape(GROUP * rows, rows), keys, ((0,), (0,)))
            dq_ref[here, columns] = dq.astype(jnp.bfloat16)
            dk = contract(side_by_side(score_grad), stacked(queries), ((1,), (0,)))
            dk_ref[here, columns] = dk.astype(jnp.bfloat16)
            dv = contract(side_by_side(low), stacked(upstream), ((1,), (0,)))
            dv_ref[here, columns] = dv.astype(jnp.bfloat16)

    grads = jnp.concatenate([dq_ref[...], dk_ref[...], dv_ref[...]], axis=1)
    total = contract(grads, w_qkv_ref[...], ((1,), (1,)))
    unit, inverse = statistics(raw.astype(jnp.float32))
    grad = inverse * (
        total
        - jnp.mean(total, axis=-1, keepdims=True)
        - unit * jnp.mean(total * unit, axis=-1, keepdims=True)
    )
    dx = (cot_ref[...].astype(jnp.float32) + grad).astype(jnp.bfloat16)
    for k in range(n_pieces):
        if before:
            dx_refs[k][:at] = before[k][...]
        for clip in range(n_clips):
            start = clip * rows + k * span
            dx_refs[k][at + clip] = dx[start : start + span]


def sublayer(pieces, at, n_clips, w_qkv, w_out, n_positions, before):
    _, _, span, width = pieces[0].shape
    rows = n_clips * len(pieces) * span
    flat = jax.ShapeDtypeStruct((rows, width), jnp.bfloat16)
    dx = jax.ShapeDtypeStruct((at + n_clips, span, width), jnp.bfloat16)
    operands = (*pieces, w_qkv, w_out, *before)
    return pl.pallas_call(
        functools.partial(sublayer_kernel, at, n_clips, n_positions, len(pieces), len(before)),
        out_shape=[flat] * 6 + [dx] * len(pieces),
        in_specs=[pl.BlockSpec(memory_space=pltpu.VMEM)] * len(operands),
        out_specs=[pl.BlockSpec(memory_space=pltpu.VMEM)] * (6 + len(pieces)),
        compiler_params=pltpu.CompilerParams(vmem_limit_bytes=32 * MIB),
        cost_estimate=pl.CostEstimate(
            flops=2 * rows * width * (7 * width + 24 * 128),
            bytes_accessed=16 * rows * width + 8 * width * width,
            transcendentals=rows * 128 * HEADS,
        ),
    )(*operands)


def swap(block, axis, size, distance):
    return lax.ppermute(block, axis, [(i, i ^ distance) for i in range(size)])


def after(values, done):
    values, _ = lax.optimization_barrier((values, done))
    return values


def inbound(near, far, n_tm):
    half = n_tm // 2
    near = [near[0]] + [swap(near[k], "tm", n_tm, k) for k in range(1, half)]
    arrived = []
    for blocks in far:
        gates = arrived[-1] if arrived else [near[2]] + [None] * (half - 1)
        blocks = [block if gate is None else after(block, gate) for block, gate in zip(blocks, gates)]
        done = {i: swap(blocks[i], "tm", n_tm, half + i) for i in reversed(range(half))}
        arrived.append([done[i] for i in range(half)])
    return near, arrived


def shards(n_clip_devices, n_tm, clips, w_qkv, w_out, cotangent):
    n_clips, _, n_patches, width = clips.shape
    n_positions = n_patches // n_tm
    n_x, n_z = n_clip_devices // CORES, n_tm // N_Y
    joined = n_positions % 16 != 0
    ids = jnp.stack([lax.axis_index("clip"), lax.axis_index("tm")]).astype(jnp.int32)

    near, far = inbound(*pick(ids, clips, cotangent, n_tm, CHUNKS), n_tm)
    depth = n_clips // CHUNKS
    factors, dx = [], []
    for chunk in range(CHUNKS):
        at = chunk * depth
        pieces = near + far[chunk]
        if joined:
            pieces = [p[:, at : at + depth] for p in near] + far[chunk]
            pieces = [jnp.stack(pieces, axis=2).reshape(2, depth, -1, width)]
        out = sublayer(pieces, at, depth, w_qkv, w_out, n_positions, dx)
        factors.append(out[:6])
        dx = list(out[6:])
    normed, cot, mixed, dq, dk, dv = zip(*factors)
    if joined:
        cut = dx[0].reshape(n_clips, n_tm, n_positions, width)
        dx = [cut[:, k] for k in range(n_tm)]

    cut = int(4 * width * FIRST) - 2 * width
    first_parts = ([normed], [dq, dk, dv]), ((0, 0, width), (0, 0, width), (0, 0, cut))
    second_parts = ([normed, mixed], [dv, cot]), ((0, cut, width - cut), (1, 0, width))
    sent_second = products(ids, 1, n_x, n_z, *second_parts[0], second_parts[1])
    second = swap(sent_second, "clip", n_clip_devices, 1)
    sent_first = products(ids, 1, n_x, n_z, *after(first_parts[0], sent_second), first_parts[1])
    first = swap(sent_first, "clip", n_clip_devices, 1)
    own_second = products(ids, 0, n_x, n_z, *after(second_parts[0], sent_first), second_parts[1])
    sent, own_second = halve(ids, (own_second, second), 2, 1, 1)
    second = swap(sent, "tm", n_tm, 1)
    own_first = products(ids, 0, n_x, n_z, *after(first_parts[0], own_second), first_parts[1])
    sent, own_first = halve(ids, (own_first, first), 0, 0, CORES)
    first = swap(sent, "clip", n_clip_devices, CORES)
    dx = after(dx, sent_first)
    late = (1, 3)
    back = {}
    for k in reversed([k for k in range(1, n_tm) if k not in late]):
        block = after(dx[k], back[k + 3]) if k + 3 in back else dx[k]
        back[k] = swap(block, "tm", n_tm, k)
    first, second = after((first, second), back)
    sent, own_first = halve(ids, (own_first, first), 1, 1, 1)
    first = swap(sent, "tm", n_tm, 1)
    sent, own_second = halve(ids, (own_second, second), 0, 0, CORES)
    second = swap(sent, "clip", n_clip_devices, CORES)
    total, *sent = join(ids, (own_first, first), (own_second, second), n_z)
    others = [swap(block, "tm", n_tm, (j + 1) * N_Y) for j, block in enumerate(sent)]
    back[0] = dx[0]
    for k in late:
        back[k] = swap(after(dx[k], sent), "tm", n_tm, k)
    grad_clips = place(ids, [back[k] for k in range(n_tm)]).reshape(clips.shape)
    grad_qkv, grad_out = finish((total, *others))
    return (grad_clips, grad_qkv, grad_out)


def solution(mesh):
    return jax.shard_map(
        functools.partial(shards, mesh.shape["clip"], mesh.shape["tm"]),
        mesh=mesh,
        in_specs=(P("clip", "tm", None, None), P(), P(), P("clip", "tm", None, None)),
        out_specs=(P("clip", "tm", None, None), P(("clip", "tm"), None), P(("clip", "tm"), None)),
        check_vma=False,
    )
```

time: 155 us -> 153 us (0.987)
  starting transfers between devices: 46.2 us -> 40.8 us
  waiting for transfers between devices: 66.1 us -> 71.4 us
  Pallas kernels: 35.1 us -> 33.2 us
    ppermute x27, starting transfers between devices: 46.2 us -> 40.8 us  [swap(): return lax.ppermute(block, axis, [(i, i ^ distance) for i in range(size)])]
    ppermute x27, waiting for transfers between devices: 66.1 us -> 71.4 us  [swap(): return lax.ppermute(block, axis, [(i, i ^ distance) for i in range(size)])]
    pallas_call x6, Pallas kernels: 27.6 us -> 24.5 us  [the longest x2 17 us: sublayer(): pl.pallas_call(functools.partial(sublayer_kernel, at, n_clips, n_position...]
  transfers between devices with their start and end apart: 27 -> 27, of which waited for: 11 -> 15; matrix products, arithmetic and copies ran while one was open for 0% -> 0% of each run, Pallas kernels for 12% -> 10%
where the time goes in v8:
time: 153 us; the launch traced here: 152 us
  waiting for transfers between devices  71.4 us (47%)
  starting transfers between devices  40.8 us (27%)
  Pallas kernels  33.2 us (22%)
  local copies, waits for them, and re-layouts  5.24 us (3%)
    ppermute x27, waiting for transfers between devices, swap(): return lax.ppermute(block, axis, [(i, i ^ distance) for i in range(size)])  71.4 us
    ppermute x27, starting transfers between devices, swap(): return lax.ppermute(block, axis, [(i, i ^ distance) for i in range(size)])  40.8 us
    pallas_call x2, Pallas kernels, sublayer(): pl.pallas_call(functools.partial(sublayer_kernel, at, n_clips, n_position...  17 us
    pallas_call x4, Pallas kernels, products(): pl.pallas_call(functools.partial(product_kernel, n_x, flip, n_chunks, spa...  7.54 us
    unnamed x10, local copies, waits for them, and re-layouts  5.24 us
    pallas_call x4, Pallas kernels, halve(): pl.pallas_call(functools.partial(halve_kernel, dim, axis, stride), out_sh...  3.58 us
  transfers between devices with their start and end apart: 27, of which 15 were waited for; matrix products, arithmetic and copies ran while one was open for 0% of the time, Pallas kernels for 10%

profile of v8, /device:TPU:0, one launch (start us, length us, event | category | flops | bytes accessed | tf_op | source)
XLA Modules:
  0.0 151.6 jit_solution(14871424760535970198)
XLA Ops:
  5.0 3.1 %collective-permute-start.1 = (bf16[2,4,16,1024]{3,2,1,0:T(8,128)(2,1)S(1)}, bf16[2,4,16,1024]{3,2,1,0:T(8,128)(2,1)S(1)}, u32[]{:S(2)}, u32[]{:S(2)}) collective-permute-start(bf16[2,4,16,1024]{3,2,1,0:T(8,128)(2,1)S(1)} %get-tuple-element.102), channel_id=1, source_target_pairs={{0,2},{1,3},{2,0},{3,1},{4,6},{5,7},{6,4},{7,5},{8,10},{9,11},{10,... | collective-permute-start | bytes 786440 | tf_op jit(solution)/shard_map/ppermute | solution.py:307
  8.1 3.5 %collective-permute-start.5 = (bf16[2,2,16,1024]{3,2,1,0:T(8,128)(2,1)S(1)}, bf16[2,2,16,1024]{3,2,1,0:T(8,128)(2,1)S(1)}, u32[]{:S(2)}, u32[]{:S(2)}) collective-permute-start(bf16[2,2,16,1024]{3,2,1,0:T(8,128)(2,1)S(1)} %get-tuple-element.109), channel_id=1, source_target_pairs={{0,5},{1,4},{2,7},{3,6},{4,1},{5,0},{6,3},{7,2},{8,13},{9,12},{10,... | collective-permute-start | bytes 393224 | tf_op jit(solution)/shard_map/ppermute | solution.py:307
  14.9 3.1 %collective-permute-done.1.refs_2_ = bf16[2,4,16,1024]{3,2,1,0:T(8,128)(2,1)S(1)} collective-permute-done((bf16[2,4,16,1024]{3,2,1,0:T(8,128)(2,1)S(1)}, bf16[2,4,16,1024]{3,2,1,0:T(8,128)(2,1)S(1)}, u32[]{:S(2)}, u32[]{:S(2)}) %collective-permute-start.1) | collective-permute-done | bytes 262176 | tf_op jit(solution)/shard_map/ppermute | solution.py:307
  18.1 5.0 %collective-permute-start.9 = (bf16[2,2,16,1024]{3,2,1,0:T(8,128)(2,1)S(1)}, bf16[2,2,16,1024]{3,2,1,0:T(8,128)(2,1)S(1)}, u32[]{:S(2)}, u32[]{:S(2)}) collective-permute-start(bf16[2,2,16,1024]{3,2,1,0:T(8,128)(2,1)S(1)} %get-tuple-element.115), channel_id=1, source_target_pairs={{0,7},{1,6},{2,5},{3,4},{4,3},{5,2},{6,1},{7,0},{8,15},{9,14},{10,... | collective-permute-start | bytes 393224 | tf_op jit(solution)/shard_map/ppermute | solution.py:307
  23.1 7.4 %collective-permute-done.7.refs_6_ = bf16[2,2,16,1024]{3,2,1,0:T(8,128)(2,1)S(1)} collective-permute-done((bf16[2,2,16,1024]{3,2,1,0:T(8,128)(2,1)S(1)}, bf16[2,2,16,1024]{3,2,1,0:T(8,128)(2,1)S(1)}, u32[]{:S(2)}, u32[]{:S(2)}) %collective-permute-start.7) | collective-permute-done | bytes 131104 | tf_op jit(solution)/shard_map/ppermute | solution.py:307
  30.5 4.4 %collective-permute-done.9.refs_7_ = bf16[2,2,16,1024]{3,2,1,0:T(8,128)(2,1)S(1)} collective-permute-done((bf16[2,2,16,1024]{3,2,1,0:T(8,128)(2,1)S(1)}, bf16[2,2,16,1024]{3,2,1,0:T(8,128)(2,1)S(1)}, u32[]{:S(2)}, u32[]{:S(2)}) %collective-permute-start.9) | collective-permute-done | bytes 131104 | tf_op jit(solution)/shard_map/ppermute | solution.py:307
  34.9 1.9 %collective-permute-start.8 = (bf16[2,2,16,1024]{3,2,1,0:T(8,128)(2,1)S(1)}, bf16[2,2,16,1024]{3,2,1,0:T(8,128)(2,1)S(1)}, u32[]{:S(2)}, u32[]{:S(2)}) collective-permute-start(bf16[2,2,16,1024]{3,2,1,0:T(8,128)(2,1)S(1)} %get-tuple-element.113), channel_id=1, source_target_pairs={{0,6},{1,7},{2,4},{3,5},{4,2},{5,3},{6,0},{7,1},{8,14},{9,15},{10,... | collective-permute-start | bytes 393224 | tf_op jit(solution)/shard_map/ppermute | solution.py:307
  36.8 9.2 %collective-permute-done.3.refs_4_ = bf16[2,2,16,1024]{3,2,1,0:T(8,128)(2,1)S(1)} collective-permute-done((bf16[2,2,16,1024]{3,2,1,0:T(8,128)(2,1)S(1)}, bf16[2,2,16,1024]{3,2,1,0:T(8,128)(2,1)S(1)}, u32[]{:S(2)}, u32[]{:S(2)}) %collective-permute-start.3) | collective-permute-done | bytes 131104 | tf_op jit(solution)/shard_map/ppermute | solution.py:307
  46.1 2.8 %copy-done.2 = bf16[1024,3072]{1,0:T(8,128)(2,1)S(1)} copy-done((bf16[1024,3072]{1,0:T(8,128)(2,1)S(1)}, bf16[1024,3072]{1,0:T(8,128)(2,1)}, u32[]{:S(2)}) %copy-start.2) | copy-done | bytes 6291480
  48.8 8.4 %shard_map.68 = (bf16[256,1024]{1,0:T(8,128)(2,1)S(1)}, bf16[256,1024]{1,0:T(8,128)(2,1)S(1)}, bf16[256,1024]{1,0:T(8,128)(2,1)S(1)}, bf16[256,1024]{1,0:T(8,128...) custom-call(bf16[2,4,16,1024]{3,2,1,0:T(8,128)(2,1)S(1)} %get-tuple-, ...), custom_call_target="tpu_custom_call" | custom-call | flops 5368709120 | bytes 12582912 | tf_op jit(solution)/shard_map/pallas_call | solution.py:292
  58.7 8.6 %shard_map.69 = (bf16[256,1024]{1,0:T(8,128)(2,1)S(1)}, bf16[256,1024]{1,0:T(8,128)(2,1)S(1)}, bf16[256,1024]{1,0:T(8,128)(2,1)S(1)}, bf16[256,1024]{1,0:T(8,128...) custom-call(bf16[2,4,16,1024]{3,2,1,0:T(8,128)(2,1)S(1)} %get-tuple-, ...), custom_call_target="tpu_custom_call" | custom-call | flops 5368709120 | bytes 12582912 | tf_op jit(solution)/shard_map/pallas_call | solution.py:292
  69.1 2.0 %shard_map.71 = bf16[2,4,2,32,2304]{4,3,2,1,0:T(8,128)(2,1)S(1)} custom-call(s32[2]{0:T(128)S(1)} %pad_add_fusion.ids_ref, bf16[256,1024]{1,0:T(8,128)(2,1)S(1)} %get-tuple-element.164.refs_0_, bf16[256,1024]{1,0:T(8,128)(2,1)S(1)} %get-tuple-element.165.refs_1_, bf16[256,1024]{1,0:T(8,128)(2,1)S(1)} %get-tuple-element.166.refs_2_, ...), custom_call_target="tpu_custom_call" | custom-call | flops 1207959552 | bytes 5767168 | tf_op jit(solution)/shard_map/pallas_call | solution.py:112
  73.5 4.9 %collective-permute-done.11.refs_1_ = bf16[2,4,2,32,1792]{4,3,2,1,0:T(8,128)(2,1)S(1)} collective-permute-done((bf16[2,4,2,32,1792]{4,3,2,1,0:T(8,128)(2,1)S(1)}, bf16[2,4,2,32,1792]{4,3,2,1,0:T(8,128)(2,1)S(1)}, u32[]{:S(2)}, u32[]{:S(2)}) %collective-permute-start.11) | collective-permute-done | bytes 1835040 | tf_op jit(solution)/shard_map/ppermute | solution.py:307
  79.4 2.0 %shard_map.74.refs_0_ = bf16[2,4,2,32,2304]{4,3,2,1,0:T(8,128)(2,1)S(1)} custom-call(s32[2]{0:T(128)S(1)} %pad_add_fusion.ids_ref, bf16[256,1024]{1,0:T(8,128)(2,1)S(1)} %get-tuple-element.164.refs_0_, bf16[256,1024]{1,0:T(8,128)(2,1)S(1)} %get-tuple-element.165.refs_1_, bf16[256,1024]{1,0:T(8,128)(2,1)S(1)} %get-tuple-element.166.refs_2_, ...), custom_call_target="tpu_custom_call" | custom-call | flops 1207959552 | bytes 5767168 | tf_op jit(solution)/shard_map/pallas_call | solution.py:112
  87.0 4.7 %collective-permute-start.17 = (bf16[4,16,1024]{2,1,0:T(8,128)(2,1)S(1)}, bf16[4,16,1024]{2,1,0:T(8,128)(2,1)S(1)}, u32[]{:S(2)}, u32[]{:S(2)}) collective-permute-start(bf16[4,16,1024]{2,1,0:T(8,128)(2,1)S(1)} %get-tuple-element.179), channel_id=1, source_target_pairs={{0,7},{1,6},{2,5},{3,4},{4,3},{5,2},{6,1},{7,0},{8,15},{9,14},{10,... | collective-permute-start | bytes 393224 | tf_op jit(solution)/shard_map/ppermute | solution.py:307
  92.2 9.4 %collective-permute-done.15.refs_5_ = bf16[4,16,1024]{2,1,0:T(8,128)(2,1)S(1)} collective-permute-done((bf16[4,16,1024]{2,1,0:T(8,128)(2,1)S(1)}, bf16[4,16,1024]{2,1,0:T(8,128)(2,1)S(1)}, u32[]{:S(2)}, u32[]{:S(2)}) %collective-permute-start.15) | collective-permute-done | bytes 131104 | tf_op jit(solution)/shard_map/ppermute | solution.py:307
  101.7 4.0 %collective-permute-start.18 = (bf16[4,16,1024]{2,1,0:T(8,128)(2,1)S(1)}, bf16[4,16,1024]{2,1,0:T(8,128)(2,1)S(1)}, u32[]{:S(2)}, u32[]{:S(2)}) collective-permute-start(bf16[4,16,1024]{2,1,0:T(8,128)(2,1)S(1)} %get-tuple-element.180), channel_id=1, source_target_pairs={{0,4},{1,5},{2,6},{3,7},{4,0},{5,1},{6,2},{7,3},{8,12},{9,13},{10,... | collective-permute-start | bytes 393224 | tf_op jit(solution)/shard_map/ppermute | solution.py:307
  105.7 2.1 %collective-permute-done.16.refs_2_ = bf16[4,16,1024]{2,1,0:T(8,128)(2,1)S(1)} collective-permute-done((bf16[4,16,1024]{2,1,0:T(8,128)(2,1)S(1)}, bf16[4,16,1024]{2,1,0:T(8,128)(2,1)S(1)}, u32[]{:S(2)}, u32[]{:S(2)}) %collective-permute-start.16) | collective-permute-done | bytes 131104 | tf_op jit(solution)/shard_map/ppermute | solution.py:307
  107.8 3.3 %collective-permute-done.18.refs_4_ = bf16[4,16,1024]{2,1,0:T(8,128)(2,1)S(1)} collective-permute-done((bf16[4,16,1024]{2,1,0:T(8,128)(2,1)S(1)}, bf16[4,16,1024]{2,1,0:T(8,128)(2,1)S(1)}, u32[]{:S(2)}, u32[]{:S(2)}) %collective-permute-start.18) | collective-permute-done | bytes 131104 | tf_op jit(solution)/shard_map/ppermute | solution.py:307
  115.2 10.6 %collective-permute-done.21.refs_3_ = bf16[4,32,1792]{2,1,0:T(8,128)(2,1)S(1)} collective-permute-done((bf16[4,32,1792]{2,1,0:T(8,128)(2,1)S(1)}, bf16[4,32,1792]{2,1,0:T(8,128)(2,1)S(1)}, u32[]{:S(2)}, u32[]{:S(2)}) %collective-permute-start.21) | collective-permute-done | bytes 458784 | tf_op jit(solution)/shard_map/ppermute | solution.py:307
  127.5 2.8 %collective-permute-start.24 = (bf16[32,4096]{1,0:T(8,128)(2,1)S(1)}, bf16[32,4096]{1,0:T(8,128)(2,1)S(1)}, u32[]{:S(2)}, u32[]{:S(2)}) collective-permute-start(bf16[32,4096]{1,0:T(8,128)(2,1)S(1)} %get-tuple-element.188), channel_id=1, source_target_pairs={{0,2},{1,3},{2,0},{3,1},{4,6},{5,7},{6,4},{7,5},{8,10},{9,11},{10,... | collective-permute-start | bytes 786440 | tf_op jit(solution)/shard_map/ppermute | solution.py:307
  130.3 2.4 %collective-permute-start.26 = (bf16[32,4096]{1,0:T(8,128)(2,1)S(1)}, bf16[32,4096]{1,0:T(8,128)(2,1)S(1)}, u32[]{:S(2)}, u32[]{:S(2)}) collective-permute-start(bf16[32,4096]{1,0:T(8,128)(2,1)S(1)} %get-tuple-element.190), channel_id=1, source_target_pairs={{0,6},{1,7},{2,4},{3,5},{4,2},{5,3},{6,0},{7,1},{8,14},{9,15},{10,... | collective-permute-start | bytes 786440 | tf_op jit(solution)/shard_map/ppermute | solution.py:307
  135.2 2.9 %collective-permute-done.22.refs_1_ = bf16[4,16,1024]{2,1,0:T(8,128)(2,1)S(1)} collective-permute-done((bf16[4,16,1024]{2,1,0:T(8,128)(2,1)S(1)}, bf16[4,16,1024]{2,1,0:T(8,128)(2,1)S(1)}, u32[]{:S(2)}, u32[]{:S(2)}) %collective-permute-start.22) | collective-permute-done | bytes 131104 | tf_op jit(solution)/shard_map/ppermute | solution.py:307
  138.2 10.0 %collective-permute-done.23.refs_3_ = bf16[4,16,1024]{2,1,0:T(8,128)(2,1)S(1)} collective-permute-done((bf16[4,16,1024]{2,1,0:T(8,128)(2,1)S(1)}, bf16[4,16,1024]{2,1,0:T(8,128)(2,1)S(1)}, u32[]{:S(2)}, u32[]{:S(2)}) %collective-permute-start.23) | collective-permute-done | bytes 131104 | tf_op jit(solution)/shard_map/ppermute | solution.py:307
  (55 shorter events, 32.1 us)
Async XLA Ops:
  5.0 13.0 %collective-permute-start.1 = (bf16[2,4,16,1024]{3,2,1,0:T(8,128)(2,1)S(1)}, bf16[2,4,16,1024]{3,2,1,0:T(8,128)(2,1)S(1)}, u32[]{:S(2)}, u32[]{:S(2)}) collective-permute-start(bf16[2,4,16,1024]{3,2,1,0:T(8,128)(2,1)S(1)} %get-tuple-element.102), channel_id=1, source_target_pairs={{0,2},{1,3},{2,0},{3,1},{4,6},{5,7},{6,4},{7,5},{8,10},{9,11},{10,... | collective-permute-start | bytes 786440 | tf_op jit(solution)/shard_map/ppermute | solution.py:307
  8.1 15.0 %collective-permute-start.5 = (bf16[2,2,16,1024]{3,2,1,0:T(8,128)(2,1)S(1)}, bf16[2,2,16,1024]{3,2,1,0:T(8,128)(2,1)S(1)}, u32[]{:S(2)}, u32[]{:S(2)}) collective-permute-start(bf16[2,2,16,1024]{3,2,1,0:T(8,128)(2,1)S(1)} %get-tuple-element.109), channel_id=1, source_target_pairs={{0,5},{1,4},{2,7},{3,6},{4,1},{5,0},{6,3},{7,2},{8,13},{9,12},{10,... | collective-permute-start | bytes 393224 | tf_op jit(solution)/shard_map/ppermute | solution.py:307
  11.7 34.4 %collective-permute-start = (bf16[2,4,16,1024]{3,2,1,0:T(8,128)(2,1)S(1)}, bf16[2,4,16,1024]{3,2,1,0:T(8,128)(2,1)S(1)}, u32[]{:S(2)}, u32[]{:S(2)}) collective-permute-start(bf16[2,4,16,1024]{3,2,1,0:T(8,128)(2,1)S(1)} %get-tuple-element.101), channel_id=1, source_target_pairs={{0,1},{1,0},{2,3},{3,2},{4,5},{5,4},{6,7},{7,6},{8,9},{9,8},{10,11... | collective-permute-start | bytes 786440 | tf_op jit(solution)/shard_map/ppermute | solution.py:307
  12.2 33.9 %collective-permute-start.2 = (bf16[2,4,16,1024]{3,2,1,0:T(8,128)(2,1)S(1)}, bf16[2,4,16,1024]{3,2,1,0:T(8,128)(2,1)S(1)}, u32[]{:S(2)}, u32[]{:S(2)}) collective-permute-start(bf16[2,4,16,1024]{3,2,1,0:T(8,128)(2,1)S(1)} %get-tuple-element.103), channel_id=1, source_target_pairs={{0,3},{1,2},{2,1},{3,0},{4,7},{5,6},{6,5},{7,4},{8,11},{9,10},{10,... | collective-permute-start | bytes 786440 | tf_op jit(solution)/shard_map/ppermute | solution.py:307
  13.6 16.9 %collective-permute-start.7 = (bf16[2,2,16,1024]{3,2,1,0:T(8,128)(2,1)S(1)}, bf16[2,2,16,1024]{3,2,1,0:T(8,128)(2,1)S(1)}, u32[]{:S(2)}, u32[]{:S(2)}) collective-permute-start(bf16[2,2,16,1024]{3,2,1,0:T(8,128)(2,1)S(1)} %get-tuple-element.112), channel_id=1, source_target_pairs={{0,6},{1,7},{2,4},{3,5},{4,2},{5,3},{6,0},{7,1},{8,14},{9,15},{10,... | collective-permute-start | bytes 393224 | tf_op jit(solution)/shard_map/ppermute | solution.py:307
  18.1 16.8 %collective-permute-start.9 = (bf16[2,2,16,1024]{3,2,1,0:T(8,128)(2,1)S(1)}, bf16[2,2,16,1024]{3,2,1,0:T(8,128)(2,1)S(1)}, u32[]{:S(2)}, u32[]{:S(2)}) collective-permute-start(bf16[2,2,16,1024]{3,2,1,0:T(8,128)(2,1)S(1)} %get-tuple-element.115), channel_id=1, source_target_pairs={{0,7},{1,6},{2,5},{3,4},{4,3},{5,2},{6,1},{7,0},{8,15},{9,14},{10,... | collective-permute-start | bytes 393224 | tf_op jit(solution)/shard_map/ppermute | solution.py:307
  23.1 22.9 %collective-permute-start.3 = (bf16[2,2,16,1024]{3,2,1,0:T(8,128)(2,1)S(1)}, bf16[2,2,16,1024]{3,2,1,0:T(8,128)(2,1)S(1)}, u32[]{:S(2)}, u32[]{:S(2)}) collective-permute-start(bf16[2,2,16,1024]{3,2,1,0:T(8,128)(2,1)S(1)} %get-tuple-element.106), channel_id=1, source_target_pairs={{0,4},{1,5},{2,6},{3,7},{4,0},{5,1},{6,2},{7,3},{8,12},{9,13},{10,... | collective-permute-start | bytes 393224 | tf_op jit(solution)/shard_map/ppermute | solution.py:307
  30.5 26.8 %collective-permute-start.6 = (bf16[2,2,16,1024]{3,2,1,0:T(8,128)(2,1)S(1)}, bf16[2,2,16,1024]{3,2,1,0:T(8,128)(2,1)S(1)}, u32[]{:S(2)}, u32[]{:S(2)}) collective-permute-start(bf16[2,2,16,1024]{3,2,1,0:T(8,128)(2,1)S(1)} %get-tuple-element.110), channel_id=1, source_target_pairs={{0,5},{1,4},{2,7},{3,6},{4,1},{5,0},{6,3},{7,2},{8,13},{9,12},{10,... | collective-permute-start | bytes 393224 | tf_op jit(solution)/shard_map/ppermute | solution.py:307
  34.9 22.4 %collective-permute-start.8 = (bf16[2,2,16,1024]{3,2,1,0:T(8,128)(2,1)S(1)}, bf16[2,2,16,1024]{3,2,1,0:T(8,128)(2,1)S(1)}, u32[]{:S(2)}, u32[]{:S(2)}) collective-permute-start(bf16[2,2,16,1024]{3,2,1,0:T(8,128)(2,1)S(1)} %get-tuple-element.113), channel_id=1, source_target_pairs={{0,6},{1,7},{2,4},{3,5},{4,2},{5,3},{6,0},{7,1},{8,14},{9,15},{10,... | collective-permute-start | bytes 393224 | tf_op jit(solution)/shard_map/ppermute | solution.py:307
  46.0 11.3 %collective-permute-start.10 = (bf16[2,2,16,1024]{3,2,1,0:T(8,128)(2,1)S(1)}, bf16[2,2,16,1024]{3,2,1,0:T(8,128)(2,1)S(1)}, u32[]{:S(2)}, u32[]{:S(2)}) collective-permute-start(bf16[2,2,16,1024]{3,2,1,0:T(8,128)(2,1)S(1)} %get-tuple-element.116), channel_id=1, source_target_pairs={{0,7},{1,6},{2,5},{3,4},{4,3},{5,2},{6,1},{7,0},{8,15},{9,14},{10,... | collective-permute-start | bytes 393224 | tf_op jit(solution)/shard_map/ppermute | solution.py:307
  46.0 12.7 %collective-permute-start.4 = (bf16[2,2,16,1024]{3,2,1,0:T(8,128)(2,1)S(1)}, bf16[2,2,16,1024]{3,2,1,0:T(8,128)(2,1)S(1)}, u32[]{:S(2)}, u32[]{:S(2)}) collective-permute-start(bf16[2,2,16,1024]{3,2,1,0:T(8,128)(2,1)S(1)} %get-tuple-element.107), channel_id=1, source_target_pairs={{0,4},{1,5},{2,6},{3,7},{4,0},{5,1},{6,2},{7,3},{8,12},{9,13},{10,... | collective-permute-start | bytes 393224 | tf_op jit(solution)/shard_map/ppermute | solution.py:307
  71.2 10.3 %collective-permute-start.12 = (bf16[2,4,2,32,2304]{4,3,2,1,0:T(8,128)(2,1)S(1)}, bf16[2,4,2,32,2304]{4,3,2,1,0:T(8,128)(2,1)S(1)}, u32[]{:S(2)}, u32[]{:S(2)}) collective-permute-start(bf16[2,4,2,32,2304]{4,3,2,1,0:T(8,128)(2,1)S(1)} %shard_map.71), channel_id=1, source_target_pairs={{0,8},{8,0},{16,24},{24,16},{1,9},{9,1},{17,25},{25,17},{2,10},{10... | collective-permute-start | bytes 7077896 | tf_op jit(solution)/shard_map/ppermute | solution.py:307
  82.5 29.3 %collective-permute-start.13 = (bf16[4,2,32,2304]{3,2,1,0:T(8,128)(2,1)S(1)}, bf16[4,2,32,2304]{3,2,1,0:T(8,128)(2,1)S(1)}, u32[]{:S(2)}, u32[]{:S(2)}) collective-permute-start(bf16[4,2,32,2304]{3,2,1,0:T(8,128)(2,1)S(1)} %get-tuple-element.173), channel_id=1, source_target_pairs={{0,16},{8,24},{16,0},{24,8},{1,17},{9,25},{17,1},{25,9},{2,18},{10... | collective-permute-start | bytes 3538952 | tf_op jit(solution)/shard_map/ppermute | solution.py:307
  84.1 27.7 %collective-permute-start.14 = (bf16[2,4,32,1792]{3,2,1,0:T(8,128)(2,1)S(1)}, bf16[2,4,32,1792]{3,2,1,0:T(8,128)(2,1)S(1)}, u32[]{:S(2)}, u32[]{:S(2)}) collective-permute-start(bf16[2,4,32,1792]{3,2,1,0:T(8,128)(2,1)S(1)} %get-tuple-element.174), channel_id=1, source_target_pairs={{0,1},{1,0},{2,3},{3,2},{4,5},{5,4},{6,7},{7,6},{8,9},{9,8},{10,11... | collective-permute-start | bytes 2752520 | tf_op jit(solution)/shard_map/ppermute | solution.py:307
  85.3 16.3 %collective-permute-start.15 = (bf16[4,16,1024]{2,1,0:T(8,128)(2,1)S(1)}, bf16[4,16,1024]{2,1,0:T(8,128)(2,1)S(1)}, u32[]{:S(2)}, u32[]{:S(2)}) collective-permute-start(bf16[4,16,1024]{2,1,0:T(8,128)(2,1)S(1)} %get-tuple-element.176), channel_id=1, source_target_pairs={{0,5},{1,4},{2,7},{3,6},{4,1},{5,0},{6,3},{7,2},{8,13},{9,12},{10,... | collective-permute-start | bytes 393224 | tf_op jit(solution)/shard_map/ppermute | solution.py:307
  87.0 14.7 %collective-permute-start.17 = (bf16[4,16,1024]{2,1,0:T(8,128)(2,1)S(1)}, bf16[4,16,1024]{2,1,0:T(8,128)(2,1)S(1)}, u32[]{:S(2)}, u32[]{:S(2)}) collective-permute-start(bf16[4,16,1024]{2,1,0:T(8,128)(2,1)S(1)} %get-tuple-element.179), channel_id=1, source_target_pairs={{0,7},{1,6},{2,5},{3,4},{4,3},{5,2},{6,1},{7,0},{8,15},{9,14},{10,... | collective-permute-start | bytes 393224 | tf_op jit(solution)/shard_map/ppermute | solution.py:307
  91.7 14.0 %collective-permute-start.19 = (bf16[4,16,1024]{2,1,0:T(8,128)(2,1)S(1)}, bf16[4,16,1024]{2,1,0:T(8,128)(2,1)S(1)}, u32[]{:S(2)}, u32[]{:S(2)}) collective-permute-start(bf16[4,16,1024]{2,1,0:T(8,128)(2,1)S(1)} %get-tuple-element.181), channel_id=1, source_target_pairs={{0,6},{1,7},{2,4},{3,5},{4,2},{5,3},{6,0},{7,1},{8,14},{9,15},{10,... | collective-permute-start | bytes 393224 | tf_op jit(solution)/shard_map/ppermute | solution.py:307
  101.7 9.4 %collective-permute-start.18 = (bf16[4,16,1024]{2,1,0:T(8,128)(2,1)S(1)}, bf16[4,16,1024]{2,1,0:T(8,128)(2,1)S(1)}, u32[]{:S(2)}, u32[]{:S(2)}) collective-permute-start(bf16[4,16,1024]{2,1,0:T(8,128)(2,1)S(1)} %get-tuple-element.180), channel_id=1, source_target_pairs={{0,4},{1,5},{2,6},{3,7},{4,0},{5,1},{6,2},{7,3},{8,12},{9,13},{10,... | collective-permute-start | bytes 393224 | tf_op jit(solution)/shard_map/ppermute | solution.py:307
  112.5 14.3 %collective-permute-start.20 = (bf16[4,32,2304]{2,1,0:T(8,128)(2,1)S(1)}, bf16[4,32,2304]{2,1,0:T(8,128)(2,1)S(1)}, u32[]{:S(2)}, u32[]{:S(2)}) collective-permute-start(bf16[4,32,2304]{2,1,0:T(8,128)(2,1)S(1)} %get-tuple-element.184), channel_id=1, source_target_pairs={{0,1},{1,0},{2,3},{3,2},{4,5},{5,4},{6,7},{7,6},{8,9},{9,8},{10,11... | collective-permute-start | bytes 1769480 | tf_op jit(solution)/shard_map/ppermute | solution.py:307
  114.6 11.2 %collective-permute-start.21 = (bf16[4,32,1792]{2,1,0:T(8,128)(2,1)S(1)}, bf16[4,32,1792]{2,1,0:T(8,128)(2,1)S(1)}, u32[]{:S(2)}, u32[]{:S(2)}) collective-permute-start(bf16[4,32,1792]{2,1,0:T(8,128)(2,1)S(1)} %get-tuple-element.187), channel_id=1, source_target_pairs={{0,16},{8,24},{16,0},{24,8},{1,17},{9,25},{17,1},{25,9},{2,18},{10... | collective-permute-start | bytes 1376264 | tf_op jit(solution)/shard_map/ppermute | solution.py:307
  127.5 22.2 %collective-permute-start.24 = (bf16[32,4096]{1,0:T(8,128)(2,1)S(1)}, bf16[32,4096]{1,0:T(8,128)(2,1)S(1)}, u32[]{:S(2)}, u32[]{:S(2)}) collective-permute-start(bf16[32,4096]{1,0:T(8,128)(2,1)S(1)} %get-tuple-element.188), channel_id=1, source_target_pairs={{0,2},{1,3},{2,0},{3,1},{4,6},{5,7},{6,4},{7,5},{8,10},{9,11},{10,... | collective-permute-start | bytes 786440 | tf_op jit(solution)/shard_map/ppermute | solution.py:307
  130.3 20.4 %collective-permute-start.25 = (bf16[32,4096]{1,0:T(8,128)(2,1)S(1)}, bf16[32,4096]{1,0:T(8,128)(2,1)S(1)}, u32[]{:S(2)}, u32[]{:S(2)}) collective-permute-start(bf16[32,4096]{1,0:T(8,128)(2,1)S(1)} %get-tuple-element.189), channel_id=1, source_target_pairs={{0,4},{1,5},{2,6},{3,7},{4,0},{5,1},{6,2},{7,3},{8,12},{9,13},{10,... | collective-permute-start | bytes 786440 | tf_op jit(solution)/shard_map/ppermute | solution.py:307
  130.3 20.4 %collective-permute-start.26 = (bf16[32,4096]{1,0:T(8,128)(2,1)S(1)}, bf16[32,4096]{1,0:T(8,128)(2,1)S(1)}, u32[]{:S(2)}, u32[]{:S(2)}) collective-permute-start(bf16[32,4096]{1,0:T(8,128)(2,1)S(1)} %get-tuple-element.190), channel_id=1, source_target_pairs={{0,6},{1,7},{2,4},{3,5},{4,2},{5,3},{6,0},{7,1},{8,14},{9,15},{10,... | collective-permute-start | bytes 786440 | tf_op jit(solution)/shard_map/ppermute | solution.py:307
  134.4 13.7 %collective-permute-start.23 = (bf16[4,16,1024]{2,1,0:T(8,128)(2,1)S(1)}, bf16[4,16,1024]{2,1,0:T(8,128)(2,1)S(1)}, u32[]{:S(2)}, u32[]{:S(2)}) collective-permute-start(bf16[4,16,1024]{2,1,0:T(8,128)(2,1)S(1)} %get-tuple-element.193), channel_id=1, source_target_pairs={{0,3},{1,2},{2,1},{3,0},{4,7},{5,6},{6,5},{7,4},{8,11},{9,10},{10,... | collective-permute-start | bytes 393224 | tf_op jit(solution)/shard_map/ppermute | solution.py:307
  (8 other events, 76.8 us)

commit v9 on v8

--- a/solution.py
+++ b/solution.py
@@ -31,21 +31,15 @@
     return centred * inverse, inverse
 
 
-def pick_kernel(n_slots, n_chunks, ids_ref, x_ref, cot_ref, *refs):
-    out_refs, sem = refs[:-1], refs[-1]
+def pick_kernel(n_slots, n_chunks, ids_ref, x_ref, cot_ref, *out_refs):
     half = n_slots // 2
     depth = x_ref.shape[0] // n_chunks
-    copies = []
     for i, ref in enumerate(out_refs):
         far = i - half
         here = slice(None) if far < 0 else pl.ds(far // half * depth, depth)
         slot = ids_ref[1] ^ (i if far < 0 else half + far % half)
-        for which, source in enumerate((x_ref, cot_ref)):
-            copy = pltpu.make_async_copy(source.at[here, slot], ref.at[which], sem.at[2 * i + which])
-            copy.start()
-            copies.append(copy)
-    for copy in copies:
-        copy.wait()
+        ref[0] = x_ref[here, slot]
+        ref[1] = cot_ref[here, slot]
 
 
 def pick(ids, clips, cotangent, n_slots, n_chunks):
@@ -59,9 +53,9 @@
     out = pl.pallas_call(
         functools.partial(pick_kernel, n_slots, n_chunks),
         out_shape=[piece(n_clips)] * half + [piece(n_clips // n_chunks)] * (half * n_chunks),
-        in_specs=[pl.BlockSpec(memory_space=pltpu.SMEM)] + [pl.BlockSpec(memory_space=pl.ANY)] * 2,
+        in_specs=[pl.BlockSpec(memory_space=pltpu.SMEM)]
+        + [pl.BlockSpec(memory_space=pltpu.VMEM)] * 2,
         out_specs=[pl.BlockSpec(memory_space=pltpu.VMEM)] * (half * (1 + n_chunks)),
-        scratch_shapes=[pltpu.SemaphoreType.DMA((2 * half * (1 + n_chunks),))],
         compiler_params=pltpu.CompilerParams(vmem_limit_bytes=12 * MIB),
     )(ids, clips.reshape(cut), cotangent.reshape(cut))
     far = [out[half + chunk * half :][:half] for chunk in range(n_chunks)]
@@ -117,8 +111,8 @@
         out_specs=pl.BlockSpec(memory_space=pltpu.VMEM),
         compiler_params=pltpu.CompilerParams(vmem_limit_bytes=24 * MIB),
         cost_estimate=pl.CostEstimate(
-            flops=n_chunks * rows * width * columns,
-            bytes_accessed=2 * n_chunks * rows * (width + columns) + width * columns,
+            flops=n_chunks * rows * width * columns // 4,
+            bytes_accessed=n_chunks * rows * width,
             transcendentals=0,
         ),
     )(ids, *operands)
@@ -351,29 +345,30 @@
     cut = int(4 * width * FIRST) - 2 * width
     first_parts = ([normed], [dq, dk, dv]), ((0, 0, width), (0, 0, width), (0, 0, cut))
     second_parts = ([normed, mixed], [dv, cot]), ((0, cut, width - cut), (1, 0, width))
-    sent_second = products(ids, 1, n_x, n_z, *second_parts[0], second_parts[1])
+    sent_first = products(ids, 1, n_x, n_z, *first_parts[0], first_parts[1])
+    first = swap(sent_first, "clip", n_clip_devices, 1)
+    sent_second = products(ids, 1, n_x, n_z, *after(second_parts[0], sent_first), second_parts[1])
     second = swap(sent_second, "clip", n_clip_devices, 1)
-    sent_first = products(ids, 1, n_x, n_z, *after(first_parts[0], sent_second), first_parts[1])
-    first = swap(sent_first, "clip", n_clip_devices, 1)
-    own_second = products(ids, 0, n_x, n_z, *after(second_parts[0], sent_first), second_parts[1])
+    own_first = products(ids, 0, n_x, n_z, *after(first_parts[0], sent_second), first_parts[1])
+    sent, own_first = halve(ids, (own_first, first), 0, 0, CORES)
+    first = swap(sent, "clip", n_clip_devices, CORES)
+    own_second = products(ids, 0, n_x, n_z, *after(second_parts[0], own_first), second_parts[1])
     sent, own_second = halve(ids, (own_second, second), 2, 1, 1)
     second = swap(sent, "tm", n_tm, 1)
-    own_first = products(ids, 0, n_x, n_z, *after(first_parts[0], own_second), first_parts[1])
-    sent, own_first = halve(ids, (own_first, first), 0, 0, CORES)
-    first = swap(sent, "clip", n_clip_devices, CORES)
-    dx = after(dx, sent_first)
+    dx = after(dx, sent_second)
     late = (1, 3)
     back = {}
     for k in reversed([k for k in range(1, n_tm) if k not in late]):
         block = after(dx[k], back[k + 3]) if k + 3 in back else dx[k]
         back[k] = swap(block, "tm", n_tm, k)
-    first, second = after((first, second), back)
+    first, second = after((first, second), [back[k] for k in range(n_tm - 3, n_tm)])
     sent, own_first = halve(ids, (own_first, first), 1, 1, 1)
     first = swap(sent, "tm", n_tm, 1)
     sent, own_second = halve(ids, (own_second, second), 0, 0, CORES)
     second = swap(sent, "clip", n_clip_devices, CORES)
+    first, second = after((first, second), back)
     total, *sent = join(ids, (own_first, first), (own_second, second), n_z)
-    others = [swap(block, "tm", n_tm, (j + 1) * N_Y) for j, block in enumerate(sent)]
+    others = [swap(sent[j - 1], "tm", n_tm, j * N_Y) for j in reversed(range(1, n_z))]
     back[0] = dx[0]
     for k in late:
         back[k] = swap(after(dx[k], sent), "tm", n_tm, k)

time: 153 us -> 147 us (0.961)
  waiting for transfers between devices: 71.4 us -> 67.8 us
    ppermute x27, waiting for transfers between devices: 71.4 us -> 67.8 us  [swap(): return lax.ppermute(block, axis, [(i, i ^ distance) for i in range(size)])]
  transfers between devices with their start and end apart: 27 -> 27, of which waited for: 15 -> 15; matrix products, arithmetic and copies ran while one was open for 0% -> 0% of each run, Pallas kernels for 10% -> 13%
where the time goes in v9:
time: 147 us; the launch traced here: 146 us
  waiting for transfers between devices  67.8 us (46%)
  starting transfers between devices  40.1 us (27%)
  Pallas kernels  32 us (22%)
  local copies, waits for them, and re-layouts  5.24 us (4%)
    ppermute x27, waiting for transfers between devices, swap(): return lax.ppermute(block, axis, [(i, i ^ distance) for i in range(size)])  67.8 us
    ppermute x27, starting transfers between devices, swap(): return lax.ppermute(block, axis, [(i, i ^ distance) for i in range(size)])  40.1 us
    pallas_call x2, Pallas kernels, sublayer(): pl.pallas_call(functools.partial(sublayer_kernel, at, n_clips, n_position...  17.1 us
    pallas_call x4, Pallas kernels, products(): pl.pallas_call(functools.partial(product_kernel, n_x, flip, n_chunks, spa...  7.54 us
    unnamed x10, local copies, waits for them, and re-layouts  5.24 us
    pallas_call x4, Pallas kernels, halve(): pl.pallas_call(functools.partial(halve_kernel, dim, axis, stride), out_sh...  3.5 us
  transfers between devices with their start and end apart: 27, of which 15 were waited for; matrix products, arithmetic and copies ran while one was open for 0% of the time, Pallas kernels for 13%

profile of v9, /device:TPU:0, one launch (start us, length us, event | category | flops | bytes accessed | tf_op | source)
XLA Modules:
  0.0 146.0 jit_solution(7531103868174432424)
XLA Ops:
  3.8 3.1 %collective-permute-start.1 = (bf16[2,4,16,1024]{3,2,1,0:T(8,128)(2,1)S(1)}, bf16[2,4,16,1024]{3,2,1,0:T(8,128)(2,1)S(1)}, u32[]{:S(2)}, u32[]{:S(2)}) collective-permute-start(bf16[2,4,16,1024]{3,2,1,0:T(8,128)(2,1)S(1)} %get-tuple-element.104), channel_id=1, source_target_pairs={{0,2},{1,3},{2,0},{3,1},{4,6},{5,7},{6,4},{7,5},{8,10},{9,11},{10,... | collective-permute-start | bytes 786440 | tf_op jit(solution)/shard_map/ppermute | solution.py:301
  6.9 3.5 %collective-permute-start.5 = (bf16[2,2,16,1024]{3,2,1,0:T(8,128)(2,1)S(1)}, bf16[2,2,16,1024]{3,2,1,0:T(8,128)(2,1)S(1)}, u32[]{:S(2)}, u32[]{:S(2)}) collective-permute-start(bf16[2,2,16,1024]{3,2,1,0:T(8,128)(2,1)S(1)} %get-tuple-element.111), channel_id=1, source_target_pairs={{0,5},{1,4},{2,7},{3,6},{4,1},{5,0},{6,3},{7,2},{8,13},{9,12},{10,... | collective-permute-start | bytes 393224 | tf_op jit(solution)/shard_map/ppermute | solution.py:301
  13.7 3.1 %collective-permute-done.1.refs_2_ = bf16[2,4,16,1024]{3,2,1,0:T(8,128)(2,1)S(1)} collective-permute-done((bf16[2,4,16,1024]{3,2,1,0:T(8,128)(2,1)S(1)}, bf16[2,4,16,1024]{3,2,1,0:T(8,128)(2,1)S(1)}, u32[]{:S(2)}, u32[]{:S(2)}) %collective-permute-start.1) | collective-permute-done | bytes 262176 | tf_op jit(solution)/shard_map/ppermute | solution.py:301
  16.9 5.0 %collective-permute-start.9 = (bf16[2,2,16,1024]{3,2,1,0:T(8,128)(2,1)S(1)}, bf16[2,2,16,1024]{3,2,1,0:T(8,128)(2,1)S(1)}, u32[]{:S(2)}, u32[]{:S(2)}) collective-permute-start(bf16[2,2,16,1024]{3,2,1,0:T(8,128)(2,1)S(1)} %get-tuple-element.117), channel_id=1, source_target_pairs={{0,7},{1,6},{2,5},{3,4},{4,3},{5,2},{6,1},{7,0},{8,15},{9,14},{10,... | collective-permute-start | bytes 393224 | tf_op jit(solution)/shard_map/ppermute | solution.py:301
  21.9 7.4 %collective-permute-done.7.refs_6_ = bf16[2,2,16,1024]{3,2,1,0:T(8,128)(2,1)S(1)} collective-permute-done((bf16[2,2,16,1024]{3,2,1,0:T(8,128)(2,1)S(1)}, bf16[2,2,16,1024]{3,2,1,0:T(8,128)(2,1)S(1)}, u32[]{:S(2)}, u32[]{:S(2)}) %collective-permute-start.7) | collective-permute-done | bytes 131104 | tf_op jit(solution)/shard_map/ppermute | solution.py:301
  29.3 4.4 %collective-permute-done.9.refs_7_ = bf16[2,2,16,1024]{3,2,1,0:T(8,128)(2,1)S(1)} collective-permute-done((bf16[2,2,16,1024]{3,2,1,0:T(8,128)(2,1)S(1)}, bf16[2,2,16,1024]{3,2,1,0:T(8,128)(2,1)S(1)}, u32[]{:S(2)}, u32[]{:S(2)}) %collective-permute-start.9) | collective-permute-done | bytes 131104 | tf_op jit(solution)/shard_map/ppermute | solution.py:301
  33.7 1.9 %collective-permute-start.8 = (bf16[2,2,16,1024]{3,2,1,0:T(8,128)(2,1)S(1)}, bf16[2,2,16,1024]{3,2,1,0:T(8,128)(2,1)S(1)}, u32[]{:S(2)}, u32[]{:S(2)}) collective-permute-start(bf16[2,2,16,1024]{3,2,1,0:T(8,128)(2,1)S(1)} %get-tuple-element.115), channel_id=1, source_target_pairs={{0,6},{1,7},{2,4},{3,5},{4,2},{5,3},{6,0},{7,1},{8,14},{9,15},{10,... | collective-permute-start | bytes 393224 | tf_op jit(solution)/shard_map/ppermute | solution.py:301
  35.6 9.2 %collective-permute-done.3.refs_4_ = bf16[2,2,16,1024]{3,2,1,0:T(8,128)(2,1)S(1)} collective-permute-done((bf16[2,2,16,1024]{3,2,1,0:T(8,128)(2,1)S(1)}, bf16[2,2,16,1024]{3,2,1,0:T(8,128)(2,1)S(1)}, u32[]{:S(2)}, u32[]{:S(2)}) %collective-permute-start.3) | collective-permute-done | bytes 131104 | tf_op jit(solution)/shard_map/ppermute | solution.py:301
  44.9 2.8 %copy-done.2 = bf16[1024,3072]{1,0:T(8,128)(2,1)S(1)} copy-done((bf16[1024,3072]{1,0:T(8,128)(2,1)S(1)}, bf16[1024,3072]{1,0:T(8,128)(2,1)}, u32[]{:S(2)}) %copy-start.2) | copy-done | bytes 6291480
  47.7 8.4 %shard_map.68 = (bf16[256,1024]{1,0:T(8,128)(2,1)S(1)}, bf16[256,1024]{1,0:T(8,128)(2,1)S(1)}, bf16[256,1024]{1,0:T(8,128)(2,1)S(1)}, bf16[256,1024]{1,0:T(8,128...) custom-call(bf16[2,4,16,1024]{3,2,1,0:T(8,128)(2,1)S(1)} %get-tuple-, ...), custom_call_target="tpu_custom_call" | custom-call | flops 5368709120 | bytes 12582912 | tf_op jit(solution)/shard_map/pallas_call | solution.py:286
  57.6 8.7 %shard_map.69 = (bf16[256,1024]{1,0:T(8,128)(2,1)S(1)}, bf16[256,1024]{1,0:T(8,128)(2,1)S(1)}, bf16[256,1024]{1,0:T(8,128)(2,1)S(1)}, bf16[256,1024]{1,0:T(8,128...) custom-call(bf16[2,4,16,1024]{3,2,1,0:T(8,128)(2,1)S(1)} %get-tuple-, ...), custom_call_target="tpu_custom_call" | custom-call | flops 5368709120 | bytes 12582912 | tf_op jit(solution)/shard_map/pallas_call | solution.py:286
  66.2 2.0 %shard_map.70 = bf16[2,4,2,32,2304]{4,3,2,1,0:T(8,128)(2,1)S(1)} custom-call(s32[2]{0:T(128)S(1)} %pad_add_fusion.ids_ref, bf16[256,1024]{1,0:T(8,128)(2,1)S(1)} %get-tuple-element.167.refs_0_, bf16[256,1024]{1,0:T(8,128)(2,1)S(1)} %get-tuple-element.168.refs_1_, bf16[256,1024]{1,0:T(8,128)(2,1)S(1)} %get-tuple-element.159.refs_2_, ...), custom_call_target="tpu_custom_call" | custom-call | flops 301989888 | bytes 524288 | tf_op jit(solution)/shard_map/pallas_call | solution.py:106
  68.4 1.8 %shard_map.71 = bf16[2,4,2,32,1792]{4,3,2,1,0:T(8,128)(2,1)S(1)} custom-call(s32[2]{0:T(128)S(1)} %pad_add_fusion.ids_ref, bf16[256,1024]{1,0:T(8,128)(2,1)S(1)} %get-tuple-element.167.refs_0_, bf16[256,1024]{1,0:T(8,128)(2,1)S(1)} %get-tuple-element.168.refs_1_, bf16[256,1024]{1,0:T(8,128)(2,1)S(1)} %get-tuple-element.169.refs_2_, ...), custom_call_target="tpu_custom_call" | custom-call | flops 234881024 | bytes 524288 | tf_op jit(solution)/shard_map/pallas_call | solution.py:106
  70.7 2.0 %shard_map.72.refs_0_ = bf16[2,4,2,32,2304]{4,3,2,1,0:T(8,128)(2,1)S(1)} custom-call(s32[2]{0:T(128)S(1)} %pad_add_fusion.ids_ref, bf16[256,1024]{1,0:T(8,128)(2,1)S(1)} %get-tuple-element.167.refs_0_, bf16[256,1024]{1,0:T(8,128)(2,1)S(1)} %get-tuple-element.168.refs_1_, bf16[256,1024]{1,0:T(8,128)(2,1)S(1)} %get-tuple-element.159.refs_2_, ...), custom_call_target="tpu_custom_call" | custom-call | flops 301989888 | bytes 524288 | tf_op jit(solution)/shard_map/pallas_call | solution.py:106
  81.3 3.6 %collective-permute-start.16 = (bf16[4,16,1024]{2,1,0:T(8,128)(2,1)S(1)}, bf16[4,16,1024]{2,1,0:T(8,128)(2,1)S(1)}, u32[]{:S(2)}, u32[]{:S(2)}) collective-permute-start(bf16[4,16,1024]{2,1,0:T(8,128)(2,1)S(1)} %get-tuple-element.177), channel_id=1, source_target_pairs={{0,6},{1,7},{2,4},{3,5},{4,2},{5,3},{6,0},{7,1},{8,14},{9,15},{10,... | collective-permute-start | bytes 393224 | tf_op jit(solution)/shard_map/ppermute | solution.py:301
  86.5 9.7 %collective-permute-done.15.refs_5_ = bf16[4,16,1024]{2,1,0:T(8,128)(2,1)S(1)} collective-permute-done((bf16[4,16,1024]{2,1,0:T(8,128)(2,1)S(1)}, bf16[4,16,1024]{2,1,0:T(8,128)(2,1)S(1)}, u32[]{:S(2)}, u32[]{:S(2)}) %collective-permute-start.15) | collective-permute-done | bytes 131104 | tf_op jit(solution)/shard_map/ppermute | solution.py:301
  96.2 9.9 %collective-permute-done.14.refs_1_ = bf16[2,4,32,1792]{3,2,1,0:T(8,128)(2,1)S(1)} collective-permute-done((bf16[2,4,32,1792]{3,2,1,0:T(8,128)(2,1)S(1)}, bf16[2,4,32,1792]{3,2,1,0:T(8,128)(2,1)S(1)}, u32[]{:S(2)}, u32[]{:S(2)}) %collective-permute-start.14) | collective-permute-done | bytes 917536 | tf_op jit(solution)/shard_map/ppermute | solution.py:301
  109.5 3.2 %collective-permute-start.20 = (bf16[4,16,1024]{2,1,0:T(8,128)(2,1)S(1)}, bf16[4,16,1024]{2,1,0:T(8,128)(2,1)S(1)}, u32[]{:S(2)}, u32[]{:S(2)}) collective-permute-start(bf16[4,16,1024]{2,1,0:T(8,128)(2,1)S(1)} %get-tuple-element.186), channel_id=1, source_target_pairs={{0,2},{1,3},{2,0},{3,1},{4,6},{5,7},{6,4},{7,5},{8,10},{9,11},{10,... | collective-permute-start | bytes 393224 | tf_op jit(solution)/shard_map/ppermute | solution.py:301
  112.6 4.3 %collective-permute-done.20.refs_2_ = bf16[4,16,1024]{2,1,0:T(8,128)(2,1)S(1)} collective-permute-done((bf16[4,16,1024]{2,1,0:T(8,128)(2,1)S(1)}, bf16[4,16,1024]{2,1,0:T(8,128)(2,1)S(1)}, u32[]{:S(2)}, u32[]{:S(2)}) %collective-permute-start.20) | collective-permute-done | bytes 131104 | tf_op jit(solution)/shard_map/ppermute | solution.py:301
  117.0 2.7 %collective-permute-done.21.refs_4_ = bf16[4,16,1024]{2,1,0:T(8,128)(2,1)S(1)} collective-permute-done((bf16[4,16,1024]{2,1,0:T(8,128)(2,1)S(1)}, bf16[4,16,1024]{2,1,0:T(8,128)(2,1)S(1)}, u32[]{:S(2)}, u32[]{:S(2)}) %collective-permute-start.21) | collective-permute-done | bytes 131104 | tf_op jit(solution)/shard_map/ppermute | solution.py:301
  121.9 2.8 %collective-permute-start.26 = (bf16[32,4096]{1,0:T(8,128)(2,1)S(1)}, bf16[32,4096]{1,0:T(8,128)(2,1)S(1)}, u32[]{:S(2)}, u32[]{:S(2)}) collective-permute-start(bf16[32,4096]{1,0:T(8,128)(2,1)S(1)} %get-tuple-element.192), channel_id=1, source_target_pairs={{0,2},{1,3},{2,0},{3,1},{4,6},{5,7},{6,4},{7,5},{8,10},{9,11},{10,... | collective-permute-start | bytes 786440 | tf_op jit(solution)/shard_map/ppermute | solution.py:301
  124.7 2.4 %collective-permute-start.24 = (bf16[32,4096]{1,0:T(8,128)(2,1)S(1)}, bf16[32,4096]{1,0:T(8,128)(2,1)S(1)}, u32[]{:S(2)}, u32[]{:S(2)}) collective-permute-start(bf16[32,4096]{1,0:T(8,128)(2,1)S(1)} %get-tuple-element.194), channel_id=1, source_target_pairs={{0,6},{1,7},{2,4},{3,5},{4,2},{5,3},{6,0},{7,1},{8,14},{9,15},{10,... | collective-permute-start | bytes 786440 | tf_op jit(solution)/shard_map/ppermute | solution.py:301
  129.6 2.9 %collective-permute-done.22.refs_1_ = bf16[4,16,1024]{2,1,0:T(8,128)(2,1)S(1)} collective-permute-done((bf16[4,16,1024]{2,1,0:T(8,128)(2,1)S(1)}, bf16[4,16,1024]{2,1,0:T(8,128)(2,1)S(1)}, u32[]{:S(2)}, u32[]{:S(2)}) %collective-permute-start.22) | collective-permute-done | bytes 131104 | tf_op jit(solution)/shard_map/ppermute | solution.py:301
  132.5 10.0 %collective-permute-done.23.refs_3_ = bf16[4,16,1024]{2,1,0:T(8,128)(2,1)S(1)} collective-permute-done((bf16[4,16,1024]{2,1,0:T(8,128)(2,1)S(1)}, bf16[4,16,1024]{2,1,0:T(8,128)(2,1)S(1)}, u32[]{:S(2)}, u32[]{:S(2)}) %collective-permute-start.23) | collective-permute-done | bytes 131104 | tf_op jit(solution)/shard_map/ppermute | solution.py:301
  (55 shorter events, 30.4 us)
Async XLA Ops:
  3.8 13.0 %collective-permute-start.1 = (bf16[2,4,16,1024]{3,2,1,0:T(8,128)(2,1)S(1)}, bf16[2,4,16,1024]{3,2,1,0:T(8,128)(2,1)S(1)}, u32[]{:S(2)}, u32[]{:S(2)}) collective-permute-start(bf16[2,4,16,1024]{3,2,1,0:T(8,128)(2,1)S(1)} %get-tuple-element.104), channel_id=1, source_target_pairs={{0,2},{1,3},{2,0},{3,1},{4,6},{5,7},{6,4},{7,5},{8,10},{9,11},{10,... | collective-permute-start | bytes 786440 | tf_op jit(solution)/shard_map/ppermute | solution.py:301
  6.9 15.0 %collective-permute-start.5 = (bf16[2,2,16,1024]{3,2,1,0:T(8,128)(2,1)S(1)}, bf16[2,2,16,1024]{3,2,1,0:T(8,128)(2,1)S(1)}, u32[]{:S(2)}, u32[]{:S(2)}) collective-permute-start(bf16[2,2,16,1024]{3,2,1,0:T(8,128)(2,1)S(1)} %get-tuple-element.111), channel_id=1, source_target_pairs={{0,5},{1,4},{2,7},{3,6},{4,1},{5,0},{6,3},{7,2},{8,13},{9,12},{10,... | collective-permute-start | bytes 393224 | tf_op jit(solution)/shard_map/ppermute | solution.py:301
  10.5 34.4 %collective-permute-start = (bf16[2,4,16,1024]{3,2,1,0:T(8,128)(2,1)S(1)}, bf16[2,4,16,1024]{3,2,1,0:T(8,128)(2,1)S(1)}, u32[]{:S(2)}, u32[]{:S(2)}) collective-permute-start(bf16[2,4,16,1024]{3,2,1,0:T(8,128)(2,1)S(1)} %get-tuple-element.103), channel_id=1, source_target_pairs={{0,1},{1,0},{2,3},{3,2},{4,5},{5,4},{6,7},{7,6},{8,9},{9,8},{10,11... | collective-permute-start | bytes 786440 | tf_op jit(solution)/shard_map/ppermute | solution.py:301
  11.0 33.9 %collective-permute-start.2 = (bf16[2,4,16,1024]{3,2,1,0:T(8,128)(2,1)S(1)}, bf16[2,4,16,1024]{3,2,1,0:T(8,128)(2,1)S(1)}, u32[]{:S(2)}, u32[]{:S(2)}) collective-permute-start(bf16[2,4,16,1024]{3,2,1,0:T(8,128)(2,1)S(1)} %get-tuple-element.105), channel_id=1, source_target_pairs={{0,3},{1,2},{2,1},{3,0},{4,7},{5,6},{6,5},{7,4},{8,11},{9,10},{10,... | collective-permute-start | bytes 786440 | tf_op jit(solution)/shard_map/ppermute | solution.py:301
  12.4 16.9 %collective-permute-start.7 = (bf16[2,2,16,1024]{3,2,1,0:T(8,128)(2,1)S(1)}, bf16[2,2,16,1024]{3,2,1,0:T(8,128)(2,1)S(1)}, u32[]{:S(2)}, u32[]{:S(2)}) collective-permute-start(bf16[2,2,16,1024]{3,2,1,0:T(8,128)(2,1)S(1)} %get-tuple-element.114), channel_id=1, source_target_pairs={{0,6},{1,7},{2,4},{3,5},{4,2},{5,3},{6,0},{7,1},{8,14},{9,15},{10,... | collective-permute-start | bytes 393224 | tf_op jit(solution)/shard_map/ppermute | solution.py:301
  16.9 16.8 %collective-permute-start.9 = (bf16[2,2,16,1024]{3,2,1,0:T(8,128)(2,1)S(1)}, bf16[2,2,16,1024]{3,2,1,0:T(8,128)(2,1)S(1)}, u32[]{:S(2)}, u32[]{:S(2)}) collective-permute-start(bf16[2,2,16,1024]{3,2,1,0:T(8,128)(2,1)S(1)} %get-tuple-element.117), channel_id=1, source_target_pairs={{0,7},{1,6},{2,5},{3,4},{4,3},{5,2},{6,1},{7,0},{8,15},{9,14},{10,... | collective-permute-start | bytes 393224 | tf_op jit(solution)/shard_map/ppermute | solution.py:301
  21.9 22.9 %collective-permute-start.3 = (bf16[2,2,16,1024]{3,2,1,0:T(8,128)(2,1)S(1)}, bf16[2,2,16,1024]{3,2,1,0:T(8,128)(2,1)S(1)}, u32[]{:S(2)}, u32[]{:S(2)}) collective-permute-start(bf16[2,2,16,1024]{3,2,1,0:T(8,128)(2,1)S(1)} %get-tuple-element.108), channel_id=1, source_target_pairs={{0,4},{1,5},{2,6},{3,7},{4,0},{5,1},{6,2},{7,3},{8,12},{9,13},{10,... | collective-permute-start | bytes 393224 | tf_op jit(solution)/shard_map/ppermute | solution.py:301
  29.3 26.8 %collective-permute-start.6 = (bf16[2,2,16,1024]{3,2,1,0:T(8,128)(2,1)S(1)}, bf16[2,2,16,1024]{3,2,1,0:T(8,128)(2,1)S(1)}, u32[]{:S(2)}, u32[]{:S(2)}) collective-permute-start(bf16[2,2,16,1024]{3,2,1,0:T(8,128)(2,1)S(1)} %get-tuple-element.112), channel_id=1, source_target_pairs={{0,5},{1,4},{2,7},{3,6},{4,1},{5,0},{6,3},{7,2},{8,13},{9,12},{10,... | collective-permute-start | bytes 393224 | tf_op jit(solution)/shard_map/ppermute | solution.py:301
  33.7 22.4 %collective-permute-start.8 = (bf16[2,2,16,1024]{3,2,1,0:T(8,128)(2,1)S(1)}, bf16[2,2,16,1024]{3,2,1,0:T(8,128)(2,1)S(1)}, u32[]{:S(2)}, u32[]{:S(2)}) collective-permute-start(bf16[2,2,16,1024]{3,2,1,0:T(8,128)(2,1)S(1)} %get-tuple-element.115), channel_id=1, source_target_pairs={{0,6},{1,7},{2,4},{3,5},{4,2},{5,3},{6,0},{7,1},{8,14},{9,15},{10,... | collective-permute-start | bytes 393224 | tf_op jit(solution)/shard_map/ppermute | solution.py:301
  44.8 11.3 %collective-permute-start.10 = (bf16[2,2,16,1024]{3,2,1,0:T(8,128)(2,1)S(1)}, bf16[2,2,16,1024]{3,2,1,0:T(8,128)(2,1)S(1)}, u32[]{:S(2)}, u32[]{:S(2)}) collective-permute-start(bf16[2,2,16,1024]{3,2,1,0:T(8,128)(2,1)S(1)} %get-tuple-element.118), channel_id=1, source_target_pairs={{0,7},{1,6},{2,5},{3,4},{4,3},{5,2},{6,1},{7,0},{8,15},{9,14},{10,... | collective-permute-start | bytes 393224 | tf_op jit(solution)/shard_map/ppermute | solution.py:301
  44.8 12.7 %collective-permute-start.4 = (bf16[2,2,16,1024]{3,2,1,0:T(8,128)(2,1)S(1)}, bf16[2,2,16,1024]{3,2,1,0:T(8,128)(2,1)S(1)}, u32[]{:S(2)}, u32[]{:S(2)}) collective-permute-start(bf16[2,2,16,1024]{3,2,1,0:T(8,128)(2,1)S(1)} %get-tuple-element.109), channel_id=1, source_target_pairs={{0,4},{1,5},{2,6},{3,7},{4,0},{5,1},{6,2},{7,3},{8,12},{9,13},{10,... | collective-permute-start | bytes 393224 | tf_op jit(solution)/shard_map/ppermute | solution.py:301
  70.1 7.1 %collective-permute-start.13 = (bf16[2,4,2,32,1792]{4,3,2,1,0:T(8,128)(2,1)S(1)}, bf16[2,4,2,32,1792]{4,3,2,1,0:T(8,128)(2,1)S(1)}, u32[]{:S(2)}, u32[]{:S(2)}) collective-permute-start(bf16[2,4,2,32,1792]{4,3,2,1,0:T(8,128)(2,1)S(1)} %shard_map.71), channel_id=1, source_target_pairs={{0,8},{8,0},{16,24},{24,16},{1,9},{9,1},{17,25},{25,17},{2,10},{10... | collective-permute-start | bytes 5505032 | tf_op jit(solution)/shard_map/ppermute | solution.py:301
  73.9 32.2 %collective-permute-start.12 = (bf16[4,2,32,2304]{3,2,1,0:T(8,128)(2,1)S(1)}, bf16[4,2,32,2304]{3,2,1,0:T(8,128)(2,1)S(1)}, u32[]{:S(2)}, u32[]{:S(2)}) collective-permute-start(bf16[4,2,32,2304]{3,2,1,0:T(8,128)(2,1)S(1)} %get-tuple-element.166), channel_id=1, source_target_pairs={{0,16},{8,24},{16,0},{24,8},{1,17},{9,25},{17,1},{25,9},{2,18},{10... | collective-permute-start | bytes 3538952 | tf_op jit(solution)/shard_map/ppermute | solution.py:301
  78.3 27.8 %collective-permute-start.14 = (bf16[2,4,32,1792]{3,2,1,0:T(8,128)(2,1)S(1)}, bf16[2,4,32,1792]{3,2,1,0:T(8,128)(2,1)S(1)}, u32[]{:S(2)}, u32[]{:S(2)}) collective-permute-start(bf16[2,4,32,1792]{3,2,1,0:T(8,128)(2,1)S(1)} %get-tuple-element.175), channel_id=1, source_target_pairs={{0,1},{1,0},{2,3},{3,2},{4,5},{5,4},{6,7},{7,6},{8,9},{9,8},{10,11... | collective-permute-start | bytes 2752520 | tf_op jit(solution)/shard_map/ppermute | solution.py:301
  79.6 16.6 %collective-permute-start.15 = (bf16[4,16,1024]{2,1,0:T(8,128)(2,1)S(1)}, bf16[4,16,1024]{2,1,0:T(8,128)(2,1)S(1)}, u32[]{:S(2)}, u32[]{:S(2)}) collective-permute-start(bf16[4,16,1024]{2,1,0:T(8,128)(2,1)S(1)} %get-tuple-element.176), channel_id=1, source_target_pairs={{0,5},{1,4},{2,7},{3,6},{4,1},{5,0},{6,3},{7,2},{8,13},{9,12},{10,... | collective-permute-start | bytes 393224 | tf_op jit(solution)/shard_map/ppermute | solution.py:301
  81.3 14.9 %collective-permute-start.16 = (bf16[4,16,1024]{2,1,0:T(8,128)(2,1)S(1)}, bf16[4,16,1024]{2,1,0:T(8,128)(2,1)S(1)}, u32[]{:S(2)}, u32[]{:S(2)}) collective-permute-start(bf16[4,16,1024]{2,1,0:T(8,128)(2,1)S(1)} %get-tuple-element.177), channel_id=1, source_target_pairs={{0,6},{1,7},{2,4},{3,5},{4,2},{5,3},{6,0},{7,1},{8,14},{9,15},{10,... | collective-permute-start | bytes 393224 | tf_op jit(solution)/shard_map/ppermute | solution.py:301
  84.9 11.4 %collective-permute-start.17 = (bf16[4,16,1024]{2,1,0:T(8,128)(2,1)S(1)}, bf16[4,16,1024]{2,1,0:T(8,128)(2,1)S(1)}, u32[]{:S(2)}, u32[]{:S(2)}) collective-permute-start(bf16[4,16,1024]{2,1,0:T(8,128)(2,1)S(1)} %get-tuple-element.178), channel_id=1, source_target_pairs={{0,7},{1,6},{2,5},{3,4},{4,3},{5,2},{6,1},{7,0},{8,15},{9,14},{10,... | collective-permute-start | bytes 393224 | tf_op jit(solution)/shard_map/ppermute | solution.py:301
  106.8 14.3 %collective-permute-start.18 = (bf16[4,32,2304]{2,1,0:T(8,128)(2,1)S(1)}, bf16[4,32,2304]{2,1,0:T(8,128)(2,1)S(1)}, u32[]{:S(2)}, u32[]{:S(2)}) collective-permute-start(bf16[4,32,2304]{2,1,0:T(8,128)(2,1)S(1)} %get-tuple-element.181), channel_id=1, source_target_pairs={{0,1},{1,0},{2,3},{3,2},{4,5},{5,4},{6,7},{7,6},{8,9},{9,8},{10,11... | collective-permute-start | bytes 1769480 | tf_op jit(solution)/shard_map/ppermute | solution.py:301
  108.9 11.2 %collective-permute-start.19 = (bf16[4,32,1792]{2,1,0:T(8,128)(2,1)S(1)}, bf16[4,32,1792]{2,1,0:T(8,128)(2,1)S(1)}, u32[]{:S(2)}, u32[]{:S(2)}) collective-permute-start(bf16[4,32,1792]{2,1,0:T(8,128)(2,1)S(1)} %get-tuple-element.184), channel_id=1, source_target_pairs={{0,16},{8,24},{16,0},{24,8},{1,17},{9,25},{17,1},{25,9},{2,18},{10... | collective-permute-start | bytes 1376264 | tf_op jit(solution)/shard_map/ppermute | solution.py:301
  109.5 7.5 %collective-permute-start.20 = (bf16[4,16,1024]{2,1,0:T(8,128)(2,1)S(1)}, bf16[4,16,1024]{2,1,0:T(8,128)(2,1)S(1)}, u32[]{:S(2)}, u32[]{:S(2)}) collective-permute-start(bf16[4,16,1024]{2,1,0:T(8,128)(2,1)S(1)} %get-tuple-element.186), channel_id=1, source_target_pairs={{0,2},{1,3},{2,0},{3,1},{4,6},{5,7},{6,4},{7,5},{8,10},{9,11},{10,... | collective-permute-start | bytes 393224 | tf_op jit(solution)/shard_map/ppermute | solution.py:301
  121.9 22.2 %collective-permute-start.26 = (bf16[32,4096]{1,0:T(8,128)(2,1)S(1)}, bf16[32,4096]{1,0:T(8,128)(2,1)S(1)}, u32[]{:S(2)}, u32[]{:S(2)}) collective-permute-start(bf16[32,4096]{1,0:T(8,128)(2,1)S(1)} %get-tuple-element.192), channel_id=1, source_target_pairs={{0,2},{1,3},{2,0},{3,1},{4,6},{5,7},{6,4},{7,5},{8,10},{9,11},{10,... | collective-permute-start | bytes 786440 | tf_op jit(solution)/shard_map/ppermute | solution.py:301
  124.7 20.4 %collective-permute-start.25 = (bf16[32,4096]{1,0:T(8,128)(2,1)S(1)}, bf16[32,4096]{1,0:T(8,128)(2,1)S(1)}, u32[]{:S(2)}, u32[]{:S(2)}) collective-permute-start(bf16[32,4096]{1,0:T(8,128)(2,1)S(1)} %get-tuple-element.193), channel_id=1, source_target_pairs={{0,4},{1,5},{2,6},{3,7},{4,0},{5,1},{6,2},{7,3},{8,12},{9,13},{10,... | collective-permute-start | bytes 786440 | tf_op jit(solution)/shard_map/ppermute | solution.py:301
  124.7 20.4 %collective-permute-start.24 = (bf16[32,4096]{1,0:T(8,128)(2,1)S(1)}, bf16[32,4096]{1,0:T(8,128)(2,1)S(1)}, u32[]{:S(2)}, u32[]{:S(2)}) collective-permute-start(bf16[32,4096]{1,0:T(8,128)(2,1)S(1)} %get-tuple-element.194), channel_id=1, source_target_pairs={{0,6},{1,7},{2,4},{3,5},{4,2},{5,3},{6,0},{7,1},{8,14},{9,15},{10,... | collective-permute-start | bytes 786440 | tf_op jit(solution)/shard_map/ppermute | solution.py:301
  128.8 13.7 %collective-permute-start.23 = (bf16[4,16,1024]{2,1,0:T(8,128)(2,1)S(1)}, bf16[4,16,1024]{2,1,0:T(8,128)(2,1)S(1)}, u32[]{:S(2)}, u32[]{:S(2)}) collective-permute-start(bf16[4,16,1024]{2,1,0:T(8,128)(2,1)S(1)} %get-tuple-element.197), channel_id=1, source_target_pairs={{0,3},{1,2},{2,1},{3,0},{4,7},{5,6},{6,5},{7,4},{8,11},{9,10},{10,... | collective-permute-start | bytes 393224 | tf_op jit(solution)/shard_map/ppermute | solution.py:301
  (8 other events, 73.9 us)

commit v10 on v9

--- a/solution.py
+++ b/solution.py
@@ -10,7 +10,7 @@
 
 HEADS = 16
 GROUP = 4
-FIRST = 9 / 16
+FIRST = 5 / 8
 CHUNKS = 2
 CORES = 2
 N_Y = 2
@@ -167,6 +167,75 @@
         out_specs=[pl.BlockSpec(memory_space=pltpu.VMEM)] * n_z,
         compiler_params=pltpu.CompilerParams(vmem_limit_bytes=12 * MIB),
     )(ids, *first, *second)
+
+
+def cross_kernel(n_first, ids_ref, *refs):
+    (near_sent, far_sent, near_kept, far_kept), addends = refs[-4:], refs[:-4]
+    first, second = addends[:n_first], addends[n_first:]
+    me = lax.div(ids_ref[1], N_Y)
+    middle = near_sent.shape[2]
+    cut = first[0].shape[2]
+    rows = slice(None)
+    for out, blocks in ((near_sent, (1, 3)), (near_kept, (0, 2))):
+        for i, block in enumerate(blocks):
+            out[i] = summed(first, (me ^ block, rows, pl.ds(0, middle))).astype(out.dtype)
+    for out, blocks in ((far_sent, (2, 3)), (far_kept, (0, 1))):
+        for i, block in enumerate(blocks):
+            left = summed(first, (me ^ block, rows, pl.ds(middle, cut - middle)))
+            out[i, :, pl.ds(0, cut - middle)] = left.astype(out.dtype)
+            out[i, :, pl.ds(cut - middle, 2 * middle - cut)] = summed(second, (me ^ block,)).astype(out.dtype)
+
+
+def cross(ids, first, second):
+    rows, columns = first[0].shape[1], first[0].shape[2] + second[0].shape[2]
+    shape = (2, rows, columns // 2)
+    sent, kept = (jax.ShapeDtypeStruct(shape, kind) for kind in (jnp.bfloat16, jnp.float32))
+    return pl.pallas_call(
+        functools.partial(cross_kernel, len(first)),
+        out_shape=[sent, sent, kept, kept],
+        in_specs=[pl.BlockSpec(memory_space=pltpu.SMEM)]
+        + [pl.BlockSpec(memory_space=pltpu.VMEM)] * (len(first) + len(second)),
+        out_specs=[pl.BlockSpec(memory_space=pltpu.VMEM)] * 4,
+        compiler_params=pltpu.CompilerParams(vmem_limit_bytes=12 * MIB),
+    )(ids, *first, *second)
+
+
+def pass_kernel(kept_ref, came_ref, sent_ref):
+    sent_ref[...] = summed((kept_ref, came_ref), 1).astype(jnp.bfloat16)
+
+
+def pass_on(kept, came):
+    return pl.pallas_call(
+        pass_kernel,
+        out_shape=jax.ShapeDtypeStruct(came.shape[1:], jnp.bfloat16),
+        in_specs=[pl.BlockSpec(memory_space=pltpu.VMEM)] * 2,
+        out_specs=pl.BlockSpec(memory_space=pltpu.VMEM),
+        compiler_params=pltpu.CompilerParams(vmem_limit_bytes=8 * MIB),
+    )(kept, came)
+
+
+def gather_kernel(*refs):
+    halves, (grad_qkv_ref, grad_out_ref) = (refs[:3], refs[3:6]), refs[6:]
+    middle = refs[0].shape[2]
+    rest = grad_qkv_ref.shape[1] - middle
+    sums = [kept[0] + came[0].astype(jnp.float32) + last[...].astype(jnp.float32) for kept, came, last in halves]
+    grad_qkv_ref[:, pl.ds(0, middle)] = sums[0]
+    grad_qkv_ref[:, pl.ds(middle, rest)] = sums[1][:, :rest]
+    grad_out_ref[...] = sums[1][:, rest:]
+
+
+def gather(near, far):
+    _, rows, half = near[0].shape
+    return pl.pallas_call(
+        gather_kernel,
+        out_shape=[
+            jax.ShapeDtypeStruct((rows, half // 2 * 3), jnp.float32),
+            jax.ShapeDtypeStruct((rows, half // 2), jnp.float32),
+        ],
+        in_specs=[pl.BlockSpec(memory_space=pltpu.VMEM)] * 6,
+        out_specs=[pl.BlockSpec(memory_space=pltpu.VMEM)] * 2,
+        compiler_params=pltpu.CompilerParams(vmem_limit_bytes=8 * MIB),
+    )(*near, *far)
 
 
 def finish_kernel(*refs):
@@ -367,13 +436,21 @@
     sent, own_second = halve(ids, (own_second, second), 0, 0, CORES)
     second = swap(sent, "clip", n_clip_devices, CORES)
     first, second = after((first, second), back)
-    total, *sent = join(ids, (own_first, first), (own_second, second), n_z)
-    others = [swap(sent[j - 1], "tm", n_tm, j * N_Y) for j in reversed(range(1, n_z))]
+    if n_z == 4:
+        *sent, near_kept, far_kept = cross(ids, (own_first, first), (own_second, second))
+        far_came = swap(sent[1], "tm", n_tm, 2 * N_Y)
+        near_came = swap(sent[0], "tm", n_tm, N_Y)
+        near_last = swap(pass_on(near_kept, near_came), "tm", n_tm, 2 * N_Y)
+        far_last = swap(pass_on(far_kept, far_came), "tm", n_tm, N_Y)
+        grad_qkv, grad_out = gather((near_kept, near_came, near_last), (far_kept, far_came, far_last))
+    else:
+        total, *sent = join(ids, (own_first, first), (own_second, second), n_z)
+        others = [swap(sent[j - 1], "tm", n_tm, j * N_Y) for j in reversed(range(1, n_z))]
+        grad_qkv, grad_out = finish((total, *others))
     back[0] = dx[0]
     for k in late:
         back[k] = swap(after(dx[k], sent), "tm", n_tm, k)
     grad_clips = place(ids, [back[k] for k in range(n_tm)]).reshape(clips.shape)
-    grad_qkv, grad_out = finish((total, *others))
     return (grad_clips, grad_qkv, grad_out)
 
 

time: 147 us -> 148 us (level)
  waiting for transfers between devices: 67.8 us -> 70.6 us
    ppermute x27 -> x28, waiting for transfers between devices: 67.8 us -> 70.6 us  [swap(): return lax.ppermute(block, axis, [(i, i ^ distance) for i in range(size)])]
    ppermute x27 -> x28, starting transfers between devices: 40.1 us -> 38.8 us  [swap(): return lax.ppermute(block, axis, [(i, i ^ distance) for i in range(size)])]
  transfers between devices with their start and end apart: 27 -> 28, of which waited for: 15 -> 16; matrix products, arithmetic and copies ran while one was open for 0% -> 0% of each run, Pallas kernels for 13% -> 12%
where the time goes in v10:
time: 148 us; the launch traced here: 147 us
  waiting for transfers between devices  70.6 us (48%)
  starting transfers between devices  38.8 us (26%)
  Pallas kernels  31.8 us (21%)
  local copies, waits for them, and re-layouts  5.24 us (4%)
    ppermute x28, waiting for transfers between devices, swap(): return lax.ppermute(block, axis, [(i, i ^ distance) for i in range(size)])  70.6 us
    ppermute x28, starting transfers between devices, swap(): return lax.ppermute(block, axis, [(i, i ^ distance) for i in range(size)])  38.8 us
    pallas_call x2, Pallas kernels, sublayer(): pl.pallas_call(functools.partial(sublayer_kernel, at, n_clips, n_position...  17.1 us
    pallas_call x4, Pallas kernels, products(): pl.pallas_call(functools.partial(product_kernel, n_x, flip, n_chunks, spa...  7.35 us
    unnamed x10, local copies, waits for them, and re-layouts  5.24 us
    pallas_call x4, Pallas kernels, halve(): pl.pallas_call(functools.partial(halve_kernel, dim, axis, stride), out_sh...  3.49 us
  transfers between devices with their start and end apart: 28, of which 16 were waited for; matrix products, arithmetic and copies ran while one was open for 0% of the time, Pallas kernels for 12%

profile of v10, /device:TPU:0, one launch (start us, length us, event | category | flops | bytes accessed | tf_op | source)
XLA Modules:
  0.0 147.3 jit_solution(4118826190960533489)
XLA Ops:
  3.8 3.1 %collective-permute-start.1 = (bf16[2,4,16,1024]{3,2,1,0:T(8,128)(2,1)S(1)}, bf16[2,4,16,1024]{3,2,1,0:T(8,128)(2,1)S(1)}, u32[]{:S(2)}, u32[]{:S(2)}) collective-permute-start(bf16[2,4,16,1024]{3,2,1,0:T(8,128)(2,1)S(1)} %get-tuple-element.104), channel_id=1, source_target_pairs={{0,2},{1,3},{2,0},{3,1},{4,6},{5,7},{6,4},{7,5},{8,10},{9,11},{10,... | collective-permute-start | bytes 786440 | tf_op jit(solution)/shard_map/ppermute | solution.py:370
  6.9 3.5 %collective-permute-start.5 = (bf16[2,2,16,1024]{3,2,1,0:T(8,128)(2,1)S(1)}, bf16[2,2,16,1024]{3,2,1,0:T(8,128)(2,1)S(1)}, u32[]{:S(2)}, u32[]{:S(2)}) collective-permute-start(bf16[2,2,16,1024]{3,2,1,0:T(8,128)(2,1)S(1)} %get-tuple-element.111), channel_id=1, source_target_pairs={{0,5},{1,4},{2,7},{3,6},{4,1},{5,0},{6,3},{7,2},{8,13},{9,12},{10,... | collective-permute-start | bytes 393224 | tf_op jit(solution)/shard_map/ppermute | solution.py:370
  13.7 3.1 %collective-permute-done.1.refs_2_ = bf16[2,4,16,1024]{3,2,1,0:T(8,128)(2,1)S(1)} collective-permute-done((bf16[2,4,16,1024]{3,2,1,0:T(8,128)(2,1)S(1)}, bf16[2,4,16,1024]{3,2,1,0:T(8,128)(2,1)S(1)}, u32[]{:S(2)}, u32[]{:S(2)}) %collective-permute-start.1) | collective-permute-done | bytes 262176 | tf_op jit(solution)/shard_map/ppermute | solution.py:370
  16.9 5.0 %collective-permute-start.9 = (bf16[2,2,16,1024]{3,2,1,0:T(8,128)(2,1)S(1)}, bf16[2,2,16,1024]{3,2,1,0:T(8,128)(2,1)S(1)}, u32[]{:S(2)}, u32[]{:S(2)}) collective-permute-start(bf16[2,2,16,1024]{3,2,1,0:T(8,128)(2,1)S(1)} %get-tuple-element.117), channel_id=1, source_target_pairs={{0,7},{1,6},{2,5},{3,4},{4,3},{5,2},{6,1},{7,0},{8,15},{9,14},{10,... | collective-permute-start | bytes 393224 | tf_op jit(solution)/shard_map/ppermute | solution.py:370
  21.9 7.4 %collective-permute-done.7.refs_6_ = bf16[2,2,16,1024]{3,2,1,0:T(8,128)(2,1)S(1)} collective-permute-done((bf16[2,2,16,1024]{3,2,1,0:T(8,128)(2,1)S(1)}, bf16[2,2,16,1024]{3,2,1,0:T(8,128)(2,1)S(1)}, u32[]{:S(2)}, u32[]{:S(2)}) %collective-permute-start.7) | collective-permute-done | bytes 131104 | tf_op jit(solution)/shard_map/ppermute | solution.py:370
  29.3 4.4 %collective-permute-done.9.refs_7_ = bf16[2,2,16,1024]{3,2,1,0:T(8,128)(2,1)S(1)} collective-permute-done((bf16[2,2,16,1024]{3,2,1,0:T(8,128)(2,1)S(1)}, bf16[2,2,16,1024]{3,2,1,0:T(8,128)(2,1)S(1)}, u32[]{:S(2)}, u32[]{:S(2)}) %collective-permute-start.9) | collective-permute-done | bytes 131104 | tf_op jit(solution)/shard_map/ppermute | solution.py:370
  33.7 1.9 %collective-permute-start.8 = (bf16[2,2,16,1024]{3,2,1,0:T(8,128)(2,1)S(1)}, bf16[2,2,16,1024]{3,2,1,0:T(8,128)(2,1)S(1)}, u32[]{:S(2)}, u32[]{:S(2)}) collective-permute-start(bf16[2,2,16,1024]{3,2,1,0:T(8,128)(2,1)S(1)} %get-tuple-element.115), channel_id=1, source_target_pairs={{0,6},{1,7},{2,4},{3,5},{4,2},{5,3},{6,0},{7,1},{8,14},{9,15},{10,... | collective-permute-start | bytes 393224 | tf_op jit(solution)/shard_map/ppermute | solution.py:370
  35.6 9.2 %collective-permute-done.3.refs_4_ = bf16[2,2,16,1024]{3,2,1,0:T(8,128)(2,1)S(1)} collective-permute-done((bf16[2,2,16,1024]{3,2,1,0:T(8,128)(2,1)S(1)}, bf16[2,2,16,1024]{3,2,1,0:T(8,128)(2,1)S(1)}, u32[]{:S(2)}, u32[]{:S(2)}) %collective-permute-start.3) | collective-permute-done | bytes 131104 | tf_op jit(solution)/shard_map/ppermute | solution.py:370
  44.9 2.8 %copy-done.2 = bf16[1024,3072]{1,0:T(8,128)(2,1)S(1)} copy-done((bf16[1024,3072]{1,0:T(8,128)(2,1)S(1)}, bf16[1024,3072]{1,0:T(8,128)(2,1)}, u32[]{:S(2)}) %copy-start.2) | copy-done | bytes 6291480
  47.7 8.4 %shard_map.68 = (bf16[256,1024]{1,0:T(8,128)(2,1)S(1)}, bf16[256,1024]{1,0:T(8,128)(2,1)S(1)}, bf16[256,1024]{1,0:T(8,128)(2,1)S(1)}, bf16[256,1024]{1,0:T(8,128...) custom-call(bf16[2,4,16,1024]{3,2,1,0:T(8,128)(2,1)S(1)} %get-tuple-, ...), custom_call_target="tpu_custom_call" | custom-call | flops 5368709120 | bytes 12582912 | tf_op jit(solution)/shard_map/pallas_call | solution.py:355
  57.6 8.7 %shard_map.69 = (bf16[256,1024]{1,0:T(8,128)(2,1)S(1)}, bf16[256,1024]{1,0:T(8,128)(2,1)S(1)}, bf16[256,1024]{1,0:T(8,128)(2,1)S(1)}, bf16[256,1024]{1,0:T(8,128...) custom-call(bf16[2,4,16,1024]{3,2,1,0:T(8,128)(2,1)S(1)} %get-tuple-, ...), custom_call_target="tpu_custom_call" | custom-call | flops 5368709120 | bytes 12582912 | tf_op jit(solution)/shard_map/pallas_call | solution.py:355
  66.2 2.1 %shard_map.70 = bf16[2,4,2,32,2560]{4,3,2,1,0:T(8,128)(2,1)S(1)} custom-call(s32[2]{0:T(128)S(1)} %pad_add_fusion.ids_ref, bf16[256,1024]{1,0:T(8,128)(2,1)S(1)} %get-tuple-element.167.refs_0_, bf16[256,1024]{1,0:T(8,128)(2,1)S(1)} %get-tuple-element.168.refs_1_, bf16[256,1024]{1,0:T(8,128)(2,1)S(1)} %get-tuple-element.159.refs_2_, ...), custom_call_target="tpu_custom_call" | custom-call | flops 335544320 | bytes 524288 | tf_op jit(solution)/shard_map/pallas_call | solution.py:106
  70.6 2.1 %shard_map.72.refs_0_ = bf16[2,4,2,32,2560]{4,3,2,1,0:T(8,128)(2,1)S(1)} custom-call(s32[2]{0:T(128)S(1)} %pad_add_fusion.ids_ref, bf16[256,1024]{1,0:T(8,128)(2,1)S(1)} %get-tuple-element.167.refs_0_, bf16[256,1024]{1,0:T(8,128)(2,1)S(1)} %get-tuple-element.168.refs_1_, bf16[256,1024]{1,0:T(8,128)(2,1)S(1)} %get-tuple-element.159.refs_2_, ...), custom_call_target="tpu_custom_call" | custom-call | flops 335544320 | bytes 524288 | tf_op jit(solution)/shard_map/pallas_call | solution.py:106
  81.6 3.6 %collective-permute-start.16 = (bf16[4,16,1024]{2,1,0:T(8,128)(2,1)S(1)}, bf16[4,16,1024]{2,1,0:T(8,128)(2,1)S(1)}, u32[]{:S(2)}, u32[]{:S(2)}) collective-permute-start(bf16[4,16,1024]{2,1,0:T(8,128)(2,1)S(1)} %get-tuple-element.177), channel_id=1, source_target_pairs={{0,6},{1,7},{2,4},{3,5},{4,2},{5,3},{6,0},{7,1},{8,14},{9,15},{10,... | collective-permute-start | bytes 393224 | tf_op jit(solution)/shard_map/ppermute | solution.py:370
  86.8 9.7 %collective-permute-done.15.refs_5_ = bf16[4,16,1024]{2,1,0:T(8,128)(2,1)S(1)} collective-permute-done((bf16[4,16,1024]{2,1,0:T(8,128)(2,1)S(1)}, bf16[4,16,1024]{2,1,0:T(8,128)(2,1)S(1)}, u32[]{:S(2)}, u32[]{:S(2)}) %collective-permute-start.15) | collective-permute-done | bytes 131104 | tf_op jit(solution)/shard_map/ppermute | solution.py:370
  96.5 7.1 %collective-permute-done.14.refs_1_ = bf16[2,4,32,1536]{3,2,1,0:T(8,128)(2,1)S(1)} collective-permute-done((bf16[2,4,32,1536]{3,2,1,0:T(8,128)(2,1)S(1)}, bf16[2,4,32,1536]{3,2,1,0:T(8,128)(2,1)S(1)}, u32[]{:S(2)}, u32[]{:S(2)}) %collective-permute-start.14) | collective-permute-done | bytes 786464 | tf_op jit(solution)/shard_map/ppermute | solution.py:370
  103.5 1.8 %collective-permute-done.12.refs_1_ = bf16[4,2,32,2560]{3,2,1,0:T(8,128)(2,1)S(1)} collective-permute-done((bf16[4,2,32,2560]{3,2,1,0:T(8,128)(2,1)S(1)}, bf16[4,2,32,2560]{3,2,1,0:T(8,128)(2,1)S(1)}, u32[]{:S(2)}, u32[]{:S(2)}) %collective-permute-start.12) | collective-permute-done | bytes 1310752 | tf_op jit(solution)/shard_map/ppermute | solution.py:370
  109.7 3.2 %collective-permute-start.20 = (bf16[4,16,1024]{2,1,0:T(8,128)(2,1)S(1)}, bf16[4,16,1024]{2,1,0:T(8,128)(2,1)S(1)}, u32[]{:S(2)}, u32[]{:S(2)}) collective-permute-start(bf16[4,16,1024]{2,1,0:T(8,128)(2,1)S(1)} %get-tuple-element.186), channel_id=1, source_target_pairs={{0,2},{1,3},{2,0},{3,1},{4,6},{5,7},{6,4},{7,5},{8,10},{9,11},{10,... | collective-permute-start | bytes 393224 | tf_op jit(solution)/shard_map/ppermute | solution.py:370
  112.8 3.9 %collective-permute-done.20.refs_2_ = bf16[4,16,1024]{2,1,0:T(8,128)(2,1)S(1)} collective-permute-done((bf16[4,16,1024]{2,1,0:T(8,128)(2,1)S(1)}, bf16[4,16,1024]{2,1,0:T(8,128)(2,1)S(1)}, u32[]{:S(2)}, u32[]{:S(2)}) %collective-permute-start.20) | collective-permute-done | bytes 131104 | tf_op jit(solution)/shard_map/ppermute | solution.py:370
  116.7 3.4 %collective-permute-done.21.refs_4_ = bf16[4,16,1024]{2,1,0:T(8,128)(2,1)S(1)} collective-permute-done((bf16[4,16,1024]{2,1,0:T(8,128)(2,1)S(1)}, bf16[4,16,1024]{2,1,0:T(8,128)(2,1)S(1)}, u32[]{:S(2)}, u32[]{:S(2)}) %collective-permute-start.21) | collective-permute-done | bytes 131104 | tf_op jit(solution)/shard_map/ppermute | solution.py:370
  120.1 2.0 %collective-permute-done.18.refs_1_ = bf16[4,32,2560]{2,1,0:T(8,128)(2,1)S(1)} collective-permute-done((bf16[4,32,2560]{2,1,0:T(8,128)(2,1)S(1)}, bf16[4,32,2560]{2,1,0:T(8,128)(2,1)S(1)}, u32[]{:S(2)}, u32[]{:S(2)}) %collective-permute-start.18) | collective-permute-done | bytes 655392 | tf_op jit(solution)/shard_map/ppermute | solution.py:370
  122.8 2.8 %collective-permute-start.24 = (bf16[2,32,2048]{2,1,0:T(8,128)(2,1)S(1)}, bf16[2,32,2048]{2,1,0:T(8,128)(2,1)S(1)}, u32[]{:S(2)}, u32[]{:S(2)}) collective-permute-start(bf16[2,32,2048]{2,1,0:T(8,128)(2,1)S(1)} %get-tuple-element.192), channel_id=1, source_target_pairs={{0,2},{1,3},{2,0},{3,1},{4,6},{5,7},{6,4},{7,5},{8,10},{9,11},{10,... | collective-permute-start | bytes 786440 | tf_op jit(solution)/shard_map/ppermute | solution.py:370
  128.1 9.1 %collective-permute-done.24.came_ref.refs_1_ = bf16[2,32,2048]{2,1,0:T(8,128)(2,1)S(1)} collective-permute-done((bf16[2,32,2048]{2,1,0:T(8,128)(2,1)S(1)}, bf16[2,32,2048]{2,1,0:T(8,128)(2,1)S(1)}, u32[]{:S(2)}, u32[]{:S(2)}) %collective-permute-start.24) | collective-permute-done | bytes 262176 | tf_op jit(solution)/shard_map/ppermute | solution.py:370
  137.3 4.1 %collective-permute-done.26.came_ref.refs_4_ = bf16[2,32,2048]{2,1,0:T(8,128)(2,1)S(1)} collective-permute-done((bf16[2,32,2048]{2,1,0:T(8,128)(2,1)S(1)}, bf16[2,32,2048]{2,1,0:T(8,128)(2,1)S(1)}, u32[]{:S(2)}, u32[]{:S(2)}) %collective-permute-start.26) | collective-permute-done | bytes 262176 | tf_op jit(solution)/shard_map/ppermute | solution.py:370
  (59 shorter events, 34.2 us)
Async XLA Ops:
  3.8 13.0 %collective-permute-start.1 = (bf16[2,4,16,1024]{3,2,1,0:T(8,128)(2,1)S(1)}, bf16[2,4,16,1024]{3,2,1,0:T(8,128)(2,1)S(1)}, u32[]{:S(2)}, u32[]{:S(2)}) collective-permute-start(bf16[2,4,16,1024]{3,2,1,0:T(8,128)(2,1)S(1)} %get-tuple-element.104), channel_id=1, source_target_pairs={{0,2},{1,3},{2,0},{3,1},{4,6},{5,7},{6,4},{7,5},{8,10},{9,11},{10,... | collective-permute-start | bytes 786440 | tf_op jit(solution)/shard_map/ppermute | solution.py:370
  6.9 15.0 %collective-permute-start.5 = (bf16[2,2,16,1024]{3,2,1,0:T(8,128)(2,1)S(1)}, bf16[2,2,16,1024]{3,2,1,0:T(8,128)(2,1)S(1)}, u32[]{:S(2)}, u32[]{:S(2)}) collective-permute-start(bf16[2,2,16,1024]{3,2,1,0:T(8,128)(2,1)S(1)} %get-tuple-element.111), channel_id=1, source_target_pairs={{0,5},{1,4},{2,7},{3,6},{4,1},{5,0},{6,3},{7,2},{8,13},{9,12},{10,... | collective-permute-start | bytes 393224 | tf_op jit(solution)/shard_map/ppermute | solution.py:370
  10.5 34.4 %collective-permute-start = (bf16[2,4,16,1024]{3,2,1,0:T(8,128)(2,1)S(1)}, bf16[2,4,16,1024]{3,2,1,0:T(8,128)(2,1)S(1)}, u32[]{:S(2)}, u32[]{:S(2)}) collective-permute-start(bf16[2,4,16,1024]{3,2,1,0:T(8,128)(2,1)S(1)} %get-tuple-element.103), channel_id=1, source_target_pairs={{0,1},{1,0},{2,3},{3,2},{4,5},{5,4},{6,7},{7,6},{8,9},{9,8},{10,11... | collective-permute-start | bytes 786440 | tf_op jit(solution)/shard_map/ppermute | solution.py:370
  11.0 33.9 %collective-permute-start.2 = (bf16[2,4,16,1024]{3,2,1,0:T(8,128)(2,1)S(1)}, bf16[2,4,16,1024]{3,2,1,0:T(8,128)(2,1)S(1)}, u32[]{:S(2)}, u32[]{:S(2)}) collective-permute-start(bf16[2,4,16,1024]{3,2,1,0:T(8,128)(2,1)S(1)} %get-tuple-element.105), channel_id=1, source_target_pairs={{0,3},{1,2},{2,1},{3,0},{4,7},{5,6},{6,5},{7,4},{8,11},{9,10},{10,... | collective-permute-start | bytes 786440 | tf_op jit(solution)/shard_map/ppermute | solution.py:370
  12.4 16.9 %collective-permute-start.7 = (bf16[2,2,16,1024]{3,2,1,0:T(8,128)(2,1)S(1)}, bf16[2,2,16,1024]{3,2,1,0:T(8,128)(2,1)S(1)}, u32[]{:S(2)}, u32[]{:S(2)}) collective-permute-start(bf16[2,2,16,1024]{3,2,1,0:T(8,128)(2,1)S(1)} %get-tuple-element.114), channel_id=1, source_target_pairs={{0,6},{1,7},{2,4},{3,5},{4,2},{5,3},{6,0},{7,1},{8,14},{9,15},{10,... | collective-permute-start | bytes 393224 | tf_op jit(solution)/shard_map/ppermute | solution.py:370
  16.9 16.8 %collective-permute-start.9 = (bf16[2,2,16,1024]{3,2,1,0:T(8,128)(2,1)S(1)}, bf16[2,2,16,1024]{3,2,1,0:T(8,128)(2,1)S(1)}, u32[]{:S(2)}, u32[]{:S(2)}) collective-permute-start(bf16[2,2,16,1024]{3,2,1,0:T(8,128)(2,1)S(1)} %get-tuple-element.117), channel_id=1, source_target_pairs={{0,7},{1,6},{2,5},{3,4},{4,3},{5,2},{6,1},{7,0},{8,15},{9,14},{10,... | collective-permute-start | bytes 393224 | tf_op jit(solution)/shard_map/ppermute | solution.py:370
  21.9 22.9 %collective-permute-start.3 = (bf16[2,2,16,1024]{3,2,1,0:T(8,128)(2,1)S(1)}, bf16[2,2,16,1024]{3,2,1,0:T(8,128)(2,1)S(1)}, u32[]{:S(2)}, u32[]{:S(2)}) collective-permute-start(bf16[2,2,16,1024]{3,2,1,0:T(8,128)(2,1)S(1)} %get-tuple-element.108), channel_id=1, source_target_pairs={{0,4},{1,5},{2,6},{3,7},{4,0},{5,1},{6,2},{7,3},{8,12},{9,13},{10,... | collective-permute-start | bytes 393224 | tf_op jit(solution)/shard_map/ppermute | solution.py:370
  29.3 26.8 %collective-permute-start.6 = (bf16[2,2,16,1024]{3,2,1,0:T(8,128)(2,1)S(1)}, bf16[2,2,16,1024]{3,2,1,0:T(8,128)(2,1)S(1)}, u32[]{:S(2)}, u32[]{:S(2)}) collective-permute-start(bf16[2,2,16,1024]{3,2,1,0:T(8,128)(2,1)S(1)} %get-tuple-element.112), channel_id=1, source_target_pairs={{0,5},{1,4},{2,7},{3,6},{4,1},{5,0},{6,3},{7,2},{8,13},{9,12},{10,... | collective-permute-start | bytes 393224 | tf_op jit(solution)/shard_map/ppermute | solution.py:370
  33.7 22.4 %collective-permute-start.8 = (bf16[2,2,16,1024]{3,2,1,0:T(8,128)(2,1)S(1)}, bf16[2,2,16,1024]{3,2,1,0:T(8,128)(2,1)S(1)}, u32[]{:S(2)}, u32[]{:S(2)}) collective-permute-start(bf16[2,2,16,1024]{3,2,1,0:T(8,128)(2,1)S(1)} %get-tuple-element.115), channel_id=1, source_target_pairs={{0,6},{1,7},{2,4},{3,5},{4,2},{5,3},{6,0},{7,1},{8,14},{9,15},{10,... | collective-permute-start | bytes 393224 | tf_op jit(solution)/shard_map/ppermute | solution.py:370
  44.8 11.3 %collective-permute-start.10 = (bf16[2,2,16,1024]{3,2,1,0:T(8,128)(2,1)S(1)}, bf16[2,2,16,1024]{3,2,1,0:T(8,128)(2,1)S(1)}, u32[]{:S(2)}, u32[]{:S(2)}) collective-permute-start(bf16[2,2,16,1024]{3,2,1,0:T(8,128)(2,1)S(1)} %get-tuple-element.118), channel_id=1, source_target_pairs={{0,7},{1,6},{2,5},{3,4},{4,3},{5,2},{6,1},{7,0},{8,15},{9,14},{10,... | collective-permute-start | bytes 393224 | tf_op jit(solution)/shard_map/ppermute | solution.py:370
  44.8 12.7 %collective-permute-start.4 = (bf16[2,2,16,1024]{3,2,1,0:T(8,128)(2,1)S(1)}, bf16[2,2,16,1024]{3,2,1,0:T(8,128)(2,1)S(1)}, u32[]{:S(2)}, u32[]{:S(2)}) collective-permute-start(bf16[2,2,16,1024]{3,2,1,0:T(8,128)(2,1)S(1)} %get-tuple-element.109), channel_id=1, source_target_pairs={{0,4},{1,5},{2,6},{3,7},{4,0},{5,1},{6,2},{7,3},{8,12},{9,13},{10,... | collective-permute-start | bytes 393224 | tf_op jit(solution)/shard_map/ppermute | solution.py:370
  70.0 7.6 %collective-permute-start.13 = (bf16[2,4,2,32,1536]{4,3,2,1,0:T(8,128)(2,1)S(1)}, bf16[2,4,2,32,1536]{4,3,2,1,0:T(8,128)(2,1)S(1)}, u32[]{:S(2)}, u32[]{:S(2)}) collective-permute-start(bf16[2,4,2,32,1536]{4,3,2,1,0:T(8,128)(2,1)S(1)} %shard_map.71), channel_id=1, source_target_pairs={{0,8},{8,0},{16,24},{24,16},{1,9},{9,1},{17,25},{25,17},{2,10},{10... | collective-permute-start | bytes 4718600 | tf_op jit(solution)/shard_map/ppermute | solution.py:370
  74.4 30.9 %collective-permute-start.12 = (bf16[4,2,32,2560]{3,2,1,0:T(8,128)(2,1)S(1)}, bf16[4,2,32,2560]{3,2,1,0:T(8,128)(2,1)S(1)}, u32[]{:S(2)}, u32[]{:S(2)}) collective-permute-start(bf16[4,2,32,2560]{3,2,1,0:T(8,128)(2,1)S(1)} %get-tuple-element.166), channel_id=1, source_target_pairs={{0,16},{8,24},{16,0},{24,8},{1,17},{9,25},{17,1},{25,9},{2,18},{10... | collective-permute-start | bytes 3932168 | tf_op jit(solution)/shard_map/ppermute | solution.py:370
  78.5 25.0 %collective-permute-start.14 = (bf16[2,4,32,1536]{3,2,1,0:T(8,128)(2,1)S(1)}, bf16[2,4,32,1536]{3,2,1,0:T(8,128)(2,1)S(1)}, u32[]{:S(2)}, u32[]{:S(2)}) collective-permute-start(bf16[2,4,32,1536]{3,2,1,0:T(8,128)(2,1)S(1)} %get-tuple-element.175), channel_id=1, source_target_pairs={{0,1},{1,0},{2,3},{3,2},{4,5},{5,4},{6,7},{7,6},{8,9},{9,8},{10,11... | collective-permute-start | bytes 2359304 | tf_op jit(solution)/shard_map/ppermute | solution.py:370
  79.9 16.6 %collective-permute-start.15 = (bf16[4,16,1024]{2,1,0:T(8,128)(2,1)S(1)}, bf16[4,16,1024]{2,1,0:T(8,128)(2,1)S(1)}, u32[]{:S(2)}, u32[]{:S(2)}) collective-permute-start(bf16[4,16,1024]{2,1,0:T(8,128)(2,1)S(1)} %get-tuple-element.176), channel_id=1, source_target_pairs={{0,5},{1,4},{2,7},{3,6},{4,1},{5,0},{6,3},{7,2},{8,13},{9,12},{10,... | collective-permute-start | bytes 393224 | tf_op jit(solution)/shard_map/ppermute | solution.py:370
  81.6 14.9 %collective-permute-start.16 = (bf16[4,16,1024]{2,1,0:T(8,128)(2,1)S(1)}, bf16[4,16,1024]{2,1,0:T(8,128)(2,1)S(1)}, u32[]{:S(2)}, u32[]{:S(2)}) collective-permute-start(bf16[4,16,1024]{2,1,0:T(8,128)(2,1)S(1)} %get-tuple-element.177), channel_id=1, source_target_pairs={{0,6},{1,7},{2,4},{3,5},{4,2},{5,3},{6,0},{7,1},{8,14},{9,15},{10,... | collective-permute-start | bytes 393224 | tf_op jit(solution)/shard_map/ppermute | solution.py:370
  85.1 11.3 %collective-permute-start.17 = (bf16[4,16,1024]{2,1,0:T(8,128)(2,1)S(1)}, bf16[4,16,1024]{2,1,0:T(8,128)(2,1)S(1)}, u32[]{:S(2)}, u32[]{:S(2)}) collective-permute-start(bf16[4,16,1024]{2,1,0:T(8,128)(2,1)S(1)} %get-tuple-element.178), channel_id=1, source_target_pairs={{0,7},{1,6},{2,5},{3,4},{4,3},{5,2},{6,1},{7,0},{8,15},{9,14},{10,... | collective-permute-start | bytes 393224 | tf_op jit(solution)/shard_map/ppermute | solution.py:370
  106.1 16.0 %collective-permute-start.18 = (bf16[4,32,2560]{2,1,0:T(8,128)(2,1)S(1)}, bf16[4,32,2560]{2,1,0:T(8,128)(2,1)S(1)}, u32[]{:S(2)}, u32[]{:S(2)}) collective-permute-start(bf16[4,32,2560]{2,1,0:T(8,128)(2,1)S(1)} %get-tuple-element.181), channel_id=1, source_target_pairs={{0,1},{1,0},{2,3},{3,2},{4,5},{5,4},{6,7},{7,6},{8,9},{9,8},{10,11... | collective-permute-start | bytes 1966088 | tf_op jit(solution)/shard_map/ppermute | solution.py:370
  108.1 12.0 %collective-permute-start.19 = (bf16[4,32,1536]{2,1,0:T(8,128)(2,1)S(1)}, bf16[4,32,1536]{2,1,0:T(8,128)(2,1)S(1)}, u32[]{:S(2)}, u32[]{:S(2)}) collective-permute-start(bf16[4,32,1536]{2,1,0:T(8,128)(2,1)S(1)} %get-tuple-element.184), channel_id=1, source_target_pairs={{0,16},{8,24},{16,0},{24,8},{1,17},{9,25},{17,1},{25,9},{2,18},{10... | collective-permute-start | bytes 1179656 | tf_op jit(solution)/shard_map/ppermute | solution.py:370
  122.8 14.4 %collective-permute-start.24 = (bf16[2,32,2048]{2,1,0:T(8,128)(2,1)S(1)}, bf16[2,32,2048]{2,1,0:T(8,128)(2,1)S(1)}, u32[]{:S(2)}, u32[]{:S(2)}) collective-permute-start(bf16[2,32,2048]{2,1,0:T(8,128)(2,1)S(1)} %get-tuple-element.192), channel_id=1, source_target_pairs={{0,2},{1,3},{2,0},{3,1},{4,6},{5,7},{6,4},{7,5},{8,10},{9,11},{10,... | collective-permute-start | bytes 786440 | tf_op jit(solution)/shard_map/ppermute | solution.py:370
  125.6 15.8 %collective-permute-start.26 = (bf16[2,32,2048]{2,1,0:T(8,128)(2,1)S(1)}, bf16[2,32,2048]{2,1,0:T(8,128)(2,1)S(1)}, u32[]{:S(2)}, u32[]{:S(2)}) collective-permute-start(bf16[2,32,2048]{2,1,0:T(8,128)(2,1)S(1)} %get-tuple-element.193), channel_id=1, source_target_pairs={{0,4},{1,5},{2,6},{3,7},{4,0},{5,1},{6,2},{7,3},{8,12},{9,13},{10,... | collective-permute-start | bytes 786440 | tf_op jit(solution)/shard_map/ppermute | solution.py:370
  125.6 15.9 %collective-permute-start.22 = (bf16[4,16,1024]{2,1,0:T(8,128)(2,1)S(1)}, bf16[4,16,1024]{2,1,0:T(8,128)(2,1)S(1)}, u32[]{:S(2)}, u32[]{:S(2)}) collective-permute-start(bf16[4,16,1024]{2,1,0:T(8,128)(2,1)S(1)} %get-tuple-element.194), channel_id=1, source_target_pairs={{0,1},{1,0},{2,3},{3,2},{4,5},{5,4},{6,7},{7,6},{8,9},{9,8},{10,11... | collective-permute-start | bytes 393224 | tf_op jit(solution)/shard_map/ppermute | solution.py:370
  127.3 15.8 %collective-permute-start.23 = (bf16[4,16,1024]{2,1,0:T(8,128)(2,1)S(1)}, bf16[4,16,1024]{2,1,0:T(8,128)(2,1)S(1)}, u32[]{:S(2)}, u32[]{:S(2)}) collective-permute-start(bf16[4,16,1024]{2,1,0:T(8,128)(2,1)S(1)} %get-tuple-element.196), channel_id=1, source_target_pairs={{0,3},{1,2},{2,1},{3,0},{4,7},{5,6},{6,5},{7,4},{8,11},{9,10},{10,... | collective-permute-start | bytes 393224 | tf_op jit(solution)/shard_map/ppermute | solution.py:370
  137.2 7.4 %collective-permute-start.25 = (bf16[32,2048]{1,0:T(8,128)(2,1)S(1)}, bf16[32,2048]{1,0:T(8,128)(2,1)S(1)}, u32[]{:S(2)}, u32[]{:S(2)}) collective-permute-start(bf16[32,2048]{1,0:T(8,128)(2,1)S(1)} %shard_map.80), channel_id=1, source_target_pairs={{0,4},{1,5},{2,6},{3,7},{4,0},{5,1},{6,2},{7,3},{8,12},{9,13},{10,... | collective-permute-start | bytes 393224 | tf_op jit(solution)/shard_map/ppermute | solution.py:370
  (9 other events, 81.2 us)

commit v11 on v9

--- a/solution.py
+++ b/solution.py
@@ -60,6 +60,23 @@
     )(ids, clips.reshape(cut), cotangent.reshape(cut))
     far = [out[half + chunk * half :][:half] for chunk in range(n_chunks)]
     return out[:half], far
+
+
+def fetch_kernel(w_ref, out_ref, sem):
+    copy = pltpu.make_async_copy(w_ref, out_ref, sem)
+    copy.start()
+    copy.wait()
+
+
+def fetch(weights):
+    return pl.pallas_call(
+        fetch_kernel,
+        out_shape=jax.ShapeDtypeStruct(weights.shape, weights.dtype),
+        in_specs=[pl.BlockSpec(memory_space=pltpu.HBM)],
+        out_specs=pl.BlockSpec(memory_space=pltpu.VMEM),
+        scratch_shapes=[pltpu.SemaphoreType.DMA],
+        compiler_params=pltpu.CompilerParams(vmem_limit_bytes=42 * MIB),
+    )(weights)
 
 
 def place_kernel(ids_ref, *refs):
@@ -306,15 +323,24 @@
     return values
 
 
-def inbound(near, far, n_tm):
+def inbound(near, far, ready, n_tm):
     half = n_tm // 2
-    near = [near[0]] + [swap(near[k], "tm", n_tm, k) for k in range(1, half)]
-    arrived = []
-    for blocks in far:
-        gates = arrived[-1] if arrived else [near[2]] + [None] * (half - 1)
-        blocks = [block if gate is None else after(block, gate) for block, gate in zip(blocks, gates)]
-        done = {i: swap(blocks[i], "tm", n_tm, half + i) for i in reversed(range(half))}
-        arrived.append([done[i] for i in range(half)])
+    order, gates = list(range(1, n_tm)), {}
+    if half == 4:
+        order, gates = [3, 2, 5, 7, 1, 4, 6], {7: 5}
+    near = list(near)
+    blocks = near + list(far[0])
+    for k in order:
+        block = after(blocks[k], blocks[gates[k]]) if k in gates else blocks[k]
+        blocks[k] = swap(block, "tm", n_tm, k)
+    near, arrived = blocks[:half], [blocks[half:]]
+    extra = {0: [ready], 3: [near[-1]]}
+    for chunk in far[1:]:
+        done = list(chunk)
+        for i in (0, *reversed(range(1, half))):
+            gate = (arrived[-1][i], extra.get(i, [near[1]]))
+            done[i] = swap(after(chunk[i], gate), "tm", n_tm, half + i)
+        arrived.append(done)
     return near, arrived
 
 
@@ -325,7 +351,9 @@
     joined = n_positions % 16 != 0
     ids = jnp.stack([lax.axis_index("clip"), lax.axis_index("tm")]).astype(jnp.int32)
 
-    near, far = inbound(*pick(ids, clips, cotangent, n_tm, CHUNKS), n_tm)
+    near, far = pick(ids, clips, cotangent, n_tm, CHUNKS)
+    w_qkv = fetch(w_qkv)
+    near, far = inbound(near, far, w_qkv, n_tm)
     depth = n_clips // CHUNKS
     factors, dx = [], []
     for chunk in range(CHUNKS):

time: 147 us -> 144 us (0.980)
  waiting for transfers between devices: 67.8 us -> 50 us
  starting transfers between devices: 40.1 us -> 54.8 us
  Pallas kernels: 32 us -> 34.8 us
  local copies, waits for them, and re-layouts: 5.24 us -> 2.45 us
    ppermute x27, waiting for transfers between devices: 67.8 us -> 50 us  [swap(): return lax.ppermute(block, axis, [(i, i ^ distance) for i in range(size)])]
    ppermute x27, starting transfers between devices: 40.1 us -> 54.8 us  [swap(): return lax.ppermute(block, axis, [(i, i ^ distance) for i in range(size)])]
    pallas_call x0 -> x1, Pallas kernels: none -> 2.79 us  [fetch(): pl.pallas_call(fetch_kernel, out_shape=jax.ShapeDtypeStruct(weights.shape...]
    unnamed x10 -> x6, local copies, waits for them, and re-layouts: 5.24 us -> 2.45 us
  transfers between devices with their start and end apart: 27 -> 27, of which waited for: 15 -> 11; matrix products, arithmetic and copies ran while one was open for 0% -> 0% of each run, Pallas kernels for 13% -> 15%
where the time goes in v11:
time: 144 us; the launch traced here: 143 us
  starting transfers between devices  54.8 us (38%)
  waiting for transfers between devices  50 us (35%)
  Pallas kernels  34.8 us (24%)
  local copies, waits for them, and re-layouts  2.45 us (2%)
    ppermute x27, starting transfers between devices, swap(): return lax.ppermute(block, axis, [(i, i ^ distance) for i in range(size)])  54.8 us
    ppermute x27, waiting for transfers between devices, swap(): return lax.ppermute(block, axis, [(i, i ^ distance) for i in range(size)])  50 us
    pallas_call x2, Pallas kernels, sublayer(): pl.pallas_call(functools.partial(sublayer_kernel, at, n_clips, n_position...  17.1 us
    pallas_call x4, Pallas kernels, products(): pl.pallas_call(functools.partial(product_kernel, n_x, flip, n_chunks, spa...  7.55 us
    pallas_call x4, Pallas kernels, halve(): pl.pallas_call(functools.partial(halve_kernel, dim, axis, stride), out_sh...  3.5 us
  transfers between devices with their start and end apart: 27, of which 11 were waited for; matrix products, arithmetic and copies ran while one was open for 0% of the time, Pallas kernels for 15%

profile of v11, /device:TPU:0, one launch (start us, length us, event | category | flops | bytes accessed | tf_op | source)
XLA Modules:
  0.0 142.9 jit_solution(8860993031329512786)
XLA Ops:
  3.8 5.1 %collective-permute-start.5 = (bf16[2,2,16,1024]{3,2,1,0:T(8,128)(2,1)S(1)}, bf16[2,2,16,1024]{3,2,1,0:T(8,128)(2,1)S(1)}, u32[]{:S(2)}, u32[]{:S(2)}) collective-permute-start(bf16[2,2,16,1024]{3,2,1,0:T(8,128)(2,1)S(1)} %get-tuple-element.110), channel_id=1, source_target_pairs={{0,5},{1,4},{2,7},{3,6},{4,1},{5,0},{6,3},{7,2},{8,13},{9,12},{10,... | collective-permute-start | bytes 393224 | tf_op jit(solution)/shard_map/ppermute | solution.py:318
  9.5 2.7 %collective-permute-start.2 = (bf16[2,4,16,1024]{3,2,1,0:T(8,128)(2,1)S(1)}, bf16[2,4,16,1024]{3,2,1,0:T(8,128)(2,1)S(1)}, u32[]{:S(2)}, u32[]{:S(2)}) collective-permute-start(bf16[2,4,16,1024]{3,2,1,0:T(8,128)(2,1)S(1)} %get-tuple-element.105), channel_id=1, source_target_pairs={{0,3},{1,2},{2,1},{3,0},{4,7},{5,6},{6,5},{7,4},{8,11},{9,10},{10,... | collective-permute-start | bytes 786440 | tf_op jit(solution)/shard_map/ppermute | solution.py:318
  12.7 6.1 %collective-permute-done.5.refs_5_ = bf16[2,2,16,1024]{3,2,1,0:T(8,128)(2,1)S(1)} collective-permute-done((bf16[2,2,16,1024]{3,2,1,0:T(8,128)(2,1)S(1)}, bf16[2,2,16,1024]{3,2,1,0:T(8,128)(2,1)S(1)}, u32[]{:S(2)}, u32[]{:S(2)}) %collective-permute-start.5) | collective-permute-done | bytes 131104 | tf_op jit(solution)/shard_map/ppermute | solution.py:318
  18.8 2.8 %collective-permute-start.7 = (bf16[2,2,16,1024]{3,2,1,0:T(8,128)(2,1)S(1)}, bf16[2,2,16,1024]{3,2,1,0:T(8,128)(2,1)S(1)}, u32[]{:S(2)}, u32[]{:S(2)}) collective-permute-start(bf16[2,2,16,1024]{3,2,1,0:T(8,128)(2,1)S(1)} %get-tuple-element.113), channel_id=1, source_target_pairs={{0,6},{1,7},{2,4},{3,5},{4,2},{5,3},{6,0},{7,1},{8,14},{9,15},{10,... | collective-permute-start | bytes 393224 | tf_op jit(solution)/shard_map/ppermute | solution.py:318
  21.7 2.7 %collective-permute-start.9 = (bf16[2,2,16,1024]{3,2,1,0:T(8,128)(2,1)S(1)}, bf16[2,2,16,1024]{3,2,1,0:T(8,128)(2,1)S(1)}, u32[]{:S(2)}, u32[]{:S(2)}) collective-permute-start(bf16[2,2,16,1024]{3,2,1,0:T(8,128)(2,1)S(1)} %get-tuple-element.117), channel_id=1, source_target_pairs={{0,7},{1,6},{2,5},{3,4},{4,3},{5,2},{6,1},{7,0},{8,15},{9,14},{10,... | collective-permute-start | bytes 393224 | tf_op jit(solution)/shard_map/ppermute | solution.py:318
  24.4 2.8 %shard_map.68.refs_8_ = bf16[1024,3072]{1,0:T(8,128)(2,1)S(1)} custom-call(bf16[1024,3072]{1,0:T(8,128)(2,1)} %w_ref.1), custom_call_target="tpu_custom_call" | custom-call | tf_op jit(solution)/shard_map/pallas_call | solution.py:72
  27.2 4.6 %collective-permute-done.7.refs_6_ = bf16[2,2,16,1024]{3,2,1,0:T(8,128)(2,1)S(1)} collective-permute-done((bf16[2,2,16,1024]{3,2,1,0:T(8,128)(2,1)S(1)}, bf16[2,2,16,1024]{3,2,1,0:T(8,128)(2,1)S(1)}, u32[]{:S(2)}, u32[]{:S(2)}) %collective-permute-start.7) | collective-permute-done | bytes 131104 | tf_op jit(solution)/shard_map/ppermute | solution.py:318
  31.9 3.5 %collective-permute-start.6 = (bf16[2,2,16,1024]{3,2,1,0:T(8,128)(2,1)S(1)}, bf16[2,2,16,1024]{3,2,1,0:T(8,128)(2,1)S(1)}, u32[]{:S(2)}, u32[]{:S(2)}) collective-permute-start(bf16[2,2,16,1024]{3,2,1,0:T(8,128)(2,1)S(1)} %get-tuple-element.111), channel_id=1, source_target_pairs={{0,5},{1,4},{2,7},{3,6},{4,1},{5,0},{6,3},{7,2},{8,13},{9,12},{10,... | collective-permute-start | bytes 393224 | tf_op jit(solution)/shard_map/ppermute | solution.py:318
  37.0 2.5 %collective-permute-start.10 = (bf16[2,2,16,1024]{3,2,1,0:T(8,128)(2,1)S(1)}, bf16[2,2,16,1024]{3,2,1,0:T(8,128)(2,1)S(1)}, u32[]{:S(2)}, u32[]{:S(2)}) collective-permute-start(bf16[2,2,16,1024]{3,2,1,0:T(8,128)(2,1)S(1)} %get-tuple-element.118), channel_id=1, source_target_pairs={{0,7},{1,6},{2,5},{3,4},{4,3},{5,2},{6,1},{7,0},{8,15},{9,14},{10,... | collective-permute-start | bytes 393224 | tf_op jit(solution)/shard_map/ppermute | solution.py:318
  39.5 8.4 %shard_map.69 = (bf16[256,1024]{1,0:T(8,128)(2,1)S(1)}, bf16[256,1024]{1,0:T(8,128)(2,1)S(1)}, bf16[256,1024]{1,0:T(8,128)(2,1)S(1)}, bf16[256,1024]{1,0:T(8,128...) custom-call(bf16[2,4,16,1024]{3,2,1,0:T(8,128)(2,1)S(1)} %get-tuple-, ...), custom_call_target="tpu_custom_call" | custom-call | flops 5368709120 | bytes 12582912 | tf_op jit(solution)/shard_map/pallas_call | solution.py:303
  48.0 3.1 %collective-permute-done.6.refs_5_ = bf16[2,2,16,1024]{3,2,1,0:T(8,128)(2,1)S(1)} collective-permute-done((bf16[2,2,16,1024]{3,2,1,0:T(8,128)(2,1)S(1)}, bf16[2,2,16,1024]{3,2,1,0:T(8,128)(2,1)S(1)}, u32[]{:S(2)}, u32[]{:S(2)}) %collective-permute-start.6) | collective-permute-done | bytes 131104 | tf_op jit(solution)/shard_map/ppermute | solution.py:318
  51.1 8.6 %shard_map.70 = (bf16[256,1024]{1,0:T(8,128)(2,1)S(1)}, bf16[256,1024]{1,0:T(8,128)(2,1)S(1)}, bf16[256,1024]{1,0:T(8,128)(2,1)S(1)}, bf16[256,1024]{1,0:T(8,128...) custom-call(bf16[2,4,16,1024]{3,2,1,0:T(8,128)(2,1)S(1)} %get-tuple-, ...), custom_call_target="tpu_custom_call" | custom-call | flops 5368709120 | bytes 12582912 | tf_op jit(solution)/shard_map/pallas_call | solution.py:303
  59.8 2.0 %shard_map.71 = bf16[2,4,2,32,2304]{4,3,2,1,0:T(8,128)(2,1)S(1)} custom-call(s32[2]{0:T(128)S(1)} %pad_add_fusion.ids_ref, bf16[256,1024]{1,0:T(8,128)(2,1)S(1)} %get-tuple-element.167.refs_0_, bf16[256,1024]{1,0:T(8,128)(2,1)S(1)} %get-tuple-element.168.refs_1_, bf16[256,1024]{1,0:T(8,128)(2,1)S(1)} %get-tuple-element.159.refs_2_, ...), custom_call_target="tpu_custom_call" | custom-call | flops 301989888 | bytes 524288 | tf_op jit(solution)/shard_map/pallas_call | solution.py:123
  64.2 2.0 %shard_map.73.refs_0_ = bf16[2,4,2,32,2304]{4,3,2,1,0:T(8,128)(2,1)S(1)} custom-call(s32[2]{0:T(128)S(1)} %pad_add_fusion.ids_ref, bf16[256,1024]{1,0:T(8,128)(2,1)S(1)} %get-tuple-element.167.refs_0_, bf16[256,1024]{1,0:T(8,128)(2,1)S(1)} %get-tuple-element.168.refs_1_, bf16[256,1024]{1,0:T(8,128)(2,1)S(1)} %get-tuple-element.159.refs_2_, ...), custom_call_target="tpu_custom_call" | custom-call | flops 301989888 | bytes 524288 | tf_op jit(solution)/shard_map/pallas_call | solution.py:123
  72.7 6.7 %collective-permute-start.15 = (bf16[4,16,1024]{2,1,0:T(8,128)(2,1)S(1)}, bf16[4,16,1024]{2,1,0:T(8,128)(2,1)S(1)}, u32[]{:S(2)}, u32[]{:S(2)}) collective-permute-start(bf16[4,16,1024]{2,1,0:T(8,128)(2,1)S(1)} %get-tuple-element.176), channel_id=1, source_target_pairs={{0,5},{1,4},{2,7},{3,6},{4,1},{5,0},{6,3},{7,2},{8,13},{9,12},{10,... | collective-permute-start | bytes 393224 | tf_op jit(solution)/shard_map/ppermute | solution.py:318
  81.5 2.8 %collective-permute-start.17 = (bf16[4,16,1024]{2,1,0:T(8,128)(2,1)S(1)}, bf16[4,16,1024]{2,1,0:T(8,128)(2,1)S(1)}, u32[]{:S(2)}, u32[]{:S(2)}) collective-permute-start(bf16[4,16,1024]{2,1,0:T(8,128)(2,1)S(1)} %get-tuple-element.178), channel_id=1, source_target_pairs={{0,7},{1,6},{2,5},{3,4},{4,3},{5,2},{6,1},{7,0},{8,15},{9,14},{10,... | collective-permute-start | bytes 393224 | tf_op jit(solution)/shard_map/ppermute | solution.py:318
  84.2 8.0 %collective-permute-done.15.refs_5_ = bf16[4,16,1024]{2,1,0:T(8,128)(2,1)S(1)} collective-permute-done((bf16[4,16,1024]{2,1,0:T(8,128)(2,1)S(1)}, bf16[4,16,1024]{2,1,0:T(8,128)(2,1)S(1)}, u32[]{:S(2)}, u32[]{:S(2)}) %collective-permute-start.15) | collective-permute-done | bytes 131104 | tf_op jit(solution)/shard_map/ppermute | solution.py:318
  92.2 7.4 %collective-permute-done.14.refs_1_ = bf16[2,4,32,1792]{3,2,1,0:T(8,128)(2,1)S(1)} collective-permute-done((bf16[2,4,32,1792]{3,2,1,0:T(8,128)(2,1)S(1)}, bf16[2,4,32,1792]{3,2,1,0:T(8,128)(2,1)S(1)}, u32[]{:S(2)}, u32[]{:S(2)}) %collective-permute-start.14) | collective-permute-done | bytes 917536 | tf_op jit(solution)/shard_map/ppermute | solution.py:318
  102.6 5.7 %collective-permute-start.20 = (bf16[4,16,1024]{2,1,0:T(8,128)(2,1)S(1)}, bf16[4,16,1024]{2,1,0:T(8,128)(2,1)S(1)}, u32[]{:S(2)}, u32[]{:S(2)}) collective-permute-start(bf16[4,16,1024]{2,1,0:T(8,128)(2,1)S(1)} %get-tuple-element.186), channel_id=1, source_target_pairs={{0,2},{1,3},{2,0},{3,1},{4,6},{5,7},{6,4},{7,5},{8,10},{9,11},{10,... | collective-permute-start | bytes 393224 | tf_op jit(solution)/shard_map/ppermute | solution.py:318
  109.4 3.3 %collective-permute-done.20.refs_2_ = bf16[4,16,1024]{2,1,0:T(8,128)(2,1)S(1)} collective-permute-done((bf16[4,16,1024]{2,1,0:T(8,128)(2,1)S(1)}, bf16[4,16,1024]{2,1,0:T(8,128)(2,1)S(1)}, u32[]{:S(2)}, u32[]{:S(2)}) %collective-permute-start.20) | collective-permute-done | bytes 131104 | tf_op jit(solution)/shard_map/ppermute | solution.py:318
  112.7 3.1 %collective-permute-done.21.refs_4_ = bf16[4,16,1024]{2,1,0:T(8,128)(2,1)S(1)} collective-permute-done((bf16[4,16,1024]{2,1,0:T(8,128)(2,1)S(1)}, bf16[4,16,1024]{2,1,0:T(8,128)(2,1)S(1)}, u32[]{:S(2)}, u32[]{:S(2)}) %collective-permute-start.21) | collective-permute-done | bytes 131104 | tf_op jit(solution)/shard_map/ppermute | solution.py:318
  116.4 4.8 %collective-permute-start.26 = (bf16[32,4096]{1,0:T(8,128)(2,1)S(1)}, bf16[32,4096]{1,0:T(8,128)(2,1)S(1)}, u32[]{:S(2)}, u32[]{:S(2)}) collective-permute-start(bf16[32,4096]{1,0:T(8,128)(2,1)S(1)} %get-tuple-element.192), channel_id=1, source_target_pairs={{0,2},{1,3},{2,0},{3,1},{4,6},{5,7},{6,4},{7,5},{8,10},{9,11},{10,... | collective-permute-start | bytes 786440 | tf_op jit(solution)/shard_map/ppermute | solution.py:318
  126.2 3.3 %collective-permute-done.22.refs_1_ = bf16[4,16,1024]{2,1,0:T(8,128)(2,1)S(1)} collective-permute-done((bf16[4,16,1024]{2,1,0:T(8,128)(2,1)S(1)}, bf16[4,16,1024]{2,1,0:T(8,128)(2,1)S(1)}, u32[]{:S(2)}, u32[]{:S(2)}) %collective-permute-start.22) | collective-permute-done | bytes 131104 | tf_op jit(solution)/shard_map/ppermute | solution.py:318
  129.5 9.6 %collective-permute-done.23.refs_3_ = bf16[4,16,1024]{2,1,0:T(8,128)(2,1)S(1)} collective-permute-done((bf16[4,16,1024]{2,1,0:T(8,128)(2,1)S(1)}, bf16[4,16,1024]{2,1,0:T(8,128)(2,1)S(1)}, u32[]{:S(2)}, u32[]{:S(2)}) %collective-permute-start.23) | collective-permute-done | bytes 131104 | tf_op jit(solution)/shard_map/ppermute | solution.py:318
  (52 shorter events, 30.2 us)
Async XLA Ops:
  3.8 15.0 %collective-permute-start.5 = (bf16[2,2,16,1024]{3,2,1,0:T(8,128)(2,1)S(1)}, bf16[2,2,16,1024]{3,2,1,0:T(8,128)(2,1)S(1)}, u32[]{:S(2)}, u32[]{:S(2)}) collective-permute-start(bf16[2,2,16,1024]{3,2,1,0:T(8,128)(2,1)S(1)} %get-tuple-element.110), channel_id=1, source_target_pairs={{0,5},{1,4},{2,7},{3,6},{4,1},{5,0},{6,3},{7,2},{8,13},{9,12},{10,... | collective-permute-start | bytes 393224 | tf_op jit(solution)/shard_map/ppermute | solution.py:318
  8.9 23.0 %collective-permute-start = (bf16[2,4,16,1024]{3,2,1,0:T(8,128)(2,1)S(1)}, bf16[2,4,16,1024]{3,2,1,0:T(8,128)(2,1)S(1)}, u32[]{:S(2)}, u32[]{:S(2)}) collective-permute-start(bf16[2,4,16,1024]{3,2,1,0:T(8,128)(2,1)S(1)} %get-tuple-element.103), channel_id=1, source_target_pairs={{0,1},{1,0},{2,3},{3,2},{4,5},{5,4},{6,7},{7,6},{8,9},{9,8},{10,11... | collective-permute-start | bytes 786440 | tf_op jit(solution)/shard_map/ppermute | solution.py:318
  9.4 12.3 %collective-permute-start.3 = (bf16[2,2,16,1024]{3,2,1,0:T(8,128)(2,1)S(1)}, bf16[2,2,16,1024]{3,2,1,0:T(8,128)(2,1)S(1)}, u32[]{:S(2)}, u32[]{:S(2)}) collective-permute-start(bf16[2,2,16,1024]{3,2,1,0:T(8,128)(2,1)S(1)} %get-tuple-element.107), channel_id=1, source_target_pairs={{0,4},{1,5},{2,6},{3,7},{4,0},{5,1},{6,2},{7,3},{8,12},{9,13},{10,... | collective-permute-start | bytes 393224 | tf_op jit(solution)/shard_map/ppermute | solution.py:318
  9.5 27.5 %collective-permute-start.2 = (bf16[2,4,16,1024]{3,2,1,0:T(8,128)(2,1)S(1)}, bf16[2,4,16,1024]{3,2,1,0:T(8,128)(2,1)S(1)}, u32[]{:S(2)}, u32[]{:S(2)}) collective-permute-start(bf16[2,4,16,1024]{3,2,1,0:T(8,128)(2,1)S(1)} %get-tuple-element.105), channel_id=1, source_target_pairs={{0,3},{1,2},{2,1},{3,0},{4,7},{5,6},{6,5},{7,4},{8,11},{9,10},{10,... | collective-permute-start | bytes 786440 | tf_op jit(solution)/shard_map/ppermute | solution.py:318
  12.3 27.2 %collective-permute-start.1 = (bf16[2,4,16,1024]{3,2,1,0:T(8,128)(2,1)S(1)}, bf16[2,4,16,1024]{3,2,1,0:T(8,128)(2,1)S(1)}, u32[]{:S(2)}, u32[]{:S(2)}) collective-permute-start(bf16[2,4,16,1024]{3,2,1,0:T(8,128)(2,1)S(1)} %get-tuple-element.104), channel_id=1, source_target_pairs={{0,2},{1,3},{2,0},{3,1},{4,6},{5,7},{6,4},{7,5},{8,10},{9,11},{10,... | collective-permute-start | bytes 786440 | tf_op jit(solution)/shard_map/ppermute | solution.py:318
  18.8 13.0 %collective-permute-start.7 = (bf16[2,2,16,1024]{3,2,1,0:T(8,128)(2,1)S(1)}, bf16[2,2,16,1024]{3,2,1,0:T(8,128)(2,1)S(1)}, u32[]{:S(2)}, u32[]{:S(2)}) collective-permute-start(bf16[2,2,16,1024]{3,2,1,0:T(8,128)(2,1)S(1)} %get-tuple-element.113), channel_id=1, source_target_pairs={{0,6},{1,7},{2,4},{3,5},{4,2},{5,3},{6,0},{7,1},{8,14},{9,15},{10,... | collective-permute-start | bytes 393224 | tf_op jit(solution)/shard_map/ppermute | solution.py:318
  21.7 13.7 %collective-permute-start.9 = (bf16[2,2,16,1024]{3,2,1,0:T(8,128)(2,1)S(1)}, bf16[2,2,16,1024]{3,2,1,0:T(8,128)(2,1)S(1)}, u32[]{:S(2)}, u32[]{:S(2)}) collective-permute-start(bf16[2,2,16,1024]{3,2,1,0:T(8,128)(2,1)S(1)} %get-tuple-element.117), channel_id=1, source_target_pairs={{0,7},{1,6},{2,5},{3,4},{4,3},{5,2},{6,1},{7,0},{8,15},{9,14},{10,... | collective-permute-start | bytes 393224 | tf_op jit(solution)/shard_map/ppermute | solution.py:318
  31.9 16.1 %collective-permute-start.4 = (bf16[2,2,16,1024]{3,2,1,0:T(8,128)(2,1)S(1)}, bf16[2,2,16,1024]{3,2,1,0:T(8,128)(2,1)S(1)}, u32[]{:S(2)}, u32[]{:S(2)}) collective-permute-start(bf16[2,2,16,1024]{3,2,1,0:T(8,128)(2,1)S(1)} %get-tuple-element.108), channel_id=1, source_target_pairs={{0,4},{1,5},{2,6},{3,7},{4,0},{5,1},{6,2},{7,3},{8,12},{9,13},{10,... | collective-permute-start | bytes 393224 | tf_op jit(solution)/shard_map/ppermute | solution.py:318
  31.9 19.3 %collective-permute-start.6 = (bf16[2,2,16,1024]{3,2,1,0:T(8,128)(2,1)S(1)}, bf16[2,2,16,1024]{3,2,1,0:T(8,128)(2,1)S(1)}, u32[]{:S(2)}, u32[]{:S(2)}) collective-permute-start(bf16[2,2,16,1024]{3,2,1,0:T(8,128)(2,1)S(1)} %get-tuple-element.111), channel_id=1, source_target_pairs={{0,5},{1,4},{2,7},{3,6},{4,1},{5,0},{6,3},{7,2},{8,13},{9,12},{10,... | collective-permute-start | bytes 393224 | tf_op jit(solution)/shard_map/ppermute | solution.py:318
  35.4 15.7 %collective-permute-start.8 = (bf16[2,2,16,1024]{3,2,1,0:T(8,128)(2,1)S(1)}, bf16[2,2,16,1024]{3,2,1,0:T(8,128)(2,1)S(1)}, u32[]{:S(2)}, u32[]{:S(2)}) collective-permute-start(bf16[2,2,16,1024]{3,2,1,0:T(8,128)(2,1)S(1)} %get-tuple-element.114), channel_id=1, source_target_pairs={{0,6},{1,7},{2,4},{3,5},{4,2},{5,3},{6,0},{7,1},{8,14},{9,15},{10,... | collective-permute-start | bytes 393224 | tf_op jit(solution)/shard_map/ppermute | solution.py:318
  37.0 14.1 %collective-permute-start.10 = (bf16[2,2,16,1024]{3,2,1,0:T(8,128)(2,1)S(1)}, bf16[2,2,16,1024]{3,2,1,0:T(8,128)(2,1)S(1)}, u32[]{:S(2)}, u32[]{:S(2)}) collective-permute-start(bf16[2,2,16,1024]{3,2,1,0:T(8,128)(2,1)S(1)} %get-tuple-element.118), channel_id=1, source_target_pairs={{0,7},{1,6},{2,5},{3,4},{4,3},{5,2},{6,1},{7,0},{8,15},{9,14},{10,... | collective-permute-start | bytes 393224 | tf_op jit(solution)/shard_map/ppermute | solution.py:318
  67.5 32.2 %collective-permute-start.12 = (bf16[4,2,32,2304]{3,2,1,0:T(8,128)(2,1)S(1)}, bf16[4,2,32,2304]{3,2,1,0:T(8,128)(2,1)S(1)}, u32[]{:S(2)}, u32[]{:S(2)}) collective-permute-start(bf16[4,2,32,2304]{3,2,1,0:T(8,128)(2,1)S(1)} %get-tuple-element.166), channel_id=1, source_target_pairs={{0,16},{8,24},{16,0},{24,8},{1,17},{9,25},{17,1},{25,9},{2,18},{10... | collective-permute-start | bytes 3538952 | tf_op jit(solution)/shard_map/ppermute | solution.py:318
  71.8 27.8 %collective-permute-start.14 = (bf16[2,4,32,1792]{3,2,1,0:T(8,128)(2,1)S(1)}, bf16[2,4,32,1792]{3,2,1,0:T(8,128)(2,1)S(1)}, u32[]{:S(2)}, u32[]{:S(2)}) collective-permute-start(bf16[2,4,32,1792]{3,2,1,0:T(8,128)(2,1)S(1)} %get-tuple-element.175), channel_id=1, source_target_pairs={{0,1},{1,0},{2,3},{3,2},{4,5},{5,4},{6,7},{7,6},{8,9},{9,8},{10,11... | collective-permute-start | bytes 2752520 | tf_op jit(solution)/shard_map/ppermute | solution.py:318
  72.7 19.5 %collective-permute-start.15 = (bf16[4,16,1024]{2,1,0:T(8,128)(2,1)S(1)}, bf16[4,16,1024]{2,1,0:T(8,128)(2,1)S(1)}, u32[]{:S(2)}, u32[]{:S(2)}) collective-permute-start(bf16[4,16,1024]{2,1,0:T(8,128)(2,1)S(1)} %get-tuple-element.176), channel_id=1, source_target_pairs={{0,5},{1,4},{2,7},{3,6},{4,1},{5,0},{6,3},{7,2},{8,13},{9,12},{10,... | collective-permute-start | bytes 393224 | tf_op jit(solution)/shard_map/ppermute | solution.py:318
  79.5 12.8 %collective-permute-start.16 = (bf16[4,16,1024]{2,1,0:T(8,128)(2,1)S(1)}, bf16[4,16,1024]{2,1,0:T(8,128)(2,1)S(1)}, u32[]{:S(2)}, u32[]{:S(2)}) collective-permute-start(bf16[4,16,1024]{2,1,0:T(8,128)(2,1)S(1)} %get-tuple-element.177), channel_id=1, source_target_pairs={{0,6},{1,7},{2,4},{3,5},{4,2},{5,3},{6,0},{7,1},{8,14},{9,15},{10,... | collective-permute-start | bytes 393224 | tf_op jit(solution)/shard_map/ppermute | solution.py:318
  81.5 10.8 %collective-permute-start.17 = (bf16[4,16,1024]{2,1,0:T(8,128)(2,1)S(1)}, bf16[4,16,1024]{2,1,0:T(8,128)(2,1)S(1)}, u32[]{:S(2)}, u32[]{:S(2)}) collective-permute-start(bf16[4,16,1024]{2,1,0:T(8,128)(2,1)S(1)} %get-tuple-element.178), channel_id=1, source_target_pairs={{0,7},{1,6},{2,5},{3,4},{4,3},{5,2},{6,1},{7,0},{8,15},{9,14},{10,... | collective-permute-start | bytes 393224 | tf_op jit(solution)/shard_map/ppermute | solution.py:318
  100.4 15.3 %collective-permute-start.18 = (bf16[4,32,2304]{2,1,0:T(8,128)(2,1)S(1)}, bf16[4,32,2304]{2,1,0:T(8,128)(2,1)S(1)}, u32[]{:S(2)}, u32[]{:S(2)}) collective-permute-start(bf16[4,32,2304]{2,1,0:T(8,128)(2,1)S(1)} %get-tuple-element.181), channel_id=1, source_target_pairs={{0,1},{1,0},{2,3},{3,2},{4,5},{5,4},{6,7},{7,6},{8,9},{9,8},{10,11... | collective-permute-start | bytes 1769480 | tf_op jit(solution)/shard_map/ppermute | solution.py:318
  102.0 13.7 %collective-permute-start.19 = (bf16[4,32,1792]{2,1,0:T(8,128)(2,1)S(1)}, bf16[4,32,1792]{2,1,0:T(8,128)(2,1)S(1)}, u32[]{:S(2)}, u32[]{:S(2)}) collective-permute-start(bf16[4,32,1792]{2,1,0:T(8,128)(2,1)S(1)} %get-tuple-element.184), channel_id=1, source_target_pairs={{0,16},{8,24},{16,0},{24,8},{1,17},{9,25},{17,1},{25,9},{2,18},{10... | collective-permute-start | bytes 1376264 | tf_op jit(solution)/shard_map/ppermute | solution.py:318
  102.6 10.1 %collective-permute-start.20 = (bf16[4,16,1024]{2,1,0:T(8,128)(2,1)S(1)}, bf16[4,16,1024]{2,1,0:T(8,128)(2,1)S(1)}, u32[]{:S(2)}, u32[]{:S(2)}) collective-permute-start(bf16[4,16,1024]{2,1,0:T(8,128)(2,1)S(1)} %get-tuple-element.186), channel_id=1, source_target_pairs={{0,2},{1,3},{2,0},{3,1},{4,6},{5,7},{6,4},{7,5},{8,10},{9,11},{10,... | collective-permute-start | bytes 393224 | tf_op jit(solution)/shard_map/ppermute | solution.py:318
  108.3 7.4 %collective-permute-start.21 = (bf16[4,16,1024]{2,1,0:T(8,128)(2,1)S(1)}, bf16[4,16,1024]{2,1,0:T(8,128)(2,1)S(1)}, u32[]{:S(2)}, u32[]{:S(2)}) collective-permute-start(bf16[4,16,1024]{2,1,0:T(8,128)(2,1)S(1)} %get-tuple-element.188), channel_id=1, source_target_pairs={{0,4},{1,5},{2,6},{3,7},{4,0},{5,1},{6,2},{7,3},{8,12},{9,13},{10,... | collective-permute-start | bytes 393224 | tf_op jit(solution)/shard_map/ppermute | solution.py:318
  116.4 24.3 %collective-permute-start.26 = (bf16[32,4096]{1,0:T(8,128)(2,1)S(1)}, bf16[32,4096]{1,0:T(8,128)(2,1)S(1)}, u32[]{:S(2)}, u32[]{:S(2)}) collective-permute-start(bf16[32,4096]{1,0:T(8,128)(2,1)S(1)} %get-tuple-element.192), channel_id=1, source_target_pairs={{0,2},{1,3},{2,0},{3,1},{4,6},{5,7},{6,4},{7,5},{8,10},{9,11},{10,... | collective-permute-start | bytes 786440 | tf_op jit(solution)/shard_map/ppermute | solution.py:318
  121.2 20.7 %collective-permute-start.25 = (bf16[32,4096]{1,0:T(8,128)(2,1)S(1)}, bf16[32,4096]{1,0:T(8,128)(2,1)S(1)}, u32[]{:S(2)}, u32[]{:S(2)}) collective-permute-start(bf16[32,4096]{1,0:T(8,128)(2,1)S(1)} %get-tuple-element.193), channel_id=1, source_target_pairs={{0,4},{1,5},{2,6},{3,7},{4,0},{5,1},{6,2},{7,3},{8,12},{9,13},{10,... | collective-permute-start | bytes 786440 | tf_op jit(solution)/shard_map/ppermute | solution.py:318
  121.7 20.3 %collective-permute-start.24 = (bf16[32,4096]{1,0:T(8,128)(2,1)S(1)}, bf16[32,4096]{1,0:T(8,128)(2,1)S(1)}, u32[]{:S(2)}, u32[]{:S(2)}) collective-permute-start(bf16[32,4096]{1,0:T(8,128)(2,1)S(1)} %get-tuple-element.194), channel_id=1, source_target_pairs={{0,6},{1,7},{2,4},{3,5},{4,2},{5,3},{6,0},{7,1},{8,14},{9,15},{10,... | collective-permute-start | bytes 786440 | tf_op jit(solution)/shard_map/ppermute | solution.py:318
  124.6 14.5 %collective-permute-start.23 = (bf16[4,16,1024]{2,1,0:T(8,128)(2,1)S(1)}, bf16[4,16,1024]{2,1,0:T(8,128)(2,1)S(1)}, u32[]{:S(2)}, u32[]{:S(2)}) collective-permute-start(bf16[4,16,1024]{2,1,0:T(8,128)(2,1)S(1)} %get-tuple-element.197), channel_id=1, source_target_pairs={{0,3},{1,2},{2,1},{3,0},{4,7},{5,6},{6,5},{7,4},{8,11},{9,10},{10,... | collective-permute-start | bytes 393224 | tf_op jit(solution)/shard_map/ppermute | solution.py:318
  (6 other events, 37.8 us)

commit v12 on v11

--- a/solution.py
+++ b/solution.py
@@ -208,12 +208,17 @@
     )(*addends)
 
 
-def sublayer_kernel(at, n_clips, n_positions, n_pieces, n_before, *refs):
+def raw_rows(pieces, at, n_clips):
+    parts = []
+    for clip in range(n_clips):
+        parts += [p[0, clip if p.shape[1] == n_clips else at + clip] for p in pieces]
+    return jnp.concatenate(parts, axis=0).astype(jnp.float32)
+
+
+def sublayer_kernel(at, n_clips, n_positions, n_pieces, *refs):
     pieces, refs = refs[:n_pieces], refs[n_pieces:]
     w_qkv_ref, w_out_ref = refs[:2]
-    before, refs = refs[2 : 2 + n_before], refs[2 + n_before :]
-    normed_ref, cot_ref, mixed_ref, dq_ref, dk_ref, dv_ref = refs[:6]
-    dx_refs = refs[6:]
+    normed_ref, cot_ref, mixed_ref, dq_ref, dk_ref, dv_ref = refs[2:]
     rows = normed_ref.shape[0] // n_clips
     span = rows // n_pieces
     width = w_out_ref.shape[0]
@@ -221,15 +226,12 @@
     depth = wide // GROUP
     scaling = depth**-0.5
 
-    def piece(k, which, clip):
-        return pieces[k][which, clip if pieces[k].shape[1] == n_clips else at + clip]
-
-    raw = jnp.concatenate([piece(k, 0, clip) for clip in range(n_clips) for k in range(n_pieces)], axis=0)
-    unit, _ = statistics(raw.astype(jnp.float32))
+    unit, _ = statistics(raw_rows(pieces, at, n_clips))
     normed_ref[...] = unit.astype(jnp.bfloat16)
     for clip in range(n_clips):
-        for k in range(n_pieces):
-            cot_ref[pl.ds(clip * rows + k * span, span)] = piece(k, 1, clip)
+        for k, piece in enumerate(pieces):
+            source = clip if piece.shape[1] == n_clips else at + clip
+            cot_ref[pl.ds(clip * rows + k * span, span)] = piece[1, source]
 
     lane_head = lax.broadcasted_iota(jnp.int32, (rows, wide), 1) // depth
     head_masks = [(lane_head == h).astype(jnp.float32).astype(jnp.bfloat16) for h in range(GROUP)]
@@ -277,9 +279,35 @@
             dv = contract(side_by_side(low), stacked(upstream), ((1,), (0,)))
             dv_ref[here, columns] = dv.astype(jnp.bfloat16)
 
+
+def sublayer(pieces, at, n_clips, w_qkv, w_out, n_positions):
+    _, _, span, width = pieces[0].shape
+    rows = n_clips * len(pieces) * span
+    flat = jax.ShapeDtypeStruct((rows, width), jnp.bfloat16)
+    operands = (*pieces, w_qkv, w_out)
+    return pl.pallas_call(
+        functools.partial(sublayer_kernel, at, n_clips, n_positions, len(pieces)),
+        out_shape=[flat] * 6,
+        in_specs=[pl.BlockSpec(memory_space=pltpu.VMEM)] * len(operands),
+        out_specs=[pl.BlockSpec(memory_space=pltpu.VMEM)] * 6,
+        compiler_params=pltpu.CompilerParams(vmem_limit_bytes=30 * MIB),
+        cost_estimate=pl.CostEstimate(
+            flops=2 * rows * width * (4 * width + 24 * 128),
+            bytes_accessed=16 * rows * width + 8 * width * width,
+            transcendentals=rows * 128 * HEADS,
+        ),
+    )(*operands)
+
+
+def input_kernel(at, n_clips, n_pieces, n_before, *refs):
+    pieces, refs = refs[:n_pieces], refs[n_pieces:]
+    w_qkv_ref, cot_ref, dq_ref, dk_ref, dv_ref = refs[:5]
+    before, dx_refs = refs[5 : 5 + n_before], refs[5 + n_before :]
+    rows = cot_ref.shape[0] // n_clips
+    span = rows // n_pieces
     grads = jnp.concatenate([dq_ref[...], dk_ref[...], dv_ref[...]], axis=1)
     total = contract(grads, w_qkv_ref[...], ((1,), (1,)))
-    unit, inverse = statistics(raw.astype(jnp.float32))
+    unit, inverse = statistics(raw_rows(pieces, at, n_clips))
     grad = inverse * (
         total
         - jnp.mean(total, axis=-1, keepdims=True)
@@ -294,22 +322,20 @@
             dx_refs[k][at + clip] = dx[start : start + span]
 
 
-def sublayer(pieces, at, n_clips, w_qkv, w_out, n_positions, before):
+def input_gradient(pieces, at, n_clips, w_qkv, cot, dq, dk, dv, before):
     _, _, span, width = pieces[0].shape
-    rows = n_clips * len(pieces) * span
-    flat = jax.ShapeDtypeStruct((rows, width), jnp.bfloat16)
     dx = jax.ShapeDtypeStruct((at + n_clips, span, width), jnp.bfloat16)
-    operands = (*pieces, w_qkv, w_out, *before)
-    return pl.pallas_call(
-        functools.partial(sublayer_kernel, at, n_clips, n_positions, len(pieces), len(before)),
-        out_shape=[flat] * 6 + [dx] * len(pieces),
+    operands = (*pieces, w_qkv, cot, dq, dk, dv, *before)
+    return pl.pallas_call(
+        functools.partial(input_kernel, at, n_clips, len(pieces), len(before)),
+        out_shape=[dx] * len(pieces),
         in_specs=[pl.BlockSpec(memory_space=pltpu.VMEM)] * len(operands),
-        out_specs=[pl.BlockSpec(memory_space=pltpu.VMEM)] * (6 + len(pieces)),
-        compiler_params=pltpu.CompilerParams(vmem_limit_bytes=32 * MIB),
+        out_specs=[pl.BlockSpec(memory_space=pltpu.VMEM)] * len(pieces),
+        compiler_params=pltpu.CompilerParams(vmem_limit_bytes=24 * MIB),
         cost_estimate=pl.CostEstimate(
-            flops=2 * rows * width * (7 * width + 24 * 128),
-            bytes_accessed=16 * rows * width + 8 * width * width,
-            transcendentals=rows * 128 * HEADS,
+            flops=6 * cot.shape[0] * width * width,
+            bytes_accessed=8 * cot.shape[0] * width + 6 * width * width,
+            transcendentals=0,
         ),
     )(*operands)
 
@@ -362,14 +388,11 @@
         if joined:
             pieces = [p[:, at : at + depth] for p in near] + far[chunk]
             pieces = [jnp.stack(pieces, axis=2).reshape(2, depth, -1, width)]
-        out = sublayer(pieces, at, depth, w_qkv, w_out, n_positions, dx)
-        factors.append(out[:6])
-        dx = list(out[6:])
+        factors.append(sublayer(after(pieces, dx), at, depth, w_qkv, w_out, n_positions))
+        later = (pieces, [w_qkv, *(factors[-1][i] for i in (1, 3, 4, 5))])
+        if chunk < CHUNKS - 1:
+            dx = input_gradient(pieces, at, depth, *later[1], dx)
     normed, cot, mixed, dq, dk, dv = zip(*factors)
-    if joined:
-        cut = dx[0].reshape(n_clips, n_tm, n_positions, width)
-        dx = [cut[:, k] for k in range(n_tm)]
-
     cut = int(4 * width * FIRST) - 2 * width
     first_parts = ([normed], [dq, dk, dv]), ((0, 0, width), (0, 0, width), (0, 0, cut))
     second_parts = ([normed, mixed], [dv, cot]), ((0, cut, width - cut), (1, 0, width))
@@ -383,7 +406,11 @@
     own_second = products(ids, 0, n_x, n_z, *after(second_parts[0], own_first), second_parts[1])
     sent, own_second = halve(ids, (own_second, second), 2, 1, 1)
     second = swap(sent, "tm", n_tm, 1)
-    dx = after(dx, sent_second)
+    pieces, operands = after(later, sent)
+    dx = input_gradient(pieces, n_clips - depth, depth, *operands, dx)
+    if joined:
+        cut = dx[0].reshape(n_clips, n_tm, n_positions, width)
+        dx = [cut[:, k] for k in range(n_tm)]
     late = (1, 3)
     back = {}
     for k in reversed([k for k in range(1, n_tm) if k not in late]):

time: 144 us -> 143 us (level)
  waiting for transfers between devices: 50 us -> 45.4 us
  starting transfers between devices: 54.8 us -> 57.5 us
    ppermute x27, waiting for transfers between devices: 50 us -> 45.4 us  [swap(): return lax.ppermute(block, axis, [(i, i ^ distance) for i in range(size)])]
    pallas_call x0 -> x2, Pallas kernels: none -> 4.34 us  [input_gradient(): pl.pallas_call(functools.partial(input_kernel, at, n_clips, len(pieces),...]
    pallas_call x2, Pallas kernels: 17.1 us -> 13.2 us  [sublayer(): pl.pallas_call(functools.partial(sublayer_kernel, at, n_clips, n_position...]
    ppermute x27, starting transfers between devices: 54.8 us -> 57.5 us  [swap(): return lax.ppermute(block, axis, [(i, i ^ distance) for i in range(size)])]
  transfers between devices with their start and end apart: 27 -> 27, of which waited for: 11 -> 12; matrix products, arithmetic and copies ran while one was open for 0% -> 0% of each run, Pallas kernels for 15% -> 17%
where the time goes in v12:
time: 143 us; the launch traced here: 141 us
  starting transfers between devices  57.5 us (40%)
  waiting for transfers between devices  45.4 us (32%)
  Pallas kernels  35.2 us (25%)
  local copies, waits for them, and re-layouts  2.45 us (2%)
    ppermute x27, starting transfers between devices, swap(): return lax.ppermute(block, axis, [(i, i ^ distance) for i in range(size)])  57.5 us
    ppermute x27, waiting for transfers between devices, swap(): return lax.ppermute(block, axis, [(i, i ^ distance) for i in range(size)])  45.4 us
    pallas_call x2, Pallas kernels, sublayer(): pl.pallas_call(functools.partial(sublayer_kernel, at, n_clips, n_position...  13.2 us
    pallas_call x4, Pallas kernels, products(): pl.pallas_call(functools.partial(product_kernel, n_x, flip, n_chunks, spa...  7.54 us
    pallas_call x2, Pallas kernels, input_gradient(): pl.pallas_call(functools.partial(input_kernel, at, n_clips, len(pieces),...  4.34 us
    pallas_call x4, Pallas kernels, halve(): pl.pallas_call(functools.partial(halve_kernel, dim, axis, stride), out_sh...  3.42 us
  transfers between devices with their start and end apart: 27, of which 12 were waited for; matrix products, arithmetic and copies ran while one was open for 0% of the time, Pallas kernels for 17%

profile of v12, /device:TPU:0, one launch (start us, length us, event | category | flops | bytes accessed | tf_op | source)
XLA Modules:
  0.0 141.3 jit_solution(6509073283571115996)
XLA Ops:
  3.8 5.1 %collective-permute-start.5 = (bf16[2,2,16,1024]{3,2,1,0:T(8,128)(2,1)S(1)}, bf16[2,2,16,1024]{3,2,1,0:T(8,128)(2,1)S(1)}, u32[]{:S(2)}, u32[]{:S(2)}) collective-permute-start(bf16[2,2,16,1024]{3,2,1,0:T(8,128)(2,1)S(1)} %get-tuple-element.131), channel_id=1, source_target_pairs={{0,5},{1,4},{2,7},{3,6},{4,1},{5,0},{6,3},{7,2},{8,13},{9,12},{10,... | collective-permute-start | bytes 393224 | tf_op jit(solution)/shard_map/ppermute | solution.py:344
  12.7 6.1 %collective-permute-done.5.refs_5_ = bf16[2,2,16,1024]{3,2,1,0:T(8,128)(2,1)S(1)} collective-permute-done((bf16[2,2,16,1024]{3,2,1,0:T(8,128)(2,1)S(1)}, bf16[2,2,16,1024]{3,2,1,0:T(8,128)(2,1)S(1)}, u32[]{:S(2)}, u32[]{:S(2)}) %collective-permute-start.5) | collective-permute-done | bytes 131104 | tf_op jit(solution)/shard_map/ppermute | solution.py:344
  18.9 2.8 %collective-permute-start.7 = (bf16[2,2,16,1024]{3,2,1,0:T(8,128)(2,1)S(1)}, bf16[2,2,16,1024]{3,2,1,0:T(8,128)(2,1)S(1)}, u32[]{:S(2)}, u32[]{:S(2)}) collective-permute-start(bf16[2,2,16,1024]{3,2,1,0:T(8,128)(2,1)S(1)} %get-tuple-element.134), channel_id=1, source_target_pairs={{0,6},{1,7},{2,4},{3,5},{4,2},{5,3},{6,0},{7,1},{8,14},{9,15},{10,... | collective-permute-start | bytes 393224 | tf_op jit(solution)/shard_map/ppermute | solution.py:344
  21.7 2.7 %collective-permute-start.9 = (bf16[2,2,16,1024]{3,2,1,0:T(8,128)(2,1)S(1)}, bf16[2,2,16,1024]{3,2,1,0:T(8,128)(2,1)S(1)}, u32[]{:S(2)}, u32[]{:S(2)}) collective-permute-start(bf16[2,2,16,1024]{3,2,1,0:T(8,128)(2,1)S(1)} %get-tuple-element.138), channel_id=1, source_target_pairs={{0,7},{1,6},{2,5},{3,4},{4,3},{5,2},{6,1},{7,0},{8,15},{9,14},{10,... | collective-permute-start | bytes 393224 | tf_op jit(solution)/shard_map/ppermute | solution.py:344
  24.4 2.8 %shard_map.68.refs_8_ = bf16[1024,3072]{1,0:T(8,128)(2,1)S(1)} custom-call(bf16[1024,3072]{1,0:T(8,128)(2,1)} %w_ref.1), custom_call_target="tpu_custom_call" | custom-call | tf_op jit(solution)/shard_map/pallas_call | solution.py:72
  27.2 4.6 %collective-permute-done.7.refs_6_ = bf16[2,2,16,1024]{3,2,1,0:T(8,128)(2,1)S(1)} collective-permute-done((bf16[2,2,16,1024]{3,2,1,0:T(8,128)(2,1)S(1)}, bf16[2,2,16,1024]{3,2,1,0:T(8,128)(2,1)S(1)}, u32[]{:S(2)}, u32[]{:S(2)}) %collective-permute-start.7) | collective-permute-done | bytes 131104 | tf_op jit(solution)/shard_map/ppermute | solution.py:344
  31.8 3.6 %collective-permute-start.6 = (bf16[2,2,16,1024]{3,2,1,0:T(8,128)(2,1)S(1)}, bf16[2,2,16,1024]{3,2,1,0:T(8,128)(2,1)S(1)}, u32[]{:S(2)}, u32[]{:S(2)}) collective-permute-start(bf16[2,2,16,1024]{3,2,1,0:T(8,128)(2,1)S(1)} %get-tuple-element.132), channel_id=1, source_target_pairs={{0,5},{1,4},{2,7},{3,6},{4,1},{5,0},{6,3},{7,2},{8,13},{9,12},{10,... | collective-permute-start | bytes 393224 | tf_op jit(solution)/shard_map/ppermute | solution.py:344
  35.4 2.4 %collective-permute-start.8 = (bf16[2,2,16,1024]{3,2,1,0:T(8,128)(2,1)S(1)}, bf16[2,2,16,1024]{3,2,1,0:T(8,128)(2,1)S(1)}, u32[]{:S(2)}, u32[]{:S(2)}) collective-permute-start(bf16[2,2,16,1024]{3,2,1,0:T(8,128)(2,1)S(1)} %get-tuple-element.135), channel_id=1, source_target_pairs={{0,6},{1,7},{2,4},{3,5},{4,2},{5,3},{6,0},{7,1},{8,14},{9,15},{10,... | collective-permute-start | bytes 393224 | tf_op jit(solution)/shard_map/ppermute | solution.py:344
  39.7 6.5 %shard_map.69 = (bf16[256,1024]{1,0:T(8,128)(2,1)S(1)}, bf16[256,1024]{1,0:T(8,128)(2,1)S(1)}, bf16[256,1024]{1,0:T(8,128)(2,1)S(1)}, bf16[256,1024]{1,0:T(8,128...) custom-call(bf16[2,4,16,1024]{3,2,1,0:T(8,128)(2,1)S(1)} %get-tuple-element.202.refs_0_, ...), custom_call_target="tpu_custom_call" | custom-call | flops 3758096384 | bytes 12582912 | tf_op jit(solution)/shard_map/pallas_call | solution.py:288
  46.2 2.2 %shard_map.70 = (bf16[2,16,1024]{2,1,0:T(8,128)(2,1)S(1)}, bf16[2,16,1024]{2,1,0:T(8,128)(2,1)S(1)}, bf16[2,16,1024]{2,1,0:T(8,128)(2,1)S(1)}, bf16[2,16,1024]{2...) custom-call(bf16[2,4,16,1024]{3,2,1,0:T(8,128)(2,1)S(1)} %get-tuple-, ...), custom_call_target="tpu_custom_call" | custom-call | flops 1610612736 | bytes 8388608 | tf_op jit(solution)/shard_map/pallas_call | solution.py:329
  48.6 3.3 %collective-permute-done.6.refs_5_ = bf16[2,2,16,1024]{3,2,1,0:T(8,128)(2,1)S(1)} collective-permute-done((bf16[2,2,16,1024]{3,2,1,0:T(8,128)(2,1)S(1)}, bf16[2,2,16,1024]{3,2,1,0:T(8,128)(2,1)S(1)}, u32[]{:S(2)}, u32[]{:S(2)}) %collective-permute-start.6) | collective-permute-done | bytes 131104 | tf_op jit(solution)/shard_map/ppermute | solution.py:344
  52.0 6.7 %shard_map.71 = (bf16[256,1024]{1,0:T(8,128)(2,1)S(1)}, bf16[256,1024]{1,0:T(8,128)(2,1)S(1)}, bf16[256,1024]{1,0:T(8,128)(2,1)S(1)}, bf16[256,1024]{1,0:T(8,128...) custom-call(bf16[2,4,16,1024]{3,2,1,0:T(8,128)(2,1)S(1)} %get-tuple-element.202.refs_0_, ...), custom_call_target="tpu_custom_call" | custom-call | flops 3758096384 | bytes 12582912 | tf_op jit(solution)/shard_map/pallas_call | solution.py:288
  71.6 2.2 %shard_map.78 = (bf16[4,16,1024]{2,1,0:T(8,128)(2,1)S(1)}, bf16[4,16,1024]{2,1,0:T(8,128)(2,1)S(1)}, bf16[4,16,1024]{2,1,0:T(8,128)(2,1)S(1)}, bf16[4,16,1024]{2...) custom-call(bf16[2,4,16,1024]{3,2,1,0:T(8,128)(2,1)S(1)} %get-tuple-, ...), custom_call_target="tpu_custom_call" | custom-call | flops 1610612736 | bytes 8388608 | tf_op jit(solution)/shard_map/pallas_call | solution.py:329
  73.8 7.1 %collective-permute-start.15 = (bf16[4,16,1024]{2,1,0:T(8,128)(2,1)S(1)}, bf16[4,16,1024]{2,1,0:T(8,128)(2,1)S(1)}, u32[]{:S(2)}, u32[]{:S(2)}) collective-permute-start(bf16[4,16,1024]{2,1,0:T(8,128)(2,1)S(1)} %get-tuple-element.218), channel_id=1, source_target_pairs={{0,5},{1,4},{2,7},{3,6},{4,1},{5,0},{6,3},{7,2},{8,13},{9,12},{10,... | collective-permute-start | bytes 393224 | tf_op jit(solution)/shard_map/ppermute | solution.py:344
  81.9 4.3 %collective-permute-start.17 = (bf16[4,16,1024]{2,1,0:T(8,128)(2,1)S(1)}, bf16[4,16,1024]{2,1,0:T(8,128)(2,1)S(1)}, u32[]{:S(2)}, u32[]{:S(2)}) collective-permute-start(bf16[4,16,1024]{2,1,0:T(8,128)(2,1)S(1)} %get-tuple-element.220), channel_id=1, source_target_pairs={{0,7},{1,6},{2,5},{3,4},{4,3},{5,2},{6,1},{7,0},{8,15},{9,14},{10,... | collective-permute-start | bytes 393224 | tf_op jit(solution)/shard_map/ppermute | solution.py:344
  86.1 7.3 %collective-permute-done.15.refs_5_ = bf16[4,16,1024]{2,1,0:T(8,128)(2,1)S(1)} collective-permute-done((bf16[4,16,1024]{2,1,0:T(8,128)(2,1)S(1)}, bf16[4,16,1024]{2,1,0:T(8,128)(2,1)S(1)}, u32[]{:S(2)}, u32[]{:S(2)}) %collective-permute-start.15) | collective-permute-done | bytes 131104 | tf_op jit(solution)/shard_map/ppermute | solution.py:344
  93.4 5.1 %collective-permute-done.14.refs_1_ = bf16[2,4,32,1792]{3,2,1,0:T(8,128)(2,1)S(1)} collective-permute-done((bf16[2,4,32,1792]{3,2,1,0:T(8,128)(2,1)S(1)}, bf16[2,4,32,1792]{3,2,1,0:T(8,128)(2,1)S(1)}, u32[]{:S(2)}, u32[]{:S(2)}) %collective-permute-start.14) | collective-permute-done | bytes 917536 | tf_op jit(solution)/shard_map/ppermute | solution.py:344
  101.5 4.8 %collective-permute-start.20 = (bf16[4,16,1024]{2,1,0:T(8,128)(2,1)S(1)}, bf16[4,16,1024]{2,1,0:T(8,128)(2,1)S(1)}, u32[]{:S(2)}, u32[]{:S(2)}) collective-permute-start(bf16[4,16,1024]{2,1,0:T(8,128)(2,1)S(1)} %get-tuple-element.228), channel_id=1, source_target_pairs={{0,2},{1,3},{2,0},{3,1},{4,6},{5,7},{6,4},{7,5},{8,10},{9,11},{10,... | collective-permute-start | bytes 393224 | tf_op jit(solution)/shard_map/ppermute | solution.py:344
  106.3 2.8 %collective-permute-start.21 = (bf16[4,16,1024]{2,1,0:T(8,128)(2,1)S(1)}, bf16[4,16,1024]{2,1,0:T(8,128)(2,1)S(1)}, u32[]{:S(2)}, u32[]{:S(2)}) collective-permute-start(bf16[4,16,1024]{2,1,0:T(8,128)(2,1)S(1)} %get-tuple-element.230), channel_id=1, source_target_pairs={{0,4},{1,5},{2,6},{3,7},{4,0},{5,1},{6,2},{7,3},{8,12},{9,13},{10,... | collective-permute-start | bytes 393224 | tf_op jit(solution)/shard_map/ppermute | solution.py:344
  110.6 2.9 %collective-permute-done.21.refs_4_ = bf16[4,16,1024]{2,1,0:T(8,128)(2,1)S(1)} collective-permute-done((bf16[4,16,1024]{2,1,0:T(8,128)(2,1)S(1)}, bf16[4,16,1024]{2,1,0:T(8,128)(2,1)S(1)}, u32[]{:S(2)}, u32[]{:S(2)}) %collective-permute-start.21) | collective-permute-done | bytes 131104 | tf_op jit(solution)/shard_map/ppermute | solution.py:344
  114.3 5.1 %collective-permute-start.26 = (bf16[32,4096]{1,0:T(8,128)(2,1)S(1)}, bf16[32,4096]{1,0:T(8,128)(2,1)S(1)}, u32[]{:S(2)}, u32[]{:S(2)}) collective-permute-start(bf16[32,4096]{1,0:T(8,128)(2,1)S(1)} %get-tuple-element.234), channel_id=1, source_target_pairs={{0,2},{1,3},{2,0},{3,1},{4,6},{5,7},{6,4},{7,5},{8,10},{9,11},{10,... | collective-permute-start | bytes 786440 | tf_op jit(solution)/shard_map/ppermute | solution.py:344
  119.4 2.0 %collective-permute-start.25 = (bf16[32,4096]{1,0:T(8,128)(2,1)S(1)}, bf16[32,4096]{1,0:T(8,128)(2,1)S(1)}, u32[]{:S(2)}, u32[]{:S(2)}) collective-permute-start(bf16[32,4096]{1,0:T(8,128)(2,1)S(1)} %get-tuple-element.235), channel_id=1, source_target_pairs={{0,4},{1,5},{2,6},{3,7},{4,0},{5,1},{6,2},{7,3},{8,12},{9,13},{10,... | collective-permute-start | bytes 786440 | tf_op jit(solution)/shard_map/ppermute | solution.py:344
  124.9 3.8 %collective-permute-done.22.refs_1_ = bf16[4,16,1024]{2,1,0:T(8,128)(2,1)S(1)} collective-permute-done((bf16[4,16,1024]{2,1,0:T(8,128)(2,1)S(1)}, bf16[4,16,1024]{2,1,0:T(8,128)(2,1)S(1)}, u32[]{:S(2)}, u32[]{:S(2)}) %collective-permute-start.22) | collective-permute-done | bytes 131104 | tf_op jit(solution)/shard_map/ppermute | solution.py:344
  128.6 8.6 %collective-permute-done.23.refs_3_ = bf16[4,16,1024]{2,1,0:T(8,128)(2,1)S(1)} collective-permute-done((bf16[4,16,1024]{2,1,0:T(8,128)(2,1)S(1)}, bf16[4,16,1024]{2,1,0:T(8,128)(2,1)S(1)}, u32[]{:S(2)}, u32[]{:S(2)}) %collective-permute-start.23) | collective-permute-done | bytes 131104 | tf_op jit(solution)/shard_map/ppermute | solution.py:344
  (54 shorter events, 35.9 us)
Async XLA Ops:
  3.8 15.0 %collective-permute-start.5 = (bf16[2,2,16,1024]{3,2,1,0:T(8,128)(2,1)S(1)}, bf16[2,2,16,1024]{3,2,1,0:T(8,128)(2,1)S(1)}, u32[]{:S(2)}, u32[]{:S(2)}) collective-permute-start(bf16[2,2,16,1024]{3,2,1,0:T(8,128)(2,1)S(1)} %get-tuple-element.131), channel_id=1, source_target_pairs={{0,5},{1,4},{2,7},{3,6},{4,1},{5,0},{6,3},{7,2},{8,13},{9,12},{10,... | collective-permute-start | bytes 393224 | tf_op jit(solution)/shard_map/ppermute | solution.py:344
  8.9 22.9 %collective-permute-start = (bf16[2,4,16,1024]{3,2,1,0:T(8,128)(2,1)S(1)}, bf16[2,4,16,1024]{3,2,1,0:T(8,128)(2,1)S(1)}, u32[]{:S(2)}, u32[]{:S(2)}) collective-permute-start(bf16[2,4,16,1024]{3,2,1,0:T(8,128)(2,1)S(1)} %get-tuple-element.124), channel_id=1, source_target_pairs={{0,1},{1,0},{2,3},{3,2},{4,5},{5,4},{6,7},{7,6},{8,9},{9,8},{10,11... | collective-permute-start | bytes 786440 | tf_op jit(solution)/shard_map/ppermute | solution.py:344
  9.4 12.3 %collective-permute-start.3 = (bf16[2,2,16,1024]{3,2,1,0:T(8,128)(2,1)S(1)}, bf16[2,2,16,1024]{3,2,1,0:T(8,128)(2,1)S(1)}, u32[]{:S(2)}, u32[]{:S(2)}) collective-permute-start(bf16[2,2,16,1024]{3,2,1,0:T(8,128)(2,1)S(1)} %get-tuple-element.128), channel_id=1, source_target_pairs={{0,4},{1,5},{2,6},{3,7},{4,0},{5,1},{6,2},{7,3},{8,12},{9,13},{10,... | collective-permute-start | bytes 393224 | tf_op jit(solution)/shard_map/ppermute | solution.py:344
  9.5 28.2 %collective-permute-start.1 = (bf16[2,4,16,1024]{3,2,1,0:T(8,128)(2,1)S(1)}, bf16[2,4,16,1024]{3,2,1,0:T(8,128)(2,1)S(1)}, u32[]{:S(2)}, u32[]{:S(2)}) collective-permute-start(bf16[2,4,16,1024]{3,2,1,0:T(8,128)(2,1)S(1)} %get-tuple-element.125), channel_id=1, source_target_pairs={{0,2},{1,3},{2,0},{3,1},{4,6},{5,7},{6,4},{7,5},{8,10},{9,11},{10,... | collective-permute-start | bytes 786440 | tf_op jit(solution)/shard_map/ppermute | solution.py:344
  11.3 26.4 %collective-permute-start.2 = (bf16[2,4,16,1024]{3,2,1,0:T(8,128)(2,1)S(1)}, bf16[2,4,16,1024]{3,2,1,0:T(8,128)(2,1)S(1)}, u32[]{:S(2)}, u32[]{:S(2)}) collective-permute-start(bf16[2,4,16,1024]{3,2,1,0:T(8,128)(2,1)S(1)} %get-tuple-element.126), channel_id=1, source_target_pairs={{0,3},{1,2},{2,1},{3,0},{4,7},{5,6},{6,5},{7,4},{8,11},{9,10},{10,... | collective-permute-start | bytes 786440 | tf_op jit(solution)/shard_map/ppermute | solution.py:344
  18.9 12.9 %collective-permute-start.7 = (bf16[2,2,16,1024]{3,2,1,0:T(8,128)(2,1)S(1)}, bf16[2,2,16,1024]{3,2,1,0:T(8,128)(2,1)S(1)}, u32[]{:S(2)}, u32[]{:S(2)}) collective-permute-start(bf16[2,2,16,1024]{3,2,1,0:T(8,128)(2,1)S(1)} %get-tuple-element.134), channel_id=1, source_target_pairs={{0,6},{1,7},{2,4},{3,5},{4,2},{5,3},{6,0},{7,1},{8,14},{9,15},{10,... | collective-permute-start | bytes 393224 | tf_op jit(solution)/shard_map/ppermute | solution.py:344
  21.7 13.7 %collective-permute-start.9 = (bf16[2,2,16,1024]{3,2,1,0:T(8,128)(2,1)S(1)}, bf16[2,2,16,1024]{3,2,1,0:T(8,128)(2,1)S(1)}, u32[]{:S(2)}, u32[]{:S(2)}) collective-permute-start(bf16[2,2,16,1024]{3,2,1,0:T(8,128)(2,1)S(1)} %get-tuple-element.138), channel_id=1, source_target_pairs={{0,7},{1,6},{2,5},{3,4},{4,3},{5,2},{6,1},{7,0},{8,15},{9,14},{10,... | collective-permute-start | bytes 393224 | tf_op jit(solution)/shard_map/ppermute | solution.py:344
  31.8 16.8 %collective-permute-start.4 = (bf16[2,2,16,1024]{3,2,1,0:T(8,128)(2,1)S(1)}, bf16[2,2,16,1024]{3,2,1,0:T(8,128)(2,1)S(1)}, u32[]{:S(2)}, u32[]{:S(2)}) collective-permute-start(bf16[2,2,16,1024]{3,2,1,0:T(8,128)(2,1)S(1)} %get-tuple-element.129), channel_id=1, source_target_pairs={{0,4},{1,5},{2,6},{3,7},{4,0},{5,1},{6,2},{7,3},{8,12},{9,13},{10,... | collective-permute-start | bytes 393224 | tf_op jit(solution)/shard_map/ppermute | solution.py:344
  31.8 20.2 %collective-permute-start.6 = (bf16[2,2,16,1024]{3,2,1,0:T(8,128)(2,1)S(1)}, bf16[2,2,16,1024]{3,2,1,0:T(8,128)(2,1)S(1)}, u32[]{:S(2)}, u32[]{:S(2)}) collective-permute-start(bf16[2,2,16,1024]{3,2,1,0:T(8,128)(2,1)S(1)} %get-tuple-element.132), channel_id=1, source_target_pairs={{0,5},{1,4},{2,7},{3,6},{4,1},{5,0},{6,3},{7,2},{8,13},{9,12},{10,... | collective-permute-start | bytes 393224 | tf_op jit(solution)/shard_map/ppermute | solution.py:344
  35.4 16.6 %collective-permute-start.8 = (bf16[2,2,16,1024]{3,2,1,0:T(8,128)(2,1)S(1)}, bf16[2,2,16,1024]{3,2,1,0:T(8,128)(2,1)S(1)}, u32[]{:S(2)}, u32[]{:S(2)}) collective-permute-start(bf16[2,2,16,1024]{3,2,1,0:T(8,128)(2,1)S(1)} %get-tuple-element.135), channel_id=1, source_target_pairs={{0,6},{1,7},{2,4},{3,5},{4,2},{5,3},{6,0},{7,1},{8,14},{9,15},{10,... | collective-permute-start | bytes 393224 | tf_op jit(solution)/shard_map/ppermute | solution.py:344
  37.8 14.2 %collective-permute-start.10 = (bf16[2,2,16,1024]{3,2,1,0:T(8,128)(2,1)S(1)}, bf16[2,2,16,1024]{3,2,1,0:T(8,128)(2,1)S(1)}, u32[]{:S(2)}, u32[]{:S(2)}) collective-permute-start(bf16[2,2,16,1024]{3,2,1,0:T(8,128)(2,1)S(1)} %get-tuple-element.139), channel_id=1, source_target_pairs={{0,7},{1,6},{2,5},{3,4},{4,3},{5,2},{6,1},{7,0},{8,15},{9,14},{10,... | collective-permute-start | bytes 393224 | tf_op jit(solution)/shard_map/ppermute | solution.py:344
  66.4 32.1 %collective-permute-start.13 = (bf16[4,2,32,2304]{3,2,1,0:T(8,128)(2,1)S(1)}, bf16[4,2,32,2304]{3,2,1,0:T(8,128)(2,1)S(1)}, u32[]{:S(2)}, u32[]{:S(2)}) collective-permute-start(bf16[4,2,32,2304]{3,2,1,0:T(8,128)(2,1)S(1)} %get-tuple-element.217), channel_id=1, source_target_pairs={{0,16},{8,24},{16,0},{24,8},{1,17},{9,25},{17,1},{25,9},{2,18},{10... | collective-permute-start | bytes 3538952 | tf_op jit(solution)/shard_map/ppermute | solution.py:344
  70.6 27.8 %collective-permute-start.14 = (bf16[2,4,32,1792]{3,2,1,0:T(8,128)(2,1)S(1)}, bf16[2,4,32,1792]{3,2,1,0:T(8,128)(2,1)S(1)}, u32[]{:S(2)}, u32[]{:S(2)}) collective-permute-start(bf16[2,4,32,1792]{3,2,1,0:T(8,128)(2,1)S(1)} %get-tuple-element.201), channel_id=1, source_target_pairs={{0,1},{1,0},{2,3},{3,2},{4,5},{5,4},{6,7},{7,6},{8,9},{9,8},{10,11... | collective-permute-start | bytes 2752520 | tf_op jit(solution)/shard_map/ppermute | solution.py:344
  73.8 19.6 %collective-permute-start.15 = (bf16[4,16,1024]{2,1,0:T(8,128)(2,1)S(1)}, bf16[4,16,1024]{2,1,0:T(8,128)(2,1)S(1)}, u32[]{:S(2)}, u32[]{:S(2)}) collective-permute-start(bf16[4,16,1024]{2,1,0:T(8,128)(2,1)S(1)} %get-tuple-element.218), channel_id=1, source_target_pairs={{0,5},{1,4},{2,7},{3,6},{4,1},{5,0},{6,3},{7,2},{8,13},{9,12},{10,... | collective-permute-start | bytes 393224 | tf_op jit(solution)/shard_map/ppermute | solution.py:344
  80.9 12.5 %collective-permute-start.16 = (bf16[4,16,1024]{2,1,0:T(8,128)(2,1)S(1)}, bf16[4,16,1024]{2,1,0:T(8,128)(2,1)S(1)}, u32[]{:S(2)}, u32[]{:S(2)}) collective-permute-start(bf16[4,16,1024]{2,1,0:T(8,128)(2,1)S(1)} %get-tuple-element.219), channel_id=1, source_target_pairs={{0,6},{1,7},{2,4},{3,5},{4,2},{5,3},{6,0},{7,1},{8,14},{9,15},{10,... | collective-permute-start | bytes 393224 | tf_op jit(solution)/shard_map/ppermute | solution.py:344
  81.9 11.6 %collective-permute-start.17 = (bf16[4,16,1024]{2,1,0:T(8,128)(2,1)S(1)}, bf16[4,16,1024]{2,1,0:T(8,128)(2,1)S(1)}, u32[]{:S(2)}, u32[]{:S(2)}) collective-permute-start(bf16[4,16,1024]{2,1,0:T(8,128)(2,1)S(1)} %get-tuple-element.220), channel_id=1, source_target_pairs={{0,7},{1,6},{2,5},{3,4},{4,3},{5,2},{6,1},{7,0},{8,15},{9,14},{10,... | collective-permute-start | bytes 393224 | tf_op jit(solution)/shard_map/ppermute | solution.py:344
  99.2 14.4 %collective-permute-start.18 = (bf16[4,32,2304]{2,1,0:T(8,128)(2,1)S(1)}, bf16[4,32,2304]{2,1,0:T(8,128)(2,1)S(1)}, u32[]{:S(2)}, u32[]{:S(2)}) collective-permute-start(bf16[4,32,2304]{2,1,0:T(8,128)(2,1)S(1)} %get-tuple-element.223), channel_id=1, source_target_pairs={{0,1},{1,0},{2,3},{3,2},{4,5},{5,4},{6,7},{7,6},{8,9},{9,8},{10,11... | collective-permute-start | bytes 1769480 | tf_op jit(solution)/shard_map/ppermute | solution.py:344
  100.9 12.7 %collective-permute-start.19 = (bf16[4,32,1792]{2,1,0:T(8,128)(2,1)S(1)}, bf16[4,32,1792]{2,1,0:T(8,128)(2,1)S(1)}, u32[]{:S(2)}, u32[]{:S(2)}) collective-permute-start(bf16[4,32,1792]{2,1,0:T(8,128)(2,1)S(1)} %get-tuple-element.226), channel_id=1, source_target_pairs={{0,16},{8,24},{16,0},{24,8},{1,17},{9,25},{17,1},{25,9},{2,18},{10... | collective-permute-start | bytes 1376264 | tf_op jit(solution)/shard_map/ppermute | solution.py:344
  101.5 9.1 %collective-permute-start.20 = (bf16[4,16,1024]{2,1,0:T(8,128)(2,1)S(1)}, bf16[4,16,1024]{2,1,0:T(8,128)(2,1)S(1)}, u32[]{:S(2)}, u32[]{:S(2)}) collective-permute-start(bf16[4,16,1024]{2,1,0:T(8,128)(2,1)S(1)} %get-tuple-element.228), channel_id=1, source_target_pairs={{0,2},{1,3},{2,0},{3,1},{4,6},{5,7},{6,4},{7,5},{8,10},{9,11},{10,... | collective-permute-start | bytes 393224 | tf_op jit(solution)/shard_map/ppermute | solution.py:344
  106.3 7.3 %collective-permute-start.21 = (bf16[4,16,1024]{2,1,0:T(8,128)(2,1)S(1)}, bf16[4,16,1024]{2,1,0:T(8,128)(2,1)S(1)}, u32[]{:S(2)}, u32[]{:S(2)}) collective-permute-start(bf16[4,16,1024]{2,1,0:T(8,128)(2,1)S(1)} %get-tuple-element.230), channel_id=1, source_target_pairs={{0,4},{1,5},{2,6},{3,7},{4,0},{5,1},{6,2},{7,3},{8,12},{9,13},{10,... | collective-permute-start | bytes 393224 | tf_op jit(solution)/shard_map/ppermute | solution.py:344
  114.3 24.5 %collective-permute-start.26 = (bf16[32,4096]{1,0:T(8,128)(2,1)S(1)}, bf16[32,4096]{1,0:T(8,128)(2,1)S(1)}, u32[]{:S(2)}, u32[]{:S(2)}) collective-permute-start(bf16[32,4096]{1,0:T(8,128)(2,1)S(1)} %get-tuple-element.234), channel_id=1, source_target_pairs={{0,2},{1,3},{2,0},{3,1},{4,6},{5,7},{6,4},{7,5},{8,10},{9,11},{10,... | collective-permute-start | bytes 786440 | tf_op jit(solution)/shard_map/ppermute | solution.py:344
  119.4 21.0 %collective-permute-start.25 = (bf16[32,4096]{1,0:T(8,128)(2,1)S(1)}, bf16[32,4096]{1,0:T(8,128)(2,1)S(1)}, u32[]{:S(2)}, u32[]{:S(2)}) collective-permute-start(bf16[32,4096]{1,0:T(8,128)(2,1)S(1)} %get-tuple-element.235), channel_id=1, source_target_pairs={{0,4},{1,5},{2,6},{3,7},{4,0},{5,1},{6,2},{7,3},{8,12},{9,13},{10,... | collective-permute-start | bytes 786440 | tf_op jit(solution)/shard_map/ppermute | solution.py:344
  121.4 19.0 %collective-permute-start.24 = (bf16[32,4096]{1,0:T(8,128)(2,1)S(1)}, bf16[32,4096]{1,0:T(8,128)(2,1)S(1)}, u32[]{:S(2)}, u32[]{:S(2)}) collective-permute-start(bf16[32,4096]{1,0:T(8,128)(2,1)S(1)} %get-tuple-element.236), channel_id=1, source_target_pairs={{0,6},{1,7},{2,4},{3,5},{4,2},{5,3},{6,0},{7,1},{8,14},{9,15},{10,... | collective-permute-start | bytes 786440 | tf_op jit(solution)/shard_map/ppermute | solution.py:344
  124.3 13.0 %collective-permute-start.23 = (bf16[4,16,1024]{2,1,0:T(8,128)(2,1)S(1)}, bf16[4,16,1024]{2,1,0:T(8,128)(2,1)S(1)}, u32[]{:S(2)}, u32[]{:S(2)}) collective-permute-start(bf16[4,16,1024]{2,1,0:T(8,128)(2,1)S(1)} %get-tuple-element.239), channel_id=1, source_target_pairs={{0,3},{1,2},{2,1},{3,0},{4,7},{5,6},{6,5},{7,4},{8,11},{9,10},{10,... | collective-permute-start | bytes 393224 | tf_op jit(solution)/shard_map/ppermute | solution.py:344
  (6 other events, 38.0 us)

commit v13 on v12

--- a/solution.py
+++ b/solution.py
@@ -423,10 +423,11 @@
     second = swap(sent, "clip", n_clip_devices, CORES)
     first, second = after((first, second), back)
     total, *sent = join(ids, (own_first, first), (own_second, second), n_z)
-    others = [swap(sent[j - 1], "tm", n_tm, j * N_Y) for j in reversed(range(1, n_z))]
     back[0] = dx[0]
     for k in late:
         back[k] = swap(after(dx[k], sent), "tm", n_tm, k)
+    sent[0] = after(sent[0], back[1])
+    others = [swap(sent[j - 1], "tm", n_tm, j * N_Y) for j in reversed(range(1, n_z))]
     grad_clips = place(ids, [back[k] for k in range(n_tm)]).reshape(clips.shape)
     grad_qkv, grad_out = finish((total, *others))
     return (grad_clips, grad_qkv, grad_out)

time: 143 us -> 146 us (1.021)
  waiting for transfers between devices: 45.4 us -> 49 us
    ppermute x27, waiting for transfers between devices: 45.4 us -> 49 us  [swap(): return lax.ppermute(block, axis, [(i, i ^ distance) for i in range(size)])]
  transfers between devices with their start and end apart: 27 -> 27, of which waited for: 12 -> 10; matrix products, arithmetic and copies ran while one was open for 0% -> 0% of each run, Pallas kernels for 17% -> 16%
where the time goes in v13:
time: 146 us; the launch traced here: 145 us
  starting transfers between devices  57.9 us (40%)
  waiting for transfers between devices  49 us (34%)
  Pallas kernels  35.2 us (24%)
  local copies, waits for them, and re-layouts  2.45 us (2%)
    ppermute x27, starting transfers between devices, swap(): return lax.ppermute(block, axis, [(i, i ^ distance) for i in range(size)])  57.9 us
    ppermute x27, waiting for transfers between devices, swap(): return lax.ppermute(block, axis, [(i, i ^ distance) for i in range(size)])  49 us
    pallas_call x2, Pallas kernels, sublayer(): pl.pallas_call(functools.partial(sublayer_kernel, at, n_clips, n_position...  13.2 us
    pallas_call x4, Pallas kernels, products(): pl.pallas_call(functools.partial(product_kernel, n_x, flip, n_chunks, spa...  7.54 us
    pallas_call x2, Pallas kernels, input_gradient(): pl.pallas_call(functools.partial(input_kernel, at, n_clips, len(pieces),...  4.34 us
    pallas_call x4, Pallas kernels, halve(): pl.pallas_call(functools.partial(halve_kernel, dim, axis, stride), out_sh...  3.42 us
  transfers between devices with their start and end apart: 27, of which 10 were waited for; matrix products, arithmetic and copies ran while one was open for 0% of the time, Pallas kernels for 16%

profile of v13, /device:TPU:0, one launch (start us, length us, event | category | flops | bytes accessed | tf_op | source)
XLA Modules:
  0.0 145.3 jit_solution(1808095222559288423)
XLA Ops:
  3.8 5.1 %collective-permute-start.5 = (bf16[2,2,16,1024]{3,2,1,0:T(8,128)(2,1)S(1)}, bf16[2,2,16,1024]{3,2,1,0:T(8,128)(2,1)S(1)}, u32[]{:S(2)}, u32[]{:S(2)}) collective-permute-start(bf16[2,2,16,1024]{3,2,1,0:T(8,128)(2,1)S(1)} %get-tuple-element.132), channel_id=1, source_target_pairs={{0,5},{1,4},{2,7},{3,6},{4,1},{5,0},{6,3},{7,2},{8,13},{9,12},{10,... | collective-permute-start | bytes 393224 | tf_op jit(solution)/shard_map/ppermute | solution.py:344
  12.7 6.1 %collective-permute-done.5.refs_5_ = bf16[2,2,16,1024]{3,2,1,0:T(8,128)(2,1)S(1)} collective-permute-done((bf16[2,2,16,1024]{3,2,1,0:T(8,128)(2,1)S(1)}, bf16[2,2,16,1024]{3,2,1,0:T(8,128)(2,1)S(1)}, u32[]{:S(2)}, u32[]{:S(2)}) %collective-permute-start.5) | collective-permute-done | bytes 131104 | tf_op jit(solution)/shard_map/ppermute | solution.py:344
  18.9 2.8 %collective-permute-start.7 = (bf16[2,2,16,1024]{3,2,1,0:T(8,128)(2,1)S(1)}, bf16[2,2,16,1024]{3,2,1,0:T(8,128)(2,1)S(1)}, u32[]{:S(2)}, u32[]{:S(2)}) collective-permute-start(bf16[2,2,16,1024]{3,2,1,0:T(8,128)(2,1)S(1)} %get-tuple-element.135), channel_id=1, source_target_pairs={{0,6},{1,7},{2,4},{3,5},{4,2},{5,3},{6,0},{7,1},{8,14},{9,15},{10,... | collective-permute-start | bytes 393224 | tf_op jit(solution)/shard_map/ppermute | solution.py:344
  21.7 2.7 %collective-permute-start.9 = (bf16[2,2,16,1024]{3,2,1,0:T(8,128)(2,1)S(1)}, bf16[2,2,16,1024]{3,2,1,0:T(8,128)(2,1)S(1)}, u32[]{:S(2)}, u32[]{:S(2)}) collective-permute-start(bf16[2,2,16,1024]{3,2,1,0:T(8,128)(2,1)S(1)} %get-tuple-element.139), channel_id=1, source_target_pairs={{0,7},{1,6},{2,5},{3,4},{4,3},{5,2},{6,1},{7,0},{8,15},{9,14},{10,... | collective-permute-start | bytes 393224 | tf_op jit(solution)/shard_map/ppermute | solution.py:344
  24.4 2.8 %shard_map.68.refs_8_ = bf16[1024,3072]{1,0:T(8,128)(2,1)S(1)} custom-call(bf16[1024,3072]{1,0:T(8,128)(2,1)} %w_ref.1), custom_call_target="tpu_custom_call" | custom-call | tf_op jit(solution)/shard_map/pallas_call | solution.py:72
  27.2 4.6 %collective-permute-done.7.refs_6_ = bf16[2,2,16,1024]{3,2,1,0:T(8,128)(2,1)S(1)} collective-permute-done((bf16[2,2,16,1024]{3,2,1,0:T(8,128)(2,1)S(1)}, bf16[2,2,16,1024]{3,2,1,0:T(8,128)(2,1)S(1)}, u32[]{:S(2)}, u32[]{:S(2)}) %collective-permute-start.7) | collective-permute-done | bytes 131104 | tf_op jit(solution)/shard_map/ppermute | solution.py:344
  31.8 3.6 %collective-permute-start.6 = (bf16[2,2,16,1024]{3,2,1,0:T(8,128)(2,1)S(1)}, bf16[2,2,16,1024]{3,2,1,0:T(8,128)(2,1)S(1)}, u32[]{:S(2)}, u32[]{:S(2)}) collective-permute-start(bf16[2,2,16,1024]{3,2,1,0:T(8,128)(2,1)S(1)} %get-tuple-element.133), channel_id=1, source_target_pairs={{0,5},{1,4},{2,7},{3,6},{4,1},{5,0},{6,3},{7,2},{8,13},{9,12},{10,... | collective-permute-start | bytes 393224 | tf_op jit(solution)/shard_map/ppermute | solution.py:344
  35.4 2.4 %collective-permute-start.8 = (bf16[2,2,16,1024]{3,2,1,0:T(8,128)(2,1)S(1)}, bf16[2,2,16,1024]{3,2,1,0:T(8,128)(2,1)S(1)}, u32[]{:S(2)}, u32[]{:S(2)}) collective-permute-start(bf16[2,2,16,1024]{3,2,1,0:T(8,128)(2,1)S(1)} %get-tuple-element.136), channel_id=1, source_target_pairs={{0,6},{1,7},{2,4},{3,5},{4,2},{5,3},{6,0},{7,1},{8,14},{9,15},{10,... | collective-permute-start | bytes 393224 | tf_op jit(solution)/shard_map/ppermute | solution.py:344
  39.7 6.5 %shard_map.69 = (bf16[256,1024]{1,0:T(8,128)(2,1)S(1)}, bf16[256,1024]{1,0:T(8,128)(2,1)S(1)}, bf16[256,1024]{1,0:T(8,128)(2,1)S(1)}, bf16[256,1024]{1,0:T(8,128...) custom-call(bf16[2,4,16,1024]{3,2,1,0:T(8,128)(2,1)S(1)} %get-tuple-element.203.refs_0_, ...), custom_call_target="tpu_custom_call" | custom-call | flops 3758096384 | bytes 12582912 | tf_op jit(solution)/shard_map/pallas_call | solution.py:288
  46.2 2.2 %shard_map.70 = (bf16[2,16,1024]{2,1,0:T(8,128)(2,1)S(1)}, bf16[2,16,1024]{2,1,0:T(8,128)(2,1)S(1)}, bf16[2,16,1024]{2,1,0:T(8,128)(2,1)S(1)}, bf16[2,16,1024]{2...) custom-call(bf16[2,4,16,1024]{3,2,1,0:T(8,128)(2,1)S(1)} %get-tuple-, ...), custom_call_target="tpu_custom_call" | custom-call | flops 1610612736 | bytes 8388608 | tf_op jit(solution)/shard_map/pallas_call | solution.py:329
  48.6 3.3 %collective-permute-done.6.refs_5_ = bf16[2,2,16,1024]{3,2,1,0:T(8,128)(2,1)S(1)} collective-permute-done((bf16[2,2,16,1024]{3,2,1,0:T(8,128)(2,1)S(1)}, bf16[2,2,16,1024]{3,2,1,0:T(8,128)(2,1)S(1)}, u32[]{:S(2)}, u32[]{:S(2)}) %collective-permute-start.6) | collective-permute-done | bytes 131104 | tf_op jit(solution)/shard_map/ppermute | solution.py:344
  52.0 6.7 %shard_map.71 = (bf16[256,1024]{1,0:T(8,128)(2,1)S(1)}, bf16[256,1024]{1,0:T(8,128)(2,1)S(1)}, bf16[256,1024]{1,0:T(8,128)(2,1)S(1)}, bf16[256,1024]{1,0:T(8,128...) custom-call(bf16[2,4,16,1024]{3,2,1,0:T(8,128)(2,1)S(1)} %get-tuple-element.203.refs_0_, ...), custom_call_target="tpu_custom_call" | custom-call | flops 3758096384 | bytes 12582912 | tf_op jit(solution)/shard_map/pallas_call | solution.py:288
  58.7 2.0 %shard_map.72 = bf16[2,4,2,32,2304]{4,3,2,1,0:T(8,128)(2,1)S(1)} custom-call(s32[2]{0:T(128)S(1)} %pad_add_fusion.ids_ref, bf16[256,1024]{1,0:T(8,128)(2,1)S(1)} %get-tuple-element.194.refs_0_, bf16[256,1024]{1,0:T(8,128)(2,1)S(1)} %get-tuple-element.195.refs_1_, bf16[256,1024]{1,0:T(8,128)(2,1)S(1)} %get-tuple-element.187.refs_10_.refs_2_, ...), custom_call_target="tpu_custom_call" | custom-call | flops 301989888 | bytes 524288 | tf_op jit(solution)/shard_map/pallas_call | solution.py:123
  63.1 2.0 %shard_map.74.refs_0_ = bf16[2,4,2,32,2304]{4,3,2,1,0:T(8,128)(2,1)S(1)} custom-call(s32[2]{0:T(128)S(1)} %pad_add_fusion.ids_ref, bf16[256,1024]{1,0:T(8,128)(2,1)S(1)} %get-tuple-element.194.refs_0_, bf16[256,1024]{1,0:T(8,128)(2,1)S(1)} %get-tuple-element.195.refs_1_, bf16[256,1024]{1,0:T(8,128)(2,1)S(1)} %get-tuple-element.187.refs_10_.refs_2_, ...), custom_call_target="tpu_custom_call" | custom-call | flops 301989888 | bytes 524288 | tf_op jit(solution)/shard_map/pallas_call | solution.py:123
  71.6 2.2 %shard_map.78 = (bf16[4,16,1024]{2,1,0:T(8,128)(2,1)S(1)}, bf16[4,16,1024]{2,1,0:T(8,128)(2,1)S(1)}, bf16[4,16,1024]{2,1,0:T(8,128)(2,1)S(1)}, bf16[4,16,1024]{2...) custom-call(bf16[2,4,16,1024]{3,2,1,0:T(8,128)(2,1)S(1)} %get-tuple-, ...), custom_call_target="tpu_custom_call" | custom-call | flops 1610612736 | bytes 8388608 | tf_op jit(solution)/shard_map/pallas_call | solution.py:329
  73.8 7.1 %collective-permute-start.15 = (bf16[4,16,1024]{2,1,0:T(8,128)(2,1)S(1)}, bf16[4,16,1024]{2,1,0:T(8,128)(2,1)S(1)}, u32[]{:S(2)}, u32[]{:S(2)}) collective-permute-start(bf16[4,16,1024]{2,1,0:T(8,128)(2,1)S(1)} %get-tuple-element.219), channel_id=1, source_target_pairs={{0,5},{1,4},{2,7},{3,6},{4,1},{5,0},{6,3},{7,2},{8,13},{9,12},{10,... | collective-permute-start | bytes 393224 | tf_op jit(solution)/shard_map/ppermute | solution.py:344
  81.9 4.3 %collective-permute-start.17 = (bf16[4,16,1024]{2,1,0:T(8,128)(2,1)S(1)}, bf16[4,16,1024]{2,1,0:T(8,128)(2,1)S(1)}, u32[]{:S(2)}, u32[]{:S(2)}) collective-permute-start(bf16[4,16,1024]{2,1,0:T(8,128)(2,1)S(1)} %get-tuple-element.221), channel_id=1, source_target_pairs={{0,7},{1,6},{2,5},{3,4},{4,3},{5,2},{6,1},{7,0},{8,15},{9,14},{10,... | collective-permute-start | bytes 393224 | tf_op jit(solution)/shard_map/ppermute | solution.py:344
  86.1 7.3 %collective-permute-done.15.refs_5_ = bf16[4,16,1024]{2,1,0:T(8,128)(2,1)S(1)} collective-permute-done((bf16[4,16,1024]{2,1,0:T(8,128)(2,1)S(1)}, bf16[4,16,1024]{2,1,0:T(8,128)(2,1)S(1)}, u32[]{:S(2)}, u32[]{:S(2)}) %collective-permute-start.15) | collective-permute-done | bytes 131104 | tf_op jit(solution)/shard_map/ppermute | solution.py:344
  93.4 5.1 %collective-permute-done.14.refs_1_ = bf16[2,4,32,1792]{3,2,1,0:T(8,128)(2,1)S(1)} collective-permute-done((bf16[2,4,32,1792]{3,2,1,0:T(8,128)(2,1)S(1)}, bf16[2,4,32,1792]{3,2,1,0:T(8,128)(2,1)S(1)}, u32[]{:S(2)}, u32[]{:S(2)}) %collective-permute-start.14) | collective-permute-done | bytes 917536 | tf_op jit(solution)/shard_map/ppermute | solution.py:344
  101.5 4.8 %collective-permute-start.20 = (bf16[4,16,1024]{2,1,0:T(8,128)(2,1)S(1)}, bf16[4,16,1024]{2,1,0:T(8,128)(2,1)S(1)}, u32[]{:S(2)}, u32[]{:S(2)}) collective-permute-start(bf16[4,16,1024]{2,1,0:T(8,128)(2,1)S(1)} %get-tuple-element.229), channel_id=1, source_target_pairs={{0,2},{1,3},{2,0},{3,1},{4,6},{5,7},{6,4},{7,5},{8,10},{9,11},{10,... | collective-permute-start | bytes 393224 | tf_op jit(solution)/shard_map/ppermute | solution.py:344
  106.3 2.8 %collective-permute-start.21 = (bf16[4,16,1024]{2,1,0:T(8,128)(2,1)S(1)}, bf16[4,16,1024]{2,1,0:T(8,128)(2,1)S(1)}, u32[]{:S(2)}, u32[]{:S(2)}) collective-permute-start(bf16[4,16,1024]{2,1,0:T(8,128)(2,1)S(1)} %get-tuple-element.231), channel_id=1, source_target_pairs={{0,4},{1,5},{2,6},{3,7},{4,0},{5,1},{6,2},{7,3},{8,12},{9,13},{10,... | collective-permute-start | bytes 393224 | tf_op jit(solution)/shard_map/ppermute | solution.py:344
  110.6 2.9 %collective-permute-done.21.refs_4_ = bf16[4,16,1024]{2,1,0:T(8,128)(2,1)S(1)} collective-permute-done((bf16[4,16,1024]{2,1,0:T(8,128)(2,1)S(1)}, bf16[4,16,1024]{2,1,0:T(8,128)(2,1)S(1)}, u32[]{:S(2)}, u32[]{:S(2)}) %collective-permute-start.21) | collective-permute-done | bytes 131104 | tf_op jit(solution)/shard_map/ppermute | solution.py:344
  115.2 7.5 %collective-permute-start.25 = (bf16[32,4096]{1,0:T(8,128)(2,1)S(1)}, bf16[32,4096]{1,0:T(8,128)(2,1)S(1)}, u32[]{:S(2)}, u32[]{:S(2)}) collective-permute-start(bf16[32,4096]{1,0:T(8,128)(2,1)S(1)} %get-tuple-element.236), channel_id=1, source_target_pairs={{0,4},{1,5},{2,6},{3,7},{4,0},{5,1},{6,2},{7,3},{8,12},{9,13},{10,... | collective-permute-start | bytes 786440 | tf_op jit(solution)/shard_map/ppermute | solution.py:344
  125.3 17.6 %collective-permute-done.23.refs_3_ = bf16[4,16,1024]{2,1,0:T(8,128)(2,1)S(1)} collective-permute-done((bf16[4,16,1024]{2,1,0:T(8,128)(2,1)S(1)}, bf16[4,16,1024]{2,1,0:T(8,128)(2,1)S(1)}, u32[]{:S(2)}, u32[]{:S(2)}) %collective-permute-start.23) | collective-permute-done | bytes 131104 | tf_op jit(solution)/shard_map/ppermute | solution.py:344
  (54 shorter events, 30.3 us)
Async XLA Ops:
  3.8 15.0 %collective-permute-start.5 = (bf16[2,2,16,1024]{3,2,1,0:T(8,128)(2,1)S(1)}, bf16[2,2,16,1024]{3,2,1,0:T(8,128)(2,1)S(1)}, u32[]{:S(2)}, u32[]{:S(2)}) collective-permute-start(bf16[2,2,16,1024]{3,2,1,0:T(8,128)(2,1)S(1)} %get-tuple-element.132), channel_id=1, source_target_pairs={{0,5},{1,4},{2,7},{3,6},{4,1},{5,0},{6,3},{7,2},{8,13},{9,12},{10,... | collective-permute-start | bytes 393224 | tf_op jit(solution)/shard_map/ppermute | solution.py:344
  8.9 22.9 %collective-permute-start = (bf16[2,4,16,1024]{3,2,1,0:T(8,128)(2,1)S(1)}, bf16[2,4,16,1024]{3,2,1,0:T(8,128)(2,1)S(1)}, u32[]{:S(2)}, u32[]{:S(2)}) collective-permute-start(bf16[2,4,16,1024]{3,2,1,0:T(8,128)(2,1)S(1)} %get-tuple-element.125), channel_id=1, source_target_pairs={{0,1},{1,0},{2,3},{3,2},{4,5},{5,4},{6,7},{7,6},{8,9},{9,8},{10,11... | collective-permute-start | bytes 786440 | tf_op jit(solution)/shard_map/ppermute | solution.py:344
  9.4 12.3 %collective-permute-start.3 = (bf16[2,2,16,1024]{3,2,1,0:T(8,128)(2,1)S(1)}, bf16[2,2,16,1024]{3,2,1,0:T(8,128)(2,1)S(1)}, u32[]{:S(2)}, u32[]{:S(2)}) collective-permute-start(bf16[2,2,16,1024]{3,2,1,0:T(8,128)(2,1)S(1)} %get-tuple-element.129), channel_id=1, source_target_pairs={{0,4},{1,5},{2,6},{3,7},{4,0},{5,1},{6,2},{7,3},{8,12},{9,13},{10,... | collective-permute-start | bytes 393224 | tf_op jit(solution)/shard_map/ppermute | solution.py:344
  9.5 28.2 %collective-permute-start.1 = (bf16[2,4,16,1024]{3,2,1,0:T(8,128)(2,1)S(1)}, bf16[2,4,16,1024]{3,2,1,0:T(8,128)(2,1)S(1)}, u32[]{:S(2)}, u32[]{:S(2)}) collective-permute-start(bf16[2,4,16,1024]{3,2,1,0:T(8,128)(2,1)S(1)} %get-tuple-element.126), channel_id=1, source_target_pairs={{0,2},{1,3},{2,0},{3,1},{4,6},{5,7},{6,4},{7,5},{8,10},{9,11},{10,... | collective-permute-start | bytes 786440 | tf_op jit(solution)/shard_map/ppermute | solution.py:344
  11.3 26.4 %collective-permute-start.2 = (bf16[2,4,16,1024]{3,2,1,0:T(8,128)(2,1)S(1)}, bf16[2,4,16,1024]{3,2,1,0:T(8,128)(2,1)S(1)}, u32[]{:S(2)}, u32[]{:S(2)}) collective-permute-start(bf16[2,4,16,1024]{3,2,1,0:T(8,128)(2,1)S(1)} %get-tuple-element.127), channel_id=1, source_target_pairs={{0,3},{1,2},{2,1},{3,0},{4,7},{5,6},{6,5},{7,4},{8,11},{9,10},{10,... | collective-permute-start | bytes 786440 | tf_op jit(solution)/shard_map/ppermute | solution.py:344
  18.9 12.9 %collective-permute-start.7 = (bf16[2,2,16,1024]{3,2,1,0:T(8,128)(2,1)S(1)}, bf16[2,2,16,1024]{3,2,1,0:T(8,128)(2,1)S(1)}, u32[]{:S(2)}, u32[]{:S(2)}) collective-permute-start(bf16[2,2,16,1024]{3,2,1,0:T(8,128)(2,1)S(1)} %get-tuple-element.135), channel_id=1, source_target_pairs={{0,6},{1,7},{2,4},{3,5},{4,2},{5,3},{6,0},{7,1},{8,14},{9,15},{10,... | collective-permute-start | bytes 393224 | tf_op jit(solution)/shard_map/ppermute | solution.py:344
  21.7 13.7 %collective-permute-start.9 = (bf16[2,2,16,1024]{3,2,1,0:T(8,128)(2,1)S(1)}, bf16[2,2,16,1024]{3,2,1,0:T(8,128)(2,1)S(1)}, u32[]{:S(2)}, u32[]{:S(2)}) collective-permute-start(bf16[2,2,16,1024]{3,2,1,0:T(8,128)(2,1)S(1)} %get-tuple-element.139), channel_id=1, source_target_pairs={{0,7},{1,6},{2,5},{3,4},{4,3},{5,2},{6,1},{7,0},{8,15},{9,14},{10,... | collective-permute-start | bytes 393224 | tf_op jit(solution)/shard_map/ppermute | solution.py:344
  31.8 16.8 %collective-permute-start.4 = (bf16[2,2,16,1024]{3,2,1,0:T(8,128)(2,1)S(1)}, bf16[2,2,16,1024]{3,2,1,0:T(8,128)(2,1)S(1)}, u32[]{:S(2)}, u32[]{:S(2)}) collective-permute-start(bf16[2,2,16,1024]{3,2,1,0:T(8,128)(2,1)S(1)} %get-tuple-element.130), channel_id=1, source_target_pairs={{0,4},{1,5},{2,6},{3,7},{4,0},{5,1},{6,2},{7,3},{8,12},{9,13},{10,... | collective-permute-start | bytes 393224 | tf_op jit(solution)/shard_map/ppermute | solution.py:344
  31.8 20.2 %collective-permute-start.6 = (bf16[2,2,16,1024]{3,2,1,0:T(8,128)(2,1)S(1)}, bf16[2,2,16,1024]{3,2,1,0:T(8,128)(2,1)S(1)}, u32[]{:S(2)}, u32[]{:S(2)}) collective-permute-start(bf16[2,2,16,1024]{3,2,1,0:T(8,128)(2,1)S(1)} %get-tuple-element.133), channel_id=1, source_target_pairs={{0,5},{1,4},{2,7},{3,6},{4,1},{5,0},{6,3},{7,2},{8,13},{9,12},{10,... | collective-permute-start | bytes 393224 | tf_op jit(solution)/shard_map/ppermute | solution.py:344
  35.4 16.6 %collective-permute-start.8 = (bf16[2,2,16,1024]{3,2,1,0:T(8,128)(2,1)S(1)}, bf16[2,2,16,1024]{3,2,1,0:T(8,128)(2,1)S(1)}, u32[]{:S(2)}, u32[]{:S(2)}) collective-permute-start(bf16[2,2,16,1024]{3,2,1,0:T(8,128)(2,1)S(1)} %get-tuple-element.136), channel_id=1, source_target_pairs={{0,6},{1,7},{2,4},{3,5},{4,2},{5,3},{6,0},{7,1},{8,14},{9,15},{10,... | collective-permute-start | bytes 393224 | tf_op jit(solution)/shard_map/ppermute | solution.py:344
  37.8 14.2 %collective-permute-start.10 = (bf16[2,2,16,1024]{3,2,1,0:T(8,128)(2,1)S(1)}, bf16[2,2,16,1024]{3,2,1,0:T(8,128)(2,1)S(1)}, u32[]{:S(2)}, u32[]{:S(2)}) collective-permute-start(bf16[2,2,16,1024]{3,2,1,0:T(8,128)(2,1)S(1)} %get-tuple-element.140), channel_id=1, source_target_pairs={{0,7},{1,6},{2,5},{3,4},{4,3},{5,2},{6,1},{7,0},{8,15},{9,14},{10,... | collective-permute-start | bytes 393224 | tf_op jit(solution)/shard_map/ppermute | solution.py:344
  66.4 32.1 %collective-permute-start.13 = (bf16[4,2,32,2304]{3,2,1,0:T(8,128)(2,1)S(1)}, bf16[4,2,32,2304]{3,2,1,0:T(8,128)(2,1)S(1)}, u32[]{:S(2)}, u32[]{:S(2)}) collective-permute-start(bf16[4,2,32,2304]{3,2,1,0:T(8,128)(2,1)S(1)} %get-tuple-element.218), channel_id=1, source_target_pairs={{0,16},{8,24},{16,0},{24,8},{1,17},{9,25},{17,1},{25,9},{2,18},{10... | collective-permute-start | bytes 3538952 | tf_op jit(solution)/shard_map/ppermute | solution.py:344
  70.6 27.8 %collective-permute-start.14 = (bf16[2,4,32,1792]{3,2,1,0:T(8,128)(2,1)S(1)}, bf16[2,4,32,1792]{3,2,1,0:T(8,128)(2,1)S(1)}, u32[]{:S(2)}, u32[]{:S(2)}) collective-permute-start(bf16[2,4,32,1792]{3,2,1,0:T(8,128)(2,1)S(1)} %get-tuple-element.202), channel_id=1, source_target_pairs={{0,1},{1,0},{2,3},{3,2},{4,5},{5,4},{6,7},{7,6},{8,9},{9,8},{10,11... | collective-permute-start | bytes 2752520 | tf_op jit(solution)/shard_map/ppermute | solution.py:344
  73.8 19.6 %collective-permute-start.15 = (bf16[4,16,1024]{2,1,0:T(8,128)(2,1)S(1)}, bf16[4,16,1024]{2,1,0:T(8,128)(2,1)S(1)}, u32[]{:S(2)}, u32[]{:S(2)}) collective-permute-start(bf16[4,16,1024]{2,1,0:T(8,128)(2,1)S(1)} %get-tuple-element.219), channel_id=1, source_target_pairs={{0,5},{1,4},{2,7},{3,6},{4,1},{5,0},{6,3},{7,2},{8,13},{9,12},{10,... | collective-permute-start | bytes 393224 | tf_op jit(solution)/shard_map/ppermute | solution.py:344
  80.9 12.5 %collective-permute-start.16 = (bf16[4,16,1024]{2,1,0:T(8,128)(2,1)S(1)}, bf16[4,16,1024]{2,1,0:T(8,128)(2,1)S(1)}, u32[]{:S(2)}, u32[]{:S(2)}) collective-permute-start(bf16[4,16,1024]{2,1,0:T(8,128)(2,1)S(1)} %get-tuple-element.220), channel_id=1, source_target_pairs={{0,6},{1,7},{2,4},{3,5},{4,2},{5,3},{6,0},{7,1},{8,14},{9,15},{10,... | collective-permute-start | bytes 393224 | tf_op jit(solution)/shard_map/ppermute | solution.py:344
  81.9 11.6 %collective-permute-start.17 = (bf16[4,16,1024]{2,1,0:T(8,128)(2,1)S(1)}, bf16[4,16,1024]{2,1,0:T(8,128)(2,1)S(1)}, u32[]{:S(2)}, u32[]{:S(2)}) collective-permute-start(bf16[4,16,1024]{2,1,0:T(8,128)(2,1)S(1)} %get-tuple-element.221), channel_id=1, source_target_pairs={{0,7},{1,6},{2,5},{3,4},{4,3},{5,2},{6,1},{7,0},{8,15},{9,14},{10,... | collective-permute-start | bytes 393224 | tf_op jit(solution)/shard_map/ppermute | solution.py:344
  99.2 14.4 %collective-permute-start.18 = (bf16[4,32,2304]{2,1,0:T(8,128)(2,1)S(1)}, bf16[4,32,2304]{2,1,0:T(8,128)(2,1)S(1)}, u32[]{:S(2)}, u32[]{:S(2)}) collective-permute-start(bf16[4,32,2304]{2,1,0:T(8,128)(2,1)S(1)} %get-tuple-element.224), channel_id=1, source_target_pairs={{0,1},{1,0},{2,3},{3,2},{4,5},{5,4},{6,7},{7,6},{8,9},{9,8},{10,11... | collective-permute-start | bytes 1769480 | tf_op jit(solution)/shard_map/ppermute | solution.py:344
  100.9 12.7 %collective-permute-start.19 = (bf16[4,32,1792]{2,1,0:T(8,128)(2,1)S(1)}, bf16[4,32,1792]{2,1,0:T(8,128)(2,1)S(1)}, u32[]{:S(2)}, u32[]{:S(2)}) collective-permute-start(bf16[4,32,1792]{2,1,0:T(8,128)(2,1)S(1)} %get-tuple-element.227), channel_id=1, source_target_pairs={{0,16},{8,24},{16,0},{24,8},{1,17},{9,25},{17,1},{25,9},{2,18},{10... | collective-permute-start | bytes 1376264 | tf_op jit(solution)/shard_map/ppermute | solution.py:344
  101.5 9.1 %collective-permute-start.20 = (bf16[4,16,1024]{2,1,0:T(8,128)(2,1)S(1)}, bf16[4,16,1024]{2,1,0:T(8,128)(2,1)S(1)}, u32[]{:S(2)}, u32[]{:S(2)}) collective-permute-start(bf16[4,16,1024]{2,1,0:T(8,128)(2,1)S(1)} %get-tuple-element.229), channel_id=1, source_target_pairs={{0,2},{1,3},{2,0},{3,1},{4,6},{5,7},{6,4},{7,5},{8,10},{9,11},{10,... | collective-permute-start | bytes 393224 | tf_op jit(solution)/shard_map/ppermute | solution.py:344
  114.3 8.5 %collective-permute-start.22 = (bf16[4,16,1024]{2,1,0:T(8,128)(2,1)S(1)}, bf16[4,16,1024]{2,1,0:T(8,128)(2,1)S(1)}, u32[]{:S(2)}, u32[]{:S(2)}) collective-permute-start(bf16[4,16,1024]{2,1,0:T(8,128)(2,1)S(1)} %get-tuple-element.238), channel_id=1, source_target_pairs={{0,1},{1,0},{2,3},{3,2},{4,5},{5,4},{6,7},{7,6},{8,9},{9,8},{10,11... | collective-permute-start | bytes 393224 | tf_op jit(solution)/shard_map/ppermute | solution.py:344
  115.2 29.2 %collective-permute-start.25 = (bf16[32,4096]{1,0:T(8,128)(2,1)S(1)}, bf16[32,4096]{1,0:T(8,128)(2,1)S(1)}, u32[]{:S(2)}, u32[]{:S(2)}) collective-permute-start(bf16[32,4096]{1,0:T(8,128)(2,1)S(1)} %get-tuple-element.236), channel_id=1, source_target_pairs={{0,4},{1,5},{2,6},{3,7},{4,0},{5,1},{6,2},{7,3},{8,12},{9,13},{10,... | collective-permute-start | bytes 786440 | tf_op jit(solution)/shard_map/ppermute | solution.py:344
  122.8 21.6 %collective-permute-start.24 = (bf16[32,4096]{1,0:T(8,128)(2,1)S(1)}, bf16[32,4096]{1,0:T(8,128)(2,1)S(1)}, u32[]{:S(2)}, u32[]{:S(2)}) collective-permute-start(bf16[32,4096]{1,0:T(8,128)(2,1)S(1)} %get-tuple-element.237), channel_id=1, source_target_pairs={{0,6},{1,7},{2,4},{3,5},{4,2},{5,3},{6,0},{7,1},{8,14},{9,15},{10,... | collective-permute-start | bytes 786440 | tf_op jit(solution)/shard_map/ppermute | solution.py:344
  122.8 21.6 %collective-permute-start.26 = (bf16[32,4096]{1,0:T(8,128)(2,1)S(1)}, bf16[32,4096]{1,0:T(8,128)(2,1)S(1)}, u32[]{:S(2)}, u32[]{:S(2)}) collective-permute-start(bf16[32,4096]{1,0:T(8,128)(2,1)S(1)} %get-tuple-element.242), channel_id=1, source_target_pairs={{0,2},{1,3},{2,0},{3,1},{4,6},{5,7},{6,4},{7,5},{8,10},{9,11},{10,... | collective-permute-start | bytes 786440 | tf_op jit(solution)/shard_map/ppermute | solution.py:344
  124.4 18.5 %collective-permute-start.23 = (bf16[4,16,1024]{2,1,0:T(8,128)(2,1)S(1)}, bf16[4,16,1024]{2,1,0:T(8,128)(2,1)S(1)}, u32[]{:S(2)}, u32[]{:S(2)}) collective-permute-start(bf16[4,16,1024]{2,1,0:T(8,128)(2,1)S(1)} %get-tuple-element.240), channel_id=1, source_target_pairs={{0,3},{1,2},{2,1},{3,0},{4,7},{5,6},{6,5},{7,4},{8,11},{9,10},{10,... | collective-permute-start | bytes 393224 | tf_op jit(solution)/shard_map/ppermute | solution.py:344
  (6 other events, 39.4 us)
